TPU v7x, 32 devices: a whole 2x2x4 slice. The times are simulated.
32 devices in a mesh: dp: 32 (over z, y, x, core).
Axes of the slice: x: 2, y: 2, z: 4, core: 2. Of those that a mesh axis runs over, the one named last changes fastest.
Arguments:
- tokens: bfloat16 [8192, 2560], P('dp'), may hold values from -6 to 6
- doc_positions: int32 [8192], P('dp'), may hold values from 0 to 255, as said below
- attn_gain: bfloat16 [2560], P('dp'), may hold values from 0.099609375 to 1.8984375
- q_weight: bfloat16 [2560, 2560], P('dp'), may hold values from -0.125 to 0.125
- kv_weight: bfloat16 [2560, 512], P('dp'), may hold values from -0.125 to 0.125
- out_weight: bfloat16 [2560, 2560], P('dp'), may hold values from -0.5 to 0.5
- ffn_gain: bfloat16 [2560], P('dp'), may hold values from 0.099609375 to 1.8984375
- gate_weight: bfloat16 [7680, 2560], P('dp'), may hold values from -0.125 to 0.125
- gate_bias: bfloat16 [7680], P('dp'), may hold values from -3 to 3
- up_weight: bfloat16 [7680, 2560], P('dp'), may hold values from -0.125 to 0.125
- up_bias: bfloat16 [7680], P('dp'), may hold values from -3 to 3
- down_weight: bfloat16 [7680, 2560], P('dp'), may hold values from -0.0625 to 0.0625
- down_bias: bfloat16 [2560], P('dp'), may hold values from -3 to 3
- cotangent: bfloat16 [8192, 2560], P('dp'), may hold values from -6 to 6
Outputs:
- output: bfloat16 [8192, 2560], P('dp')
- input_grad: bfloat16 [8192, 2560], P('dp')
- attn_gain_grad: float32 [2560], P('dp')
- q_grad: float32 [2560, 2560], P('dp')
- kv_grad: float32 [2560, 512], P('dp')
- out_grad: float32 [2560, 2560], P('dp')
- ffn_gain_grad: float32 [2560], P('dp')
- gate_grad: float32 [7680, 2560], P('dp')
- gate_bias_grad: float32 [7680], P('dp')
- up_grad: float32 [7680, 2560], P('dp')
- up_bias_grad: float32 [7680], P('dp')
- down_grad: float32 [7680, 2560], P('dp')
- down_bias_grad: float32 [2560], P('dp')
Inputs may be any that keep to these rules, and one draw needn't show every extreme that they name: doc_positions[t] is token t's index within its document; documents lie within one sequence of 256 tokens and a token's position is 0 or one more than the previous token's; in one sequence of every draw a single document fills the whole sequence.
All inputs are finite; a program needn't handle non-finite values.
Results may differ from a plain program's by a relative error of at most 0.014.
Values may be sent and summed in bfloat16 or wider, within the bound.
No kernel may reach another device: no remote copies, remote signals or barrier semaphores. Data moves between devices by JAX's collectives and lax.ppermute only.
A program may use at most 832 MiB of HBM per device.

v0:
```python
import jax
import jax.numpy as jnp
from jax import lax
from jax.sharding import PartitionSpec as P

D = 2560
H = 10
HD = 256
LENGTH = 256


epsilon = 1e-06


def rms_scale(values, gain):
    return values * lax.rsqrt(jnp.mean(values * values, axis=-1, keepdims=True) + epsilon) * gain


def angles(positions):
    quarter = HD // 4
    ladder = jnp.arange(quarter, dtype=jnp.float32)
    freq = 10000.0 ** (-2.0 * ladder / (HD // 2))
    angle = positions.astype(jnp.float32)[:, None] * freq[None, :]
    return (jnp.cos(angle), jnp.sin(angle))


def rotate(values, cosine, sine):
    quarter = cosine.shape[-1]
    first = values[..., :quarter]
    second = values[..., quarter : 2 * quarter]
    rest = values[..., 2 * quarter :]
    return jnp.concatenate(
        [first * cosine - second * sine, second * cosine + first * sine, rest], -1
    )


def contract_rows(left, right):
    return lax.dot_general(
        left, right, (((0,), (0,)), ((), ())), preferred_element_type=jnp.float32
    )


def times_transposed(left, right):
    return lax.dot_general(
        left, right, (((1,), (1,)), ((), ())), preferred_element_type=jnp.float32
    )


def glu_tanh(gate, up):
    return jax.nn.gelu(gate, approximate=True) * up


def attention_scores(query_block_rows, key_block_rows, allowed):
    logit_matrix = jnp.einsum(
        "ropc,rvc->rpov", query_block_rows, key_block_rows, preferred_element_type=jnp.float32
    )
    return jnp.where(allowed[:, None], logit_matrix, -1e30)


def body(
    tokens,
    doc_positions,
    attn_gain,
    q_weight,
    kv_weight,
    out_weight,
    ffn_gain,
    gate_weight,
    gate_bias,
    up_weight,
    up_bias,
    down_weight,
    down_bias,
    cotangent,
):
    widened_window = jnp.float32
    narrow = jnp.bfloat16
    tok_rows = tokens.shape[0]
    seq_count = tok_rows // LENGTH
    head_scale = HD ** (-0.5)
    gathered = (
        lax.all_gather(attn_gain, "dp", axis=0, tiled=True),
        lax.all_gather(ffn_gain, "dp", axis=0, tiled=True),
        lax.all_gather(down_bias, "dp", axis=0, tiled=True),
        lax.all_gather(q_weight, "dp", axis=0, tiled=True),
        lax.all_gather(kv_weight, "dp", axis=0, tiled=True),
        lax.all_gather(out_weight, "dp", axis=0, tiled=True),
    )
    gain_one = gathered[0].astype(widened_window)
    gain_two = gathered[1].astype(widened_window)
    bias_down = gathered[2].astype(widened_window)
    w_query, w_keyval, w_out = (gathered[3], gathered[4], gathered[5])
    x_value = tokens.astype(widened_window)
    norm_one_b = rms_scale(x_value, gain_one).astype(narrow)
    cosine, sine = angles(doc_positions)
    q_lin = jnp.dot(norm_one_b, w_query, preferred_element_type=widened_window).reshape(
        tok_rows, H, HD
    )
    kv_lin = jnp.dot(norm_one_b, w_keyval, preferred_element_type=widened_window)
    query_block_rows = (
        (rotate(q_lin, cosine[:, None, :], sine[:, None, :]) * head_scale)
        .astype(narrow)
        .reshape(seq_count, LENGTH, H, HD)
    )
    key_block_rows = (
        rotate(kv_lin[:, :HD], cosine, sine).astype(narrow).reshape(seq_count, LENGTH, HD)
    )
    value_block_rows = kv_lin[:, HD:].astype(narrow).reshape(seq_count, LENGTH, HD)
    index = jnp.arange(LENGTH)
    distance = index[:, None] - index[None, :]
    allowed = (distance[None] >= 0) & (
        distance[None] <= doc_positions.reshape(seq_count, LENGTH)[:, :, None]
    )
    logit_matrix = attention_scores(query_block_rows, key_block_rows, allowed)
    top = jnp.max(logit_matrix, axis=-1, keepdims=True)
    weights = jnp.exp(logit_matrix - top)
    total = jnp.sum(weights, axis=-1, keepdims=True)
    log_total = top + jnp.log(total)
    block_probabilities = (weights / total).astype(narrow)
    attended_b = (
        jnp.einsum(
            "fmtw,fwy->ftmy",
            block_probabilities,
            value_block_rows,
            preferred_element_type=widened_window,
        )
        .reshape(tok_rows, H * HD)
        .astype(narrow)
    )
    hidden_one = x_value + jnp.dot(attended_b, w_out, preferred_element_type=widened_window)
    norm_two_b = rms_scale(hidden_one, gain_two).astype(narrow)
    gate_piece = lax.all_gather(gate_weight, "dp", axis=0, tiled=True)
    up_piece = lax.all_gather(up_weight, "dp", axis=0, tiled=True)
    down_piece = lax.all_gather(down_weight, "dp", axis=0, tiled=True)
    gate_shift = lax.all_gather(gate_bias, "dp", axis=0, tiled=True)
    up_shift = lax.all_gather(up_bias, "dp", axis=0, tiled=True)
    gate_part = times_transposed(norm_two_b, gate_piece) + gate_shift.astype(widened_window)
    up_part = times_transposed(norm_two_b, up_piece) + up_shift.astype(widened_window)
    act_part = glu_tanh(gate_part, up_part).astype(narrow)
    summed = jnp.dot(act_part, down_piece, preferred_element_type=widened_window)
    ffn_gate_all = gate_part
    ffn_up_all = up_part
    branch_out = summed
    output = (hidden_one + branch_out + bias_down).astype(narrow)
    gate_piece = lax.all_gather(gate_weight, "dp", axis=0, tiled=True)
    up_piece = lax.all_gather(up_weight, "dp", axis=0, tiled=True)
    down_piece = lax.all_gather(down_weight, "dp", axis=0, tiled=True)
    gate_part = ffn_gate_all
    up_part = ffn_up_all
    grad_act = times_transposed(cotangent, down_piece)
    _, act_back = jax.vjp(glu_tanh, gate_part, up_part)
    grad_gate, grad_up = act_back(grad_act)
    grad_gate_part = grad_gate.astype(narrow)
    grad_up_part = grad_up.astype(narrow)
    summed = jnp.dot(grad_gate_part, gate_piece, preferred_element_type=widened_window) + jnp.dot(
        grad_up_part, up_piece, preferred_element_type=widened_window
    )
    grad_norm_two = summed
    _, norm_two_back = jax.vjp(rms_scale, hidden_one, gain_two)
    grad_rms_two, grad_gain_two = norm_two_back(grad_norm_two)
    grad_hidden = cotangent.astype(widened_window) + grad_rms_two
    grad_hidden_b = grad_hidden.astype(narrow)
    grad_w_out = contract_rows(attended_b, grad_hidden_b)
    attended_block_gradient = (
        times_transposed(grad_hidden_b, w_out).astype(narrow).reshape(seq_count, LENGTH, H, HD)
    )
    logit_matrix = attention_scores(query_block_rows, key_block_rows, allowed)
    soft = jnp.exp(logit_matrix - log_total)
    recomputed_probabilities = soft.astype(narrow)
    probability_gradient = jnp.einsum(
        "ropc,rvc->rpov",
        attended_block_gradient,
        value_block_rows,
        preferred_element_type=widened_window,
    )
    grad_value = jnp.einsum(
        "yexn,yxeg->yng",
        recomputed_probabilities,
        attended_block_gradient,
        preferred_element_type=widened_window,
    ).reshape(tok_rows, HD)
    score_block_gradient = (
        soft * (probability_gradient - jnp.sum(probability_gradient * soft, axis=-1, keepdims=True))
    ).astype(narrow)
    grad_query = jnp.einsum(
        "fmtw,fwy->ftmy",
        score_block_gradient,
        key_block_rows,
        preferred_element_type=widened_window,
    ).reshape(tok_rows, H, HD)
    grad_key = jnp.einsum(
        "yexn,yxeg->yng",
        score_block_gradient,
        query_block_rows,
        preferred_element_type=widened_window,
    ).reshape(tok_rows, HD)
    grad_kv_lin_b = jnp.concatenate([rotate(grad_key, cosine, -sine), grad_value], 1).astype(narrow)
    grad_q_lin_b = (
        rotate(grad_query * head_scale, cosine[:, None, :], -sine[:, None, :])
        .reshape(tok_rows, H * HD)
        .astype(narrow)
    )
    grad_w_query = contract_rows(norm_one_b, grad_q_lin_b)
    grad_w_keyval = contract_rows(norm_one_b, grad_kv_lin_b)
    grad_norm_one = times_transposed(grad_q_lin_b, w_query) + times_transposed(
        grad_kv_lin_b, w_keyval
    )
    _, norm_one_back = jax.vjp(rms_scale, x_value, gain_one)
    grad_rms_one, grad_gain_one = norm_one_back(grad_norm_one)
    input_grad = (grad_hidden + grad_rms_one).astype(narrow)
    unit_sums = lax.psum_scatter(
        jnp.concatenate(
            [
                contract_rows(grad_gate_part, norm_two_b),
                contract_rows(grad_up_part, norm_two_b),
                contract_rows(act_part, cotangent),
            ],
            1,
        ),
        "dp",
        scatter_dimension=0,
        tiled=True,
    )
    gate_grad = unit_sums[:, :D]
    up_grad = unit_sums[:, D : 2 * D]
    down_grad = unit_sums[:, 2 * D :]
    gate_bias_sum = jnp.sum(grad_gate_part, axis=0, dtype=widened_window)
    up_bias_sum = jnp.sum(grad_up_part, axis=0, dtype=widened_window)
    down_bias_sum = jnp.sum(cotangent, axis=0, dtype=widened_window)
    summed = (
        lax.psum_scatter(grad_w_query, "dp", scatter_dimension=0, tiled=True),
        lax.psum_scatter(grad_w_keyval, "dp", scatter_dimension=0, tiled=True),
        lax.psum_scatter(grad_w_out, "dp", scatter_dimension=0, tiled=True),
        lax.psum_scatter(grad_gain_one, "dp", scatter_dimension=0, tiled=True),
        lax.psum_scatter(grad_gain_two, "dp", scatter_dimension=0, tiled=True),
        lax.psum_scatter(down_bias_sum, "dp", scatter_dimension=0, tiled=True),
        lax.psum_scatter(gate_bias_sum, "dp", scatter_dimension=0, tiled=True),
        lax.psum_scatter(up_bias_sum, "dp", scatter_dimension=0, tiled=True),
    )
    return (
        output,
        input_grad,
        summed[3],
        summed[0],
        summed[1],
        summed[2],
        summed[4],
        gate_grad,
        summed[6],
        up_grad,
        summed[7],
        down_grad,
        summed[5],
    )


def solution(mesh):
    return jax.shard_map(
        body,
        mesh=mesh,
        in_specs=(
            P("dp", None),
            P("dp"),
            P("dp"),
            P("dp", None),
            P("dp", None),
            P("dp", None),
            P("dp"),
            P("dp", None),
            P("dp"),
            P("dp", None),
            P("dp"),
            P("dp", None),
            P("dp"),
            P("dp", None),
        ),
        out_specs=(
            P("dp", None),
            P("dp", None),
            P("dp"),
            P("dp", None),
            P("dp", None),
            P("dp", None),
            P("dp"),
            P("dp", None),
            P("dp"),
            P("dp", None),
            P("dp"),
            P("dp", None),
            P("dp"),
        ),
        check_vma=False,
    )
```

profile of v0, /device:TPU:0, one launch (start us, length us, event | category | flops | bytes accessed | tf_op | source)
XLA Modules:
  0.0 4059.7 jit_solution(7174769357263801829)
XLA Ops:
  12.6 43.4 %all-reduce.11 = (bf16[2560]{0:T(1024)(128)(2,1)S(1)}, bf16[2560]{0:T(1024)(128)(2,1)S(1)}, bf16[7680]{0:T(1024)(128)(2,1)S(1)}, bf16[7680]{0:T(1024)(128)(2,1)S(1)}, bf16[2560]{0:T(1024)(128)(2,1)}) all-reduce(bf16[2560]{0:T(1024)(128)(2,1)S(1)} %dynamic-update-slice, ...), channel_id=1, replica_groups=mesh['dp'=32] {'dp'}, use_global_device_ids=true, to_apply=%add | all-reduce | flops 23040 | bytes 92160
  57.7 13.9 all-gather.7.cloned.1.call-done
  71.6 2.6 fusion.83
  76.4 95.5 %all-gather.9.cloned.1.call-done = bf16[2560,2560]{1,0:T(8,128)(2,1)} async-done(((bf16[80,2560]{1,0:T(8,128)(2,1)}), bf16[2560,2560]{1,0:T(8,128)(2,1)}) %all-gather.9.cloned.1.call-update) | async-done | bytes 13107216 | tf_op jit(solution)/shard_map/all_gather | solution.py:85
  171.9 8.5 fusion.76
  180.5 1.5 copy-done.21
  183.5 2.3 multiply_subtract_fusion
  185.8 2.7 copy.103
  188.5 1.5 copy.104
  189.9 2.8 fusion.22
  195.2 76.3 %all-gather.11.cloned.1.call-done = bf16[2560,2560]{1,0:T(8,128)(2,1)} async-done(((bf16[80,2560]{1,0:T(8,128)(2,1)}), bf16[2560,2560]{1,0:T(8,128)(2,1)}) %all-gather.11.cloned.1.call-update) | async-done | bytes 13107216 | tf_op jit(solution)/shard_map/all_gather | solution.py:87
  271.5 6.9 multiply_reduce_fusion.2
  278.5 1.5 copy-done.6
  280.3 214.7 %all-gather.15.cloned.1.call-done = bf16[7680,2560]{1,0:T(8,128)(2,1)} async-done(((bf16[240,2560]{1,0:T(8,128)(2,1)}), bf16[7680,2560]{1,0:T(8,128)(2,1)}) %all-gather.15.cloned.1.call-update) | async-done | bytes 39321616 | tf_op jit(solution)/shard_map/all_gather | solution.py:133
  495.0 20.9 convolution_add_fusion
  516.0 202.5 %all-gather.13.cloned.1.call-done = bf16[7680,2560]{1,0:T(8,128)(2,1)} async-done(((bf16[240,2560]{1,0:T(8,128)(2,1)}), bf16[7680,2560]{1,0:T(8,128)(2,1)}) %all-gather.13.cloned.1.call-update) | async-done | bytes 39321616 | tf_op jit(solution)/shard_map/all_gather | solution.py:132
  718.5 20.5 convolution_add_fusion.1
  739.0 202.9 %all-gather.17.cloned.1.call-done = bf16[7680,2560]{1,0:T(8,128)(2,1)} async-done(((bf16[240,2560]{1,0:T(8,128)(2,1)}), bf16[7680,2560]{1,0:T(8,128)(2,1)}) %all-gather.17.cloned.1.call-update) | async-done | bytes 39321616 | tf_op jit(solution)/shard_map/all_gather | solution.py:134
  941.9 26.8 convert_reduce_fusion
  968.8 20.2 fusion.84
  989.0 21.1 multiply_reduce_fusion
  1010.1 3.8 convert_reduce_fusion.2
  1013.9 1.5 copy-done.5
  1015.4 9.5 convolution_convert_fusion
  1024.8 2.7 copy.107
  1027.6 2.1 fusion.36
  1032.7 1.7 convolution_bitcast_fusion
  1034.8 2.2 multiply_bitcast_fusion
  1037.0 29.1 fusion.87
  1066.1 29.2 fusion.86
  1095.2 1.5 slice.105
  1096.8 1.5 subtract_convert_fusion
  1098.3 29.2 fusion.88
  1127.6 7.5 fusion.85
  1135.2 3.4 fusion.12
  1138.7 156.8 %pad_maximum_fusion = f32[7680,7680]{0,1:T(8,128)} fusion(f32[7680,2560]{0,1:T(8,128)} %fusion.88, f32[7680,2560]{0,1:T(8,128)} %fusion.87, f32[7680,2560]{0,1:T(8,128)} %fusion.86), kind=kLoop, calls=%fused_computation | loop fusion | flops 117964800 | bytes 471859200 | tf_op jit(solution)/shard_map/concatenate | solution.py:212
  1295.4 227.2 %copy.128 = f32[7680,7680]{1,0:T(8,128)} copy(f32[7680,7680]{0,1:T(8,128)} %pad_maximum_fusion) | data formatting | bytes 471859200
  1524.0 4.0 fusion.61
  1529.3 19.0 fusion.39
  1548.4 1.6 copy-done.13
  1549.9 17.0 fusion.74
  1567.7 5.7 fusion.14
  1573.4 30.6 fusion.8
  1610.5 1732.0 %reduce-scatter.13.cloned.1.call-done = f32[240,7680]{1,0:T(8,128)} async-done(((f32[7680,7680]{1,0:T(8,128)}), f32[240,7680]{1,0:T(8,128)}) %reduce-scatter.13.cloned.1.call-update) | async-done | bytes 7372816
  3342.5 6.4 fusion.81
  3348.9 138.4 %reduce-scatter.9.cloned.1.call-done = f32[80,512]{1,0:T(8,128)} async-done(((f32[2560,512]{1,0:T(8,128)}), f32[80,512]{1,0:T(8,128)}) %reduce-scatter.9.cloned.1.call-update) | async-done | bytes 163856 | tf_op jit(solution)/shard_map/reduce_scatter | solution.py:232
  3487.3 277.3 %reduce-scatter.11.cloned.1.call-done = f32[80,2560]{1,0:T(8,128)} async-done(((f32[2560,2560]{1,0:T(8,128)}), f32[80,2560]{1,0:T(8,128)}) %reduce-scatter.11.cloned.1.call-update) | async-done | bytes 819216 | tf_op jit(solution)/shard_map/reduce_scatter | solution.py:233
  3764.6 288.1 %reduce-scatter.7.cloned.1.call-done = f32[80,2560]{1,0:T(8,128)} async-done(((f32[2560,2560]{1,0:T(8,128)}), f32[80,2560]{1,0:T(8,128)}) %reduce-scatter.7.cloned.1.call-update) | async-done | bytes 819216 | tf_op jit(solution)/shard_map/reduce_scatter | solution.py:231
  (181 shorter events, 26.6 us)
Async XLA Ops:
  7.2 4.1 copy-start.50
  7.2 4.1 copy-start.53
  7.2 4.4 copy-start.54
  7.2 4.6 copy-start.55
  7.2 4.9 copy-start.56
  7.2 5.1 copy-start.57
  7.2 50.1 %copy-start = (bf16[256,2560]{1,0:T(8,128)(2,1)S(1)}, bf16[256,2560]{1,0:T(8,128)(2,1)}, u32[]{:S(2)}) copy-start(bf16[256,2560]{1,0:T(8,128)(2,1)} %param.14) | copy-start | bytes 3932164
  7.3 64.4 %all-gather.7.cloned.1.call-start = ((), (), s32[]{:S(2)}) async-start(), calls=%async_computation.4 | async-start | bytes 2703360 | tf_op jit(solution)/shard_map/all_gather | solution.py:86
  8.0 164.0 %all-gather.9.cloned.1.call-start = ((), (), s32[]{:S(2)}) async-start(), calls=%async_computation.5 | async-start | bytes 13516800 | tf_op jit(solution)/shard_map/all_gather | solution.py:85
  8.7 262.8 %all-gather.11.cloned.1.call-start = ((), (), s32[]{:S(2)}) async-start(), calls=%async_computation.6 | async-start | bytes 13516800 | tf_op jit(solution)/shard_map/all_gather | solution.py:87
  9.5 485.5 %all-gather.15.cloned.1.call-start = ((), (), s32[]{:S(2)}) async-start(), calls=%async_computation.8 | async-start | bytes 40550400 | tf_op jit(solution)/shard_map/all_gather | solution.py:133
  10.0 708.4 %all-gather.13.cloned.1.call-start = ((), (), s32[]{:S(2)}) async-start(), calls=%async_computation.7 | async-start | bytes 40550400 | tf_op jit(solution)/shard_map/all_gather | solution.py:132
  10.6 931.3 %all-gather.17.cloned.1.call-start = ((), (), s32[]{:S(2)}) async-start(), calls=%async_computation.9 | async-start | bytes 40550400 | tf_op jit(solution)/shard_map/all_gather | solution.py:134
  11.2 1592.8 %all-reduce.14.cloned.1.call-start = ((), (), s32[]{:S(2)}) async-start(), calls=%async_computation.14 | async-start | bytes 204800
  11.3 63.3 %copy-start.44 = (f32[256]{0:T(256)}, f32[256]{0:T(256)S(1)}, u32[]{:S(2)}) copy-start(f32[256]{0:T(256)S(1)} %convert_element_type.98) | copy-start | bytes 3076
  56.0 115.9 %copy-start.23 = (f32[2560]{0:T(1024)}, f32[2560]{0:T(1024)S(1)}, u32[]{:S(2)}) copy-start(f32[2560]{0:T(1024)S(1)} %convert_element_type.96) | copy-start | bytes 30724
  57.3 17.3 copy-start.51
  57.6 16.6 copy-start.46
  57.7 114.3 %copy-start.39 = (f32[256]{0:T(256)}, f32[256]{0:T(256)S(1)}, u32[]{:S(2)}) copy-start(f32[256]{0:T(256)S(1)} %fusion.63) | copy-start | bytes 3076
  74.3 106.2 %copy-start.37 = (bf16[256,512]{1,0:T(8,128)(2,1)}, bf16[256,512]{1,0:T(8,128)(2,1)S(1)}, u32[]{:S(2)}) copy-start(bf16[256,512]{1,0:T(8,128)(2,1)S(1)} %get-tuple-element.106) | copy-start | bytes 786436
  75.6 107.9 %copy-start.28 = (f32[256,64]{0,1:T(8,128)}, f32[256,64]{0,1:T(8,128)S(1)}, u32[]{:S(2)}) copy-start(f32[256,64]{0,1:T(8,128)S(1)} %get-tuple-element.102) | copy-start | bytes 196612
  185.8 4.1 copy-start.15
  185.8 4.1 copy-start.30
  195.2 83.3 %copy-start.10 = (bf16[256,10,256]{2,0,1:T(8,128)(2,1)}, bf16[256,10,256]{2,0,1:T(8,128)(2,1)S(1)}, u32[]{:S(2)}) copy-start(bf16[256,10,256]{2,0,1:T(8,128)(2,1)S(1)} %convolution_convert_fusion.1) | copy-start | bytes 3932164
  278.5 216.5 %copy-start.43 = (f32[7680]{0:T(1024)S(1)}, f32[7680]{0:T(1024)}, u32[]{:S(2)}) copy-start(f32[7680]{0:T(1024)} %convert_element_type.108) | copy-start | bytes 92164
  280.3 438.2 %copy-start.8 = (bf16[256,2560]{1,0:T(8,128)(2,1)}, bf16[256,2560]{1,0:T(8,128)(2,1)S(1)}, u32[]{:S(2)}) copy-start(bf16[256,2560]{1,0:T(8,128)(2,1)S(1)} %multiply_convert_fusion.2) | copy-start | bytes 3932164
  280.3 438.2 %copy-start.42 = (f32[7680]{0:T(1024)S(1)}, f32[7680]{0:T(1024)}, u32[]{:S(2)}) copy-start(f32[7680]{0:T(1024)} %convert_element_type.107) | copy-start | bytes 92164
  516.0 426.0 %copy-start.19 = (bf16[256,2560]{1,0:T(8,128)(2,1)S(1)}, bf16[256,2560]{1,0:T(8,128)(2,1)}, u32[]{:S(2)}) copy-start(bf16[256,2560]{1,0:T(8,128)(2,1)} %param.27) | copy-start | bytes 3932164
  968.8 20.2 copy-start.7
  1024.8 2.7 copy-start.4
  1027.6 2.2 copy-start.14
  1029.7 105.4 %copy-start.31 = (bf16[256,256]{0,1:T(8,128)(2,1)}, bf16[256,256]{0,1:T(8,128)(2,1)S(1)}, u32[]{:S(2)}) copy-start(bf16[256,256]{0,1:T(8,128)(2,1)S(1)} %fusion.36) | copy-start | bytes 393220
  1030.6 2.1 copy-start.18
  1034.4 2.6 copy-start.9
  1034.4 100.7 %copy-start.26 = (bf16[256,128]{0,1:T(8,128)(2,1)}, bf16[256,128]{0,1:T(8,128)(2,1)S(1)}, u32[]{:S(2)}) copy-start(bf16[256,128]{0,1:T(8,128)(2,1)S(1)} %slice.106) | copy-start | bytes 196612
  1034.8 100.4 %copy-start.33 = (bf16[256,64]{0,1:T(8,128)(2,1)}, bf16[256,64]{0,1:T(8,128)(2,1)S(1)}, u32[]{:S(2)}) copy-start(bf16[256,64]{0,1:T(8,128)(2,1)S(1)} %get-tuple-element.97) | copy-start | bytes 98308
  1034.8 100.4 %copy-start.35 = (bf16[256,64]{0,1:T(8,128)(2,1)}, bf16[256,64]{0,1:T(8,128)(2,1)S(1)}, u32[]{:S(2)}) copy-start(bf16[256,64]{0,1:T(8,128)(2,1)S(1)} %get-tuple-element.98) | copy-start | bytes 98308
  1066.1 30.7 copy-start.29
  1095.2 3.0 copy-start.20
  1127.5 7.6 copy-start.12
  1127.5 7.6 copy-start.1
  1127.6 7.6 copy-start.22
  1127.6 7.6 copy-start.24
  1127.6 7.6 copy-start.40
  1138.6 2203.9 %reduce-scatter.13.cloned.1.call-start = ((), (), s32[]{:S(2)}) async-start(), calls=%async_computation.13 | async-start | bytes 243302400
  1522.7 1964.6 %reduce-scatter.9.cloned.1.call-start = ((), (), s32[]{:S(2)}) async-start(), calls=%async_computation.11 | async-start | bytes 5406720 | tf_op jit(solution)/shard_map/reduce_scatter | solution.py:232
  1528.0 2236.6 %reduce-scatter.11.cloned.1.call-start = ((), (), s32[]{:S(2)}) async-start(), calls=%async_computation.12 | async-start | bytes 27033600 | tf_op jit(solution)/shard_map/reduce_scatter | solution.py:233
  1548.3 2504.4 %reduce-scatter.7.cloned.1.call-start = ((), (), s32[]{:S(2)}) async-start(), calls=%async_computation.10 | async-start | bytes 27033600 | tf_op jit(solution)/shard_map/reduce_scatter | solution.py:231
  (21 other events, 28.3 us)
Sparse Core Ops, SparseCore 0:
  10.9 60.6 all-gather.6
  74.5 97.3 all-gather.8
  174.8 96.6 all-gather.10
  274.3 220.6 all-gather.14
  497.8 220.6 all-gather.12
  721.2 220.6 all-gather.16
  1138.7 120.9 all-reduce.13
  1522.8 1819.6 reduce-scatter.12
  3345.4 141.8 reduce-scatter.8
  3490.0 274.5 reduce-scatter.10
  3767.5 285.2 reduce-scatter.6
where the time goes:
time: 4080 us; the launch traced here: 4060 us
  waiting for transfers between devices  3250 us (80%)
  matrix products  317 us (8%)
  local copies, waits for them, and re-layouts  264 us (6%)
  other arithmetic  174 us (4%)
  blocking collectives  43.4 us (1%)
    unnamed x13, waiting for transfers between devices  1740 us
    reduce_scatter x1, waiting for transfers between devices, body(): lax.psum_scatter(grad_w_query, 'dp', scatter_dimension=0, tiled=True)  288 us
    reduce_scatter x1, waiting for transfers between devices, body(): lax.psum_scatter(grad_w_out, 'dp', scatter_dimension=0, tiled=True)  277 us
    unnamed x135, local copies, waits for them, and re-layouts  248 us
    all_gather x1, waiting for transfers between devices, body(): up_piece = lax.all_gather(up_weight, 'dp', axis=0, tiled=True)  215 us
    all_gather x1, waiting for transfers between devices, body(): down_piece = lax.all_gather(down_weight, 'dp', axis=0, tiled=True)  203 us
    all_gather x1, waiting for transfers between devices, body(): gate_piece = lax.all_gather(gate_weight, 'dp', axis=0, tiled=True)  203 us
    concatenate x1, other arithmetic, body(): jnp.concatenate([contract_rows(grad_gate_part, norm_two_b), contract_rows...  157 us
  transfers between devices with their start and end apart: 11, of which 10 were waited for; matrix products, arithmetic and copies ran while one was open for 14% of the time, Pallas kernels for 0%

commit v1 on v0

v1 whole, which is shorter than its diff:
```python
import jax
import jax.numpy as jnp
from jax import lax
from jax.sharding import PartitionSpec as P

D = 2560
H = 10
HD = 256
LENGTH = 256
F32 = jnp.float32
BF = jnp.bfloat16
EPS = 1e-06


def rms_scale(values, gain):
    return values * lax.rsqrt(jnp.mean(values * values, axis=-1, keepdims=True) + EPS) * gain


def angles(positions):
    quarter = HD // 4
    ladder = jnp.arange(quarter, dtype=F32)
    freq = 10000.0 ** (-2.0 * ladder / (HD // 2))
    angle = positions.astype(F32)[:, None] * freq[None, :]
    return (jnp.cos(angle), jnp.sin(angle))


def rotate(values, cosine, sine):
    quarter = cosine.shape[-1]
    first = values[..., :quarter]
    second = values[..., quarter : 2 * quarter]
    rest = values[..., 2 * quarter :]
    return jnp.concatenate(
        [first * cosine - second * sine, second * cosine + first * sine, rest], -1
    )


def dot_tn(left, right, out=F32):
    return lax.dot_general(
        left, right, (((0,), (0,)), ((), ())), preferred_element_type=F32
    ).astype(out)


def dot_nt(left, right):
    return lax.dot_general(left, right, (((1,), (1,)), ((), ())), preferred_element_type=F32)


def dot_nn(left, right):
    return jnp.dot(left, right, preferred_element_type=F32)


def glu_tanh(gate, up):
    return jax.nn.gelu(gate, approximate=True) * up


class Moves:
    def __init__(self, n):
        self.n = n
        self.planes = n // 8
        me = lax.axis_index("dp")
        self.core = me % 2
        self.x = (me // 2) % 2
        self.y = (me // 4) % 2
        self.z = me // 8

    def flip(self, value, bit):
        return lax.ppermute(value, "dp", [(i, i ^ bit) for i in range(self.n)])

    def other(self, value):
        return self.flip(value, 1)

    def over_x(self, value):
        return self.flip(value, 2)

    def over_y(self, value):
        return self.flip(value, 4)

    def up(self, value, steps=1):
        return lax.ppermute(value, "dp", [(i, (i + 8 * steps) % self.n) for i in range(self.n)])


def plane_gather(mv, value):
    half = value.shape[0] // 2
    from_x = mv.over_x(value)
    from_y = mv.over_y(value)
    diag_a = mv.over_y(from_x[:half])
    diag_b = mv.over_x(from_y[half:])
    return value, from_x, from_y, diag_a, diag_b


def plane_scatter(mv, own, to_x, to_y, to_diag):
    half = own.shape[0] // 2
    diag_a = mv.over_x(to_diag[:half].astype(BF))
    diag_b = mv.over_y(to_diag[half:].astype(BF))
    x_a = mv.over_x(to_x[:half].astype(BF))
    y_b = mv.over_y(to_y[half:].astype(BF))
    x_b = mv.over_x((to_x[half:].astype(F32) + diag_b.astype(F32)).astype(BF))
    y_a = mv.over_y((to_y[:half].astype(F32) + diag_a.astype(F32)).astype(BF))
    got_x = jnp.concatenate([x_a, x_b], 0).astype(F32)
    got_y = jnp.concatenate([y_a, y_b], 0).astype(F32)
    return own.astype(F32) + got_x + got_y


def gather_rows(mv, value):
    rows, width = value.shape
    whole = jnp.zeros((mv.n * rows, width), value.dtype)
    half = rows // 2

    def place(whole, block, z, y, x, core, shift=0):
        index = ((z * 2 + y) * 2 + x) * 2 + core
        return lax.dynamic_update_slice(whole, block, (index * rows + shift, 0))

    piece = value
    for step in range(mv.planes):
        z = (mv.z - step) % mv.planes
        own, from_x, from_y, diag_a, diag_b = plane_gather(mv, piece)
        for block, y, x, shift in (
            (own, mv.y, mv.x, 0),
            (from_x, mv.y, 1 - mv.x, 0),
            (from_y, 1 - mv.y, mv.x, 0),
            (diag_a, 1 - mv.y, 1 - mv.x, 0),
            (diag_b, 1 - mv.y, 1 - mv.x, half),
        ):
            whole = place(whole, block, z, y, x, mv.core, shift)
            whole = place(whole, mv.other(block), z, y, x, 1 - mv.core, shift)
        if step < mv.planes - 1:
            piece = mv.up(piece)
    return whole


def gather_tokens(mv, value):
    pieces = []
    piece = value
    for step in range(mv.planes):
        pieces.append(jnp.concatenate([piece, mv.other(piece)], 0))
        if step < mv.planes - 1:
            piece = mv.up(piece)
    return pieces


class RingSum:
    def __init__(self, mv):
        self.mv = mv
        self.got = None
        self.given = 0

    def give(self, piece):
        rows = piece.shape[0] // 2
        total = piece[:rows] + self.mv.other(piece[rows:].astype(BF)).astype(F32)
        return self.add(total)

    def add(self, total):
        if self.got is not None:
            total = total + self.got.astype(F32)
        self.given += 1
        if self.given == self.mv.planes:
            return total
        self.got = self.mv.up(total.astype(BF))
        return None


def scatter_rows(mv, grads):
    width = grads.shape[1]
    rows = grads.shape[0] // mv.n
    blocks = grads.reshape(mv.planes, 2, 2, 2 * rows, width)

    def block(z, y, x):
        return lax.dynamic_slice(blocks, (z, y, x, 0, 0), (1, 1, 1, 2 * rows, width)).reshape(
            2 * rows, width
        )

    ring = RingSum(mv)
    total = None
    for step in range(1, mv.planes + 1):
        z = (mv.z - step) % mv.planes
        total = ring.add(
            plane_scatter(
                mv,
                block(z, mv.y, mv.x),
                block(z, mv.y, 1 - mv.x),
                block(z, 1 - mv.y, mv.x),
                block(z, 1 - mv.y, 1 - mv.x),
            )
        )
    mine = lax.dynamic_slice(total, (mv.core * rows, 0), (rows, width))
    theirs = mv.other(lax.dynamic_slice(total, ((1 - mv.core) * rows, 0), (rows, width)))
    first = jnp.where(mv.core == 0, mine, theirs)
    second = jnp.where(mv.core == 0, theirs, mine)
    return first, second


def scatter_small(mv, vectors):
    count = len(vectors)
    part = vectors[0].shape[0] // mv.n
    value = jnp.stack(vectors).reshape(count, mv.planes, 2, 2, 2, part)
    value = value.transpose(2, 3, 4, 1, 0, 5)

    def pick(value, at):
        return lax.dynamic_index_in_dim(value, at, 0, keepdims=False)

    value = pick(value, mv.y) + mv.over_y(pick(value, 1 - mv.y))
    value = pick(value, mv.x) + mv.over_x(pick(value, 1 - mv.x))
    value = pick(value, mv.core) + mv.other(pick(value, 1 - mv.core))
    total = pick(value, mv.z)
    for step in range(1, mv.planes):
        total = total + mv.up(pick(value, (mv.z + step) % mv.planes), step)
    return [total[i] for i in range(count)]


def core_half(mv, value):
    width = value.shape[1] // 2
    mine = jnp.where(mv.core == 0, value[:, :width], value[:, width:])
    theirs = jnp.where(mv.core == 0, value[:, width:], value[:, :width])
    return jnp.concatenate([mine, mv.other(theirs)], 0)


def make_body(n):
    def body(
        tokens,
        doc_positions,
        attn_gain,
        q_weight,
        kv_weight,
        out_weight,
        ffn_gain,
        gate_weight,
        gate_bias,
        up_weight,
        up_bias,
        down_weight,
        down_bias,
        cotangent,
    ):
        mv = Moves(n)
        head_scale = HD ** (-0.5)
        rows = tokens.shape[0]
        seqs = rows // LENGTH
        small = jnp.stack([attn_gain, ffn_gain, down_bias], 1)
        small = jnp.pad(small, ((0, 0), (0, 125)))
        w_qkv = gather_rows(mv, jnp.concatenate([q_weight, kv_weight, small], 1))
        w_query = w_qkv[:, :D]
        w_keyval = w_qkv[:, D : D + 2 * HD]
        small = w_qkv[:, D + 2 * HD :].T.astype(F32)
        gain_one, gain_two, bias_down = small[0], small[1], small[2]
        w_out = gather_rows(mv, out_weight)
        cot_pieces = gather_tokens(mv, cotangent)
        w_down = jnp.concatenate(plane_gather(mv, down_weight), 0)
        w_gate = jnp.concatenate(plane_gather(mv, gate_weight), 0)
        w_up = jnp.concatenate(plane_gather(mv, up_weight), 0)
        biases = jnp.stack([gate_bias, up_bias])
        bias_x = mv.over_x(biases)
        biases = jnp.concatenate(
            [biases, bias_x, mv.over_y(biases), mv.over_y(bias_x)], 1
        ).astype(F32)

        x_value = tokens.astype(F32)
        norm_one_b = rms_scale(x_value, gain_one).astype(BF)
        cosine, sine = angles(doc_positions)
        q_lin = dot_nn(norm_one_b, w_query).reshape(rows, H, HD)
        kv_lin = dot_nn(norm_one_b, w_keyval)
        query = (
            (rotate(q_lin, cosine[:, None, :], sine[:, None, :]) * head_scale)
            .astype(BF)
            .reshape(seqs, LENGTH, H, HD)
        )
        key = rotate(kv_lin[:, :HD], cosine, sine).astype(BF).reshape(seqs, LENGTH, HD)
        value = kv_lin[:, HD:].astype(BF).reshape(seqs, LENGTH, HD)
        index = jnp.arange(LENGTH)
        distance = index[:, None] - index[None, :]
        allowed = (distance[None] >= 0) & (
            distance[None] <= doc_positions.reshape(seqs, LENGTH)[:, :, None]
        )
        logits = jnp.einsum("sqhd,skd->shqk", query, key, preferred_element_type=F32)
        logits = jnp.where(allowed[:, None], logits, -1e30)
        top = jnp.max(logits, axis=-1, keepdims=True)
        weights = jnp.exp(logits - top)
        soft = weights / jnp.sum(weights, axis=-1, keepdims=True)
        probs = soft.astype(BF)
        attended = (
            jnp.einsum("shqk,skd->sqhd", probs, value, preferred_element_type=F32)
            .reshape(rows, H * HD)
            .astype(BF)
        )
        hidden_one = x_value + dot_nn(attended, w_out)
        norm_two_b = rms_scale(hidden_one, gain_two).astype(BF)

        norm_pieces = gather_tokens(mv, norm_two_b)
        out_ring, grad_ring = RingSum(mv), RingSum(mv)
        order = list(range(1, mv.planes)) + [0]
        acts, grad_gates, grad_ups = [], [], []
        for at in order:
            norm_piece, cot_piece = norm_pieces[at], cot_pieces[at]
            gate = dot_nt(norm_piece, w_gate) + biases[0]
            up = dot_nt(norm_piece, w_up) + biases[1]
            grad_act = dot_nt(cot_piece, w_down)
            act, act_back = jax.vjp(glu_tanh, gate, up)
            grad_gate, grad_up = act_back(grad_act)
            act, grad_gate, grad_up = act.astype(BF), grad_gate.astype(BF), grad_up.astype(BF)
            acts.append(act)
            grad_gates.append(grad_gate)
            grad_ups.append(grad_up)
            grad_norm_two = grad_ring.give(dot_nn(grad_gate, w_gate) + dot_nn(grad_up, w_up))
            branch = out_ring.give(dot_nn(act, w_down))
        output = (hidden_one + branch + bias_down).astype(BF)
        _, norm_two_back = jax.vjp(rms_scale, hidden_one, gain_two)
        grad_rms_two, grad_gain_two = norm_two_back(grad_norm_two)
        grad_hidden = cotangent.astype(F32) + grad_rms_two
        grad_hidden_b = grad_hidden.astype(BF)

        acts = jnp.concatenate(acts, 0)
        grad_gates = jnp.concatenate(grad_gates, 0)
        grad_ups = jnp.concatenate(grad_ups, 0)
        norm_all = jnp.concatenate([norm_pieces[i] for i in order], 0)
        cot_all = jnp.concatenate([cot_pieces[i] for i in order], 0)

        def unit_scatter(grads):
            count = grads.shape[0] // 4
            return plane_scatter(mv, *[grads[i * count : (i + 1) * count] for i in range(4)])

        down_grad = unit_scatter(dot_tn(acts, cot_all, BF))
        gate_grad = unit_scatter(dot_tn(grad_gates, norm_all, BF))
        up_grad = unit_scatter(dot_tn(grad_ups, norm_all, BF))
        bias_sums = jnp.stack(
            [jnp.sum(grad_gates, axis=0, dtype=F32), jnp.sum(grad_ups, axis=0, dtype=F32)]
        )
        units = bias_sums.shape[1] // 4
        moved = mv.over_x(
            jnp.concatenate([bias_sums[:, units : 2 * units], bias_sums[:, 3 * units :]], 1)
        )
        bias_sums = (
            bias_sums[:, :units]
            + moved[:, :units]
            + mv.over_y(bias_sums[:, 2 * units : 3 * units] + moved[:, units:])
        )

        attended_both = jnp.concatenate([attended, mv.other(attended)], 0)
        out_first, out_second = scatter_rows(
            mv, dot_tn(attended_both, core_half(mv, grad_hidden_b), BF)
        )
        out_grad = jnp.concatenate([out_first, out_second], 1)

        grad_attended = dot_nt(grad_hidden_b, w_out).astype(BF).reshape(seqs, LENGTH, H, HD)
        grad_probs = jnp.einsum(
            "sqhd,skd->shqk", grad_attended, value, preferred_element_type=F32
        )
        grad_value = jnp.einsum(
            "shqk,sqhd->skd", probs, grad_attended, preferred_element_type=F32
        ).reshape(rows, HD)
        grad_scores = (
            soft * (grad_probs - jnp.sum(grad_probs * soft, axis=-1, keepdims=True))
        ).astype(BF)
        grad_query = jnp.einsum(
            "shqk,skd->sqhd", grad_scores, key, preferred_element_type=F32
        ).reshape(rows, H, HD)
        grad_key = jnp.einsum(
            "shqk,sqhd->skd", grad_scores, query, preferred_element_type=F32
        ).reshape(rows, HD)
        grad_kv_lin = jnp.concatenate([rotate(grad_key, cosine, -sine), grad_value], 1).astype(BF)
        grad_q_lin = (
            rotate(grad_query * head_scale, cosine[:, None, :], -sine[:, None, :])
            .reshape(rows, H * HD)
            .astype(BF)
        )
        norm_both = jnp.concatenate([norm_one_b, mv.other(norm_one_b)], 0)
        lin_half = jnp.concatenate([core_half(mv, grad_q_lin), core_half(mv, grad_kv_lin)], 1)
        first, second = scatter_rows(mv, dot_tn(norm_both, lin_half, BF))
        q_grad = jnp.concatenate([first[:, : D // 2], second[:, : D // 2]], 1)
        kv_grad = jnp.concatenate([first[:, D // 2 :], second[:, D // 2 :]], 1)

        grad_norm_one = dot_nt(grad_q_lin, w_query) + dot_nt(grad_kv_lin, w_keyval)
        _, norm_one_back = jax.vjp(rms_scale, x_value, gain_one)
        grad_rms_one, grad_gain_one = norm_one_back(grad_norm_one)
        input_grad = (grad_hidden + grad_rms_one).astype(BF)
        down_bias_sum = jnp.sum(cotangent, axis=0, dtype=F32)
        attn_gain_grad, ffn_gain_grad, down_bias_grad = scatter_small(
            mv, [grad_gain_one, grad_gain_two, down_bias_sum]
        )
        return (
            output,
            input_grad,
            attn_gain_grad,
            q_grad,
            kv_grad,
            out_grad,
            ffn_gain_grad,
            gate_grad,
            bias_sums[0],
            up_grad,
            bias_sums[1],
            down_grad,
            down_bias_grad,
        )

    return body


def solution(mesh):
    matrix, vector = P("dp", None), P("dp")
    return jax.shard_map(
        make_body(mesh.shape["dp"]),
        mesh=mesh,
        in_specs=(
            matrix,
            vector,
            vector,
            matrix,
            matrix,
            matrix,
            vector,
            matrix,
            vector,
            matrix,
            vector,
            matrix,
            vector,
            matrix,
        ),
        out_specs=(
            matrix,
            matrix,
            vector,
            matrix,
            matrix,
            matrix,
            vector,
            matrix,
            vector,
            matrix,
            vector,
            matrix,
            vector,
        ),
        check_vma=False,
    )
```

time: 4080 us -> 1590 us (0.39)
  waiting for transfers between devices: 3250 us -> 448 us
  local copies, waits for them, and re-layouts: 264 us -> 656 us
  starting transfers between devices: 0.43 us -> 155 us
  other arithmetic: 174 us -> 53.5 us
  matrix products: 317 us -> 254 us
  blocking collectives: 43.4 us -> 0 us
    unnamed x13 -> x0, waiting for transfers between devices: 1740 us -> none
    all_gather x6 -> x0, waiting for transfers between devices: 806 us -> none  [the longest x1 215 us: body(): up_piece = lax.all_gather(up_weight, 'dp', axis=0, tiled=True)]
    reduce_scatter x3 -> x0, waiting for transfers between devices: 704 us -> none  [the longest x1 288 us: body(): lax.psum_scatter(grad_w_query, 'dp', scatter_dimension=0, tiled=True)]
    dynamic_update_slice x0 -> x80, local copies, waits for them, and re-layouts: none -> 460 us  [place(): return lax.dynamic_update_slice(whole, block, (index * rows + shift, 0))]
    ppermute x0 -> x208, waiting for transfers between devices: none -> 448 us  [the longest x27 240 us: up(): lax.ppermute(value, 'dp', [(i, (i + 8 * steps) % self.n) for i in range(s...]
    unnamed x135 -> x339, local copies, waits for them, and re-layouts: 248 us -> 51 us
    ppermute x0 -> x208, starting transfers between devices: none -> 155 us  [the longest x181 128 us: flip(): return lax.ppermute(value, 'dp', [(i, i ^ bit) for i in range(self.n)])]
    concatenate x1 -> x5, other arithmetic: 157 us -> 3.75 us  [the longest x1 1.09 us: body(): w_qkv = gather_rows(mv, jnp.concatenate([q_weight, kv_weight, small], 1))]
  transfers between devices with their start and end apart: 11 -> 208, of which waited for: 10 -> 67; matrix products, arithmetic and copies ran while one was open for 14% -> 54% of each run, Pallas kernels for 0% -> 0%
where the time goes in v1:
time: 1590 us; the launch traced here: 1570 us
  local copies, waits for them, and re-layouts  656 us (41%)
  waiting for transfers between devices  448 us (28%)
  matrix products  254 us (16%)
  starting transfers between devices  155 us (10%)
  other arithmetic  53.5 us (3%)
    dynamic_update_slice x80, local copies, waits for them, and re-layouts, place(): return lax.dynamic_update_slice(whole, block, (index * rows + shift, 0))  460 us
    ppermute x27, waiting for transfers between devices, up(): lax.ppermute(value, 'dp', [(i, (i + 8 * steps) % self.n) for i in range(s...  240 us
    ppermute x181, waiting for transfers between devices, flip(): return lax.ppermute(value, 'dp', [(i, i ^ bit) for i in range(self.n)])  208 us
    ppermute x181, starting transfers between devices, flip(): return lax.ppermute(value, 'dp', [(i, i ^ bit) for i in range(self.n)])  128 us
    dot_general x15, matrix products, dot_nt(): lax.dot_general(left, right, (((1,), (1,)), ((), ())), preferred_element_...  99.2 us
    dot_general x15, matrix products, dot_nn(): return jnp.dot(left, right, preferred_element_type=F32)  81.2 us
    dot_general x5, matrix products, dot_tn(): lax.dot_general(left, right, (((0,), (0,)), ((), ())), preferred_element_...  61 us
    ppermute x36, local copies, waits for them, and re-layouts, flip(): return lax.ppermute(value, 'dp', [(i, i ^ bit) for i in range(self.n)])  56.5 us
  transfers between devices with their start and end apart: 208, of which 67 were waited for; matrix products, arithmetic and copies ran while one was open for 54% of the time, Pallas kernels for 0%

profile of v1, /device:TPU:0, one launch (start us, length us, event | category | flops | bytes accessed | tf_op | source)
XLA Modules:
  0.0 1570.0 jit_solution(4314526839935722294)
XLA Ops:
  65.3 10.2 dynamic_update_slice.241
  117.7 29.7 %collective-permute-done.11 = bf16[80,3200]{1,0:T(8,128)(2,1)} collective-permute-done((bf16[80,3200]{1,0:T(8,128)(2,1)}, bf16[80,3200]{1,0:T(8,128)(2,1)}, u32[]{:S(2)}, u32[]{:S(2)}) %collective-permute-start.11) | collective-permute-done | bytes 512032 | tf_op jit(solution)/shard_map/ppermute | solution.py:66
  157.9 10.7 dynamic_update_slice.243
  202.1 10.2 dynamic_update_slice.247
  212.4 10.3 dynamic_update_slice.248
  224.0 10.2 dynamic_update_slice.249
  243.6 10.2 dynamic_update_slice.251
  255.3 10.2 dynamic_update_slice.252
  289.9 16.8 %collective-permute-done.54 = bf16[40,2560]{1,0:T(8,128)(2,1)S(1)} collective-permute-done((bf16[40,2560]{1,0:T(8,128)(2,1)S(1)}, bf16[40,2560]{1,0:T(8,128)(2,1)S(1)}, u32[]{:S(2)}, u32[]{:S(2)}) %collective-permute-start.54) | collective-permute-done | bytes 204832 | tf_op jit(solution)/shard_map/ppermute | solution.py:66
  374.3 10.7 dynamic_update_slice.253
  385.0 10.7 dynamic_update_slice.254
  397.9 10.7 dynamic_update_slice.255
  408.6 10.7 dynamic_update_slice.256
  465.9 10.2 dynamic_update_slice.261
  480.0 10.4 dynamic_update_slice.262
  597.8 10.7 dynamic_update_slice.263
  608.5 10.8 dynamic_update_slice.264
  620.5 10.8 dynamic_update_slice.265
  631.3 10.8 dynamic_update_slice.266
  643.4 10.7 dynamic_update_slice.267
  654.1 10.7 dynamic_update_slice.268
  666.0 10.7 dynamic_update_slice.269
  687.1 10.6 dynamic_update_slice.271
  699.2 10.2 dynamic_update_slice.272
  720.2 10.7 dynamic_update_slice.273
  742.3 10.8 dynamic_update_slice.275
  753.2 10.7 dynamic_update_slice.276
  765.1 10.7 dynamic_update_slice.277
  775.8 10.2 dynamic_update_slice.278
  788.3 10.7 dynamic_update_slice.279
  854.7 21.4 %collective-permute-done.95 = bf16[256,2560]{1,0:T(8,128)(2,1)S(1)} collective-permute-done((bf16[256,2560]{1,0:T(8,128)(2,1)S(1)}, bf16[256,2560]{1,0:T(8,128)(2,1)S(1)}, u32[]{:S(2)}, u32[]{:S(2)}) %collective-permute-start.95) | collective-permute-done | bytes 1310752 | tf_op jit(solution)/shard_map/ppermute | solution.py:78
  889.6 14.6 collective-permute-done.111
  915.5 16.1 %collective-permute-done.96 = bf16[256,2560]{1,0:T(8,128)(2,1)S(1)} collective-permute-done((bf16[256,2560]{1,0:T(8,128)(2,1)S(1)}, bf16[256,2560]{1,0:T(8,128)(2,1)S(1)}, u32[]{:S(2)}, u32[]{:S(2)}) %collective-permute-start.96) | collective-permute-done | bytes 1310752 | tf_op jit(solution)/shard_map/ppermute | solution.py:78
  942.8 21.9 %collective-permute-done.97 = bf16[256,2560]{1,0:T(8,128)(2,1)S(1)} collective-permute-done((bf16[256,2560]{1,0:T(8,128)(2,1)S(1)}, bf16[256,2560]{1,0:T(8,128)(2,1)S(1)}, u32[]{:S(2)}, u32[]{:S(2)}) %collective-permute-start.97) | collective-permute-done | bytes 1310752 | tf_op jit(solution)/shard_map/ppermute | solution.py:78
  992.0 16.2 %fusion.76 = (bf16[512,960]{0,1:T(8,128)(2,1)}, bf16[512,960]{0,1:T(8,128)(2,1)}, bf16[512,960]{0,1:T(8,128)(2,1)}, bf16[512,960]{0,1:T(8,128)(2,1)}, bf16[512,9...) fusion(f32[512,960]{0,1:T(8,128)} %fusion.38, ...), kind=kOutput, calls=%fused_computation.135 | convolution fusion | flops 2576875520 | bytes 40967680 | tf_op jit(solution)/shard_map/dot_general | solution.py:44
  1008.2 16.7 %convolution_convert_fusion.3 = bf16[960,2560]{1,0:T(8,128)(2,1)} fusion(bf16[2048,2560]{1,0:T(8,128)(2,1)} %constant_dynamic-update-slice_fusion.24, bf16[512,960]{0,1:T(8,128)(2,1)} %get-tuple-element.96, bf16[512,960]{0,1:T(8,128)(2,1)} %get-tuple-element.146, bf16[512,960]{0,1:T(8,128)(2,1)} %get-tuple-element.143, bf16[512,960]{0,1:T(8,128)(2,1)} %get-tuple-element.140), kind=kOutput, calls=%fused_computation.9 | convolution fusion | flops 10084515840 | bytes 19333120 | tf_op jit(solution)/shard_map/dot_general | solution.py:38
  1029.0 14.6 convolution_convert_fusion.4
  1070.3 15.2 convolution_convert_fusion.2
  1179.1 13.6 collective-permute-done.204
  1198.0 13.5 collective-permute-done.118
  1215.5 23.1 %collective-permute-done.104 = bf16[256,2560]{1,0:T(8,128)(2,1)S(1)} collective-permute-done((bf16[256,2560]{1,0:T(8,128)(2,1)S(1)}, bf16[256,2560]{1,0:T(8,128)(2,1)S(1)}, u32[]{:S(2)}, u32[]{:S(2)}) %collective-permute-start.104) | collective-permute-done | bytes 1310752 | tf_op jit(solution)/shard_map/ppermute | solution.py:78
  1245.4 26.8 %collective-permute-done.119 = bf16[256,2560]{1,0:T(8,128)(2,1)S(1)} collective-permute-done((bf16[256,2560]{1,0:T(8,128)(2,1)S(1)}, bf16[256,2560]{1,0:T(8,128)(2,1)S(1)}, u32[]{:S(2)}, u32[]{:S(2)}) %collective-permute-start.119) | collective-permute-done | bytes 1310752 | tf_op jit(solution)/shard_map/ppermute | solution.py:78
  1274.9 23.5 %collective-permute-done.105 = bf16[256,2560]{1,0:T(8,128)(2,1)S(1)} collective-permute-done((bf16[256,2560]{1,0:T(8,128)(2,1)S(1)}, bf16[256,2560]{1,0:T(8,128)(2,1)S(1)}, u32[]{:S(2)}, u32[]{:S(2)}) %collective-permute-start.105) | collective-permute-done | bytes 1310752 | tf_op jit(solution)/shard_map/ppermute | solution.py:78
  1303.0 28.9 %collective-permute-done.120 = bf16[256,2560]{1,0:T(8,128)(2,1)S(1)} collective-permute-done((bf16[256,2560]{1,0:T(8,128)(2,1)S(1)}, bf16[256,2560]{1,0:T(8,128)(2,1)S(1)}, u32[]{:S(2)}, u32[]{:S(2)}) %collective-permute-start.120) | collective-permute-done | bytes 1310752 | tf_op jit(solution)/shard_map/ppermute | solution.py:78
  1333.0 24.2 %collective-permute-done.106 = bf16[256,2560]{1,0:T(8,128)(2,1)S(1)} collective-permute-done((bf16[256,2560]{1,0:T(8,128)(2,1)S(1)}, bf16[256,2560]{1,0:T(8,128)(2,1)S(1)}, u32[]{:S(2)}, u32[]{:S(2)}) %collective-permute-start.106) | collective-permute-done | bytes 1310752 | tf_op jit(solution)/shard_map/ppermute | solution.py:78
  1394.2 10.5 fusion.17
  1444.0 10.9 collective-permute-done.179
  1555.3 10.2 collective-permute-done.156
  (1019 shorter events, 901.9 us)
Async XLA Ops:
  0.6 44.9 %collective-permute-start.39 = (bf16[80,2560]{1,0:T(8,128)(2,1)}, bf16[80,2560]{1,0:T(8,128)(2,1)}, u32[]{:S(2)}, u32[]{:S(2)}) collective-permute-start(bf16[80,2560]{1,0:T(8,128)(2,1)} %param.19), channel_id=1, source_target_pairs={{0,1},{1,0},{2,3},{3,2},{4,5},{5,4},{6,7},{7,6},{8,9},{9,8},{10,11... | collective-permute-start | bytes 1228808 | tf_op jit(solution)/shard_map/ppermute | solution.py:66
  1.2 47.9 %collective-permute-start.40 = (bf16[80,2560]{1,0:T(8,128)(2,1)}, bf16[80,2560]{1,0:T(8,128)(2,1)}, u32[]{:S(2)}, u32[]{:S(2)}) collective-permute-start(bf16[80,2560]{1,0:T(8,128)(2,1)} %param.19), channel_id=1, source_target_pairs={{0,2},{1,3},{2,0},{3,1},{4,6},{5,7},{6,4},{7,5},{8,10},{9,11},{10,... | collective-permute-start | bytes 1228808 | tf_op jit(solution)/shard_map/ppermute | solution.py:66
  3.7 46.9 %collective-permute-start.42 = (bf16[80,2560]{1,0:T(8,128)(2,1)}, bf16[80,2560]{1,0:T(8,128)(2,1)}, u32[]{:S(2)}, u32[]{:S(2)}) collective-permute-start(bf16[80,2560]{1,0:T(8,128)(2,1)} %param.19), channel_id=1, source_target_pairs={{0,4},{1,5},{2,6},{3,7},{4,0},{5,1},{6,2},{7,3},{8,12},{9,13},{10,... | collective-permute-start | bytes 1228808 | tf_op jit(solution)/shard_map/ppermute | solution.py:66
  7.2 45.1 %collective-permute-start.1 = (bf16[80,3200]{1,0:T(8,128)(2,1)S(1)}, bf16[80,3200]{1,0:T(8,128)(2,1)S(1)}, u32[]{:S(2)}, u32[]{:S(2)}) collective-permute-start(bf16[80,3200]{1,0:T(8,128)(2,1)S(1)} %fusion.142), channel_id=1, source_target_pairs={{0,2},{1,3},{2,0},{3,1},{4,6},{5,7},{6,4},{7,5},{8,10},{9,11},{10,... | collective-permute-start | bytes 1536008 | tf_op jit(solution)/shard_map/ppermute | solution.py:66
  49.0 42.4 %collective-permute-start.48 = (bf16[80,2560]{1,0:T(8,128)(2,1)}, bf16[80,2560]{1,0:T(8,128)(2,1)}, u32[]{:S(2)}, u32[]{:S(2)}) collective-permute-start(bf16[80,2560]{1,0:T(8,128)(2,1)} %param.19), channel_id=1, source_target_pairs={{0,8},{1,9},{2,10},{3,11},{4,12},{5,13},{6,14},{7,15},{8,16},{9,17... | collective-permute-start | bytes 1228808 | tf_op jit(solution)/shard_map/ppermute | solution.py:78
  52.2 41.2 %collective-permute-start.41 = (bf16[80,2560]{1,0:T(8,128)(2,1)}, bf16[80,2560]{1,0:T(8,128)(2,1)}, u32[]{:S(2)}, u32[]{:S(2)}) collective-permute-start(bf16[80,2560]{1,0:T(8,128)(2,1)} %collective-permute-done.40), channel_id=1, source_target_pairs={{0,1},{1,0},{2,3},{3,2},{4,5},{5,4},{6,7},{7,6},{8,9},{9,8},{10,11... | collective-permute-start | bytes 1228808 | tf_op jit(solution)/shard_map/ppermute | solution.py:66
  106.2 168.2 %collective-permute-start.86 = (bf16[240,2560]{1,0:T(8,128)(2,1)}, bf16[240,2560]{1,0:T(8,128)(2,1)}, u32[]{:S(2)}, u32[]{:S(2)}) collective-permute-start(bf16[240,2560]{1,0:T(8,128)(2,1)} %param.23), channel_id=1, source_target_pairs={{0,2},{1,3},{2,0},{3,1},{4,6},{5,7},{6,4},{7,5},{8,10},{9,11},{10,... | collective-permute-start | bytes 3686408 | tf_op jit(solution)/shard_map/ppermute | solution.py:66
  109.8 37.5 %collective-permute-start.11 = (bf16[80,3200]{1,0:T(8,128)(2,1)}, bf16[80,3200]{1,0:T(8,128)(2,1)}, u32[]{:S(2)}, u32[]{:S(2)}) collective-permute-start(bf16[80,3200]{1,0:T(8,128)(2,1)} %collective-permute-done.9), channel_id=1, source_target_pairs={{0,2},{1,3},{2,0},{3,1},{4,6},{5,7},{6,4},{7,5},{8,10},{9,11},{10,... | collective-permute-start | bytes 1536008 | tf_op jit(solution)/shard_map/ppermute | solution.py:66
  112.5 164.7 %collective-permute-start.87 = (bf16[240,2560]{1,0:T(8,128)(2,1)}, bf16[240,2560]{1,0:T(8,128)(2,1)}, u32[]{:S(2)}, u32[]{:S(2)}) collective-permute-start(bf16[240,2560]{1,0:T(8,128)(2,1)} %param.23), channel_id=1, source_target_pairs={{0,4},{1,5},{2,6},{3,7},{4,0},{5,1},{6,2},{7,3},{8,12},{9,13},{10,... | collective-permute-start | bytes 3686408 | tf_op jit(solution)/shard_map/ppermute | solution.py:66
  113.3 39.6 %collective-permute-start.13 = (bf16[80,3200]{1,0:T(8,128)(2,1)}, bf16[80,3200]{1,0:T(8,128)(2,1)}, u32[]{:S(2)}, u32[]{:S(2)}) collective-permute-start(bf16[80,3200]{1,0:T(8,128)(2,1)} %collective-permute-done.9), channel_id=1, source_target_pairs={{0,4},{1,5},{2,6},{3,7},{4,0},{5,1},{6,2},{7,3},{8,12},{9,13},{10,... | collective-permute-start | bytes 1536008 | tf_op jit(solution)/shard_map/ppermute | solution.py:66
  116.4 165.8 %collective-permute-start.79 = (bf16[240,2560]{1,0:T(8,128)(2,1)}, bf16[240,2560]{1,0:T(8,128)(2,1)}, u32[]{:S(2)}, u32[]{:S(2)}) collective-permute-start(bf16[240,2560]{1,0:T(8,128)(2,1)} %param.21), channel_id=1, source_target_pairs={{0,2},{1,3},{2,0},{3,1},{4,6},{5,7},{6,4},{7,5},{8,10},{9,11},{10,... | collective-permute-start | bytes 3686408 | tf_op jit(solution)/shard_map/ppermute | solution.py:66
  147.3 123.9 %collective-permute-start.19 = (bf16[80,3200]{1,0:T(8,128)(2,1)}, bf16[80,3200]{1,0:T(8,128)(2,1)}, u32[]{:S(2)}, u32[]{:S(2)}) collective-permute-start(bf16[80,3200]{1,0:T(8,128)(2,1)} %collective-permute-done.9), channel_id=1, source_target_pairs={{0,8},{1,9},{2,10},{3,11},{4,12},{5,13},{6,14},{7,15},{8,16},{9,17... | collective-permute-start | bytes 1536008 | tf_op jit(solution)/shard_map/ppermute | solution.py:78
  152.9 131.8 %collective-permute-start.80 = (bf16[240,2560]{1,0:T(8,128)(2,1)}, bf16[240,2560]{1,0:T(8,128)(2,1)}, u32[]{:S(2)}, u32[]{:S(2)}) collective-permute-start(bf16[240,2560]{1,0:T(8,128)(2,1)} %param.21), channel_id=1, source_target_pairs={{0,4},{1,5},{2,6},{3,7},{4,0},{5,1},{6,2},{7,3},{8,12},{9,13},{10,... | collective-permute-start | bytes 3686408 | tf_op jit(solution)/shard_map/ppermute | solution.py:66
  271.2 54.2 %collective-permute-start.90 = (bf16[240,2560]{1,0:T(8,128)(2,1)}, bf16[240,2560]{1,0:T(8,128)(2,1)}, u32[]{:S(2)}, u32[]{:S(2)}) collective-permute-start(bf16[240,2560]{1,0:T(8,128)(2,1)} %param.25), channel_id=1, source_target_pairs={{0,2},{1,3},{2,0},{3,1},{4,6},{5,7},{6,4},{7,5},{8,10},{9,11},{10,... | collective-permute-start | bytes 3686408 | tf_op jit(solution)/shard_map/ppermute | solution.py:66
  274.3 55.7 %collective-permute-start.91 = (bf16[240,2560]{1,0:T(8,128)(2,1)}, bf16[240,2560]{1,0:T(8,128)(2,1)S(1)}, u32[]{:S(2)}, u32[]{:S(2)}) collective-permute-start(bf16[240,2560]{1,0:T(8,128)(2,1)} %param.25), channel_id=1, source_target_pairs={{0,4},{1,5},{2,6},{3,7},{4,0},{5,1},{6,2},{7,3},{8,12},{9,13},{10,... | collective-permute-start | bytes 3686408 | tf_op jit(solution)/shard_map/ppermute | solution.py:66
  277.2 69.9 %collective-permute-start.109 = (bf16[256,2560]{1,0:T(8,128)(2,1)S(1)}, bf16[256,2560]{1,0:T(8,128)(2,1)S(1)}, u32[]{:S(2)}, u32[]{:S(2)}) collective-permute-start(bf16[256,2560]{1,0:T(8,128)(2,1)S(1)} %copy-done.7), channel_id=1, source_target_pairs={{0,8},{1,9},{2,10},{3,11},{4,12},{5,13},{6,14},{7,15},{8,16},{9,17... | collective-permute-start | bytes 3932168 | tf_op jit(solution)/shard_map/ppermute | solution.py:78
  347.1 115.5 %collective-permute-start.20 = (bf16[80,3200]{1,0:T(8,128)(2,1)}, bf16[80,3200]{1,0:T(8,128)(2,1)}, u32[]{:S(2)}, u32[]{:S(2)}) collective-permute-start(bf16[80,3200]{1,0:T(8,128)(2,1)} %collective-permute-done.19), channel_id=1, source_target_pairs={{0,1},{1,0},{2,3},{3,2},{4,5},{5,4},{6,7},{7,6},{8,9},{9,8},{10,11... | collective-permute-start | bytes 1536008 | tf_op jit(solution)/shard_map/ppermute | solution.py:66
  347.2 128.9 %collective-permute-start.21 = (bf16[80,3200]{1,0:T(8,128)(2,1)}, bf16[80,3200]{1,0:T(8,128)(2,1)S(1)}, u32[]{:S(2)}, u32[]{:S(2)}) collective-permute-start(bf16[80,3200]{1,0:T(8,128)(2,1)} %collective-permute-done.19), channel_id=1, source_target_pairs={{0,2},{1,3},{2,0},{3,1},{4,6},{5,7},{6,4},{7,5},{8,10},{9,11},{10,... | collective-permute-start | bytes 1536008 | tf_op jit(solution)/shard_map/ppermute | solution.py:66
  349.2 141.9 %collective-permute-start.23 = (bf16[80,3200]{1,0:T(8,128)(2,1)}, bf16[80,3200]{1,0:T(8,128)(2,1)S(1)}, u32[]{:S(2)}, u32[]{:S(2)}) collective-permute-start(bf16[80,3200]{1,0:T(8,128)(2,1)} %collective-permute-done.19), channel_id=1, source_target_pairs={{0,4},{1,5},{2,6},{3,7},{4,0},{5,1},{6,2},{7,3},{8,12},{9,13},{10,... | collective-permute-start | bytes 1536008 | tf_op jit(solution)/shard_map/ppermute | solution.py:66
  350.0 143.0 %collective-permute-start.29 = (bf16[80,3200]{1,0:T(8,128)(2,1)}, bf16[80,3200]{1,0:T(8,128)(2,1)}, u32[]{:S(2)}, u32[]{:S(2)}) collective-permute-start(bf16[80,3200]{1,0:T(8,128)(2,1)} %collective-permute-done.19), channel_id=1, source_target_pairs={{0,8},{1,9},{2,10},{3,11},{4,12},{5,13},{6,14},{7,15},{8,16},{9,17... | collective-permute-start | bytes 1536008 | tf_op jit(solution)/shard_map/ppermute | solution.py:78
  350.5 144.1 %collective-permute-start.61 = (bf16[80,2560]{1,0:T(8,128)(2,1)}, bf16[80,2560]{1,0:T(8,128)(2,1)}, u32[]{:S(2)}, u32[]{:S(2)}) collective-permute-start(bf16[80,2560]{1,0:T(8,128)(2,1)} %collective-permute-done.60), channel_id=1, source_target_pairs={{0,1},{1,0},{2,3},{3,2},{4,5},{5,4},{6,7},{7,6},{8,9},{9,8},{10,11... | collective-permute-start | bytes 1228808 | tf_op jit(solution)/shard_map/ppermute | solution.py:66
  462.7 82.6 %collective-permute-start.107 = (bf16[256,2560]{1,0:T(8,128)(2,1)S(1)}, bf16[256,2560]{1,0:T(8,128)(2,1)}, u32[]{:S(2)}, u32[]{:S(2)}) collective-permute-start(bf16[256,2560]{1,0:T(8,128)(2,1)S(1)} %copy-done.7), channel_id=1, source_target_pairs={{0,1},{1,0},{2,3},{3,2},{4,5},{5,4},{6,7},{7,6},{8,9},{9,8},{10,11... | collective-permute-start | bytes 3932168 | tf_op jit(solution)/shard_map/ppermute | solution.py:66
  498.2 41.9 %collective-permute-start.92 = (bf16[120,2560]{1,0:T(8,128)(2,1)}, bf16[120,2560]{1,0:T(8,128)(2,1)}, u32[]{:S(2)}, u32[]{:S(2)}) collective-permute-start(bf16[120,2560]{1,0:T(8,128)(2,1)} %slice.827), channel_id=1, source_target_pairs={{0,4},{1,5},{2,6},{3,7},{4,0},{5,1},{6,2},{7,3},{8,12},{9,13},{10,... | collective-permute-start | bytes 1843208 | tf_op jit(solution)/shard_map/ppermute | solution.py:66
  545.3 44.0 %collective-permute-start.22 = (bf16[80,3200]{1,0:T(8,128)(2,1)S(1)}, bf16[80,3200]{1,0:T(8,128)(2,1)S(1)}, u32[]{:S(2)}, u32[]{:S(2)}) collective-permute-start(bf16[80,3200]{1,0:T(8,128)(2,1)S(1)} %collective-permute-done.21), channel_id=1, source_target_pairs={{0,1},{1,0},{2,3},{3,2},{4,5},{5,4},{6,7},{7,6},{8,9},{9,8},{10,11... | collective-permute-start | bytes 1536008 | tf_op jit(solution)/shard_map/ppermute | solution.py:66
  552.1 37.2 %collective-permute-start.24 = (bf16[80,3200]{1,0:T(8,128)(2,1)S(1)}, bf16[80,3200]{1,0:T(8,128)(2,1)S(1)}, u32[]{:S(2)}, u32[]{:S(2)}) collective-permute-start(bf16[80,3200]{1,0:T(8,128)(2,1)S(1)} %collective-permute-done.23), channel_id=1, source_target_pairs={{0,1},{1,0},{2,3},{3,2},{4,5},{5,4},{6,7},{7,6},{8,9},{9,8},{10,11... | collective-permute-start | bytes 1536008 | tf_op jit(solution)/shard_map/ppermute | solution.py:66
  589.3 121.6 %collective-permute-start.77 = (bf16[40,2560]{1,0:T(8,128)(2,1)}, bf16[40,2560]{1,0:T(8,128)(2,1)}, u32[]{:S(2)}, u32[]{:S(2)}) collective-permute-start(bf16[40,2560]{1,0:T(8,128)(2,1)} %collective-permute-done.76), channel_id=1, source_target_pairs={{0,1},{1,0},{2,3},{3,2},{4,5},{5,4},{6,7},{7,6},{8,9},{9,8},{10,11... | collective-permute-start | bytes 614408 | tf_op jit(solution)/shard_map/ppermute | solution.py:66
  590.3 120.7 %collective-permute-start.35 = (bf16[40,3200]{1,0:T(8,128)(2,1)}, bf16[40,3200]{1,0:T(8,128)(2,1)}, u32[]{:S(2)}, u32[]{:S(2)}) collective-permute-start(bf16[40,3200]{1,0:T(8,128)(2,1)} %slice.799), channel_id=1, source_target_pairs={{0,4},{1,5},{2,6},{3,7},{4,0},{5,1},{6,2},{7,3},{8,12},{9,13},{10,... | collective-permute-start | bytes 768008 | tf_op jit(solution)/shard_map/ppermute | solution.py:66
  591.8 119.7 %collective-permute-start.37 = (bf16[40,3200]{1,0:T(8,128)(2,1)}, bf16[40,3200]{1,0:T(8,128)(2,1)}, u32[]{:S(2)}, u32[]{:S(2)}) collective-permute-start(bf16[40,3200]{1,0:T(8,128)(2,1)} %slice.800), channel_id=1, source_target_pairs={{0,2},{1,3},{2,0},{3,1},{4,6},{5,7},{6,4},{7,5},{8,10},{9,11},{10,... | collective-permute-start | bytes 768008 | tf_op jit(solution)/shard_map/ppermute | solution.py:66
  593.2 124.3 %collective-permute-start.32 = (bf16[80,3200]{1,0:T(8,128)(2,1)}, bf16[80,3200]{1,0:T(8,128)(2,1)}, u32[]{:S(2)}, u32[]{:S(2)}) collective-permute-start(bf16[80,3200]{1,0:T(8,128)(2,1)} %collective-permute-done.31), channel_id=1, source_target_pairs={{0,1},{1,0},{2,3},{3,2},{4,5},{5,4},{6,7},{7,6},{8,9},{9,8},{10,11... | collective-permute-start | bytes 1536008 | tf_op jit(solution)/shard_map/ppermute | solution.py:66
  594.0 147.2 %collective-permute-start.34 = (bf16[80,3200]{1,0:T(8,128)(2,1)}, bf16[80,3200]{1,0:T(8,128)(2,1)S(1)}, u32[]{:S(2)}, u32[]{:S(2)}) collective-permute-start(bf16[80,3200]{1,0:T(8,128)(2,1)} %collective-permute-done.33), channel_id=1, source_target_pairs={{0,1},{1,0},{2,3},{3,2},{4,5},{5,4},{6,7},{7,6},{8,9},{9,8},{10,11... | collective-permute-start | bytes 1536008 | tf_op jit(solution)/shard_map/ppermute | solution.py:66
  710.9 135.1 %collective-permute-start.110 = (bf16[256,2560]{1,0:T(8,128)(2,1)}, bf16[256,2560]{1,0:T(8,128)(2,1)}, u32[]{:S(2)}, u32[]{:S(2)}) collective-permute-start(bf16[256,2560]{1,0:T(8,128)(2,1)} %copy-done.26), channel_id=1, source_target_pairs={{0,8},{1,9},{2,10},{3,11},{4,12},{5,13},{6,14},{7,15},{8,16},{9,17... | collective-permute-start | bytes 3932168 | tf_op jit(solution)/shard_map/ppermute | solution.py:78
  710.9 53.0 %collective-permute-start.36 = (bf16[40,3200]{1,0:T(8,128)(2,1)}, bf16[40,3200]{1,0:T(8,128)(2,1)S(1)}, u32[]{:S(2)}, u32[]{:S(2)}) collective-permute-start(bf16[40,3200]{1,0:T(8,128)(2,1)} %collective-permute-done.35), channel_id=1, source_target_pairs={{0,1},{1,0},{2,3},{3,2},{4,5},{5,4},{6,7},{7,6},{8,9},{9,8},{10,11... | collective-permute-start | bytes 768008 | tf_op jit(solution)/shard_map/ppermute | solution.py:66
  711.5 74.6 %collective-permute-start.38 = (bf16[40,3200]{1,0:T(8,128)(2,1)}, bf16[40,3200]{1,0:T(8,128)(2,1)}, u32[]{:S(2)}, u32[]{:S(2)}) collective-permute-start(bf16[40,3200]{1,0:T(8,128)(2,1)} %collective-permute-done.37), channel_id=1, source_target_pairs={{0,1},{1,0},{2,3},{3,2},{4,5},{5,4},{6,7},{7,6},{8,9},{9,8},{10,11... | collective-permute-start | bytes 768008 | tf_op jit(solution)/shard_map/ppermute | solution.py:66
  717.5 129.0 %collective-permute-start.116 = (bf16[256,2560]{1,0:T(8,128)(2,1)}, bf16[256,2560]{1,0:T(8,128)(2,1)}, u32[]{:S(2)}, u32[]{:S(2)}) collective-permute-start(bf16[256,2560]{1,0:T(8,128)(2,1)} %copy-done.26), channel_id=1, source_target_pairs={{0,1},{1,0},{2,3},{3,2},{4,5},{5,4},{6,7},{7,6},{8,9},{9,8},{10,11... | collective-permute-start | bytes 3932168 | tf_op jit(solution)/shard_map/ppermute | solution.py:66
  845.9 58.3 %collective-permute-start.114 = (bf16[256,2560]{1,0:T(8,128)(2,1)}, bf16[256,2560]{1,0:T(8,128)(2,1)S(1)}, u32[]{:S(2)}, u32[]{:S(2)}) collective-permute-start(bf16[256,2560]{1,0:T(8,128)(2,1)} %collective-permute-done.110), channel_id=1, source_target_pairs={{0,1},{1,0},{2,3},{3,2},{4,5},{5,4},{6,7},{7,6},{8,9},{9,8},{10,11... | collective-permute-start | bytes 3932168 | tf_op jit(solution)/shard_map/ppermute | solution.py:66
  846.4 57.8 %collective-permute-start.111 = (bf16[256,2560]{1,0:T(8,128)(2,1)}, bf16[256,2560]{1,0:T(8,128)(2,1)S(1)}, u32[]{:S(2)}, u32[]{:S(2)}) collective-permute-start(bf16[256,2560]{1,0:T(8,128)(2,1)} %collective-permute-done.110), channel_id=1, source_target_pairs={{0,8},{1,9},{2,10},{3,11},{4,12},{5,13},{6,14},{7,15},{8,16},{9,17... | collective-permute-start | bytes 3932168 | tf_op jit(solution)/shard_map/ppermute | solution.py:78
  876.2 55.4 %collective-permute-start.96 = (bf16[256,2560]{1,0:T(8,128)(2,1)S(1)}, bf16[256,2560]{1,0:T(8,128)(2,1)S(1)}, u32[]{:S(2)}, u32[]{:S(2)}) collective-permute-start(bf16[256,2560]{1,0:T(8,128)(2,1)S(1)} %collective-permute-done.95), channel_id=1, source_target_pairs={{0,8},{1,9},{2,10},{3,11},{4,12},{5,13},{6,14},{7,15},{8,16},{9,17... | collective-permute-start | bytes 3932168 | tf_op jit(solution)/shard_map/ppermute | solution.py:78
  1088.6 56.9 %collective-permute-start.203 = (bf16[120,2560]{1,0:T(8,128)(2,1)}, bf16[120,2560]{1,0:T(8,128)(2,1)S(1)}, u32[]{:S(2)}, u32[]{:S(2)}) collective-permute-start(bf16[120,2560]{1,0:T(8,128)(2,1)} %get-tuple-element.74), channel_id=1, source_target_pairs={{0,4},{1,5},{2,6},{3,7},{4,0},{5,1},{6,2},{7,3},{8,12},{9,13},{10,... | collective-permute-start | bytes 1843208 | tf_op jit(solution)/shard_map/ppermute | solution.py:66
  1088.7 58.8 %collective-permute-start.205 = (bf16[120,2560]{1,0:T(8,128)(2,1)}, bf16[120,2560]{1,0:T(8,128)(2,1)}, u32[]{:S(2)}, u32[]{:S(2)}) collective-permute-start(bf16[120,2560]{1,0:T(8,128)(2,1)} %get-tuple-element.72), channel_id=1, source_target_pairs={{0,2},{1,3},{2,0},{3,1},{4,6},{5,7},{6,4},{7,5},{8,10},{9,11},{10,... | collective-permute-start | bytes 1843208 | tf_op jit(solution)/shard_map/ppermute | solution.py:66
  1089.3 89.2 %collective-permute-start.207 = (bf16[120,2560]{1,0:T(8,128)(2,1)}, bf16[120,2560]{1,0:T(8,128)(2,1)}, u32[]{:S(2)}, u32[]{:S(2)}) collective-permute-start(bf16[120,2560]{1,0:T(8,128)(2,1)} %get-tuple-element.73), channel_id=1, source_target_pairs={{0,4},{1,5},{2,6},{3,7},{4,0},{5,1},{6,2},{7,3},{8,12},{9,13},{10,... | collective-permute-start | bytes 1843208 | tf_op jit(solution)/shard_map/ppermute | solution.py:66
  1126.9 50.8 %collective-permute-start.202 = (bf16[120,2560]{1,0:T(8,128)(2,1)}, bf16[120,2560]{1,0:T(8,128)(2,1)}, u32[]{:S(2)}, u32[]{:S(2)}) collective-permute-start(bf16[120,2560]{1,0:T(8,128)(2,1)} %get-tuple-element.75), channel_id=1, source_target_pairs={{0,2},{1,3},{2,0},{3,1},{4,6},{5,7},{6,4},{7,5},{8,10},{9,11},{10,... | collective-permute-start | bytes 1843208 | tf_op jit(solution)/shard_map/ppermute | solution.py:66
  1194.0 44.7 %collective-permute-start.104 = (bf16[256,2560]{1,0:T(8,128)(2,1)S(1)}, bf16[256,2560]{1,0:T(8,128)(2,1)S(1)}, u32[]{:S(2)}, u32[]{:S(2)}) collective-permute-start(bf16[256,2560]{1,0:T(8,128)(2,1)S(1)} %fusion.28), channel_id=1, source_target_pairs={{0,8},{1,9},{2,10},{3,11},{4,12},{5,13},{6,14},{7,15},{8,16},{9,17... | collective-permute-start | bytes 3932168 | tf_op jit(solution)/shard_map/ppermute | solution.py:78
  1197.7 41.6 %collective-permute-start.201 = (bf16[120,2560]{1,0:T(8,128)(2,1)S(1)}, bf16[120,2560]{1,0:T(8,128)(2,1)}, u32[]{:S(2)}, u32[]{:S(2)}) collective-permute-start(bf16[120,2560]{1,0:T(8,128)(2,1)S(1)} %copy-done.59), channel_id=1, source_target_pairs={{0,4},{1,5},{2,6},{3,7},{4,0},{5,1},{6,2},{7,3},{8,12},{9,13},{10,... | collective-permute-start | bytes 1843208 | tf_op jit(solution)/shard_map/ppermute | solution.py:66
  1239.8 58.6 %collective-permute-start.105 = (bf16[256,2560]{1,0:T(8,128)(2,1)S(1)}, bf16[256,2560]{1,0:T(8,128)(2,1)S(1)}, u32[]{:S(2)}, u32[]{:S(2)}) collective-permute-start(bf16[256,2560]{1,0:T(8,128)(2,1)S(1)} %fusion.30), channel_id=1, source_target_pairs={{0,8},{1,9},{2,10},{3,11},{4,12},{5,13},{6,14},{7,15},{8,16},{9,17... | collective-permute-start | bytes 3932168 | tf_op jit(solution)/shard_map/ppermute | solution.py:78
  1243.8 55.1 %collective-permute-start.193 = (bf16[120,2560]{1,0:T(8,128)(2,1)S(1)}, bf16[120,2560]{1,0:T(8,128)(2,1)S(1)}, u32[]{:S(2)}, u32[]{:S(2)}) collective-permute-start(bf16[120,2560]{1,0:T(8,128)(2,1)S(1)} %copy-done.57), channel_id=1, source_target_pairs={{0,4},{1,5},{2,6},{3,7},{4,0},{5,1},{6,2},{7,3},{8,12},{9,13},{10,... | collective-permute-start | bytes 1843208 | tf_op jit(solution)/shard_map/ppermute | solution.py:66
  1299.0 113.8 %collective-permute-start.158 = (bf16[256,2560]{0,1:T(8,128)(2,1)}, bf16[256,2560]{0,1:T(8,128)(2,1)}, u32[]{:S(2)}, u32[]{:S(2)}) collective-permute-start(bf16[256,2560]{0,1:T(8,128)(2,1)} %bitcast.12), channel_id=1, source_target_pairs={{0,1},{1,0},{2,3},{3,2},{4,5},{5,4},{6,7},{7,6},{8,9},{9,8},{10,11... | collective-permute-start | bytes 3932168 | tf_op jit(solution)/shard_map/ppermute | solution.py:66
  1299.5 57.7 %collective-permute-start.106 = (bf16[256,2560]{1,0:T(8,128)(2,1)S(1)}, bf16[256,2560]{1,0:T(8,128)(2,1)S(1)}, u32[]{:S(2)}, u32[]{:S(2)}) collective-permute-start(bf16[256,2560]{1,0:T(8,128)(2,1)S(1)} %fusion.32), channel_id=1, source_target_pairs={{0,8},{1,9},{2,10},{3,11},{4,12},{5,13},{6,14},{7,15},{8,16},{9,17... | collective-permute-start | bytes 3932168 | tf_op jit(solution)/shard_map/ppermute | solution.py:78
  1302.9 118.9 %collective-permute-start.127 = (bf16[256,2560]{1,0:T(8,128)(2,1)}, bf16[256,2560]{1,0:T(8,128)(2,1)}, u32[]{:S(2)}, u32[]{:S(2)}) collective-permute-start(bf16[256,2560]{1,0:T(8,128)(2,1)} %fusion.16), channel_id=1, source_target_pairs={{0,1},{1,0},{2,3},{3,2},{4,5},{5,4},{6,7},{7,6},{8,9},{9,8},{10,11... | collective-permute-start | bytes 3932168 | tf_op jit(solution)/shard_map/ppermute | solution.py:66
  (311 other events, 7976.4 us)

commit v2 on v1

v2 whole, which is shorter than its diff:
```python
import functools

import jax
import jax.numpy as jnp
from jax import lax
from jax.experimental import pallas as pl
from jax.experimental.pallas import tpu as pltpu
from jax.experimental.layout import Layout, with_layout_constraint
from jax.sharding import PartitionSpec as P

D = 2560
H = 10
HD = 256
LENGTH = 256
F32 = jnp.float32
BF = jnp.bfloat16
EPS = 1e-06


ROWS = Layout((0, 1))


def row_major(value):
    return with_layout_constraint(value, ROWS)


def rms_scale(values, gain):
    return values * lax.rsqrt(jnp.mean(values * values, axis=-1, keepdims=True) + EPS) * gain


def angles(positions):
    quarter = HD // 4
    ladder = jnp.arange(quarter, dtype=F32)
    freq = 10000.0 ** (-2.0 * ladder / (HD // 2))
    angle = positions.astype(F32)[:, None] * freq[None, :]
    return (jnp.cos(angle), jnp.sin(angle))


def rotate(values, cosine, sine):
    quarter = cosine.shape[-1]
    first = values[..., :quarter]
    second = values[..., quarter : 2 * quarter]
    rest = values[..., 2 * quarter :]
    return jnp.concatenate(
        [first * cosine - second * sine, second * cosine + first * sine, rest], -1
    )


def dot_tn(left, right, out=F32):
    return lax.dot_general(
        left, right, (((0,), (0,)), ((), ())), preferred_element_type=F32
    ).astype(out)


def dot_nt(left, right):
    return lax.dot_general(left, right, (((1,), (1,)), ((), ())), preferred_element_type=F32)


def dot_nn(left, right):
    return jnp.dot(left, right, preferred_element_type=F32)


def glu_tanh(gate, up):
    return jax.nn.gelu(gate, approximate=True) * up


class Moves:
    def __init__(self, n):
        self.n = n
        self.planes = n // 8
        me = lax.axis_index("dp")
        self.core = me % 2
        self.x = (me // 2) % 2
        self.y = (me // 4) % 2
        self.z = me // 8

    def flip(self, value, bit):
        return lax.ppermute(value, "dp", [(i, i ^ bit) for i in range(self.n)])

    def other(self, value):
        return self.flip(value, 1)

    def over_x(self, value):
        return self.flip(value, 2)

    def over_y(self, value):
        return self.flip(value, 4)

    def lines(self):
        return [[z * 8 + at + core for z in range(self.planes) for core in (0, 1)] for at in (0, 2, 4, 6)]

    def squares(self):
        return [
            [z * 8 + at + core for at in (0, 2, 4, 6)]
            for z in range(self.planes)
            for core in (0, 1)
        ]

    def up(self, value, steps=1):
        return lax.ppermute(value, "dp", [(i, (i + 8 * steps) % self.n) for i in range(self.n)])


def fence(values):
    return lax.optimization_barrier(values)


def place_kernel(at_ref, mine, theirs, *refs):
    whole = refs[-1]

    @pl.when(pl.program_id(0) < 4)
    def _():
        whole[...] = mine[...]

    @pl.when(pl.program_id(0) >= 4)
    def _():
        whole[...] = theirs[...]


class Rows:
    def __init__(self, mv, rows, width, dtype):
        self.mv, self.rows = mv, rows
        self.shape = jax.ShapeDtypeStruct((mv.n * rows, width), dtype)
        self.whole = None

    def put(self, step, blocks):
        mv, rows = self.mv, self.rows
        z = (mv.z - step) % mv.planes
        at = [
            ((z * 2 + (mv.y ^ fy)) * 2 + (mv.x ^ fx)) * 2 + (mv.core ^ flip)
            for flip in (0, 1)
            for fy in (0, 1)
            for fx in (0, 1)
        ]
        if rows % 16:
            whole = self.whole
            if whole is None:
                whole = jnp.zeros(self.shape.shape, self.shape.dtype)
            for j in range(8):
                block = blocks[j // 4][(j % 4) * rows : (j % 4 + 1) * rows]
                whole = lax.dynamic_update_slice(whole, block, (at[j] * rows, 0))
            self.whole = whole
            return
        width = self.shape.shape[1]
        before = [] if self.whole is None else [self.whole]
        self.whole = pl.pallas_call(
            place_kernel,
            out_shape=self.shape,
            grid_spec=pltpu.PrefetchScalarGridSpec(
                num_scalar_prefetch=1,
                grid=(8,),
                in_specs=[
                    pl.BlockSpec((rows, width), lambda j, at: (jnp.minimum(j, 3), 0)),
                    pl.BlockSpec((rows, width), lambda j, at: (jnp.maximum(j - 4, 0), 0)),
                ]
                + [pl.BlockSpec(memory_space=pl.ANY)] * len(before),
                out_specs=pl.BlockSpec((rows, width), lambda j, at: (at[j], 0)),
            ),
            input_output_aliases={3: 0} if before else {},
            name="place_rows",
        )(jnp.stack(at).astype(jnp.int32), *blocks, *before)

    def done(self):
        return row_major(self.whole)


def gather_weights(mv, to_all, late, late_round, block, block_rounds):
    halves = [block[: block.shape[0] // 2], block[block.shape[0] // 2 :]]
    arrived = []
    rows = to_all[0].shape[0]
    half = rows // 2
    builders = [Rows(mv, rows, v.shape[1], v.dtype) for v in to_all]
    items = [(i, k) for i in range(len(to_all)) for k in range(mv.planes)]
    piece = list(to_all)
    first = second = whole = None
    starts = []
    for at in range(len(items) + 3):
        placed = [b.whole for b in builders]
        state = (piece, first, second, whole, halves, placed)
        if at <= late_round:
            late, state = fence((late, state))
        else:
            state = fence(state)
        piece, first, second, whole, halves, placed = state
        for builder, value in zip(builders, placed):
            builder.whole = value
        send_x, send_y = [], []
        new_first = new_second = new_whole = None
        fresh = at < len(items)
        if fresh:
            i, k = items[at]
            send_x.append(piece[i])
            send_y.append(piece[i])
        joined = fresh and first is not None and first[1].shape[1] == piece[i].shape[1]
        if first is not None:
            own, from_x, from_y = first
            diag_b, diag_a = from_y[half:rows], from_x[:half]
            if joined or not fresh:
                send_x.append(diag_b)
                send_y.append(diag_a)
            else:
                diag_b, diag_a = mv.over_x(diag_b), mv.over_y(diag_a)
        if send_x:
            got_x = mv.over_x(jnp.concatenate(send_x, 0))
            got_y = mv.over_y(jnp.concatenate(send_y, 0))
        if first is not None:
            if joined or not fresh:
                start = rows if fresh else 0
                diag_b, diag_a = got_x, got_y
            else:
                start = 0
            new_second = (own, from_x, from_y, diag_a, diag_b)
            starts.append(start)
        if fresh:
            new_first = (piece[i], got_x, got_y)
            if k < mv.planes - 1:
                piece[i] = mv.up(piece[i])
        if second is not None:
            own, from_x, from_y, diag_a, diag_b = second
            start = starts[at - 2]
            block = jnp.concatenate(
                [
                    own,
                    from_x[:rows],
                    from_y[:rows],
                    diag_a[start : start + half],
                    diag_b[start : start + half],
                ],
                0,
            )
            new_whole = (block, mv.other(block))
        if at in block_rounds:
            which = block_rounds.index(at) % 2
            halves[which] = mv.up(halves[which])
            arrived.append(halves[which])
        if whole is not None:
            i, k = items[at - 3]
            builders[i].put(k, whole)
        first, second, whole = new_first, new_second, new_whole
    arrived = [jnp.concatenate(arrived[i : i + 2], 0) for i in range(0, len(arrived), 2)]
    return [b.done() for b in builders], late, arrived


def mine_of(mv, value, axis=0):
    size = value.shape[axis] // 2
    return lax.dynamic_slice_in_dim(value, mv.core * size, size, axis)


def theirs_of(mv, value, axis=0):
    size = value.shape[axis] // 2
    return lax.dynamic_slice_in_dim(value, (1 - mv.core) * size, size, axis)


def scatter_grads(mv, arrays, arrays_rows, held, work):
    rows = arrays_rows // (mv.n // 2)
    half = rows // 2

    def block(array, step, flip_y, flip_x, shift=0, count=rows):
        index = (((mv.z - step) % mv.planes) * 2 + (mv.y ^ flip_y)) * 2 + (mv.x ^ flip_x)
        return lax.dynamic_slice(array, (index * rows + shift, 0), (count, array.shape[1]))

    items = [(i, k) for i in range(len(arrays)) for k in [*range(1, mv.planes), 0]]
    rings = [None] * len(arrays)
    sources = [None] * len(arrays)
    results = {}
    starts = []
    first = second = None
    for at in range(max(len(items) + 2, mv.planes + 6)):
        if at < len(items) and sources[items[at][0]] is None:
            sources[items[at][0]] = arrays[items[at][0]]()
        first, second, sources, rings, results, now = fence(
            (first, second, sources, rings, results, held)
        )
        held.update(now)
        new_first = new_second = None
        send_x, send_y = [], []
        fresh = at < len(items)
        if fresh:
            i, k = items[at]
            source = sources[i]
            send_x += [block(source, k, 1, 1, 0, half), block(source, k, 0, 1, 0, half)]
            send_y += [block(source, k, 1, 1, half, half), block(source, k, 1, 0, half, half)]
        if first is not None:
            i, k = items[at - 1]
            from_x, from_y = first
            last_x = block(sources[i], k, 0, 1, half, half).astype(F32) + from_y[:half].astype(F32)
            last_y = block(sources[i], k, 1, 0, 0, half).astype(F32) + from_x[:half].astype(F32)
            last_x, last_y = last_x.astype(BF), last_y.astype(BF)
            joined = fresh and source.shape[1] == last_x.shape[1]
            if joined or not fresh:
                send_x.append(last_x)
                send_y.append(last_y)
                start = 2 * half if fresh else 0
            else:
                more_x, more_y = mv.over_x(last_x), mv.over_y(last_y)
                start = 0
            starts.append(start)
        if send_x:
            got_x = mv.over_x(jnp.concatenate(send_x, 0))
            got_y = mv.over_y(jnp.concatenate(send_y, 0))
        if first is not None:
            if joined or not fresh:
                more_x, more_y = got_x, got_y
            new_second = (from_x, from_y, more_x, more_y)
        if fresh:
            new_first = (got_x, got_y)
        if second is not None:
            i, k = items[at - 2]
            from_x, from_y, more_x, more_y = second
            start = starts[at - 2]
            total = block(sources[i], k, 0, 0).astype(F32)
            total += jnp.concatenate(
                [from_x[half : 2 * half], more_x[start : start + half]], 0
            ).astype(F32)
            total += jnp.concatenate(
                [more_y[start : start + half], from_y[half : 2 * half]], 0
            ).astype(F32)
            if rings[i] is not None:
                total = total + rings[i].astype(F32)
            if k != 0:
                rings[i] = mv.up(total.astype(BF))
            else:
                results[i] = total
        work(at)
        first, second = new_first, new_second
    return [results[i] for i in range(len(arrays))]


def swap_halves(mv, total):
    rows = total.shape[0] // 2
    mine = lax.dynamic_slice(total, (mv.core * rows, 0), (rows, total.shape[1]))
    theirs = mv.other(lax.dynamic_slice(total, ((1 - mv.core) * rows, 0), (rows, total.shape[1])))
    return jnp.where(mv.core == 0, mine, theirs), jnp.where(mv.core == 0, theirs, mine)


def core_half(mv, value):
    width = value.shape[1] // 2
    mine = jnp.where(mv.core == 0, value[:, :width], value[:, width:])
    theirs = jnp.where(mv.core == 0, value[:, width:], value[:, :width])
    return jnp.concatenate([mine, mv.other(theirs)], 0)


def make_body(n):
    def body(
        tokens,
        doc_positions,
        attn_gain,
        q_weight,
        kv_weight,
        out_weight,
        ffn_gain,
        gate_weight,
        gate_bias,
        up_weight,
        up_bias,
        down_weight,
        down_bias,
        cotangent,
    ):
        mv = Moves(n)
        head_scale = HD ** (-0.5)
        rows = tokens.shape[0]
        seqs = rows // LENGTH
        small = jnp.stack([attn_gain, ffn_gain, down_bias], 1)
        small = jnp.pad(small, ((0, 0), (0, 125)))
        units = gate_weight.shape[0]
        padded = -(-(units + 2) // 128) * 128

        def pad_rows(value):
            return jnp.pad(value, ((0, padded - units), (0, 0)))

        bias_rows = jnp.pad(
            jnp.stack([gate_bias, up_bias]), ((0, padded - units - 2), (0, D - units))
        )
        ffn = jnp.concatenate(
            [pad_rows(down_weight), gate_weight, bias_rows, pad_rows(up_weight)], 0
        )
        rounds = 2 * mv.planes
        (w_qkv, w_out), ffn, cots = gather_weights(
            mv,
            [jnp.concatenate([q_weight, kv_weight, small], 1), out_weight],
            ffn,
            rounds,
            cotangent,
            list(range(rounds - 3, rounds + 3)),
        )
        cots = [cotangent, *cots]
        ffn = lax.all_gather(ffn, "dp", axis=0, tiled=True, axis_index_groups=mv.squares())
        w_query = w_qkv[:, :D]
        w_keyval = w_qkv[:, D : D + 2 * HD]
        small = w_qkv[:, D + 2 * HD :].T.astype(F32)
        gain_one, gain_two, bias_down = small[0], small[1], small[2]

        x_value = tokens.astype(F32)
        norm_one_b = rms_scale(x_value, gain_one).astype(BF)
        cosine, sine = angles(doc_positions)
        q_lin = dot_nn(norm_one_b, w_query).reshape(rows, H, HD)
        kv_lin = dot_nn(norm_one_b, w_keyval)
        query = (
            (rotate(q_lin, cosine[:, None, :], sine[:, None, :]) * head_scale)
            .astype(BF)
            .reshape(seqs, LENGTH, H, HD)
        )
        key = rotate(kv_lin[:, :HD], cosine, sine).astype(BF).reshape(seqs, LENGTH, HD)
        value = kv_lin[:, HD:].astype(BF).reshape(seqs, LENGTH, HD)
        index = jnp.arange(LENGTH)
        distance = index[:, None] - index[None, :]
        allowed = (distance[None] >= 0) & (
            distance[None] <= doc_positions.reshape(seqs, LENGTH)[:, :, None]
        )
        logits = jnp.einsum("sqhd,skd->shqk", query, key, preferred_element_type=F32)
        logits = jnp.where(allowed[:, None], logits, -1e30)
        top = jnp.max(logits, axis=-1, keepdims=True)
        weights = jnp.exp(logits - top)
        soft = weights / jnp.sum(weights, axis=-1, keepdims=True)
        probs = soft.astype(BF)
        attended = (
            jnp.einsum("shqk,skd->sqhd", probs, value, preferred_element_type=F32)
            .reshape(rows, H * HD)
            .astype(BF)
        )
        hidden_one = x_value + dot_nn(attended, w_out)
        norm_two_b = rms_scale(hidden_one, gain_two).astype(BF)

        order = [*range(1, mv.planes), 0]
        norms, cots, norm_pieces, cot_pieces = [norm_two_b], list(cots), [], []
        swap_early = [attended, norm_one_b]
        swapped = []

        def linear(step):
            return dot_nt(norm_pieces[step], w_both) + bias_both, dot_nt(cot_pieces[step], w_down)

        def pick(both, which):
            return jnp.concatenate(
                [
                    both[:, (2 * i + which) * padded : (2 * i + which + 1) * padded]
                    for i in range(4)
                ],
                1,
            )

        def nonlinear(both, grad_act):
            act, act_back = jax.vjp(glu_tanh, pick(both, 0), pick(both, 1))
            grad_gate, grad_up = act_back(grad_act)
            parts = []
            for i in range(4):
                parts.append(grad_gate[:, i * padded : (i + 1) * padded])
                parts.append(grad_up[:, i * padded : (i + 1) * padded])
            grads = jnp.concatenate(parts, 1).astype(BF)
            partial = dot_nn(grads, w_both)
            return act.astype(BF), grads, partial[:rows], partial[rows:].astype(BF)

        acts, grads_all = [], []
        sends, received, parts, gots = {}, None, {}, {}
        last = mv.planes + 1
        for at in range(last + 1):
            norms, cots, swap_early, sends, norm_pieces, cot_pieces, acts, grads_all = fence(
                (norms, cots, swap_early, sends, norm_pieces, cot_pieces, acts, grads_all)
            )
            if at == 1:
                ffn = ffn.reshape(4, 3 * padded, D)
                w_down = ffn[:, :padded].reshape(4 * padded, D)
                w_both = ffn[:, padded:].reshape(8 * padded, D)
                bias_both = ffn[:, padded + units : padded + units + 2, :padded].reshape(8 * padded)
                bias_both = bias_both.astype(F32)
                w_down, w_both, bias_both, norms = fence((w_down, w_both, bias_both, norms))
            if at <= mv.planes - 2:
                norms.append(mv.up(norms[at]))
            if 4 + at < mv.planes:
                cots.append(mv.up(cots[3 + at]))
            if at - 2 in sends:
                received = mv.up(sends.pop(at - 2))
            if at < mv.planes:
                norm_pieces.append(jnp.concatenate([norms[at], mv.other(norms[at])], 0))
                cot_pieces.append(jnp.concatenate([cots[at], mv.other(cots[at])], 0))
            if 1 <= at <= len(swap_early):
                early = swap_early[at - 1]
                swapped.append(jnp.concatenate([early, mv.other(early)], 0))
            step = at - 1
            if 0 <= step < mv.planes:
                act, grads, own_part, their_part = nonlinear(*linear(step))
                acts.append(act)
                grads_all.append(grads)
                parts[step] = own_part
                gots[step] = mv.other(their_part)
            if at == last:
                acts = jnp.concatenate(acts, 0)
                grads_all = jnp.concatenate(grads_all, 0)
                cot_all = jnp.concatenate(cot_pieces, 0)
                norm_all = jnp.concatenate(norm_pieces, 0)
                down_partial = dot_tn(acts, cot_all, BF)
                both_partial = dot_tn(grads_all, norm_all, BF)
                down_partial, both_partial = fence((down_partial, both_partial))
            norms, cots, norm_pieces, cot_pieces, swapped, acts, grads_all, parts, gots, received = (
                fence(
                    (
                        norms,
                        cots,
                        norm_pieces,
                        cot_pieces,
                        swapped,
                        acts,
                        grads_all,
                        parts,
                        gots,
                        received,
                    )
                )
            )
            if step >= 1:
                done = step if step < mv.planes else 0
                total = parts.pop(done) + gots.pop(done).astype(F32)
                if received is not None:
                    total = total + received.astype(F32)
                    received = None
                if done:
                    sends[done] = total.astype(BF)
        grad_norm_two = total
        attended_both, norm_both = swapped
        ffn_groups = mv.squares()
        down_sum = lax.psum_scatter(
            down_partial, "dp", scatter_dimension=0, tiled=True, axis_index_groups=ffn_groups
        )
        both_sum = lax.psum_scatter(
            both_partial, "dp", scatter_dimension=0, tiled=True, axis_index_groups=ffn_groups
        )
        _, norm_two_back = jax.vjp(rms_scale, hidden_one, gain_two)
        grad_rms_two, grad_gain_two = norm_two_back(grad_norm_two)
        grad_hidden = cotangent.astype(F32) + grad_rms_two
        grad_hidden_b = grad_hidden.astype(BF)

        half_columns = core_half(mv, grad_hidden_b)
        grad_attended = dot_nt(grad_hidden_b, w_out).astype(BF).reshape(seqs, LENGTH, H, HD)
        out_partial = dot_tn(attended_both, half_columns, BF)
        out_partial, grad_attended, grads_all, acts = fence(
            (out_partial, grad_attended, grads_all, acts)
        )
        held = {"grads": grads_all, "acts": acts, "attended": grad_attended}

        def scores_back(grad_attended):
            grad_probs = jnp.einsum(
                "sqhd,skd->shqk", grad_attended, value, preferred_element_type=F32
            )
            return (
                soft * (grad_probs - jnp.sum(grad_probs * soft, axis=-1, keepdims=True))
            ).astype(BF)

        def lin_back(grad_scores, grad_attended):
            grad_value = jnp.einsum(
                "shqk,sqhd->skd", probs, grad_attended, preferred_element_type=F32
            ).reshape(rows, HD)
            grad_query = jnp.einsum(
                "shqk,skd->sqhd", grad_scores, key, preferred_element_type=F32
            ).reshape(rows, H, HD)
            grad_key = jnp.einsum(
                "shqk,sqhd->skd", grad_scores, query, preferred_element_type=F32
            ).reshape(rows, HD)
            grad_kv_lin = jnp.concatenate(
                [rotate(grad_key, cosine, -sine), grad_value], 1
            ).astype(BF)
            grad_q_lin = (
                rotate(grad_query * head_scale, cosine[:, None, :], -sine[:, None, :])
                .reshape(rows, H * HD)
                .astype(BF)
            )
            return grad_q_lin, grad_kv_lin

        def work(at):
            if at == 0:
                branch = dot_nn(held.pop("acts"), w_down).reshape(mv.planes, 2, rows, D)
                held["own"] = branch[:, 0]
                held["got"] = mv.other(branch[:, 1].astype(BF))
                bias = jnp.sum(held.pop("grads"), axis=0, dtype=F32)
                held["bias"] = bias.reshape(2, 2, 2, padded)[..., :units]
            if at == 1:
                held["scores"] = scores_back(held["attended"])
            if at == 2:
                held["q"], held["kv"] = lin_back(held.pop("scores"), held.pop("attended"))
            if at == 3:
                half = jnp.concatenate([core_half(mv, held["q"]), core_half(mv, held["kv"])], 1)
                held["partial"] = dot_tn(norm_both, half, BF)
                grad_norm_one = dot_nt(held.pop("q"), w_query) + dot_nt(held.pop("kv"), w_keyval)
                _, norm_one_back = jax.vjp(rms_scale, x_value, gain_one)
                grad_rms_one, grad_gain_one = norm_one_back(grad_norm_one)
                held["input_grad"] = (grad_hidden + grad_rms_one).astype(BF)
                down_bias_sum = jnp.sum(cotangent, axis=0, dtype=F32)
                part = D // mv.n
                small = jnp.stack([grad_gain_one, grad_gain_two, down_bias_sum])
                small = small.reshape(3, mv.planes, 2, 2, 2, part).transpose(2, 3, 4, 1, 0, 5)
                held["small"] = small
            for stage, (coordinate, move) in enumerate(
                ((mv.y, mv.over_y), (mv.x, mv.over_x), (mv.core, mv.other))
            ):
                if at == 4 + stage:
                    for name in ("small", "bias")[: 2 if stage < 2 else 1]:
                        whole = held[name]
                        keep = lax.dynamic_index_in_dim(whole, coordinate, 0, keepdims=False)
                        away = lax.dynamic_index_in_dim(whole, 1 - coordinate, 0, keepdims=False)
                        held[name] = keep + move(away)
            step = at - 6
            if 0 < step < mv.planes:
                away = lax.dynamic_index_in_dim(
                    held["small"], (mv.z + step) % mv.planes, 0, keepdims=False
                )
                held["small_sum"] = held.get("small_sum", 0.0) + mv.up(away, step)
            ring = at - 1
            if 0 <= ring < mv.planes:
                at_piece = order[ring]
                branch = held["own"][at_piece] + held["got"][at_piece].astype(F32)
                if ring > 0:
                    branch = branch + held.pop("branch").astype(F32)
                if ring < mv.planes - 1:
                    held["branch"] = mv.up(branch.astype(BF))
                else:
                    held["output"] = (hidden_one + branch + bias_down).astype(BF)

        out_total, lin_total = scatter_grads(
            mv, [lambda: out_partial, lambda: held.pop("partial")], D, held, work
        )
        out_total, lin_total, down_sum, both_sum = fence((out_total, lin_total, down_sum, both_sum))
        small = held["small_sum"] + lax.dynamic_index_in_dim(
            held["small"], mv.z, 0, keepdims=False
        )
        down_grad = down_sum[:units].astype(F32)
        gate_grad = both_sum[:units].astype(F32)
        up_grad = both_sum[padded : padded + units].astype(F32)
        out_grad = jnp.concatenate(swap_halves(mv, out_total), 1)
        first, second = swap_halves(mv, lin_total)
        q_grad = jnp.concatenate([first[:, : D // 2], second[:, : D // 2]], 1)
        kv_grad = jnp.concatenate([first[:, D // 2 :], second[:, D // 2 :]], 1)

        return (
            held["output"],
            held["input_grad"],
            small[0],
            q_grad,
            kv_grad,
            out_grad,
            small[1],
            gate_grad,
            held["bias"][0],
            up_grad,
            held["bias"][1],
            down_grad,
            small[2],
        )

    return body


def solution(mesh):
    matrix, vector = P("dp", None), P("dp")
    return jax.shard_map(
        make_body(mesh.shape["dp"]),
        mesh=mesh,
        in_specs=(
            matrix,
            vector,
            vector,
            matrix,
            matrix,
            matrix,
            vector,
            matrix,
            vector,
            matrix,
            vector,
            matrix,
            vector,
            matrix,
        ),
        out_specs=(
            matrix,
            matrix,
            vector,
            matrix,
            matrix,
            matrix,
            vector,
            matrix,
            vector,
            matrix,
            vector,
            matrix,
            vector,
        ),
        check_vma=False,
    )
```

time: 1590 us -> 991 us (0.62)
  local copies, waits for them, and re-layouts: 656 us -> 149 us
  waiting for transfers between devices: 448 us -> 312 us
  other arithmetic: 53.5 us -> 136 us
  starting transfers between devices: 155 us -> 94.5 us
  Pallas kernels: 0 us -> 60 us
  matrix products: 254 us -> 215 us
    dynamic_update_slice x80 -> x0, local copies, waits for them, and re-layouts: 460 us -> none  [place(): return lax.dynamic_update_slice(whole, block, (index * rows + shift, 0))]
    ppermute x181 -> x73, waiting for transfers between devices: 208 us -> 87.5 us  [flip(): return lax.ppermute(value, 'dp', [(i, i ^ bit) for i in range(self.n)])]
    ppermute x181 -> x73, starting transfers between devices: 128 us -> 51.7 us  [flip(): return lax.ppermute(value, 'dp', [(i, i ^ bit) for i in range(self.n)])]
    ppermute x39 -> x0, local copies, waits for them, and re-layouts: 60.9 us -> none  [the longest x36 56.5 us: flip(): return lax.ppermute(value, 'dp', [(i, i ^ bit) for i in range(self.n)])]
    pallas_call x0 -> x8, Pallas kernels: none -> 60 us  [put(): pl.pallas_call(place_kernel, out_shape=self.shape, grid_spec=pltpu.Prefet...]
    concatenate x3 -> x39, other arithmetic: 2.12 us -> 52.4 us  [the longest x4 11.3 us: body(): norm_pieces.append(jnp.concatenate([norms[at], mv.other(norms[at])], 0))]
    ppermute x27 -> x30, waiting for transfers between devices: 240 us -> 204 us  [up(): lax.ppermute(value, 'dp', [(i, (i + 8 * steps) % self.n) for i in range(s...]
    convert_element_type x19 -> x28, other arithmetic: 17.4 us -> 51.2 us  [the longest x3 11.5 us: work(): held['branch'] = mv.up(branch.astype(BF))]
  transfers between devices with their start and end apart: 208 -> 106, of which waited for: 67 -> 38; matrix products, arithmetic and copies ran while one was open for 54% -> 41% of each run, Pallas kernels for 0% -> 6%
where the time goes in v2:
time: 991 us; the launch traced here: 983 us
  waiting for transfers between devices  312 us (31%)
  matrix products  215 us (22%)
  local copies, waits for them, and re-layouts  149 us (15%)
  other arithmetic  136 us (14%)
  starting transfers between devices  94.5 us (10%)
  Pallas kernels  60 us (6%)
  between operations  17.1 us (2%)
    ppermute x30, waiting for transfers between devices, up(): lax.ppermute(value, 'dp', [(i, (i + 8 * steps) % self.n) for i in range(s...  204 us
    dot_general x11, matrix products, dot_nt(): lax.dot_general(left, right, (((1,), (1,)), ((), ())), preferred_element_...  88.7 us
    ppermute x73, waiting for transfers between devices, flip(): return lax.ppermute(value, 'dp', [(i, i ^ bit) for i in range(self.n)])  87.5 us
    unnamed x378, local copies, waits for them, and re-layouts  63.7 us
    pallas_call x8, Pallas kernels, put(): pl.pallas_call(place_kernel, out_shape=self.shape, grid_spec=pltpu.Prefet...  60 us
    dot_general x4, matrix products, dot_tn(): lax.dot_general(left, right, (((0,), (0,)), ((), ())), preferred_element_...  59.6 us
    dot_general x8, matrix products, dot_nn(): return jnp.dot(left, right, preferred_element_type=F32)  57.3 us
    ppermute x73, starting transfers between devices, flip(): return lax.ppermute(value, 'dp', [(i, i ^ bit) for i in range(self.n)])  51.7 us
  transfers between devices with their start and end apart: 106, of which 38 were waited for; matrix products, arithmetic and copies ran while one was open for 41% of the time, Pallas kernels for 6%

profile of v2, /device:TPU:0, one launch (start us, length us, event | category | flops | bytes accessed | tf_op | source)
XLA Modules:
  0.0 982.9 jit_solution(6910297053811380182)
XLA Ops:
  19.6 10.7 %collective-permute-done = bf16[80,3200]{1,0:T(8,128)(2,1)S(1)} collective-permute-done((bf16[80,3200]{1,0:T(8,128)(2,1)S(1)}, bf16[80,3200]{1,0:T(8,128)(2,1)S(1)}, u32[]{:S(2)}, u32[]{:S(2)}) %collective-permute-start) | collective-permute-done | bytes 512032 | tf_op jit(solution)/shard_map/ppermute | solution.py:100
  34.8 12.6 %collective-permute-done.3 = bf16[80,3200]{1,0:T(8,128)(2,1)S(1)} collective-permute-done((bf16[80,3200]{1,0:T(8,128)(2,1)S(1)}, bf16[80,3200]{1,0:T(8,128)(2,1)S(1)}, u32[]{:S(2)}, u32[]{:S(2)}) %collective-permute-start.3) | collective-permute-done | bytes 512032 | tf_op jit(solution)/shard_map/ppermute | solution.py:100
  53.9 13.8 %collective-permute-done.6 = bf16[80,3200]{1,0:T(8,128)(2,1)S(1)} collective-permute-done((bf16[80,3200]{1,0:T(8,128)(2,1)S(1)}, bf16[80,3200]{1,0:T(8,128)(2,1)S(1)}, u32[]{:S(2)}, u32[]{:S(2)}) %collective-permute-start.6) | collective-permute-done | bytes 512032 | tf_op jit(solution)/shard_map/ppermute | solution.py:100
  79.3 7.6 place_rows.8.refs_0_
  86.9 8.7 collective-permute-done.10
  110.1 7.8 place_rows.9.refs_0_
  129.5 7.6 place_rows.10.refs_0_
  137.1 14.3 %collective-permute-done.19 = bf16[80,2560]{1,0:T(8,128)(2,1)} collective-permute-done((bf16[80,2560]{1,0:T(8,128)(2,1)S(1)}, bf16[80,2560]{1,0:T(8,128)(2,1)}, u32[]{:S(2)}, u32[]{:S(2)}) %collective-permute-start.19) | collective-permute-done | bytes 409632 | tf_op jit(solution)/shard_map/ppermute | solution.py:100
  162.7 7.8 place_rows.11
  170.5 15.0 %collective-permute-done.24 = bf16[80,2560]{1,0:T(8,128)(2,1)} collective-permute-done((bf16[80,2560]{1,0:T(8,128)(2,1)}, bf16[80,2560]{1,0:T(8,128)(2,1)}, u32[]{:S(2)}, u32[]{:S(2)}) %collective-permute-start.24) | collective-permute-done | bytes 409632 | tf_op jit(solution)/shard_map/ppermute | solution.py:100
  196.6 7.2 place_rows.12.refs_0_
  203.8 7.7 collective-permute-done.29
  219.5 7.6 place_rows.13.refs_0_
  227.1 8.4 collective-permute-done.36
  244.9 7.2 place_rows.14.refs_0_
  252.0 7.1 collective-permute-done.38
  266.5 8.6 fusion.2
  283.2 7.3 place_rows.15
  312.1 26.7 %collective-permute-done.40 = bf16[256,2560]{1,0:T(8,128)(2,1)S(1)} collective-permute-done((bf16[256,2560]{1,0:T(8,128)(2,1)S(1)}, bf16[256,2560]{1,0:T(8,128)(2,1)S(1)}, u32[]{:S(2)}, u32[]{:S(2)}) %collective-permute-start.40) | collective-permute-done | bytes 1310752 | tf_op jit(solution)/shard_map/ppermute | solution.py:100
  340.4 20.7 %all-gather.2.cloned.1.call-done = bf16[3072,2560]{1,0:T(8,128)(2,1)} async-done(((bf16[768,2560]{1,0:T(8,128)(2,1)}), bf16[3072,2560]{1,0:T(8,128)(2,1)}) %all-gather.2.cloned.1.call-update) | async-done | bytes 15728656 | tf_op jit(solution)/shard_map/all_gather | solution.py:387
  361.1 8.6 slice.888
  374.9 11.6 %collective-permute-start.43 = (bf16[256,2560]{1,0:T(8,128)(2,1)}, bf16[256,2560]{1,0:T(8,128)(2,1)}, u32[]{:S(2)}, u32[]{:S(2)}) collective-permute-start(bf16[256,2560]{1,0:T(8,128)(2,1)} %copy-done.78), channel_id=1, source_target_pairs={{0,8},{1,9},{2,10},{3,11},{4,12},{5,13},{6,14},{7,15},{8,16},{9,17... | collective-permute-start | bytes 3932168 | tf_op jit(solution)/shard_map/ppermute | solution.py:100
  386.5 7.4 convolution_add_fusion.3
  395.1 8.7 multiply_convert_fusion.7
  429.5 7.4 convolution_add_fusion.2
  438.2 8.2 multiply_convert_fusion.5
  466.5 7.4 convolution_add_fusion.1
  475.2 8.3 multiply_convert_fusion.3
  503.6 25.3 %collective-permute-done.56 = bf16[256,2560]{1,0:T(8,128)(2,1)S(1)} collective-permute-done((bf16[256,2560]{1,0:T(8,128)(2,1)S(1)}, bf16[256,2560]{1,0:T(8,128)(2,1)S(1)}, u32[]{:S(2)}, u32[]{:S(2)}) %collective-permute-start.56) | collective-permute-done | bytes 1310752 | tf_op jit(solution)/shard_map/ppermute | solution.py:100
  530.5 7.4 convolution_add_fusion
  539.1 8.4 multiply_convert_fusion.1
  560.7 30.0 %collective-permute-done.58 = bf16[256,2560]{1,0:T(8,128)(2,1)S(1)} collective-permute-done((bf16[256,2560]{1,0:T(8,128)(2,1)S(1)}, bf16[256,2560]{1,0:T(8,128)(2,1)S(1)}, u32[]{:S(2)}, u32[]{:S(2)}) %collective-permute-start.58) | collective-permute-done | bytes 1310752 | tf_op jit(solution)/shard_map/ppermute | solution.py:100
  603.9 16.2 %fusion.21 = bf16[1024,2560]{1,0:T(8,128)(2,1)} fusion(bf16[2048,1024]{1,0:T(8,128)(2,1)} %constant_dynamic-update-slice_fusion.16, bf16[512,2560]{1,0:T(8,128)(2,1)} %pad_maximum_fusion.9, bf16[512,2560]{1,0:T(8,128)(2,1)} %pad_maximum_fusion.6, bf16[512,2560]{1,0:T(8,128)(2,1)S(1)} %copy-done.36, bf16[512,2560]{1,0:T(8,128)(2,1)S(1)} %copy-done.35), kind=kOutput, calls=%fused_computation.29 | convolution fusion | flops 10781982720 | bytes 19922944 | tf_op jit(solution)/shard_map/dot_general | solution.py:50
  620.1 28.3 %convolution_convert_fusion = bf16[2048,2560]{1,0:T(8,128)(2,1)} fusion(bf16[2048,2048]{1,0:T(8,128)(2,1)} %constant_dynamic-update-slice_fusion.20, bf16[512,2560]{1,0:T(8,128)(2,1)} %pad_maximum_fusion.8, bf16[512,2560]{1,0:T(8,128)(2,1)} %pad_maximum_fusion.5, bf16[512,2560]{1,0:T(8,128)(2,1)} %pad_maximum_fusion.2, bf16[512,2560]{1,0:T(8,128)(2,1)S(1)} %copy-done.34), kind=kOutput, calls=%fused_computation.5 | convolution fusion | flops 21522022400 | bytes 29360128 | tf_op jit(solution)/shard_map/dot_general | solution.py:50
  659.9 9.8 convolution_convert_fusion.3
  672.1 8.6 convolution_convert_fusion.2
  680.7 18.7 %fusion.181 = f32[2048,2560]{1,0:T(8,128)} fusion(bf16[2048,1024]{1,0:T(8,128)(2,1)} %constant_dynamic-update-slice_fusion.16, bf16[1024,2560]{1,0:T(8,128)(2,1)} %bitcast.272), kind=kOutput, calls=%fused_computation.481 | convolution fusion | flops 10737418240 | bytes 30408704 | tf_op jit(solution)/shard_map/dot_general | solution.py:60
  699.4 6.9 fusion.24
  712.7 9.0 copy_bitcast_fusion
  737.2 25.3 %collective-permute-done.65 = bf16[240,1280]{1,0:T(8,128)(2,1)S(1)} collective-permute-done((bf16[240,1280]{1,0:T(8,128)(2,1)S(1)}, bf16[240,1280]{1,0:T(8,128)(2,1)S(1)}, u32[]{:S(2)}, u32[]{:S(2)}) %collective-permute-start.65) | collective-permute-done | bytes 614432 | tf_op jit(solution)/shard_map/ppermute | solution.py:78
  791.4 19.7 %collective-permute-done.69 = bf16[160,1280]{1,0:T(8,128)(2,1)S(1)} collective-permute-done((bf16[160,1280]{1,0:T(8,128)(2,1)S(1)}, bf16[160,1280]{1,0:T(8,128)(2,1)S(1)}, u32[]{:S(2)}, u32[]{:S(2)}) %collective-permute-start.69) | collective-permute-done | bytes 409632 | tf_op jit(solution)/shard_map/ppermute | solution.py:100
  835.5 11.7 %fusion.34 = (f32[2560]{0:T(1024)S(1)}, f32[256]{0:T(256)S(1)}, f32[256,2560]{1,0:T(8,128)}) fusion(bf16[256,2560]{1,0:T(8,128)(2,1)S(1)} %copy-done.7, f32[256]{0:T(256)S(1)} %copy-done.137, f32[2560]{0:T(1024)S(1)} %copy-done.124, f32[256,2560]{1,0:T(8,128)} %fusion.49, bf16[256,2560]{0,1:T(8,128)(2,1)} %bitcast.274, bf16[2560,3200]{1,0:T(8,128)(2,1)} %place_rows.11), kind=kOutput, calls=%fused_computation.60 | convolution fusion | flops 3360683264 | bytes 20994048 | tf_op jit(solution)/shard_map/dot_general | solution.py:56
  854.0 6.4 convolution_convert_fusion.1
  860.4 7.6 collective-permute-done.71
  885.3 7.1 collective-permute-done.79
  899.3 11.4 %collective-permute-done.85 = bf16[240,1536]{1,0:T(8,128)(2,1)S(1)} collective-permute-done((bf16[240,1536]{1,0:T(8,128)(2,1)S(1)}, bf16[240,1536]{1,0:T(8,128)(2,1)S(1)}, u32[]{:S(2)}, u32[]{:S(2)}) %collective-permute-start.85) | collective-permute-done | bytes 737312 | tf_op jit(solution)/shard_map/ppermute | solution.py:78
  920.1 7.3 collective-permute-done.90
  939.9 8.7 collective-permute-done.95
  (829 shorter events, 410.5 us)
Async XLA Ops:
  7.3 353.8 %all-gather.2.cloned.1.call-start = ((), (), s32[]{:S(2)}) async-start(), calls=%async_computation.2 | async-start | bytes 19660800 | tf_op jit(solution)/shard_map/all_gather | solution.py:387
  50.0 20.4 %collective-permute-start.9 = (bf16[320,3200]{1,0:T(8,128)(2,1)S(1)}, bf16[320,3200]{1,0:T(8,128)(2,1)S(1)}, u32[]{:S(2)}, u32[]{:S(2)}) collective-permute-start(bf16[320,3200]{1,0:T(8,128)(2,1)S(1)} %slice_dynamic-update-slice_fusion.48.mine), channel_id=1, source_target_pairs={{0,1},{1,0},{2,3},{3,2},{4,5},{5,4},{6,7},{7,6},{8,9},{9,8},{10,11... | collective-permute-start | bytes 6144008 | tf_op jit(solution)/shard_map/ppermute | solution.py:78
  50.3 19.6 %collective-permute-start.7 = (bf16[120,3200]{1,0:T(8,128)(2,1)S(1)}, bf16[120,3200]{1,0:T(8,128)(2,1)S(1)}, u32[]{:S(2)}, u32[]{:S(2)}) collective-permute-start(bf16[120,3200]{1,0:T(8,128)(2,1)S(1)} %get-tuple-element.972), channel_id=1, source_target_pairs={{0,2},{1,3},{2,0},{3,1},{4,6},{5,7},{6,4},{7,5},{8,10},{9,11},{10,... | collective-permute-start | bytes 2304008 | tf_op jit(solution)/shard_map/ppermute | solution.py:78
  51.1 19.3 %collective-permute-start.8 = (bf16[120,3200]{1,0:T(8,128)(2,1)S(1)}, bf16[120,3200]{1,0:T(8,128)(2,1)S(1)}, u32[]{:S(2)}, u32[]{:S(2)}) collective-permute-start(bf16[120,3200]{1,0:T(8,128)(2,1)S(1)} %get-tuple-element.971), channel_id=1, source_target_pairs={{0,4},{1,5},{2,6},{3,7},{4,0},{5,1},{6,2},{7,3},{8,12},{9,13},{10,... | collective-permute-start | bytes 2304008 | tf_op jit(solution)/shard_map/ppermute | solution.py:78
  74.5 22.9 %collective-permute-start.12 = (bf16[320,3200]{1,0:T(8,128)(2,1)}, bf16[320,3200]{1,0:T(8,128)(2,1)}, u32[]{:S(2)}, u32[]{:S(2)}) collective-permute-start(bf16[320,3200]{1,0:T(8,128)(2,1)} %slice_dynamic-update-slice_fusion.46.mine), channel_id=1, source_target_pairs={{0,1},{1,0},{2,3},{3,2},{4,5},{5,4},{6,7},{7,6},{8,9},{9,8},{10,11... | collective-permute-start | bytes 6144008 | tf_op jit(solution)/shard_map/ppermute | solution.py:78
  75.9 19.8 %collective-permute-start.10 = (bf16[120,3200]{1,0:T(8,128)(2,1)}, bf16[120,3200]{1,0:T(8,128)(2,1)S(1)}, u32[]{:S(2)}, u32[]{:S(2)}) collective-permute-start(bf16[120,3200]{1,0:T(8,128)(2,1)} %get-tuple-element.970), channel_id=1, source_target_pairs={{0,2},{1,3},{2,0},{3,1},{4,6},{5,7},{6,4},{7,5},{8,10},{9,11},{10,... | collective-permute-start | bytes 2304008 | tf_op jit(solution)/shard_map/ppermute | solution.py:78
  77.1 19.5 %collective-permute-start.11 = (bf16[120,3200]{1,0:T(8,128)(2,1)}, bf16[120,3200]{1,0:T(8,128)(2,1)S(1)}, u32[]{:S(2)}, u32[]{:S(2)}) collective-permute-start(bf16[120,3200]{1,0:T(8,128)(2,1)} %get-tuple-element.969), channel_id=1, source_target_pairs={{0,4},{1,5},{2,6},{3,7},{4,0},{5,1},{6,2},{7,3},{8,12},{9,13},{10,... | collective-permute-start | bytes 2304008 | tf_op jit(solution)/shard_map/ppermute | solution.py:78
  99.0 20.0 %collective-permute-start.18 = (bf16[320,3200]{1,0:T(8,128)(2,1)S(1)}, bf16[320,3200]{1,0:T(8,128)(2,1)}, u32[]{:S(2)}, u32[]{:S(2)}) collective-permute-start(bf16[320,3200]{1,0:T(8,128)(2,1)S(1)} %slice_dynamic-update-slice_fusion.44.mine), channel_id=1, source_target_pairs={{0,1},{1,0},{2,3},{3,2},{4,5},{5,4},{6,7},{7,6},{8,9},{9,8},{10,11... | collective-permute-start | bytes 6144008 | tf_op jit(solution)/shard_map/ppermute | solution.py:78
  122.3 29.1 %collective-permute-start.22 = (bf16[320,3200]{1,0:T(8,128)(2,1)S(1)}, bf16[320,3200]{1,0:T(8,128)(2,1)}, u32[]{:S(2)}, u32[]{:S(2)}) collective-permute-start(bf16[320,3200]{1,0:T(8,128)(2,1)S(1)} %constant_dynamic-update-slice_fusion.5.mine), channel_id=1, source_target_pairs={{0,1},{1,0},{2,3},{3,2},{4,5},{5,4},{6,7},{7,6},{8,9},{9,8},{10,11... | collective-permute-start | bytes 6144008 | tf_op jit(solution)/shard_map/ppermute | solution.py:78
  123.6 27.8 %collective-permute-start.23 = (bf16[128,2560]{1,0:T(8,128)(2,1)}, bf16[128,2560]{1,0:T(8,128)(2,1)}, u32[]{:S(2)}, u32[]{:S(2)}) collective-permute-start(bf16[128,2560]{1,0:T(8,128)(2,1)} %get-tuple-element.499), channel_id=1, source_target_pairs={{0,8},{1,9},{2,10},{3,11},{4,12},{5,13},{6,14},{7,15},{8,16},{9,17... | collective-permute-start | bytes 1966088 | tf_op jit(solution)/shard_map/ppermute | solution.py:100
  126.3 25.1 %collective-permute-start.20 = (bf16[120,2560]{1,0:T(8,128)(2,1)}, bf16[120,2560]{1,0:T(8,128)(2,1)}, u32[]{:S(2)}, u32[]{:S(2)}) collective-permute-start(bf16[120,2560]{1,0:T(8,128)(2,1)} %get-tuple-element.980), channel_id=1, source_target_pairs={{0,2},{1,3},{2,0},{3,1},{4,6},{5,7},{6,4},{7,5},{8,10},{9,11},{10,... | collective-permute-start | bytes 1843208 | tf_op jit(solution)/shard_map/ppermute | solution.py:78
  127.2 24.2 %collective-permute-start.21 = (bf16[120,2560]{1,0:T(8,128)(2,1)}, bf16[120,2560]{1,0:T(8,128)(2,1)}, u32[]{:S(2)}, u32[]{:S(2)}) collective-permute-start(bf16[120,2560]{1,0:T(8,128)(2,1)} %get-tuple-element.979), channel_id=1, source_target_pairs={{0,4},{1,5},{2,6},{3,7},{4,0},{5,1},{6,2},{7,3},{8,12},{9,13},{10,... | collective-permute-start | bytes 1843208 | tf_op jit(solution)/shard_map/ppermute | solution.py:78
  127.7 23.7 %collective-permute-start.19 = (bf16[80,2560]{1,0:T(8,128)(2,1)S(1)}, bf16[80,2560]{1,0:T(8,128)(2,1)}, u32[]{:S(2)}, u32[]{:S(2)}) collective-permute-start(bf16[80,2560]{1,0:T(8,128)(2,1)S(1)} %collective-permute-done.13), channel_id=1, source_target_pairs={{0,8},{1,9},{2,10},{3,11},{4,12},{5,13},{6,14},{7,15},{8,16},{9,17... | collective-permute-start | bytes 1228808 | tf_op jit(solution)/shard_map/ppermute | solution.py:100
  155.4 30.1 %collective-permute-start.27 = (bf16[320,2560]{1,0:T(8,128)(2,1)S(1)}, bf16[320,2560]{1,0:T(8,128)(2,1)S(1)}, u32[]{:S(2)}, u32[]{:S(2)}) collective-permute-start(bf16[320,2560]{1,0:T(8,128)(2,1)S(1)} %slice_dynamic-update-slice_fusion.54.mine), channel_id=1, source_target_pairs={{0,1},{1,0},{2,3},{3,2},{4,5},{5,4},{6,7},{7,6},{8,9},{9,8},{10,11... | collective-permute-start | bytes 4915208 | tf_op jit(solution)/shard_map/ppermute | solution.py:78
  157.7 27.8 %collective-permute-start.28 = (bf16[128,2560]{1,0:T(8,128)(2,1)}, bf16[128,2560]{1,0:T(8,128)(2,1)}, u32[]{:S(2)}, u32[]{:S(2)}) collective-permute-start(bf16[128,2560]{1,0:T(8,128)(2,1)} %get-tuple-element.515), channel_id=1, source_target_pairs={{0,8},{1,9},{2,10},{3,11},{4,12},{5,13},{6,14},{7,15},{8,16},{9,17... | collective-permute-start | bytes 1966088 | tf_op jit(solution)/shard_map/ppermute | solution.py:100
  159.9 25.6 %collective-permute-start.25 = (bf16[120,2560]{1,0:T(8,128)(2,1)}, bf16[120,2560]{1,0:T(8,128)(2,1)}, u32[]{:S(2)}, u32[]{:S(2)}) collective-permute-start(bf16[120,2560]{1,0:T(8,128)(2,1)} %get-tuple-element.978), channel_id=1, source_target_pairs={{0,2},{1,3},{2,0},{3,1},{4,6},{5,7},{6,4},{7,5},{8,10},{9,11},{10,... | collective-permute-start | bytes 1843208 | tf_op jit(solution)/shard_map/ppermute | solution.py:78
  160.7 24.8 %collective-permute-start.26 = (bf16[120,2560]{1,0:T(8,128)(2,1)}, bf16[120,2560]{1,0:T(8,128)(2,1)}, u32[]{:S(2)}, u32[]{:S(2)}) collective-permute-start(bf16[120,2560]{1,0:T(8,128)(2,1)} %get-tuple-element.977), channel_id=1, source_target_pairs={{0,4},{1,5},{2,6},{3,7},{4,0},{5,1},{6,2},{7,3},{8,12},{9,13},{10,... | collective-permute-start | bytes 1843208 | tf_op jit(solution)/shard_map/ppermute | solution.py:78
  161.3 24.2 %collective-permute-start.24 = (bf16[80,2560]{1,0:T(8,128)(2,1)}, bf16[80,2560]{1,0:T(8,128)(2,1)}, u32[]{:S(2)}, u32[]{:S(2)}) collective-permute-start(bf16[80,2560]{1,0:T(8,128)(2,1)} %collective-permute-done.19), channel_id=1, source_target_pairs={{0,8},{1,9},{2,10},{3,11},{4,12},{5,13},{6,14},{7,15},{8,16},{9,17... | collective-permute-start | bytes 1228808 | tf_op jit(solution)/shard_map/ppermute | solution.py:100
  190.8 21.3 %collective-permute-start.31 = (bf16[320,2560]{1,0:T(8,128)(2,1)S(1)}, bf16[320,2560]{1,0:T(8,128)(2,1)}, u32[]{:S(2)}, u32[]{:S(2)}) collective-permute-start(bf16[320,2560]{1,0:T(8,128)(2,1)S(1)} %slice_dynamic-update-slice_fusion.52.mine), channel_id=1, source_target_pairs={{0,1},{1,0},{2,3},{3,2},{4,5},{5,4},{6,7},{7,6},{8,9},{9,8},{10,11... | collective-permute-start | bytes 4915208 | tf_op jit(solution)/shard_map/ppermute | solution.py:78
  212.9 754.1 %reduce-scatter.3.cloned.1.call-start = ((), (), s32[]{:S(2)}) async-start(), calls=%async_computation.3 | async-start | bytes 6553600 | tf_op jit(solution)/shard_map/reduce_scatter | solution.py:520
  216.2 19.3 %collective-permute-start.35 = (bf16[320,2560]{1,0:T(8,128)(2,1)S(1)}, bf16[320,2560]{1,0:T(8,128)(2,1)}, u32[]{:S(2)}, u32[]{:S(2)}) collective-permute-start(bf16[320,2560]{1,0:T(8,128)(2,1)S(1)} %slice_dynamic-update-slice_fusion.50.mine), channel_id=1, source_target_pairs={{0,1},{1,0},{2,3},{3,2},{4,5},{5,4},{6,7},{7,6},{8,9},{9,8},{10,11... | collective-permute-start | bytes 4915208 | tf_op jit(solution)/shard_map/ppermute | solution.py:78
  216.2 19.2 %collective-permute-start.36 = (bf16[128,2560]{1,0:T(8,128)(2,1)}, bf16[128,2560]{1,0:T(8,128)(2,1)}, u32[]{:S(2)}, u32[]{:S(2)}) collective-permute-start(bf16[128,2560]{1,0:T(8,128)(2,1)} %collective-permute-done.28), channel_id=1, source_target_pairs={{0,8},{1,9},{2,10},{3,11},{4,12},{5,13},{6,14},{7,15},{8,16},{9,17... | collective-permute-start | bytes 1966088 | tf_op jit(solution)/shard_map/ppermute | solution.py:100
  238.7 20.5 %collective-permute-start.37 = (bf16[320,2560]{1,0:T(8,128)(2,1)S(1)}, bf16[320,2560]{1,0:T(8,128)(2,1)}, u32[]{:S(2)}, u32[]{:S(2)}) collective-permute-start(bf16[320,2560]{1,0:T(8,128)(2,1)S(1)} %constant_dynamic-update-slice_fusion.13.mine), channel_id=1, source_target_pairs={{0,1},{1,0},{2,3},{3,2},{4,5},{5,4},{6,7},{7,6},{8,9},{9,8},{10,11... | collective-permute-start | bytes 4915208 | tf_op jit(solution)/shard_map/ppermute | solution.py:78
  259.1 44.1 %collective-permute-start.39 = (bf16[128,2560]{1,0:T(8,128)(2,1)}, bf16[128,2560]{1,0:T(8,128)(2,1)}, u32[]{:S(2)}, u32[]{:S(2)}) collective-permute-start(bf16[128,2560]{1,0:T(8,128)(2,1)} %collective-permute-done.36), channel_id=1, source_target_pairs={{0,8},{1,9},{2,10},{3,11},{4,12},{5,13},{6,14},{7,15},{8,16},{9,17... | collective-permute-start | bytes 1966088 | tf_op jit(solution)/shard_map/ppermute | solution.py:100
  306.0 32.8 %collective-permute-start.40 = (bf16[256,2560]{1,0:T(8,128)(2,1)S(1)}, bf16[256,2560]{1,0:T(8,128)(2,1)S(1)}, u32[]{:S(2)}, u32[]{:S(2)}) collective-permute-start(bf16[256,2560]{1,0:T(8,128)(2,1)S(1)} %multiply_convert_fusion), channel_id=1, source_target_pairs={{0,8},{1,9},{2,10},{3,11},{4,12},{5,13},{6,14},{7,15},{8,16},{9,17... | collective-permute-start | bytes 3932168 | tf_op jit(solution)/shard_map/ppermute | solution.py:100
  339.9 74.2 %collective-permute-start.46 = (bf16[256,2560]{0,1:T(8,128)(2,1)S(1)}, bf16[256,2560]{0,1:T(8,128)(2,1)}, u32[]{:S(2)}, u32[]{:S(2)}) collective-permute-start(bf16[256,2560]{0,1:T(8,128)(2,1)S(1)} %bitcast.266), channel_id=1, source_target_pairs={{0,1},{1,0},{2,3},{3,2},{4,5},{5,4},{6,7},{7,6},{8,9},{9,8},{10,11... | collective-permute-start | bytes 3932168 | tf_op jit(solution)/shard_map/ppermute | solution.py:78
  339.9 77.2 %collective-permute-start.45 = (bf16[256,2560]{1,0:T(8,128)(2,1)}, bf16[256,2560]{1,0:T(8,128)(2,1)}, u32[]{:S(2)}, u32[]{:S(2)}) collective-permute-start(bf16[256,2560]{1,0:T(8,128)(2,1)} %pad_maximum_fusion.18), channel_id=1, source_target_pairs={{0,1},{1,0},{2,3},{3,2},{4,5},{5,4},{6,7},{7,6},{8,9},{9,8},{10,11... | collective-permute-start | bytes 3932168 | tf_op jit(solution)/shard_map/ppermute | solution.py:78
  374.8 49.2 %collective-permute-start.44 = (bf16[256,2560]{1,0:T(8,128)(2,1)}, bf16[256,2560]{1,0:T(8,128)(2,1)}, u32[]{:S(2)}, u32[]{:S(2)}) collective-permute-start(bf16[256,2560]{1,0:T(8,128)(2,1)} %copy-done.78), channel_id=1, source_target_pairs={{0,1},{1,0},{2,3},{3,2},{4,5},{5,4},{6,7},{7,6},{8,9},{9,8},{10,11... | collective-permute-start | bytes 3932168 | tf_op jit(solution)/shard_map/ppermute | solution.py:78
  374.9 52.6 %collective-permute-start.43 = (bf16[256,2560]{1,0:T(8,128)(2,1)}, bf16[256,2560]{1,0:T(8,128)(2,1)}, u32[]{:S(2)}, u32[]{:S(2)}) collective-permute-start(bf16[256,2560]{1,0:T(8,128)(2,1)} %copy-done.78), channel_id=1, source_target_pairs={{0,8},{1,9},{2,10},{3,11},{4,12},{5,13},{6,14},{7,15},{8,16},{9,17... | collective-permute-start | bytes 3932168 | tf_op jit(solution)/shard_map/ppermute | solution.py:100
  427.5 34.1 %collective-permute-start.49 = (bf16[256,2560]{1,0:T(8,128)(2,1)}, bf16[256,2560]{1,0:T(8,128)(2,1)}, u32[]{:S(2)}, u32[]{:S(2)}) collective-permute-start(bf16[256,2560]{1,0:T(8,128)(2,1)} %collective-permute-done.43), channel_id=1, source_target_pairs={{0,1},{1,0},{2,3},{3,2},{4,5},{5,4},{6,7},{7,6},{8,9},{9,8},{10,11... | collective-permute-start | bytes 3932168 | tf_op jit(solution)/shard_map/ppermute | solution.py:78
  428.0 37.0 %collective-permute-start.48 = (bf16[256,2560]{1,0:T(8,128)(2,1)}, bf16[256,2560]{1,0:T(8,128)(2,1)}, u32[]{:S(2)}, u32[]{:S(2)}) collective-permute-start(bf16[256,2560]{1,0:T(8,128)(2,1)} %collective-permute-done.43), channel_id=1, source_target_pairs={{0,8},{1,9},{2,10},{3,11},{4,12},{5,13},{6,14},{7,15},{8,16},{9,17... | collective-permute-start | bytes 3932168 | tf_op jit(solution)/shard_map/ppermute | solution.py:100
  496.3 32.6 %collective-permute-start.56 = (bf16[256,2560]{1,0:T(8,128)(2,1)S(1)}, bf16[256,2560]{1,0:T(8,128)(2,1)S(1)}, u32[]{:S(2)}, u32[]{:S(2)}) collective-permute-start(bf16[256,2560]{1,0:T(8,128)(2,1)S(1)} %copy-done.80), channel_id=1, source_target_pairs={{0,8},{1,9},{2,10},{3,11},{4,12},{5,13},{6,14},{7,15},{8,16},{9,17... | collective-permute-start | bytes 3932168 | tf_op jit(solution)/shard_map/ppermute | solution.py:100
  558.7 31.9 %collective-permute-start.58 = (bf16[256,2560]{1,0:T(8,128)(2,1)S(1)}, bf16[256,2560]{1,0:T(8,128)(2,1)S(1)}, u32[]{:S(2)}, u32[]{:S(2)}) collective-permute-start(bf16[256,2560]{1,0:T(8,128)(2,1)S(1)} %copy-done.82), channel_id=1, source_target_pairs={{0,8},{1,9},{2,10},{3,11},{4,12},{5,13},{6,14},{7,15},{8,16},{9,17... | collective-permute-start | bytes 3932168 | tf_op jit(solution)/shard_map/ppermute | solution.py:100
  594.8 53.9 %collective-permute-start.59 = (bf16[256,2560]{1,0:T(8,128)(2,1)}, bf16[256,2560]{1,0:T(8,128)(2,1)}, u32[]{:S(2)}, u32[]{:S(2)}) collective-permute-start(bf16[256,2560]{1,0:T(8,128)(2,1)} %add_convert_fusion.1), channel_id=1, source_target_pairs={{0,8},{1,9},{2,10},{3,11},{4,12},{5,13},{6,14},{7,15},{8,16},{9,17... | collective-permute-start | bytes 3932168 | tf_op jit(solution)/shard_map/ppermute | solution.py:100
  648.4 318.5 %reduce-scatter.5.cloned.1.call-start = ((), (), s32[]{:S(2)}) async-start(), calls=%async_computation.4 | async-start | bytes 13107200 | tf_op jit(solution)/shard_map/reduce_scatter | solution.py:523
  706.3 20.7 %collective-permute-start.63 = (bf16[4,256,2560]{2,1,0:T(8,128)(2,1)}, bf16[4,256,2560]{2,1,0:T(8,128)(2,1)}, u32[]{:S(2)}, u32[]{:S(2)}) collective-permute-start(bf16[4,256,2560]{2,1,0:T(8,128)(2,1)} %fusion.24), channel_id=1, source_target_pairs={{0,1},{1,0},{2,3},{3,2},{4,5},{5,4},{6,7},{7,6},{8,9},{9,8},{10,11... | collective-permute-start | bytes 15728648 | tf_op jit(solution)/shard_map/ppermute | solution.py:78
  730.1 33.8 %collective-permute-start.66 = (bf16[256,2560]{1,0:T(8,128)(2,1)S(1)}, bf16[256,2560]{1,0:T(8,128)(2,1)S(1)}, u32[]{:S(2)}, u32[]{:S(2)}) collective-permute-start(bf16[256,2560]{1,0:T(8,128)(2,1)S(1)} %fusion.90), channel_id=1, source_target_pairs={{0,8},{1,9},{2,10},{3,11},{4,12},{5,13},{6,14},{7,15},{8,16},{9,17... | collective-permute-start | bytes 3932168 | tf_op jit(solution)/shard_map/ppermute | solution.py:100
  733.1 29.4 %collective-permute-start.65 = (bf16[240,1280]{1,0:T(8,128)(2,1)S(1)}, bf16[240,1280]{1,0:T(8,128)(2,1)S(1)}, u32[]{:S(2)}, u32[]{:S(2)}) collective-permute-start(bf16[240,1280]{1,0:T(8,128)(2,1)S(1)} %pad_maximum_fusion.43), channel_id=1, source_target_pairs={{0,4},{1,5},{2,6},{3,7},{4,0},{5,1},{6,2},{7,3},{8,12},{9,13},{10,... | collective-permute-start | bytes 1843208 | tf_op jit(solution)/shard_map/ppermute | solution.py:78
  734.5 29.4 %collective-permute-start.64 = (bf16[240,1280]{1,0:T(8,128)(2,1)S(1)}, bf16[240,1280]{1,0:T(8,128)(2,1)S(1)}, u32[]{:S(2)}, u32[]{:S(2)}) collective-permute-start(bf16[240,1280]{1,0:T(8,128)(2,1)S(1)} %pad_maximum_fusion.42), channel_id=1, source_target_pairs={{0,2},{1,3},{2,0},{3,1},{4,6},{5,7},{6,4},{7,5},{8,10},{9,11},{10,... | collective-permute-start | bytes 1843208 | tf_op jit(solution)/shard_map/ppermute | solution.py:78
  770.6 40.5 %collective-permute-start.70 = (bf16[256,2560]{1,0:T(8,128)(2,1)}, bf16[256,2560]{1,0:T(8,128)(2,1)}, u32[]{:S(2)}, u32[]{:S(2)}) collective-permute-start(bf16[256,2560]{1,0:T(8,128)(2,1)} %fusion.44), channel_id=1, source_target_pairs={{0,8},{1,9},{2,10},{3,11},{4,12},{5,13},{6,14},{7,15},{8,16},{9,17... | collective-permute-start | bytes 3932168 | tf_op jit(solution)/shard_map/ppermute | solution.py:100
  774.4 36.8 %collective-permute-start.68 = (bf16[240,1280]{1,0:T(8,128)(2,1)}, bf16[240,1280]{1,0:T(8,128)(2,1)}, u32[]{:S(2)}, u32[]{:S(2)}) collective-permute-start(bf16[240,1280]{1,0:T(8,128)(2,1)} %pad_maximum_fusion.45), channel_id=1, source_target_pairs={{0,4},{1,5},{2,6},{3,7},{4,0},{5,1},{6,2},{7,3},{8,12},{9,13},{10,... | collective-permute-start | bytes 1843208 | tf_op jit(solution)/shard_map/ppermute | solution.py:78
  775.7 35.4 %collective-permute-start.67 = (bf16[240,1280]{1,0:T(8,128)(2,1)}, bf16[240,1280]{1,0:T(8,128)(2,1)}, u32[]{:S(2)}, u32[]{:S(2)}) collective-permute-start(bf16[240,1280]{1,0:T(8,128)(2,1)} %pad_maximum_fusion.44), channel_id=1, source_target_pairs={{0,2},{1,3},{2,0},{3,1},{4,6},{5,7},{6,4},{7,5},{8,10},{9,11},{10,... | collective-permute-start | bytes 1843208 | tf_op jit(solution)/shard_map/ppermute | solution.py:78
  782.1 29.1 %collective-permute-start.69 = (bf16[160,1280]{1,0:T(8,128)(2,1)S(1)}, bf16[160,1280]{1,0:T(8,128)(2,1)S(1)}, u32[]{:S(2)}, u32[]{:S(2)}) collective-permute-start(bf16[160,1280]{1,0:T(8,128)(2,1)S(1)} %copy-done.116), channel_id=1, source_target_pairs={{0,8},{1,9},{2,10},{3,11},{4,12},{5,13},{6,14},{7,15},{8,16},{9,17... | collective-permute-start | bytes 1228808 | tf_op jit(solution)/shard_map/ppermute | solution.py:100
  816.0 52.0 %collective-permute-start.76 = (bf16[256,2560]{1,0:T(8,128)(2,1)}, bf16[256,2560]{1,0:T(8,128)(2,1)}, u32[]{:S(2)}, u32[]{:S(2)}) collective-permute-start(bf16[256,2560]{1,0:T(8,128)(2,1)} %fusion.43), channel_id=1, source_target_pairs={{0,8},{1,9},{2,10},{3,11},{4,12},{5,13},{6,14},{7,15},{8,16},{9,17... | collective-permute-start | bytes 3932168 | tf_op jit(solution)/shard_map/ppermute | solution.py:100
  819.9 40.5 %collective-permute-start.75 = (bf16[160,1280]{1,0:T(8,128)(2,1)}, bf16[160,1280]{1,0:T(8,128)(2,1)S(1)}, u32[]{:S(2)}, u32[]{:S(2)}) collective-permute-start(bf16[160,1280]{1,0:T(8,128)(2,1)} %add_convert_fusion.8), channel_id=1, source_target_pairs={{0,8},{1,9},{2,10},{3,11},{4,12},{5,13},{6,14},{7,15},{8,16},{9,17... | collective-permute-start | bytes 1228808 | tf_op jit(solution)/shard_map/ppermute | solution.py:100
  826.4 27.5 %collective-permute-start.73 = (bf16[256,1280]{1,0:T(8,128)(2,1)}, bf16[256,1280]{1,0:T(8,128)(2,1)}, u32[]{:S(2)}, u32[]{:S(2)}) collective-permute-start(bf16[256,1280]{1,0:T(8,128)(2,1)} %get-tuple-element.960), channel_id=1, source_target_pairs={{0,1},{1,0},{2,3},{3,2},{4,5},{5,4},{6,7},{7,6},{8,9},{9,8},{10,11... | collective-permute-start | bytes 1966088 | tf_op jit(solution)/shard_map/ppermute | solution.py:78
  827.1 24.8 %collective-permute-start.74 = (bf16[256,256]{1,0:T(8,128)(2,1)}, bf16[256,256]{1,0:T(8,128)(2,1)}, u32[]{:S(2)}, u32[]{:S(2)}) collective-permute-start(bf16[256,256]{1,0:T(8,128)(2,1)} %get-tuple-element.984), channel_id=1, source_target_pairs={{0,1},{1,0},{2,3},{3,2},{4,5},{5,4},{6,7},{7,6},{8,9},{9,8},{10,11... | collective-permute-start | bytes 393224 | tf_op jit(solution)/shard_map/ppermute | solution.py:78
  831.2 29.2 %collective-permute-start.72 = (bf16[240,1280]{1,0:T(8,128)(2,1)}, bf16[240,1280]{1,0:T(8,128)(2,1)}, u32[]{:S(2)}, u32[]{:S(2)}) collective-permute-start(bf16[240,1280]{1,0:T(8,128)(2,1)} %pad_maximum_fusion.47), channel_id=1, source_target_pairs={{0,4},{1,5},{2,6},{3,7},{4,0},{5,1},{6,2},{7,3},{8,12},{9,13},{10,... | collective-permute-start | bytes 1843208 | tf_op jit(solution)/shard_map/ppermute | solution.py:78
  (225 other events, 2149.8 us)
Sparse Core Ops, SparseCore 0:
  212.3 148.7 all-gather.1
  648.6 61.4 reduce-scatter.2
  713.1 140.6 reduce-scatter.4

commit v3 on v2

--- a/solution.py
+++ b/solution.py
@@ -163,7 +163,7 @@
         return row_major(self.whole)
 
 
-def gather_weights(mv, to_all, late, late_round, block, block_rounds):
+def gather_weights(mv, to_all, late, late_round, block, block_rounds, held, work):
     halves = [block[: block.shape[0] // 2], block[block.shape[0] // 2 :]]
     arrived = []
     rows = to_all[0].shape[0]
@@ -175,12 +175,13 @@
     starts = []
     for at in range(len(items) + 3):
         placed = [b.whole for b in builders]
-        state = (piece, first, second, whole, halves, placed)
+        state = (piece, first, second, whole, halves, placed, held)
         if at <= late_round:
             late, state = fence((late, state))
         else:
             state = fence(state)
-        piece, first, second, whole, halves, placed = state
+        piece, first, second, whole, halves, placed, now = state
+        held.update(now)
         for builder, value in zip(builders, placed):
             builder.whole = value
         send_x, send_y = [], []
@@ -235,6 +236,7 @@
         if whole is not None:
             i, k = items[at - 3]
             builders[i].put(k, whole)
+        work(at - mv.planes - 3, placed[0])
         first, second, whole = new_first, new_second, new_whole
     arrived = [jnp.concatenate(arrived[i : i + 2], 0) for i in range(0, len(arrived), 2)]
     return [b.done() for b in builders], late, arrived
@@ -261,15 +263,12 @@
     items = [(i, k) for i in range(len(arrays)) for k in [*range(1, mv.planes), 0]]
     rings = [None] * len(arrays)
     sources = [None] * len(arrays)
-    results = {}
     starts = []
     first = second = None
-    for at in range(max(len(items) + 2, mv.planes + 6)):
+    for at in range(max(len(items) + 2, 9 + mv.planes // 2)):
         if at < len(items) and sources[items[at][0]] is None:
             sources[items[at][0]] = arrays[items[at][0]]()
-        first, second, sources, rings, results, now = fence(
-            (first, second, sources, rings, results, held)
-        )
+        first, second, sources, rings, now = fence((first, second, sources, rings, held))
         held.update(now)
         new_first = new_second = None
         send_x, send_y = [], []
@@ -295,8 +294,11 @@
                 start = 0
             starts.append(start)
         if send_x:
-            got_x = mv.over_x(jnp.concatenate(send_x, 0))
-            got_y = mv.over_y(jnp.concatenate(send_y, 0))
+            send_x, send_y, second, now = fence(
+                (jnp.concatenate(send_x, 0), jnp.concatenate(send_y, 0), second, held)
+            )
+            held.update(now)
+            got_x, got_y = mv.over_x(send_x), mv.over_y(send_y)
         if first is not None:
             if joined or not fresh:
                 more_x, more_y = got_x, got_y
@@ -319,10 +321,9 @@
             if k != 0:
                 rings[i] = mv.up(total.astype(BF))
             else:
-                results[i] = total
+                held[f"sum{i}"] = total
         work(at)
         first, second = new_first, new_second
-    return [results[i] for i in range(len(arrays))]
 
 
 def swap_halves(mv, total):
@@ -375,49 +376,69 @@
             [pad_rows(down_weight), gate_weight, bias_rows, pad_rows(up_weight)], 0
         )
         rounds = 2 * mv.planes
-        (w_qkv, w_out), ffn, cots = gather_weights(
-            mv,
-            [jnp.concatenate([q_weight, kv_weight, small], 1), out_weight],
-            ffn,
-            rounds,
-            cotangent,
-            list(range(rounds - 3, rounds + 3)),
-        )
-        cots = [cotangent, *cots]
-        ffn = lax.all_gather(ffn, "dp", axis=0, tiled=True, axis_index_groups=mv.squares())
-        w_query = w_qkv[:, :D]
-        w_keyval = w_qkv[:, D : D + 2 * HD]
-        small = w_qkv[:, D + 2 * HD :].T.astype(F32)
-        gain_one, gain_two, bias_down = small[0], small[1], small[2]
-
         x_value = tokens.astype(F32)
-        norm_one_b = rms_scale(x_value, gain_one).astype(BF)
         cosine, sine = angles(doc_positions)
-        q_lin = dot_nn(norm_one_b, w_query).reshape(rows, H, HD)
-        kv_lin = dot_nn(norm_one_b, w_keyval)
-        query = (
-            (rotate(q_lin, cosine[:, None, :], sine[:, None, :]) * head_scale)
-            .astype(BF)
-            .reshape(seqs, LENGTH, H, HD)
-        )
-        key = rotate(kv_lin[:, :HD], cosine, sine).astype(BF).reshape(seqs, LENGTH, HD)
-        value = kv_lin[:, HD:].astype(BF).reshape(seqs, LENGTH, HD)
         index = jnp.arange(LENGTH)
         distance = index[:, None] - index[None, :]
         allowed = (distance[None] >= 0) & (
             distance[None] <= doc_positions.reshape(seqs, LENGTH)[:, :, None]
         )
-        logits = jnp.einsum("sqhd,skd->shqk", query, key, preferred_element_type=F32)
-        logits = jnp.where(allowed[:, None], logits, -1e30)
-        top = jnp.max(logits, axis=-1, keepdims=True)
-        weights = jnp.exp(logits - top)
-        soft = weights / jnp.sum(weights, axis=-1, keepdims=True)
-        probs = soft.astype(BF)
-        attended = (
-            jnp.einsum("shqk,skd->sqhd", probs, value, preferred_element_type=F32)
-            .reshape(rows, H * HD)
-            .astype(BF)
+        held = {}
+
+        def split_qkv(w_qkv):
+            small = w_qkv[:, D + 2 * HD :].T.astype(F32)
+            return w_qkv[:, :D], w_qkv[:, D : D + 2 * HD], small
+
+        def attention(at, w_qkv):
+            if at == 1:
+                w_query, w_keyval, small = split_qkv(w_qkv)
+                norm_one_b = rms_scale(x_value, small[0]).astype(BF)
+                held["norm_one"] = norm_one_b
+                q_lin = dot_nn(norm_one_b, w_query).reshape(rows, H, HD)
+                query = rotate(q_lin, cosine[:, None, :], sine[:, None, :]) * head_scale
+                held["query"] = query.astype(BF).reshape(seqs, LENGTH, H, HD)
+                held["kv"] = dot_nn(norm_one_b, w_keyval)
+            if at == 2:
+                kv_lin = held.pop("kv")
+                key = rotate(kv_lin[:, :HD], cosine, sine).astype(BF)
+                held["key"] = key.reshape(seqs, LENGTH, HD)
+                held["value"] = kv_lin[:, HD:].astype(BF).reshape(seqs, LENGTH, HD)
+                logits = jnp.einsum(
+                    "sqhd,skd->shqk", held["query"], held["key"], preferred_element_type=F32
+                )
+                held["logits"] = jnp.where(allowed[:, None], logits, -1e30)
+            if at == 3:
+                logits = held.pop("logits")
+                weights = jnp.exp(logits - jnp.max(logits, axis=-1, keepdims=True))
+                held["soft"] = weights / jnp.sum(weights, axis=-1, keepdims=True)
+                held["probs"] = held["soft"].astype(BF)
+                held["attended"] = (
+                    jnp.einsum(
+                        "shqk,skd->sqhd",
+                        held["probs"],
+                        held["value"],
+                        preferred_element_type=F32,
+                    )
+                    .reshape(rows, H * HD)
+                    .astype(BF)
+                )
+
+        (w_qkv, w_out), ffn, cots = gather_weights(
+            mv,
+            [jnp.concatenate([q_weight, kv_weight, small], 1), out_weight],
+            ffn,
+            rounds - 2,
+            cotangent,
+            [mv.planes - 1, *range(rounds - 2, rounds + 3)],
+            held,
+            attention,
         )
+        cots = [cotangent, *cots]
+        w_query, w_keyval, small = split_qkv(w_qkv)
+        gain_one, gain_two, bias_down = small[0], small[1], small[2]
+        norm_one_b, query, key, value = (held[k] for k in ("norm_one", "query", "key", "value"))
+        soft, probs, attended = (held[k] for k in ("soft", "probs", "attended"))
+        ffn = lax.all_gather(ffn, "dp", axis=0, tiled=True, axis_index_groups=mv.squares())
         hidden_one = x_value + dot_nn(attended, w_out)
         norm_two_b = rms_scale(hidden_one, gain_two).astype(BF)
 
@@ -426,43 +447,36 @@
         swap_early = [attended, norm_one_b]
         swapped = []
 
-        def linear(step):
-            return dot_nt(norm_pieces[step], w_both) + bias_both, dot_nt(cot_pieces[step], w_down)
-
-        def pick(both, which):
-            return jnp.concatenate(
-                [
-                    both[:, (2 * i + which) * padded : (2 * i + which + 1) * padded]
-                    for i in range(4)
-                ],
-                1,
-            )
-
-        def nonlinear(both, grad_act):
-            act, act_back = jax.vjp(glu_tanh, pick(both, 0), pick(both, 1))
-            grad_gate, grad_up = act_back(grad_act)
-            parts = []
-            for i in range(4):
-                parts.append(grad_gate[:, i * padded : (i + 1) * padded])
-                parts.append(grad_up[:, i * padded : (i + 1) * padded])
-            grads = jnp.concatenate(parts, 1).astype(BF)
-            partial = dot_nn(grads, w_both)
-            return act.astype(BF), grads, partial[:rows], partial[rows:].astype(BF)
-
-        acts, grads_all = [], []
-        sends, received, parts, gots = {}, None, {}, {}
+        def piece_work(step):
+            gate = dot_nt(norm_pieces[step], w_gate) + b_gate
+            up = dot_nt(norm_pieces[step], w_up) + b_up
+            grad_act = dot_nt(cot_pieces[step], w_down)
+            act, act_back = jax.vjp(glu_tanh, gate, up)
+            grad_gate, grad_up = (v.astype(BF) for v in act_back(grad_act))
+            partial = dot_nn(grad_gate, w_gate) + dot_nn(grad_up, w_up)
+            return act.astype(BF), grad_gate, grad_up, partial[:rows], partial[rows:].astype(BF)
+
+        acts, grads_all = [], ([], [])
+        sends, received, parts, gots, partials = {}, None, {}, {}, None
         last = mv.planes + 1
         for at in range(last + 1):
-            norms, cots, swap_early, sends, norm_pieces, cot_pieces, acts, grads_all = fence(
-                (norms, cots, swap_early, sends, norm_pieces, cot_pieces, acts, grads_all)
+            norms, cots, swap_early, norm_pieces, cot_pieces, acts, grads_all = fence(
+                (norms, cots, swap_early, norm_pieces, cot_pieces, acts, grads_all)
             )
+            if at == last:
+                sends, norm_pieces, acts, grads_all = fence((sends, norm_pieces, acts, grads_all))
             if at == 1:
                 ffn = ffn.reshape(4, 3 * padded, D)
-                w_down = ffn[:, :padded].reshape(4 * padded, D)
-                w_both = ffn[:, padded:].reshape(8 * padded, D)
-                bias_both = ffn[:, padded + units : padded + units + 2, :padded].reshape(8 * padded)
-                bias_both = bias_both.astype(F32)
-                w_down, w_both, bias_both, norms = fence((w_down, w_both, bias_both, norms))
+                w_down, w_gate, w_up = (
+                    ffn[:, i * padded : (i + 1) * padded].reshape(4 * padded, D) for i in range(3)
+                )
+                b_gate, b_up = (
+                    ffn[:, padded + units + i, :padded].reshape(4 * padded).astype(F32)
+                    for i in range(2)
+                )
+                w_down, w_gate, w_up, b_gate, b_up, norm_pieces = fence(
+                    (w_down, w_gate, w_up, b_gate, b_up, norm_pieces)
+                )
             if at <= mv.planes - 2:
                 norms.append(mv.up(norms[at]))
             if 4 + at < mv.planes:
@@ -472,25 +486,37 @@
             if at < mv.planes:
                 norm_pieces.append(jnp.concatenate([norms[at], mv.other(norms[at])], 0))
                 cot_pieces.append(jnp.concatenate([cots[at], mv.other(cots[at])], 0))
-            if 1 <= at <= len(swap_early):
-                early = swap_early[at - 1]
+            if at in (0, mv.planes):
+                early = swap_early[min(at, 1)]
                 swapped.append(jnp.concatenate([early, mv.other(early)], 0))
             step = at - 1
             if 0 <= step < mv.planes:
-                act, grads, own_part, their_part = nonlinear(*linear(step))
+                act, grad_gate, grad_up, own_part, their_part = piece_work(step)
                 acts.append(act)
-                grads_all.append(grads)
+                grads_all[0].append(grad_gate)
+                grads_all[1].append(grad_up)
                 parts[step] = own_part
                 gots[step] = mv.other(their_part)
             if at == last:
                 acts = jnp.concatenate(acts, 0)
-                grads_all = jnp.concatenate(grads_all, 0)
+                grads_all = [jnp.concatenate(v, 0) for v in grads_all]
                 cot_all = jnp.concatenate(cot_pieces, 0)
                 norm_all = jnp.concatenate(norm_pieces, 0)
-                down_partial = dot_tn(acts, cot_all, BF)
-                both_partial = dot_tn(grads_all, norm_all, BF)
-                down_partial, both_partial = fence((down_partial, both_partial))
-            norms, cots, norm_pieces, cot_pieces, swapped, acts, grads_all, parts, gots, received = (
+                partials = [dot_tn(acts, cot_all, BF)]
+                partials += [dot_tn(v, norm_all, BF) for v in grads_all]
+            (
+                norms,
+                cots,
+                norm_pieces,
+                cot_pieces,
+                swapped,
+                acts,
+                grads_all,
+                parts,
+                gots,
+                received,
+                partials,
+            ) = (
                 fence(
                     (
                         norms,
@@ -503,6 +529,7 @@
                         parts,
                         gots,
                         received,
+                        partials,
                     )
                 )
             )
@@ -516,25 +543,23 @@
                     sends[done] = total.astype(BF)
         grad_norm_two = total
         attended_both, norm_both = swapped
-        ffn_groups = mv.squares()
-        down_sum = lax.psum_scatter(
-            down_partial, "dp", scatter_dimension=0, tiled=True, axis_index_groups=ffn_groups
-        )
-        both_sum = lax.psum_scatter(
-            both_partial, "dp", scatter_dimension=0, tiled=True, axis_index_groups=ffn_groups
-        )
+        ffn_sums = [
+            lax.psum_scatter(
+                v, "dp", scatter_dimension=0, tiled=True, axis_index_groups=mv.squares()
+            )
+            for v in partials
+        ]
+
         _, norm_two_back = jax.vjp(rms_scale, hidden_one, gain_two)
         grad_rms_two, grad_gain_two = norm_two_back(grad_norm_two)
         grad_hidden = cotangent.astype(F32) + grad_rms_two
         grad_hidden_b = grad_hidden.astype(BF)
 
-        half_columns = core_half(mv, grad_hidden_b)
-        grad_attended = dot_nt(grad_hidden_b, w_out).astype(BF).reshape(seqs, LENGTH, H, HD)
-        out_partial = dot_tn(attended_both, half_columns, BF)
-        out_partial, grad_attended, grads_all, acts = fence(
-            (out_partial, grad_attended, grads_all, acts)
+        out_partial = dot_tn(attended_both, core_half(mv, grad_hidden_b), BF)
+        out_partial, grad_hidden_b, grads_all, acts = fence(
+            (out_partial, grad_hidden_b, grads_all, acts)
         )
-        held = {"grads": grads_all, "acts": acts, "attended": grad_attended}
+        held = {"grads": grads_all, "acts": acts}
 
         def scores_back(grad_attended):
             grad_probs = jnp.einsum(
@@ -566,11 +591,16 @@
 
         def work(at):
             if at == 0:
-                branch = dot_nn(held.pop("acts"), w_down).reshape(mv.planes, 2, rows, D)
-                held["own"] = branch[:, 0]
-                held["got"] = mv.other(branch[:, 1].astype(BF))
-                bias = jnp.sum(held.pop("grads"), axis=0, dtype=F32)
-                held["bias"] = bias.reshape(2, 2, 2, padded)[..., :units]
+                grad_attended = dot_nt(grad_hidden_b, w_out).astype(BF)
+                held["attended"] = grad_attended.reshape(seqs, LENGTH, H, HD)
+                acts_two = held.pop("acts").reshape(mv.planes, 2, rows, 4 * padded)
+                mine, theirs = (
+                    dot_nn(acts_two[:, i].reshape(mv.planes * rows, 4 * padded), w_down)
+                    .astype(BF)
+                    .reshape(mv.planes, rows, D)
+                    for i in (0, 1)
+                )
+                held["branch"], held["got"] = mine, mv.other(theirs)
             if at == 1:
                 held["scores"] = scores_back(held["attended"])
             if at == 2:
@@ -578,6 +608,7 @@
             if at == 3:
                 half = jnp.concatenate([core_half(mv, held["q"]), core_half(mv, held["kv"])], 1)
                 held["partial"] = dot_tn(norm_both, half, BF)
+            if at == 4:
                 grad_norm_one = dot_nt(held.pop("q"), w_query) + dot_nt(held.pop("kv"), w_keyval)
                 _, norm_one_back = jax.vjp(rms_scale, x_value, gain_one)
                 grad_rms_one, grad_gain_one = norm_one_back(grad_norm_one)
@@ -587,44 +618,47 @@
                 small = jnp.stack([grad_gain_one, grad_gain_two, down_bias_sum])
                 small = small.reshape(3, mv.planes, 2, 2, 2, part).transpose(2, 3, 4, 1, 0, 5)
                 held["small"] = small
+                bias = jnp.stack([jnp.sum(v, axis=0, dtype=F32) for v in held.pop("grads")])
+                bias = bias.reshape(2, 2, 2, padded)[..., :units]
+                held["bias"] = bias.transpose(1, 2, 0, 3)
             for stage, (coordinate, move) in enumerate(
                 ((mv.y, mv.over_y), (mv.x, mv.over_x), (mv.core, mv.other))
             ):
-                if at == 4 + stage:
+                if at == 5 + stage:
                     for name in ("small", "bias")[: 2 if stage < 2 else 1]:
                         whole = held[name]
                         keep = lax.dynamic_index_in_dim(whole, coordinate, 0, keepdims=False)
                         away = lax.dynamic_index_in_dim(whole, 1 - coordinate, 0, keepdims=False)
                         held[name] = keep + move(away)
-            step = at - 6
-            if 0 < step < mv.planes:
-                away = lax.dynamic_index_in_dim(
-                    held["small"], (mv.z + step) % mv.planes, 0, keepdims=False
-                )
-                held["small_sum"] = held.get("small_sum", 0.0) + mv.up(away, step)
+            for step in range(1, mv.planes):
+                if at == 8 + (step - 1) // 2:
+                    away = lax.dynamic_index_in_dim(
+                        held["small"], (mv.z + step) % mv.planes, 0, keepdims=False
+                    )
+                    held["small_sum"] = held.get("small_sum", 0.0) + mv.up(away, step)
+
             ring = at - 1
             if 0 <= ring < mv.planes:
                 at_piece = order[ring]
-                branch = held["own"][at_piece] + held["got"][at_piece].astype(F32)
+                branch = held["branch"][at_piece].astype(F32) + held["got"][at_piece].astype(F32)
                 if ring > 0:
-                    branch = branch + held.pop("branch").astype(F32)
+                    branch = branch + held.pop("ring").astype(F32)
                 if ring < mv.planes - 1:
-                    held["branch"] = mv.up(branch.astype(BF))
+                    held["ring"] = mv.up(branch.astype(BF))
                 else:
                     held["output"] = (hidden_one + branch + bias_down).astype(BF)
-
-        out_total, lin_total = scatter_grads(
+            if at == mv.planes + 4:
+                held["out_grad"] = jnp.concatenate(swap_halves(mv, held.pop("sum0")), 1)
+                held["ffn"] = [v[:units].astype(F32) for v in ffn_sums]
+
+        scatter_grads(
             mv, [lambda: out_partial, lambda: held.pop("partial")], D, held, work
         )
-        out_total, lin_total, down_sum, both_sum = fence((out_total, lin_total, down_sum, both_sum))
         small = held["small_sum"] + lax.dynamic_index_in_dim(
             held["small"], mv.z, 0, keepdims=False
         )
-        down_grad = down_sum[:units].astype(F32)
-        gate_grad = both_sum[:units].astype(F32)
-        up_grad = both_sum[padded : padded + units].astype(F32)
-        out_grad = jnp.concatenate(swap_halves(mv, out_total), 1)
-        first, second = swap_halves(mv, lin_total)
+        down_grad, gate_grad, up_grad = held["ffn"]
+        first, second = swap_halves(mv, held["sum1"])
         q_grad = jnp.concatenate([first[:, : D // 2], second[:, : D // 2]], 1)
         kv_grad = jnp.concatenate([first[:, D // 2 :], second[:, D // 2 :]], 1)
 
@@ -634,7 +668,7 @@
             small[0],
             q_grad,
             kv_grad,
-            out_grad,
+            held["out_grad"],
             small[1],
             gate_grad,
             held["bias"][0],

time: 991 us -> 950 us (0.959)
  local copies, waits for them, and re-layouts: 149 us -> 126 us
  matrix products: 215 us -> 231 us
  waiting for transfers between devices: 312 us -> 297 us
  other arithmetic: 136 us -> 125 us
    dot_general x8 -> x13, matrix products: 57.3 us -> 79.2 us  [dot_nn(): return jnp.dot(left, right, preferred_element_type=F32)]
    all_gather x1, waiting for transfers between devices: 20.7 us -> 0.01 us  [body(): lax.all_gather(ffn, 'dp', axis=0, tiled=True, axis_index_groups=mv.square...]
    slice x17 -> x13, local copies, waits for them, and re-layouts: 20.2 us -> 12.8 us  [the longest x1 6.36 us: body(): ffn[:, i * padded:(i + 1) * padded].reshape(4 * padded, D)]
    dot_general x11 -> x15, matrix products: 88.7 us -> 83.4 us  [dot_nt(): lax.dot_general(left, right, (((1,), (1,)), ((), ())), preferred_element_...]
    unnamed x378 -> x312, local copies, waits for them, and re-layouts: 63.7 us -> 58.4 us
    convert_element_type x11 -> x10, other arithmetic: 25.3 us -> 20.9 us  [the longest x3 9.03 us: work(): held['ffn'] = [v[:units].astype(F32) for v in ffn_sums]]
    dot_general x4 -> x5, matrix products: 59.6 us -> 61.3 us  [dot_tn(): lax.dot_general(left, right, (((0,), (0,)), ((), ())), preferred_element_...]
  transfers between devices with their start and end apart: 106 -> 107, of which waited for: 38 -> 45; matrix products, arithmetic and copies ran while one was open for 41% -> 40% of each run, Pallas kernels for 6% -> 6%
where the time goes in v3:
time: 950 us; the launch traced here: 945 us
  waiting for transfers between devices  297 us (31%)
  matrix products  231 us (24%)
  local copies, waits for them, and re-layouts  126 us (13%)
  other arithmetic  125 us (13%)
  starting transfers between devices  89.1 us (9%)
  Pallas kernels  60 us (6%)
  between operations  16.9 us (2%)
    ppermute x30, waiting for transfers between devices, up(): lax.ppermute(value, 'dp', [(i, (i + 8 * steps) % self.n) for i in range(s...  210 us
    ppermute x73, waiting for transfers between devices, flip(): return lax.ppermute(value, 'dp', [(i, i ^ bit) for i in range(self.n)])  86.2 us
    dot_general x15, matrix products, dot_nt(): lax.dot_general(left, right, (((1,), (1,)), ((), ())), preferred_element_...  83.4 us
    dot_general x13, matrix products, dot_nn(): return jnp.dot(left, right, preferred_element_type=F32)  79.2 us
    dot_general x5, matrix products, dot_tn(): lax.dot_general(left, right, (((0,), (0,)), ((), ())), preferred_element_...  61.3 us
    pallas_call x8, Pallas kernels, put(): pl.pallas_call(place_kernel, out_shape=self.shape, grid_spec=pltpu.Prefet...  60 us
    unnamed x312, local copies, waits for them, and re-layouts  58.4 us
    ppermute x73, starting transfers between devices, flip(): return lax.ppermute(value, 'dp', [(i, i ^ bit) for i in range(self.n)])  53.5 us
  transfers between devices with their start and end apart: 107, of which 45 were waited for; matrix products, arithmetic and copies ran while one was open for 40% of the time, Pallas kernels for 6%

profile of v3, /device:TPU:0, one launch (start us, length us, event | category | flops | bytes accessed | tf_op | source)
XLA Modules:
  0.0 944.6 jit_solution(14114221530756462382)
XLA Ops:
  19.5 10.7 %collective-permute-done = bf16[80,3200]{1,0:T(8,128)(2,1)S(1)} collective-permute-done((bf16[80,3200]{1,0:T(8,128)(2,1)S(1)}, bf16[80,3200]{1,0:T(8,128)(2,1)S(1)}, u32[]{:S(2)}, u32[]{:S(2)}) %collective-permute-start) | collective-permute-done | bytes 512032 | tf_op jit(solution)/shard_map/ppermute | solution.py:100
  34.7 12.6 %collective-permute-done.3 = bf16[80,3200]{1,0:T(8,128)(2,1)S(1)} collective-permute-done((bf16[80,3200]{1,0:T(8,128)(2,1)S(1)}, bf16[80,3200]{1,0:T(8,128)(2,1)S(1)}, u32[]{:S(2)}, u32[]{:S(2)}) %collective-permute-start.3) | collective-permute-done | bytes 512032 | tf_op jit(solution)/shard_map/ppermute | solution.py:100
  53.9 13.8 %collective-permute-done.6 = bf16[80,3200]{1,0:T(8,128)(2,1)S(1)} collective-permute-done((bf16[80,3200]{1,0:T(8,128)(2,1)S(1)}, bf16[80,3200]{1,0:T(8,128)(2,1)S(1)}, u32[]{:S(2)}, u32[]{:S(2)}) %collective-permute-start.6) | collective-permute-done | bytes 512032 | tf_op jit(solution)/shard_map/ppermute | solution.py:100
  79.8 7.8 place_rows.8.refs_0_
  87.6 9.6 %collective-permute-done.13 = bf16[128,2560]{1,0:T(8,128)(2,1)} collective-permute-done((bf16[128,2560]{1,0:T(8,128)(2,1)}, bf16[128,2560]{1,0:T(8,128)(2,1)}, u32[]{:S(2)}, u32[]{:S(2)}) %collective-permute-start.13) | collective-permute-done | bytes 655392 | tf_op jit(solution)/shard_map/ppermute | solution.py:100
  104.9 5.7 collective-permute-done.17
  111.8 7.7 place_rows.9.refs_0_
  130.0 7.7 place_rows.10.refs_0_
  156.5 8.1 place_rows.11
  164.5 14.1 %collective-permute-done.24 = bf16[80,2560]{1,0:T(8,128)(2,1)S(1)} collective-permute-done((bf16[80,2560]{1,0:T(8,128)(2,1)S(1)}, bf16[80,2560]{1,0:T(8,128)(2,1)S(1)}, u32[]{:S(2)}, u32[]{:S(2)}) %collective-permute-start.24) | collective-permute-done | bytes 409632 | tf_op jit(solution)/shard_map/ppermute | solution.py:100
  192.7 7.3 place_rows.12.refs_0_
  200.0 19.7 %collective-permute-done.29 = bf16[120,2560]{1,0:T(8,128)(2,1)} collective-permute-done((bf16[120,2560]{1,0:T(8,128)(2,1)}, bf16[120,2560]{1,0:T(8,128)(2,1)}, u32[]{:S(2)}, u32[]{:S(2)}) %collective-permute-start.29) | collective-permute-done | bytes 614432 | tf_op jit(solution)/shard_map/ppermute | solution.py:78
  240.0 8.4 fusion.2
  249.5 7.1 place_rows.13.refs_0_
  272.4 7.1 place_rows.14.refs_0_
  283.5 6.1 collective-permute-done.38
  290.2 7.1 place_rows.15
  319.9 26.7 %collective-permute-done.40 = bf16[256,2560]{1,0:T(8,128)(2,1)} collective-permute-done((bf16[256,2560]{1,0:T(8,128)(2,1)S(1)}, bf16[256,2560]{1,0:T(8,128)(2,1)}, u32[]{:S(2)}, u32[]{:S(2)}) %collective-permute-start.40) | collective-permute-done | bytes 1310752 | tf_op jit(solution)/shard_map/ppermute | solution.py:100
  347.4 6.4 fusion.166
  360.4 6.0 fusion.52
  387.5 5.4 fusion.59
  392.9 16.4 %fusion.175 = f32[512,2560]{1,0:T(8,128)S(1)} fusion(bf16[512,1024]{1,0:T(8,128)(2,1)S(1)} %get-tuple-element.900, bf16[1024,2560]{1,0:T(8,128)(2,1)} %bitcast.313), kind=kOutput, calls=%fused_computation.456 | convolution fusion | flops 2684354560 | bytes 11534336 | tf_op jit(solution)/shard_map/dot_general | solution.py:60
  420.7 26.7 %collective-permute-done.48 = bf16[256,2560]{1,0:T(8,128)(2,1)} collective-permute-done((bf16[256,2560]{1,0:T(8,128)(2,1)}, bf16[256,2560]{1,0:T(8,128)(2,1)}, u32[]{:S(2)}, u32[]{:S(2)}) %collective-permute-start.48) | collective-permute-done | bytes 1310752 | tf_op jit(solution)/shard_map/ppermute | solution.py:100
  458.7 6.7 fusion.66
  465.4 5.2 fusion.178
  480.8 8.7 collective-permute-done.55
  489.5 6.7 fusion.179
  503.7 7.5 fusion.73
  511.2 5.2 fusion.181
  523.5 11.5 %collective-permute-done.58 = bf16[256,2560]{1,0:T(8,128)(2,1)} collective-permute-done((bf16[256,2560]{1,0:T(8,128)(2,1)}, bf16[256,2560]{1,0:T(8,128)(2,1)}, u32[]{:S(2)}, u32[]{:S(2)}) %collective-permute-start.58) | collective-permute-done | bytes 1310752 | tf_op jit(solution)/shard_map/ppermute | solution.py:100
  547.7 16.2 %convolution_convert_fusion.2 = bf16[1024,2560]{1,0:T(8,128)(2,1)} fusion(bf16[2048,1024]{1,0:T(8,128)(2,1)S(1)} %constant_dynamic-update-slice_fusion.24, bf16[2048,2560]{1,0:T(8,128)(2,1)} %copy-done.76), kind=kOutput, calls=%fused_computation.20 | convolution fusion | flops 10740039680 | bytes 19922944 | tf_op jit(solution)/shard_map/dot_general | solution.py:50
  572.8 15.1 %fusion.14 = bf16[1024,2560]{1,0:T(8,128)(2,1)} fusion(bf16[2048,1024]{1,0:T(8,128)(2,1)S(1)} %constant_dynamic-update-slice_fusion.16, bf16[512,2560]{1,0:T(8,128)(2,1)} %copy-done.43, bf16[512,2560]{1,0:T(8,128)(2,1)} %pad_maximum_fusion.6, bf16[512,2560]{1,0:T(8,128)(2,1)S(1)} %copy-done.41, bf16[512,2560]{1,0:T(8,128)(2,1)S(1)} %copy-done.39), kind=kOutput, calls=%fused_computation.22 | convolution fusion | flops 10781982720 | bytes 19922944 | tf_op jit(solution)/shard_map/dot_general | solution.py:50
  587.9 16.9 %convolution_convert_fusion.3 = bf16[1024,2560]{1,0:T(8,128)(2,1)} fusion(bf16[2048,1024]{1,0:T(8,128)(2,1)} %constant_dynamic-update-slice_fusion.20, bf16[2048,2560]{1,0:T(8,128)(2,1)} %copy-done.76), kind=kOutput, calls=%fused_computation.21 | convolution fusion | flops 10740039680 | bytes 19922944 | tf_op jit(solution)/shard_map/dot_general | solution.py:50
  619.5 5.7 convolution_convert_fusion.1
  629.3 10.2 %convolution_convert_fusion.4 = bf16[1024,2560]{1,0:T(8,128)(2,1)} fusion(bf16[1024,1024]{1,0:T(8,128)(2,1)S(1)} %bitcast.323, bf16[1024,2560]{1,0:T(8,128)(2,1)} %bitcast.308), kind=kOutput, calls=%fused_computation.23 | convolution fusion | flops 5371330560 | bytes 12582912 | tf_op jit(solution)/shard_map/dot_general | solution.py:60
  641.8 10.4 %convolution_convert_fusion.5 = bf16[1024,2560]{1,0:T(8,128)(2,1)} fusion(bf16[1024,1024]{1,0:T(8,128)(2,1)} %bitcast.322, bf16[1024,2560]{1,0:T(8,128)(2,1)} %bitcast.309), kind=kOutput, calls=%fused_computation.24 | convolution fusion | flops 5371330560 | bytes 12582912 | tf_op jit(solution)/shard_map/dot_general | solution.py:60
  652.3 9.4 convolution_convert_fusion.6
  680.2 20.5 %collective-permute-done.64 = bf16[240,1280]{1,0:T(8,128)(2,1)S(1)} collective-permute-done((bf16[240,1280]{1,0:T(8,128)(2,1)}, bf16[240,1280]{1,0:T(8,128)(2,1)S(1)}, u32[]{:S(2)}, u32[]{:S(2)}) %collective-permute-start.64) | collective-permute-done | bytes 614432 | tf_op jit(solution)/shard_map/ppermute | solution.py:78
  721.1 29.2 %collective-permute-done.69 = bf16[160,1280]{1,0:T(8,128)(2,1)S(1)} collective-permute-done((bf16[160,1280]{1,0:T(8,128)(2,1)S(1)}, bf16[160,1280]{1,0:T(8,128)(2,1)S(1)}, u32[]{:S(2)}, u32[]{:S(2)}) %collective-permute-start.69) | collective-permute-done | bytes 409632 | tf_op jit(solution)/shard_map/ppermute | solution.py:100
  766.7 7.3 convolution_convert_fusion
  774.0 23.7 %collective-permute-done.75 = bf16[160,1280]{1,0:T(8,128)(2,1)S(1)} collective-permute-done((bf16[160,1280]{1,0:T(8,128)(2,1)S(1)}, bf16[160,1280]{1,0:T(8,128)(2,1)S(1)}, u32[]{:S(2)}, u32[]{:S(2)}) %collective-permute-start.75) | collective-permute-done | bytes 409632 | tf_op jit(solution)/shard_map/ppermute | solution.py:100
  812.1 12.1 %fusion.26 = (f32[2560]{0:T(1024)}, f32[256]{0:T(256)S(1)}, f32[256,2560]{1,0:T(8,128)}) fusion(bf16[256,2560]{1,0:T(8,128)(2,1)S(1)} %copy-done.8, f32[256]{0:T(256)S(1)} %copy-done.111, f32[2560]{0:T(1024)S(1)} %copy-done.101, f32[256,2560]{1,0:T(8,128)} %fusion.40, bf16[256,2560]{0,1:T(8,128)(2,1)} %bitcast.303, bf16[2560,3200]{1,0:T(8,128)(2,1)} %place_rows.11), kind=kOutput, calls=%fused_computation.54 | convolution fusion | flops 3360683264 | bytes 20994048 | tf_op jit(solution)/shard_map/dot_general | solution.py:56
  824.3 6.3 fusion.28
  832.4 4.8 collective-permute-done.77
  867.1 5.5 collective-permute-start.88
  885.7 4.7 collective-permute-start.93
  901.9 7.4 collective-permute-done.91
  921.4 4.7 collective-permute-done.95
  (770 shorter events, 417.9 us)
Async XLA Ops:
  7.3 340.1 %all-gather.2.cloned.1.call-start = ((), (), s32[]{:S(2)}) async-start(), calls=%async_computation.3 | async-start | bytes 19660800 | tf_op jit(solution)/shard_map/all_gather | solution.py:441
  74.5 24.5 %collective-permute-start.12 = (bf16[320,3200]{1,0:T(8,128)(2,1)}, bf16[320,3200]{1,0:T(8,128)(2,1)}, u32[]{:S(2)}, u32[]{:S(2)}) collective-permute-start(bf16[320,3200]{1,0:T(8,128)(2,1)} %slice_dynamic-update-slice_fusion.14.mine), channel_id=1, source_target_pairs={{0,1},{1,0},{2,3},{3,2},{4,5},{5,4},{6,7},{7,6},{8,9},{9,8},{10,11... | collective-permute-start | bytes 6144008 | tf_op jit(solution)/shard_map/ppermute | solution.py:78
  75.8 21.5 %collective-permute-start.10 = (bf16[120,3200]{1,0:T(8,128)(2,1)}, bf16[120,3200]{1,0:T(8,128)(2,1)S(1)}, u32[]{:S(2)}, u32[]{:S(2)}) collective-permute-start(bf16[120,3200]{1,0:T(8,128)(2,1)} %get-tuple-element.1249), channel_id=1, source_target_pairs={{0,2},{1,3},{2,0},{3,1},{4,6},{5,7},{6,4},{7,5},{8,10},{9,11},{10,... | collective-permute-start | bytes 2304008 | tf_op jit(solution)/shard_map/ppermute | solution.py:78
  123.1 20.6 %collective-permute-start.23 = (bf16[320,3200]{1,0:T(8,128)(2,1)S(1)}, bf16[320,3200]{1,0:T(8,128)(2,1)}, u32[]{:S(2)}, u32[]{:S(2)}) collective-permute-start(bf16[320,3200]{1,0:T(8,128)(2,1)S(1)} %constant_dynamic-update-slice_fusion.5.mine), channel_id=1, source_target_pairs={{0,1},{1,0},{2,3},{3,2},{4,5},{5,4},{6,7},{7,6},{8,9},{9,8},{10,11... | collective-permute-start | bytes 6144008 | tf_op jit(solution)/shard_map/ppermute | solution.py:78
  148.7 30.0 %collective-permute-start.27 = (bf16[320,2560]{1,0:T(8,128)(2,1)S(1)}, bf16[320,2560]{1,0:T(8,128)(2,1)}, u32[]{:S(2)}, u32[]{:S(2)}) collective-permute-start(bf16[320,2560]{1,0:T(8,128)(2,1)S(1)} %slice_dynamic-update-slice_fusion.22.mine), channel_id=1, source_target_pairs={{0,1},{1,0},{2,3},{3,2},{4,5},{5,4},{6,7},{7,6},{8,9},{9,8},{10,11... | collective-permute-start | bytes 4915208 | tf_op jit(solution)/shard_map/ppermute | solution.py:78
  150.9 27.7 %collective-permute-start.28 = (bf16[128,2560]{1,0:T(8,128)(2,1)}, bf16[128,2560]{1,0:T(8,128)(2,1)}, u32[]{:S(2)}, u32[]{:S(2)}) collective-permute-start(bf16[128,2560]{1,0:T(8,128)(2,1)} %get-tuple-element.665), channel_id=1, source_target_pairs={{0,8},{1,9},{2,10},{3,11},{4,12},{5,13},{6,14},{7,15},{8,16},{9,17... | collective-permute-start | bytes 1966088 | tf_op jit(solution)/shard_map/ppermute | solution.py:100
  152.3 697.5 %reduce-scatter.8.cloned.1.call-start = ((), (), s32[]{:S(2)}) async-start(), calls=%async_computation.6 | async-start | bytes 6553600 | tf_op jit(solution)/shard_map/reduce_scatter | solution.py:547
  153.4 25.2 %collective-permute-start.25 = (bf16[120,2560]{1,0:T(8,128)(2,1)}, bf16[120,2560]{1,0:T(8,128)(2,1)}, u32[]{:S(2)}, u32[]{:S(2)}) collective-permute-start(bf16[120,2560]{1,0:T(8,128)(2,1)} %get-tuple-element.1257), channel_id=1, source_target_pairs={{0,2},{1,3},{2,0},{3,1},{4,6},{5,7},{6,4},{7,5},{8,10},{9,11},{10,... | collective-permute-start | bytes 1843208 | tf_op jit(solution)/shard_map/ppermute | solution.py:78
  154.6 24.1 %collective-permute-start.26 = (bf16[120,2560]{1,0:T(8,128)(2,1)}, bf16[120,2560]{1,0:T(8,128)(2,1)}, u32[]{:S(2)}, u32[]{:S(2)}) collective-permute-start(bf16[120,2560]{1,0:T(8,128)(2,1)} %get-tuple-element.1256), channel_id=1, source_target_pairs={{0,4},{1,5},{2,6},{3,7},{4,0},{5,1},{6,2},{7,3},{8,12},{9,13},{10,... | collective-permute-start | bytes 1843208 | tf_op jit(solution)/shard_map/ppermute | solution.py:78
  155.1 23.5 %collective-permute-start.24 = (bf16[80,2560]{1,0:T(8,128)(2,1)S(1)}, bf16[80,2560]{1,0:T(8,128)(2,1)S(1)}, u32[]{:S(2)}, u32[]{:S(2)}) collective-permute-start(bf16[80,2560]{1,0:T(8,128)(2,1)S(1)} %copy-done.48), channel_id=1, source_target_pairs={{0,8},{1,9},{2,10},{3,11},{4,12},{5,13},{6,14},{7,15},{8,16},{9,17... | collective-permute-start | bytes 1228808 | tf_op jit(solution)/shard_map/ppermute | solution.py:100
  183.5 37.0 %collective-permute-start.31 = (bf16[320,2560]{1,0:T(8,128)(2,1)S(1)}, bf16[320,2560]{1,0:T(8,128)(2,1)}, u32[]{:S(2)}, u32[]{:S(2)}) collective-permute-start(bf16[320,2560]{1,0:T(8,128)(2,1)S(1)} %slice_dynamic-update-slice_fusion.20.mine), channel_id=1, source_target_pairs={{0,1},{1,0},{2,3},{3,2},{4,5},{5,4},{6,7},{7,6},{8,9},{9,8},{10,11... | collective-permute-start | bytes 4915208 | tf_op jit(solution)/shard_map/ppermute | solution.py:78
  188.5 32.0 %collective-permute-start.32 = (bf16[128,2560]{1,0:T(8,128)(2,1)}, bf16[128,2560]{1,0:T(8,128)(2,1)}, u32[]{:S(2)}, u32[]{:S(2)}) collective-permute-start(bf16[128,2560]{1,0:T(8,128)(2,1)} %collective-permute-done.13), channel_id=1, source_target_pairs={{0,8},{1,9},{2,10},{3,11},{4,12},{5,13},{6,14},{7,15},{8,16},{9,17... | collective-permute-start | bytes 1966088 | tf_op jit(solution)/shard_map/ppermute | solution.py:100
  189.7 30.0 %collective-permute-start.29 = (bf16[120,2560]{1,0:T(8,128)(2,1)}, bf16[120,2560]{1,0:T(8,128)(2,1)}, u32[]{:S(2)}, u32[]{:S(2)}) collective-permute-start(bf16[120,2560]{1,0:T(8,128)(2,1)} %get-tuple-element.1255), channel_id=1, source_target_pairs={{0,2},{1,3},{2,0},{3,1},{4,6},{5,7},{6,4},{7,5},{8,10},{9,11},{10,... | collective-permute-start | bytes 1843208 | tf_op jit(solution)/shard_map/ppermute | solution.py:78
  190.6 29.9 %collective-permute-start.30 = (bf16[120,2560]{1,0:T(8,128)(2,1)}, bf16[120,2560]{1,0:T(8,128)(2,1)}, u32[]{:S(2)}, u32[]{:S(2)}) collective-permute-start(bf16[120,2560]{1,0:T(8,128)(2,1)} %get-tuple-element.1254), channel_id=1, source_target_pairs={{0,4},{1,5},{2,6},{3,7},{4,0},{5,1},{6,2},{7,3},{8,12},{9,13},{10,... | collective-permute-start | bytes 1843208 | tf_op jit(solution)/shard_map/ppermute | solution.py:78
  228.1 29.9 %collective-permute-start.35 = (bf16[320,2560]{1,0:T(8,128)(2,1)}, bf16[320,2560]{1,0:T(8,128)(2,1)}, u32[]{:S(2)}, u32[]{:S(2)}) collective-permute-start(bf16[320,2560]{1,0:T(8,128)(2,1)} %slice_dynamic-update-slice_fusion.18.mine), channel_id=1, source_target_pairs={{0,1},{1,0},{2,3},{3,2},{4,5},{5,4},{6,7},{7,6},{8,9},{9,8},{10,11... | collective-permute-start | bytes 4915208 | tf_op jit(solution)/shard_map/ppermute | solution.py:78
  228.1 29.9 %collective-permute-start.36 = (bf16[128,2560]{1,0:T(8,128)(2,1)}, bf16[128,2560]{1,0:T(8,128)(2,1)S(1)}, u32[]{:S(2)}, u32[]{:S(2)}) collective-permute-start(bf16[128,2560]{1,0:T(8,128)(2,1)} %collective-permute-done.28), channel_id=1, source_target_pairs={{0,8},{1,9},{2,10},{3,11},{4,12},{5,13},{6,14},{7,15},{8,16},{9,17... | collective-permute-start | bytes 1966088 | tf_op jit(solution)/shard_map/ppermute | solution.py:100
  230.2 27.7 %collective-permute-start.33 = (bf16[40,2560]{1,0:T(8,128)(2,1)}, bf16[40,2560]{1,0:T(8,128)(2,1)}, u32[]{:S(2)}, u32[]{:S(2)}) collective-permute-start(bf16[40,2560]{1,0:T(8,128)(2,1)} %slice.505), channel_id=1, source_target_pairs={{0,4},{1,5},{2,6},{3,7},{4,0},{5,1},{6,2},{7,3},{8,12},{9,13},{10,... | collective-permute-start | bytes 614408 | tf_op jit(solution)/shard_map/ppermute | solution.py:78
  233.4 24.6 %collective-permute-start.34 = (bf16[40,2560]{1,0:T(8,128)(2,1)}, bf16[40,2560]{1,0:T(8,128)(2,1)}, u32[]{:S(2)}, u32[]{:S(2)}) collective-permute-start(bf16[40,2560]{1,0:T(8,128)(2,1)} %slice.506), channel_id=1, source_target_pairs={{0,2},{1,3},{2,0},{3,1},{4,6},{5,7},{6,4},{7,5},{8,10},{9,11},{10,... | collective-permute-start | bytes 614408 | tf_op jit(solution)/shard_map/ppermute | solution.py:78
  265.6 24.0 %collective-permute-start.37 = (bf16[320,2560]{1,0:T(8,128)(2,1)}, bf16[320,2560]{1,0:T(8,128)(2,1)}, u32[]{:S(2)}, u32[]{:S(2)}) collective-permute-start(bf16[320,2560]{1,0:T(8,128)(2,1)} %constant_dynamic-update-slice_fusion.13.mine), channel_id=1, source_target_pairs={{0,1},{1,0},{2,3},{3,2},{4,5},{5,4},{6,7},{7,6},{8,9},{9,8},{10,11... | collective-permute-start | bytes 4915208 | tf_op jit(solution)/shard_map/ppermute | solution.py:78
  313.5 33.1 %collective-permute-start.40 = (bf16[256,2560]{1,0:T(8,128)(2,1)S(1)}, bf16[256,2560]{1,0:T(8,128)(2,1)}, u32[]{:S(2)}, u32[]{:S(2)}) collective-permute-start(bf16[256,2560]{1,0:T(8,128)(2,1)S(1)} %multiply_convert_fusion), channel_id=1, source_target_pairs={{0,8},{1,9},{2,10},{3,11},{4,12},{5,13},{6,14},{7,15},{8,16},{9,17... | collective-permute-start | bytes 3932168 | tf_op jit(solution)/shard_map/ppermute | solution.py:100
  346.6 29.1 %collective-permute-start.45 = (bf16[256,2560]{1,0:T(8,128)(2,1)}, bf16[256,2560]{1,0:T(8,128)(2,1)}, u32[]{:S(2)}, u32[]{:S(2)}) collective-permute-start(bf16[256,2560]{1,0:T(8,128)(2,1)} %collective-permute-done.40), channel_id=1, source_target_pairs={{0,1},{1,0},{2,3},{3,2},{4,5},{5,4},{6,7},{7,6},{8,9},{9,8},{10,11... | collective-permute-start | bytes 3932168 | tf_op jit(solution)/shard_map/ppermute | solution.py:78
  346.6 33.8 %collective-permute-start.44 = (bf16[256,2560]{1,0:T(8,128)(2,1)}, bf16[256,2560]{1,0:T(8,128)(2,1)}, u32[]{:S(2)}, u32[]{:S(2)}) collective-permute-start(bf16[256,2560]{1,0:T(8,128)(2,1)} %collective-permute-done.40), channel_id=1, source_target_pairs={{0,8},{1,9},{2,10},{3,11},{4,12},{5,13},{6,14},{7,15},{8,16},{9,17... | collective-permute-start | bytes 3932168 | tf_op jit(solution)/shard_map/ppermute | solution.py:100
  347.0 26.8 %collective-permute-start.46 = (bf16[256,2560]{1,0:T(8,128)(2,1)}, bf16[256,2560]{1,0:T(8,128)(2,1)}, u32[]{:S(2)}, u32[]{:S(2)}) collective-permute-start(bf16[256,2560]{1,0:T(8,128)(2,1)} %pad_maximum_fusion.10), channel_id=1, source_target_pairs={{0,1},{1,0},{2,3},{3,2},{4,5},{5,4},{6,7},{7,6},{8,9},{9,8},{10,11... | collective-permute-start | bytes 3932168 | tf_op jit(solution)/shard_map/ppermute | solution.py:78
  414.4 33.0 %collective-permute-start.48 = (bf16[256,2560]{1,0:T(8,128)(2,1)}, bf16[256,2560]{1,0:T(8,128)(2,1)}, u32[]{:S(2)}, u32[]{:S(2)}) collective-permute-start(bf16[256,2560]{1,0:T(8,128)(2,1)} %collective-permute-done.44), channel_id=1, source_target_pairs={{0,8},{1,9},{2,10},{3,11},{4,12},{5,13},{6,14},{7,15},{8,16},{9,17... | collective-permute-start | bytes 3932168 | tf_op jit(solution)/shard_map/ppermute | solution.py:100
  457.3 32.2 %collective-permute-start.55 = (bf16[256,2560]{1,0:T(8,128)(2,1)}, bf16[256,2560]{1,0:T(8,128)(2,1)}, u32[]{:S(2)}, u32[]{:S(2)}) collective-permute-start(bf16[256,2560]{1,0:T(8,128)(2,1)} %add_convert_fusion.3), channel_id=1, source_target_pairs={{0,8},{1,9},{2,10},{3,11},{4,12},{5,13},{6,14},{7,15},{8,16},{9,17... | collective-permute-start | bytes 3932168 | tf_op jit(solution)/shard_map/ppermute | solution.py:100
  503.7 31.3 %collective-permute-start.58 = (bf16[256,2560]{1,0:T(8,128)(2,1)}, bf16[256,2560]{1,0:T(8,128)(2,1)}, u32[]{:S(2)}, u32[]{:S(2)}) collective-permute-start(bf16[256,2560]{1,0:T(8,128)(2,1)} %add_convert_fusion.2), channel_id=1, source_target_pairs={{0,8},{1,9},{2,10},{3,11},{4,12},{5,13},{6,14},{7,15},{8,16},{9,17... | collective-permute-start | bytes 3932168 | tf_op jit(solution)/shard_map/ppermute | solution.py:100
  541.2 63.6 %collective-permute-start.59 = (bf16[256,2560]{1,0:T(8,128)(2,1)}, bf16[256,2560]{1,0:T(8,128)(2,1)}, u32[]{:S(2)}, u32[]{:S(2)}) collective-permute-start(bf16[256,2560]{1,0:T(8,128)(2,1)} %add_convert_fusion.1), channel_id=1, source_target_pairs={{0,8},{1,9},{2,10},{3,11},{4,12},{5,13},{6,14},{7,15},{8,16},{9,17... | collective-permute-start | bytes 3932168 | tf_op jit(solution)/shard_map/ppermute | solution.py:100
  604.9 247.9 %reduce-scatter.6.cloned.1.call-start = ((), (), s32[]{:S(2)}) async-start(), calls=%async_computation.5 | async-start | bytes 6553600 | tf_op jit(solution)/shard_map/reduce_scatter | solution.py:547
  617.1 276.8 %reduce-scatter.4.cloned.1.call-start = ((), (), s32[]{:S(2)}) async-start(), calls=%async_computation.4 | async-start | bytes 6553600 | tf_op jit(solution)/shard_map/reduce_scatter | solution.py:547
  639.4 24.7 %collective-permute-start.63 = (bf16[4,256,2560]{2,1,0:T(8,128)(2,1)}, bf16[4,256,2560]{2,1,0:T(8,128)(2,1)}, u32[]{:S(2)}, u32[]{:S(2)}) collective-permute-start(bf16[4,256,2560]{2,1,0:T(8,128)(2,1)} %bitcast.66), channel_id=1, source_target_pairs={{0,1},{1,0},{2,3},{3,2},{4,5},{5,4},{6,7},{7,6},{8,9},{9,8},{10,11... | collective-permute-start | bytes 15728648 | tf_op jit(solution)/shard_map/ppermute | solution.py:78
  639.4 24.7 %collective-permute-start.61 = (bf16[160,1280]{1,0:T(8,128)(2,1)}, bf16[160,1280]{1,0:T(8,128)(2,1)S(1)}, u32[]{:S(2)}, u32[]{:S(2)}) collective-permute-start(bf16[160,1280]{1,0:T(8,128)(2,1)} %pad_maximum_fusion.42), channel_id=1, source_target_pairs={{0,2},{1,3},{2,0},{3,1},{4,6},{5,7},{6,4},{7,5},{8,10},{9,11},{10,... | collective-permute-start | bytes 1228808 | tf_op jit(solution)/shard_map/ppermute | solution.py:78
  641.0 23.1 %collective-permute-start.62 = (bf16[160,1280]{1,0:T(8,128)(2,1)}, bf16[160,1280]{1,0:T(8,128)(2,1)S(1)}, u32[]{:S(2)}, u32[]{:S(2)}) collective-permute-start(bf16[160,1280]{1,0:T(8,128)(2,1)} %pad_maximum_fusion.43), channel_id=1, source_target_pairs={{0,4},{1,5},{2,6},{3,7},{4,0},{5,1},{6,2},{7,3},{8,12},{9,13},{10,... | collective-permute-start | bytes 1228808 | tf_op jit(solution)/shard_map/ppermute | solution.py:78
  671.7 33.3 %collective-permute-start.66 = (bf16[256,2560]{1,0:T(8,128)(2,1)}, bf16[256,2560]{1,0:T(8,128)(2,1)}, u32[]{:S(2)}, u32[]{:S(2)}) collective-permute-start(bf16[256,2560]{1,0:T(8,128)(2,1)} %fusion.81), channel_id=1, source_target_pairs={{0,8},{1,9},{2,10},{3,11},{4,12},{5,13},{6,14},{7,15},{8,16},{9,17... | collective-permute-start | bytes 3932168 | tf_op jit(solution)/shard_map/ppermute | solution.py:100
  674.2 26.5 %collective-permute-start.64 = (bf16[240,1280]{1,0:T(8,128)(2,1)}, bf16[240,1280]{1,0:T(8,128)(2,1)S(1)}, u32[]{:S(2)}, u32[]{:S(2)}) collective-permute-start(bf16[240,1280]{1,0:T(8,128)(2,1)} %pad_maximum_fusion.34), channel_id=1, source_target_pairs={{0,2},{1,3},{2,0},{3,1},{4,6},{5,7},{6,4},{7,5},{8,10},{9,11},{10,... | collective-permute-start | bytes 1843208 | tf_op jit(solution)/shard_map/ppermute | solution.py:78
  675.5 27.5 %collective-permute-start.65 = (bf16[240,1280]{1,0:T(8,128)(2,1)}, bf16[240,1280]{1,0:T(8,128)(2,1)S(1)}, u32[]{:S(2)}, u32[]{:S(2)}) collective-permute-start(bf16[240,1280]{1,0:T(8,128)(2,1)} %pad_maximum_fusion.35), channel_id=1, source_target_pairs={{0,4},{1,5},{2,6},{3,7},{4,0},{5,1},{6,2},{7,3},{8,12},{9,13},{10,... | collective-permute-start | bytes 1843208 | tf_op jit(solution)/shard_map/ppermute | solution.py:78
  709.9 40.5 %collective-permute-start.70 = (bf16[256,2560]{1,0:T(8,128)(2,1)S(1)}, bf16[256,2560]{1,0:T(8,128)(2,1)S(1)}, u32[]{:S(2)}, u32[]{:S(2)}) collective-permute-start(bf16[256,2560]{1,0:T(8,128)(2,1)S(1)} %fusion.36), channel_id=1, source_target_pairs={{0,8},{1,9},{2,10},{3,11},{4,12},{5,13},{6,14},{7,15},{8,16},{9,17... | collective-permute-start | bytes 3932168 | tf_op jit(solution)/shard_map/ppermute | solution.py:100
  711.8 38.6 %collective-permute-start.67 = (bf16[240,1280]{1,0:T(8,128)(2,1)S(1)}, bf16[240,1280]{1,0:T(8,128)(2,1)S(1)}, u32[]{:S(2)}, u32[]{:S(2)}) collective-permute-start(bf16[240,1280]{1,0:T(8,128)(2,1)S(1)} %pad_maximum_fusion.36), channel_id=1, source_target_pairs={{0,2},{1,3},{2,0},{3,1},{4,6},{5,7},{6,4},{7,5},{8,10},{9,11},{10,... | collective-permute-start | bytes 1843208 | tf_op jit(solution)/shard_map/ppermute | solution.py:78
  713.1 37.3 %collective-permute-start.68 = (bf16[240,1280]{1,0:T(8,128)(2,1)S(1)}, bf16[240,1280]{1,0:T(8,128)(2,1)S(1)}, u32[]{:S(2)}, u32[]{:S(2)}) collective-permute-start(bf16[240,1280]{1,0:T(8,128)(2,1)S(1)} %pad_maximum_fusion.37), channel_id=1, source_target_pairs={{0,4},{1,5},{2,6},{3,7},{4,0},{5,1},{6,2},{7,3},{8,12},{9,13},{10,... | collective-permute-start | bytes 1843208 | tf_op jit(solution)/shard_map/ppermute | solution.py:78
  716.5 33.8 %collective-permute-start.69 = (bf16[160,1280]{1,0:T(8,128)(2,1)S(1)}, bf16[160,1280]{1,0:T(8,128)(2,1)S(1)}, u32[]{:S(2)}, u32[]{:S(2)}) collective-permute-start(bf16[160,1280]{1,0:T(8,128)(2,1)S(1)} %add_convert_fusion.9), channel_id=1, source_target_pairs={{0,8},{1,9},{2,10},{3,11},{4,12},{5,13},{6,14},{7,15},{8,16},{9,17... | collective-permute-start | bytes 1228808 | tf_op jit(solution)/shard_map/ppermute | solution.py:100
  758.0 39.8 %collective-permute-start.76 = (bf16[256,2560]{1,0:T(8,128)(2,1)}, bf16[256,2560]{1,0:T(8,128)(2,1)}, u32[]{:S(2)}, u32[]{:S(2)}) collective-permute-start(bf16[256,2560]{1,0:T(8,128)(2,1)} %fusion.35), channel_id=1, source_target_pairs={{0,8},{1,9},{2,10},{3,11},{4,12},{5,13},{6,14},{7,15},{8,16},{9,17... | collective-permute-start | bytes 3932168 | tf_op jit(solution)/shard_map/ppermute | solution.py:100
  764.1 33.6 %collective-permute-start.75 = (bf16[160,1280]{1,0:T(8,128)(2,1)S(1)}, bf16[160,1280]{1,0:T(8,128)(2,1)S(1)}, u32[]{:S(2)}, u32[]{:S(2)}) collective-permute-start(bf16[160,1280]{1,0:T(8,128)(2,1)S(1)} %add_convert_fusion.8), channel_id=1, source_target_pairs={{0,8},{1,9},{2,10},{3,11},{4,12},{5,13},{6,14},{7,15},{8,16},{9,17... | collective-permute-start | bytes 1228808 | tf_op jit(solution)/shard_map/ppermute | solution.py:100
  764.2 33.5 %collective-permute-start.71 = (bf16[240,1280]{1,0:T(8,128)(2,1)S(1)}, bf16[240,1280]{1,0:T(8,128)(2,1)S(1)}, u32[]{:S(2)}, u32[]{:S(2)}) collective-permute-start(bf16[240,1280]{1,0:T(8,128)(2,1)S(1)} %copy-done.80), channel_id=1, source_target_pairs={{0,2},{1,3},{2,0},{3,1},{4,6},{5,7},{6,4},{7,5},{8,10},{9,11},{10,... | collective-permute-start | bytes 1843208 | tf_op jit(solution)/shard_map/ppermute | solution.py:78
  765.7 32.0 %collective-permute-start.72 = (bf16[240,1280]{1,0:T(8,128)(2,1)S(1)}, bf16[240,1280]{1,0:T(8,128)(2,1)S(1)}, u32[]{:S(2)}, u32[]{:S(2)}) collective-permute-start(bf16[240,1280]{1,0:T(8,128)(2,1)S(1)} %copy-done.79), channel_id=1, source_target_pairs={{0,4},{1,5},{2,6},{3,7},{4,0},{5,1},{6,2},{7,3},{8,12},{9,13},{10,... | collective-permute-start | bytes 1843208 | tf_op jit(solution)/shard_map/ppermute | solution.py:78
  806.0 26.4 %collective-permute-start.81 = (bf16[160,1280]{1,0:T(8,128)(2,1)}, bf16[160,1280]{1,0:T(8,128)(2,1)S(1)}, u32[]{:S(2)}, u32[]{:S(2)}) collective-permute-start(bf16[160,1280]{1,0:T(8,128)(2,1)} %add_convert_fusion.7), channel_id=1, source_target_pairs={{0,8},{1,9},{2,10},{3,11},{4,12},{5,13},{6,14},{7,15},{8,16},{9,17... | collective-permute-start | bytes 1228808 | tf_op jit(solution)/shard_map/ppermute | solution.py:100
  808.1 24.3 %collective-permute-start.79 = (bf16[80,1280]{1,0:T(8,128)(2,1)}, bf16[80,1280]{1,0:T(8,128)(2,1)}, u32[]{:S(2)}, u32[]{:S(2)}) collective-permute-start(bf16[80,1280]{1,0:T(8,128)(2,1)} %get-tuple-element.1194), channel_id=1, source_target_pairs={{0,2},{1,3},{2,0},{3,1},{4,6},{5,7},{6,4},{7,5},{8,10},{9,11},{10,... | collective-permute-start | bytes 614408 | tf_op jit(solution)/shard_map/ppermute | solution.py:78
  809.7 22.7 %collective-permute-start.80 = (bf16[80,1280]{1,0:T(8,128)(2,1)}, bf16[80,1280]{1,0:T(8,128)(2,1)}, u32[]{:S(2)}, u32[]{:S(2)}) collective-permute-start(bf16[80,1280]{1,0:T(8,128)(2,1)} %get-tuple-element.1193), channel_id=1, source_target_pairs={{0,4},{1,5},{2,6},{3,7},{4,0},{5,1},{6,2},{7,3},{8,12},{9,13},{10,... | collective-permute-start | bytes 614408 | tf_op jit(solution)/shard_map/ppermute | solution.py:78
  810.3 27.0 %collective-permute-start.77 = (bf16[160,1536]{1,0:T(8,128)(2,1)}, bf16[160,1536]{1,0:T(8,128)(2,1)S(1)}, u32[]{:S(2)}, u32[]{:S(2)}) collective-permute-start(bf16[160,1536]{1,0:T(8,128)(2,1)} %pad_maximum_fusion.40), channel_id=1, source_target_pairs={{0,2},{1,3},{2,0},{3,1},{4,6},{5,7},{6,4},{7,5},{8,10},{9,11},{10,... | collective-permute-start | bytes 1474568 | tf_op jit(solution)/shard_map/ppermute | solution.py:78
  811.5 27.3 %collective-permute-start.78 = (bf16[160,1536]{1,0:T(8,128)(2,1)}, bf16[160,1536]{1,0:T(8,128)(2,1)}, u32[]{:S(2)}, u32[]{:S(2)}) collective-permute-start(bf16[160,1536]{1,0:T(8,128)(2,1)} %pad_maximum_fusion.41), channel_id=1, source_target_pairs={{0,4},{1,5},{2,6},{3,7},{4,0},{5,1},{6,2},{7,3},{8,12},{9,13},{10,... | collective-permute-start | bytes 1474568 | tf_op jit(solution)/shard_map/ppermute | solution.py:78
  (202 other events, 2003.1 us)
Sparse Core Ops, SparseCore 0:
  152.4 168.6 all-gather.1
  605.0 63.9 reduce-scatter.7
  672.0 78.1 reduce-scatter.5
  753.1 86.3 reduce-scatter.3

commit v4 on v3

--- a/solution.py
+++ b/solution.py
@@ -252,80 +252,6 @@
     return lax.dynamic_slice_in_dim(value, (1 - mv.core) * size, size, axis)
 
 
-def scatter_grads(mv, arrays, arrays_rows, held, work):
-    rows = arrays_rows // (mv.n // 2)
-    half = rows // 2
-
-    def block(array, step, flip_y, flip_x, shift=0, count=rows):
-        index = (((mv.z - step) % mv.planes) * 2 + (mv.y ^ flip_y)) * 2 + (mv.x ^ flip_x)
-        return lax.dynamic_slice(array, (index * rows + shift, 0), (count, array.shape[1]))
-
-    items = [(i, k) for i in range(len(arrays)) for k in [*range(1, mv.planes), 0]]
-    rings = [None] * len(arrays)
-    sources = [None] * len(arrays)
-    starts = []
-    first = second = None
-    for at in range(max(len(items) + 2, 9 + mv.planes // 2)):
-        if at < len(items) and sources[items[at][0]] is None:
-            sources[items[at][0]] = arrays[items[at][0]]()
-        first, second, sources, rings, now = fence((first, second, sources, rings, held))
-        held.update(now)
-        new_first = new_second = None
-        send_x, send_y = [], []
-        fresh = at < len(items)
-        if fresh:
-            i, k = items[at]
-            source = sources[i]
-            send_x += [block(source, k, 1, 1, 0, half), block(source, k, 0, 1, 0, half)]
-            send_y += [block(source, k, 1, 1, half, half), block(source, k, 1, 0, half, half)]
-        if first is not None:
-            i, k = items[at - 1]
-            from_x, from_y = first
-            last_x = block(sources[i], k, 0, 1, half, half).astype(F32) + from_y[:half].astype(F32)
-            last_y = block(sources[i], k, 1, 0, 0, half).astype(F32) + from_x[:half].astype(F32)
-            last_x, last_y = last_x.astype(BF), last_y.astype(BF)
-            joined = fresh and source.shape[1] == last_x.shape[1]
-            if joined or not fresh:
-                send_x.append(last_x)
-                send_y.append(last_y)
-                start = 2 * half if fresh else 0
-            else:
-                more_x, more_y = mv.over_x(last_x), mv.over_y(last_y)
-                start = 0
-            starts.append(start)
-        if send_x:
-            send_x, send_y, second, now = fence(
-                (jnp.concatenate(send_x, 0), jnp.concatenate(send_y, 0), second, held)
-            )
-            held.update(now)
-            got_x, got_y = mv.over_x(send_x), mv.over_y(send_y)
-        if first is not None:
-            if joined or not fresh:
-                more_x, more_y = got_x, got_y
-            new_second = (from_x, from_y, more_x, more_y)
-        if fresh:
-            new_first = (got_x, got_y)
-        if second is not None:
-            i, k = items[at - 2]
-            from_x, from_y, more_x, more_y = second
-            start = starts[at - 2]
-            total = block(sources[i], k, 0, 0).astype(F32)
-            total += jnp.concatenate(
-                [from_x[half : 2 * half], more_x[start : start + half]], 0
-            ).astype(F32)
-            total += jnp.concatenate(
-                [more_y[start : start + half], from_y[half : 2 * half]], 0
-            ).astype(F32)
-            if rings[i] is not None:
-                total = total + rings[i].astype(F32)
-            if k != 0:
-                rings[i] = mv.up(total.astype(BF))
-            else:
-                held[f"sum{i}"] = total
-        work(at)
-        first, second = new_first, new_second
-
-
 def swap_halves(mv, total):
     rows = total.shape[0] // 2
     mine = lax.dynamic_slice(total, (mv.core * rows, 0), (rows, total.shape[1]))
@@ -502,8 +428,14 @@
                 grads_all = [jnp.concatenate(v, 0) for v in grads_all]
                 cot_all = jnp.concatenate(cot_pieces, 0)
                 norm_all = jnp.concatenate(norm_pieces, 0)
-                partials = [dot_tn(acts, cot_all, BF)]
-                partials += [dot_tn(v, norm_all, BF) for v in grads_all]
+                acts_two = acts.reshape(mv.planes, 2, rows, 4 * padded)
+                branch_mine, branch_other = (
+                    dot_nn(acts_two[:, i].reshape(mv.planes * rows, 4 * padded), w_down)
+                    .astype(BF)
+                    .reshape(mv.planes, rows, D)
+                    for i in (0, 1)
+                )
+                partials = (branch_mine, mv.other(branch_other), dot_tn(acts, cot_all, BF))
             (
                 norms,
                 cots,
@@ -543,12 +475,22 @@
                     sends[done] = total.astype(BF)
         grad_norm_two = total
         attended_both, norm_both = swapped
-        ffn_sums = [
-            lax.psum_scatter(
-                v, "dp", scatter_dimension=0, tiled=True, axis_index_groups=mv.squares()
+        branch_mine, branch_got, down_partial = partials
+
+        def branch_step(ring, received):
+            at_piece = order[ring]
+            branch = branch_mine[at_piece].astype(F32) + branch_got[at_piece].astype(F32)
+            return branch if received is None else branch + received.astype(F32)
+
+        def ffn_sum(value):
+            return lax.psum_scatter(
+                value, "dp", scatter_dimension=0, tiled=True, axis_index_groups=mv.squares()
             )
-            for v in partials
-        ]
+
+        down_sum = ffn_sum(down_partial)
+        branch_sent = branch_step(0, None).astype(BF)
+        grad_norm_two, branch_sent = fence((grad_norm_two, branch_sent))
+        branch_ring = mv.up(branch_sent)
 
         _, norm_two_back = jax.vjp(rms_scale, hidden_one, gain_two)
         grad_rms_two, grad_gain_two = norm_two_back(grad_norm_two)
@@ -556,10 +498,10 @@
         grad_hidden_b = grad_hidden.astype(BF)
 
         out_partial = dot_tn(attended_both, core_half(mv, grad_hidden_b), BF)
-        out_partial, grad_hidden_b, grads_all, acts = fence(
-            (out_partial, grad_hidden_b, grads_all, acts)
+        out_partial, grad_hidden_b, grads_all, norm_all, branch_ring = fence(
+            (out_partial, grad_hidden_b, grads_all, norm_all, branch_ring)
         )
-        held = {"grads": grads_all, "acts": acts}
+        held = {"grads": grads_all, "norm": norm_all, "out": out_partial, "branch": branch_ring}
 
         def scores_back(grad_attended):
             grad_probs = jnp.einsum(
@@ -589,34 +531,149 @@
             )
             return grad_q_lin, grad_kv_lin
 
-        def work(at):
+        chip = D // (n // 2)
+        plane = 4 * chip
+
+        class Scatter:
+            def __init__(self, base, chip):
+                self.base, self.chip, self.half, self.at = base, chip, chip // 2, 0
+
+            def block(self, array, flip_y, flip_x, low=True, high=True):
+                index = (mv.y ^ flip_y) * 2 + (mv.x ^ flip_x)
+                start = self.base + index * self.chip + (0 if low else self.half)
+                count = self.half * (low + high)
+                return lax.dynamic_slice(array, (start, 0), (count, array.shape[1]))
+
+            def open(self, array, send_x, send_y):
+                send_x += [
+                    self.block(array, 1, 1, high=False),
+                    self.block(array, 0, 1, high=False),
+                ]
+                send_y += [
+                    self.block(array, 1, 1, low=False),
+                    self.block(array, 1, 0, low=False),
+                ]
+
+            def close(self, array, got, send_x, send_y):
+                from_x, from_y = got
+                self.at = sum(v.shape[0] for v in send_x)
+                last_x = self.block(array, 0, 1, low=False).astype(F32)
+                last_y = self.block(array, 1, 0, high=False).astype(F32)
+                send_x.append((last_x + from_y[: self.half].astype(F32)).astype(BF))
+                send_y.append((last_y + from_x[: self.half].astype(F32)).astype(BF))
+
+            def total(self, array, got, more):
+                (from_x, from_y), (more_x, more_y) = got, more
+                last = slice(self.at, self.at + self.half)
+                kept = slice(self.half, self.chip)
+                sums = self.block(array, 0, 0).astype(F32)
+                sums += jnp.concatenate([from_x[kept], more_x[last]], 0).astype(F32)
+                sums += jnp.concatenate([more_y[last], from_y[kept]], 0).astype(F32)
+                return sums
+
+        def exchange(send_x, send_y):
+            if not send_x:
+                return None
+            send_x, send_y, now = fence(
+                (jnp.concatenate(send_x, 0), jnp.concatenate(send_y, 0), held)
+            )
+            held.update(now)
+            return mv.over_x(send_x), mv.over_y(send_y)
+
+        planes = mv.planes
+        lin_items = [Scatter(((mv.z - k) % planes) * plane, chip) for k in [*range(1, planes), 0]]
+        out_item = Scatter(0, chip)
+        ffn_items = [Scatter(0, padded), Scatter(0, padded)]
+        open_lin, open_out = 2, max(4, planes)
+        last_round = max(open_lin + planes + 1, open_out + 2, 6 + (planes - 2) // 3, 2 * planes - 3)
+        for at in range(last_round + 1):
+            now = fence(held)
+            held.update(now)
+            send_x, send_y = [], []
+            j = at - open_lin
+            if 0 <= j < planes:
+                lin_items[j].open(held["lin"], send_x, send_y)
+            if 0 <= j - 1 < planes:
+                lin_items[j - 1].close(held["lin"], held["lin1"], send_x, send_y)
+            out_x, out_y = [], []
+            if at == open_out:
+                out_item.open(held["out_b"], out_x, out_y)
+            if at == open_out + 1:
+                out_item.close(held["out_b"], held["out1"], out_x, out_y)
+            ffn_x, ffn_y = [], []
+            f = at - 1
+            if 0 <= f < 2:
+                ffn_items[f].open(held["partials"][f], ffn_x, ffn_y)
+            if 0 <= f - 1 < 2:
+                ffn_items[f - 1].close(held["partials"][f - 1], held["ffn1"], ffn_x, ffn_y)
+            got, got_out = exchange(send_x, send_y), exchange(out_x, out_y)
+            got_ffn = exchange(ffn_x, ffn_y)
+            if at < planes - 1:
+                z = (mv.z - at - 1) % planes
+                rows_out = lax.dynamic_slice(held["out"], (z * plane, 0), (plane, D // 2))
+                if at > 0:
+                    rows_out = rows_out.astype(F32) + held.pop("out_ring").astype(F32)
+                held["out_ring"] = mv.up(rows_out.astype(BF))
+            if at == planes - 1:
+                rows_out = lax.dynamic_slice(held.pop("out"), (mv.z * plane, 0), (plane, D // 2))
+                rows_out = rows_out.astype(F32) + held.pop("out_ring").astype(F32)
+                held["out_b"] = rows_out.astype(BF)
+            ring = at - (planes - 1) + 1
+            if 1 <= ring < planes:
+                branch = branch_step(ring, held.pop("branch"))
+                if ring < planes - 1:
+                    held["branch"] = mv.up(branch.astype(BF))
+                else:
+                    held["output"] = (hidden_one + branch + bias_down).astype(BF)
+            if 0 <= j - 2 < planes:
+                sums = lin_items[j - 2].total(held["lin"], held["lin2"], held["lin1"])
+                if j - 2 > 0:
+                    sums = sums + held.pop("lin_ring").astype(F32)
+                if j - 2 < planes - 1:
+                    held["lin_ring"] = mv.up(sums.astype(BF))
+                else:
+                    held["lin_sum"] = sums
+            if at == open_out + 2:
+                sums = out_item.total(held["out_b"], held["out2"], held["out1"])
+                held["out_grad"] = jnp.concatenate(swap_halves(mv, sums), 1)
+            if 0 <= f - 2 < 2:
+                sums = ffn_items[f - 2].total(
+                    held["partials"][f - 2], held["ffn2"], held["ffn1"]
+                )
+                held[f"unit_grad{f - 2}"] = sums[:units]
+            for one, two, new in (("ffn1", "ffn2", got_ffn),):
+                if one in held:
+                    held[two] = held.pop(one)
+                if new is not None:
+                    held[one] = new
+            if "lin1" in held:
+                held["lin2"] = held.pop("lin1")
+            if got is not None:
+                held["lin1"] = got
+            if "out1" in held:
+                held["out2"] = held.pop("out1")
+            if got_out is not None:
+                held["out1"] = got_out
             if at == 0:
+                held["down_sum"] = down_sum
+                partials = [dot_tn(v, held["norm"], BF) for v in held["grads"]]
+                held["partials"] = partials
+            if at == 1:
                 grad_attended = dot_nt(grad_hidden_b, w_out).astype(BF)
-                held["attended"] = grad_attended.reshape(seqs, LENGTH, H, HD)
-                acts_two = held.pop("acts").reshape(mv.planes, 2, rows, 4 * padded)
-                mine, theirs = (
-                    dot_nn(acts_two[:, i].reshape(mv.planes * rows, 4 * padded), w_down)
-                    .astype(BF)
-                    .reshape(mv.planes, rows, D)
-                    for i in (0, 1)
-                )
-                held["branch"], held["got"] = mine, mv.other(theirs)
+                grad_attended = grad_attended.reshape(seqs, LENGTH, H, HD)
+                held["q"], held["kv"] = lin_back(scores_back(grad_attended), grad_attended)
             if at == 1:
-                held["scores"] = scores_back(held["attended"])
+                both = jnp.concatenate([core_half(mv, held["q"]), core_half(mv, held["kv"])], 1)
+                held["lin"] = dot_tn(norm_both, both, BF)
             if at == 2:
-                held["q"], held["kv"] = lin_back(held.pop("scores"), held.pop("attended"))
-            if at == 3:
-                half = jnp.concatenate([core_half(mv, held["q"]), core_half(mv, held["kv"])], 1)
-                held["partial"] = dot_tn(norm_both, half, BF)
-            if at == 4:
                 grad_norm_one = dot_nt(held.pop("q"), w_query) + dot_nt(held.pop("kv"), w_keyval)
                 _, norm_one_back = jax.vjp(rms_scale, x_value, gain_one)
                 grad_rms_one, grad_gain_one = norm_one_back(grad_norm_one)
                 held["input_grad"] = (grad_hidden + grad_rms_one).astype(BF)
                 down_bias_sum = jnp.sum(cotangent, axis=0, dtype=F32)
-                part = D // mv.n
+                part = D // n
                 small = jnp.stack([grad_gain_one, grad_gain_two, down_bias_sum])
-                small = small.reshape(3, mv.planes, 2, 2, 2, part).transpose(2, 3, 4, 1, 0, 5)
+                small = small.reshape(3, planes, 2, 2, 2, part).transpose(2, 3, 4, 1, 0, 5)
                 held["small"] = small
                 bias = jnp.stack([jnp.sum(v, axis=0, dtype=F32) for v in held.pop("grads")])
                 bias = bias.reshape(2, 2, 2, padded)[..., :units]
@@ -624,41 +681,28 @@
             for stage, (coordinate, move) in enumerate(
                 ((mv.y, mv.over_y), (mv.x, mv.over_x), (mv.core, mv.other))
             ):
-                if at == 5 + stage:
+                if at == 3 + stage:
                     for name in ("small", "bias")[: 2 if stage < 2 else 1]:
                         whole = held[name]
                         keep = lax.dynamic_index_in_dim(whole, coordinate, 0, keepdims=False)
                         away = lax.dynamic_index_in_dim(whole, 1 - coordinate, 0, keepdims=False)
                         held[name] = keep + move(away)
-            for step in range(1, mv.planes):
-                if at == 8 + (step - 1) // 2:
+            for step in range(1, planes):
+                if at == min(6 + (step - 1) // 3, last_round):
                     away = lax.dynamic_index_in_dim(
-                        held["small"], (mv.z + step) % mv.planes, 0, keepdims=False
+                        held["small"], (mv.z + step) % planes, 0, keepdims=False
                     )
                     held["small_sum"] = held.get("small_sum", 0.0) + mv.up(away, step)
-
-            ring = at - 1
-            if 0 <= ring < mv.planes:
-                at_piece = order[ring]
-                branch = held["branch"][at_piece].astype(F32) + held["got"][at_piece].astype(F32)
-                if ring > 0:
-                    branch = branch + held.pop("ring").astype(F32)
-                if ring < mv.planes - 1:
-                    held["ring"] = mv.up(branch.astype(BF))
-                else:
-                    held["output"] = (hidden_one + branch + bias_down).astype(BF)
-            if at == mv.planes + 4:
-                held["out_grad"] = jnp.concatenate(swap_halves(mv, held.pop("sum0")), 1)
-                held["ffn"] = [v[:units].astype(F32) for v in ffn_sums]
-
-        scatter_grads(
-            mv, [lambda: out_partial, lambda: held.pop("partial")], D, held, work
-        )
+            if at == last_round - 1:
+                held["down_grad"] = held.pop("down_sum")[:units].astype(F32)
+
         small = held["small_sum"] + lax.dynamic_index_in_dim(
             held["small"], mv.z, 0, keepdims=False
         )
-        down_grad, gate_grad, up_grad = held["ffn"]
-        first, second = swap_halves(mv, held["sum1"])
+        down_grad, gate_grad, up_grad = (
+            held[k] for k in ("down_grad", "unit_grad0", "unit_grad1")
+        )
+        first, second = swap_halves(mv, held["lin_sum"])
         q_grad = jnp.concatenate([first[:, : D // 2], second[:, : D // 2]], 1)
         kv_grad = jnp.concatenate([first[:, D // 2 :], second[:, D // 2 :]], 1)
 

time: 950 us -> 917 us (0.965)
  matrix products: 231 us -> 202 us
  starting transfers between devices: 89.1 us -> 69.3 us
  waiting for transfers between devices: 297 us -> 314 us
    ppermute x73, waiting for transfers between devices: 86.2 us -> 123 us  [flip(): return lax.ppermute(value, 'dp', [(i, i ^ bit) for i in range(self.n)])]
    dot_general x13, matrix products: 79.2 us -> 57.4 us  [dot_nn(): return jnp.dot(left, right, preferred_element_type=F32)]
    ppermute x30, waiting for transfers between devices: 210 us -> 190 us  [up(): lax.ppermute(value, 'dp', [(i, (i + 8 * steps) % self.n) for i in range(s...]
    ppermute x30, starting transfers between devices: 35.2 us -> 17.4 us  [up(): lax.ppermute(value, 'dp', [(i, (i + 8 * steps) % self.n) for i in range(s...]
    convert_element_type x22 -> x18, other arithmetic: 43.5 us -> 27.2 us  [the longest x2 6.94 us: body(): held['out_ring'] = mv.up(rows_out.astype(BF))]
    unnamed x312 -> x297, local copies, waits for them, and re-layouts: 58.4 us -> 57.6 us
  transfers between devices with their start and end apart: 107 -> 105, of which waited for: 45 -> 48; matrix products, arithmetic and copies ran while one was open for 40% -> 39% of each run, Pallas kernels for 6% -> 7%
where the time goes in v4:
time: 917 us; the launch traced here: 907 us
  waiting for transfers between devices  314 us (34%)
  matrix products  202 us (22%)
  other arithmetic  128 us (14%)
  local copies, waits for them, and re-layouts  117 us (13%)
  starting transfers between devices  69.3 us (8%)
  Pallas kernels  60.1 us (7%)
  between operations  16.9 us (2%)
    ppermute x30, waiting for transfers between devices, up(): lax.ppermute(value, 'dp', [(i, (i + 8 * steps) % self.n) for i in range(s...  190 us
    ppermute x73, waiting for transfers between devices, flip(): return lax.ppermute(value, 'dp', [(i, i ^ bit) for i in range(self.n)])  123 us
    dot_general x15, matrix products, dot_nt(): lax.dot_general(left, right, (((1,), (1,)), ((), ())), preferred_element_...  78.3 us
    pallas_call x8, Pallas kernels, put(): pl.pallas_call(place_kernel, out_shape=self.shape, grid_spec=pltpu.Prefet...  60.1 us
    dot_general x5, matrix products, dot_tn(): lax.dot_general(left, right, (((0,), (0,)), ((), ())), preferred_element_...  59.8 us
    unnamed x297, local copies, waits for them, and re-layouts  57.6 us
    dot_general x13, matrix products, dot_nn(): return jnp.dot(left, right, preferred_element_type=F32)  57.4 us
    ppermute x73, starting transfers between devices, flip(): return lax.ppermute(value, 'dp', [(i, i ^ bit) for i in range(self.n)])  51.8 us
  transfers between devices with their start and end apart: 105, of which 48 were waited for; matrix products, arithmetic and copies ran while one was open for 39% of the time, Pallas kernels for 7%

profile of v4, /device:TPU:0, one launch (start us, length us, event | category | flops | bytes accessed | tf_op | source)
XLA Modules:
  0.0 907.3 jit_solution(6529562424673170902)
XLA Ops:
  21.3 8.6 collective-permute-done.2
  35.7 13.4 %collective-permute-done.3 = bf16[80,3200]{1,0:T(8,128)(2,1)S(1)} collective-permute-done((bf16[80,3200]{1,0:T(8,128)(2,1)S(1)}, bf16[80,3200]{1,0:T(8,128)(2,1)S(1)}, u32[]{:S(2)}, u32[]{:S(2)}) %collective-permute-start.3) | collective-permute-done | bytes 512032 | tf_op jit(solution)/shard_map/ppermute | solution.py:100
  55.0 15.3 %collective-permute-done.6 = bf16[80,3200]{1,0:T(8,128)(2,1)S(1)} collective-permute-done((bf16[80,3200]{1,0:T(8,128)(2,1)S(1)}, bf16[80,3200]{1,0:T(8,128)(2,1)S(1)}, u32[]{:S(2)}, u32[]{:S(2)}) %collective-permute-start.6) | collective-permute-done | bytes 512032 | tf_op jit(solution)/shard_map/ppermute | solution.py:100
  81.1 7.8 place_rows.8.refs_0_
  88.9 10.2 %collective-permute-done.13 = bf16[128,2560]{1,0:T(8,128)(2,1)} collective-permute-done((bf16[128,2560]{1,0:T(8,128)(2,1)}, bf16[128,2560]{1,0:T(8,128)(2,1)}, u32[]{:S(2)}, u32[]{:S(2)}) %collective-permute-start.13) | collective-permute-done | bytes 655392 | tf_op jit(solution)/shard_map/ppermute | solution.py:100
  107.5 4.9 collective-permute-done.18
  114.3 7.7 place_rows.9.refs_0_
  131.4 7.7 place_rows.10.refs_0_
  157.9 8.2 place_rows.11
  166.1 15.2 %collective-permute-done.24 = bf16[80,2560]{1,0:T(8,128)(2,1)S(1)} collective-permute-done((bf16[80,2560]{1,0:T(8,128)(2,1)S(1)}, bf16[80,2560]{1,0:T(8,128)(2,1)S(1)}, u32[]{:S(2)}, u32[]{:S(2)}) %collective-permute-start.24) | collective-permute-done | bytes 409632 | tf_op jit(solution)/shard_map/ppermute | solution.py:100
  195.3 7.3 place_rows.12.refs_0_
  202.6 19.8 %collective-permute-done.30 = bf16[120,2560]{1,0:T(8,128)(2,1)} collective-permute-done((bf16[120,2560]{1,0:T(8,128)(2,1)}, bf16[120,2560]{1,0:T(8,128)(2,1)}, u32[]{:S(2)}, u32[]{:S(2)}) %collective-permute-start.30) | collective-permute-done | bytes 614432 | tf_op jit(solution)/shard_map/ppermute | solution.py:78
  242.0 8.6 fusion.2
  251.7 7.2 place_rows.13.refs_0_
  277.8 7.1 place_rows.14.refs_0_
  295.0 7.1 place_rows.15
  324.6 26.7 %collective-permute-done.40 = bf16[256,2560]{1,0:T(8,128)(2,1)} collective-permute-done((bf16[256,2560]{1,0:T(8,128)(2,1)S(1)}, bf16[256,2560]{1,0:T(8,128)(2,1)}, u32[]{:S(2)}, u32[]{:S(2)}) %collective-permute-start.40) | collective-permute-done | bytes 1310752 | tf_op jit(solution)/shard_map/ppermute | solution.py:100
  353.0 6.4 fusion.157
  365.2 5.4 fusion.52
  391.9 5.6 fusion.59
  410.9 7.5 collective-permute-done.48
  427.5 7.1 fusion.66
  448.4 11.0 %collective-permute-done.55 = bf16[256,2560]{1,0:T(8,128)(2,1)} collective-permute-done((bf16[256,2560]{1,0:T(8,128)(2,1)}, bf16[256,2560]{1,0:T(8,128)(2,1)}, u32[]{:S(2)}, u32[]{:S(2)}) %collective-permute-start.55) | collective-permute-done | bytes 1310752 | tf_op jit(solution)/shard_map/ppermute | solution.py:100
  470.9 7.6 fusion.73
  490.0 12.5 %collective-permute-done.58 = bf16[256,2560]{1,0:T(8,128)(2,1)} collective-permute-done((bf16[256,2560]{1,0:T(8,128)(2,1)}, bf16[256,2560]{1,0:T(8,128)(2,1)}, u32[]{:S(2)}, u32[]{:S(2)}) %collective-permute-start.58) | collective-permute-done | bytes 1310752 | tf_op jit(solution)/shard_map/ppermute | solution.py:100
  510.7 7.3 convolution_convert_fusion.4
  518.7 17.0 %fusion.14 = bf16[1024,2560]{1,0:T(8,128)(2,1)} fusion(bf16[2048,1024]{1,0:T(8,128)(2,1)} %copy-done.28, bf16[512,2560]{1,0:T(8,128)(2,1)} %copy-done.45, bf16[512,2560]{1,0:T(8,128)(2,1)} %copy-done.44, bf16[512,2560]{1,0:T(8,128)(2,1)} %copy-done.43, bf16[512,2560]{1,0:T(8,128)(2,1)} %pad_maximum_fusion.4), kind=kOutput, calls=%fused_computation.23 | convolution fusion | flops 10781982720 | bytes 19922944 | tf_op jit(solution)/shard_map/dot_general | solution.py:50
  535.7 6.4 pad_maximum_fusion.1
  543.3 7.4 convolution_convert_fusion.5
  563.7 5.0 pad_maximum_fusion
  568.7 5.4 convolution_convert_fusion.1
  574.1 19.4 %collective-permute-done.62 = bf16[256,2560]{1,0:T(8,128)(2,1)} collective-permute-done((bf16[256,2560]{1,0:T(8,128)(2,1)S(1)}, bf16[256,2560]{1,0:T(8,128)(2,1)}, u32[]{:S(2)}, u32[]{:S(2)}) %collective-permute-start.62) | collective-permute-done | bytes 1310752 | tf_op jit(solution)/shard_map/ppermute | solution.py:100
  593.6 10.1 %convolution_convert_fusion.6 = bf16[256,2560]{1,0:T(8,128)(2,1)} fusion(bf16[256,2560]{1,0:T(8,128)(2,1)S(1)} %fusion.154, bf16[2560,2560]{1,0:T(8,128)(2,1)} %place_rows.15), kind=kOutput, calls=%fused_computation.43 | convolution fusion | flops 3356098560 | bytes 15728640 | tf_op jit(solution)/shard_map/dot_general | solution.py:56
  624.3 17.4 %convolution_convert_fusion.3 = bf16[1024,2560]{1,0:T(8,128)(2,1)} fusion(bf16[2048,1024]{1,0:T(8,128)(2,1)} %get-tuple-element.1036, bf16[2048,2560]{1,0:T(8,128)(2,1)} %pad_maximum_fusion), kind=kOutput, calls=%fused_computation.22 | convolution fusion | flops 10740039680 | bytes 19922944 | tf_op jit(solution)/shard_map/dot_general | solution.py:50
  641.7 13.6 %convolution_convert_fusion.2 = bf16[1024,2560]{1,0:T(8,128)(2,1)} fusion(bf16[2048,1024]{1,0:T(8,128)(2,1)S(1)} %copy-done.12, bf16[2048,2560]{1,0:T(8,128)(2,1)S(1)} %bitcast.284), kind=kOutput, calls=%fused_computation.21 | convolution fusion | flops 10740039680 | bytes 19922944 | tf_op jit(solution)/shard_map/dot_general | solution.py:50
  667.6 6.3 convolution_convert_fusion
  673.9 17.2 %collective-permute-done.64 = bf16[256,2560]{1,0:T(8,128)(2,1)} collective-permute-done((bf16[256,2560]{1,0:T(8,128)(2,1)}, bf16[256,2560]{1,0:T(8,128)(2,1)}, u32[]{:S(2)}, u32[]{:S(2)}) %collective-permute-start.64) | collective-permute-done | bytes 1310752 | tf_op jit(solution)/shard_map/ppermute | solution.py:78
  691.2 13.6 %collective-permute-done.68 = bf16[640,1280]{1,0:T(8,128)(2,1)} collective-permute-done((bf16[640,1280]{1,0:T(8,128)(2,1)}, bf16[640,1280]{1,0:T(8,128)(2,1)}, u32[]{:S(2)}, u32[]{:S(2)}) %collective-permute-start.68) | collective-permute-done | bytes 1638432 | tf_op jit(solution)/shard_map/ppermute | solution.py:100
  723.7 11.1 %fusion.26 = (f32[2560]{0:T(1024)S(1)}, f32[256]{0:T(256)S(1)}, f32[256,2560]{1,0:T(8,128)}) fusion(bf16[256,2560]{1,0:T(8,128)(2,1)S(1)} %copy-done.9, f32[256]{0:T(256)S(1)} %copy-done.110, f32[2560]{0:T(1024)S(1)} %copy-done.101, f32[256,2560]{1,0:T(8,128)} %fusion.40, bf16[256,2560]{0,1:T(8,128)(2,1)S(1)} %bitcast.298, bf16[2560,3200]{1,0:T(8,128)(2,1)} %place_rows.11), kind=kOutput, calls=%fused_computation.60 | convolution fusion | flops 3360683264 | bytes 20994048 | tf_op jit(solution)/shard_map/dot_general | solution.py:56
  737.7 6.5 convert_reduce_fusion.2
  745.2 11.1 %collective-permute-done.73 = bf16[640,1280]{1,0:T(8,128)(2,1)} collective-permute-done((bf16[640,1280]{1,0:T(8,128)(2,1)}, bf16[640,1280]{1,0:T(8,128)(2,1)}, u32[]{:S(2)}, u32[]{:S(2)}) %collective-permute-start.73) | collective-permute-done | bytes 1638432 | tf_op jit(solution)/shard_map/ppermute | solution.py:100
  756.2 5.8 collective-permute-done.69
  790.8 7.8 collective-permute-done.76
  824.0 13.3 %collective-permute-done.87 = bf16[160,1280]{1,0:T(8,128)(2,1)S(1)} collective-permute-done((bf16[160,1280]{1,0:T(8,128)(2,1)S(1)}, bf16[160,1280]{1,0:T(8,128)(2,1)S(1)}, u32[]{:S(2)}, u32[]{:S(2)}) %collective-permute-start.87) | collective-permute-done | bytes 409632 | tf_op jit(solution)/shard_map/ppermute | solution.py:78
  837.4 9.1 %collective-permute-done.85 = bf16[160,1536]{1,0:T(8,128)(2,1)S(1)} collective-permute-done((bf16[160,1536]{1,0:T(8,128)(2,1)S(1)}, bf16[160,1536]{1,0:T(8,128)(2,1)S(1)}, u32[]{:S(2)}, u32[]{:S(2)}) %collective-permute-start.85) | collective-permute-done | bytes 491552 | tf_op jit(solution)/shard_map/ppermute | solution.py:100
  855.0 17.3 %collective-permute-done.93 = bf16[80,1280]{1,0:T(8,128)(2,1)S(1)} collective-permute-done((bf16[80,1280]{1,0:T(8,128)(2,1)S(1)}, bf16[80,1280]{1,0:T(8,128)(2,1)S(1)}, u32[]{:S(2)}, u32[]{:S(2)}) %collective-permute-start.93) | collective-permute-done | bytes 204832 | tf_op jit(solution)/shard_map/ppermute | solution.py:78
  884.2 4.7 collective-permute-done.96
  888.9 7.2 collective-permute-done.97
  (741 shorter events, 404.3 us)
Async XLA Ops:
  7.2 345.0 %all-gather.2.cloned.1.call-start = ((), (), s32[]{:S(2)}) async-start(), calls=%async_computation.1 | async-start | bytes 19660800 | tf_op jit(solution)/shard_map/all_gather | solution.py:367
  77.8 23.0 %collective-permute-start.12 = (bf16[320,3200]{1,0:T(8,128)(2,1)}, bf16[320,3200]{1,0:T(8,128)(2,1)}, u32[]{:S(2)}, u32[]{:S(2)}) collective-permute-start(bf16[320,3200]{1,0:T(8,128)(2,1)} %slice_dynamic-update-slice_fusion.14.mine), channel_id=1, source_target_pairs={{0,1},{1,0},{2,3},{3,2},{4,5},{5,4},{6,7},{7,6},{8,9},{9,8},{10,11... | collective-permute-start | bytes 6144008 | tf_op jit(solution)/shard_map/ppermute | solution.py:78
  151.3 30.0 %collective-permute-start.27 = (bf16[320,2560]{1,0:T(8,128)(2,1)S(1)}, bf16[320,2560]{1,0:T(8,128)(2,1)}, u32[]{:S(2)}, u32[]{:S(2)}) collective-permute-start(bf16[320,2560]{1,0:T(8,128)(2,1)S(1)} %slice_dynamic-update-slice_fusion.22.mine), channel_id=1, source_target_pairs={{0,1},{1,0},{2,3},{3,2},{4,5},{5,4},{6,7},{7,6},{8,9},{9,8},{10,11... | collective-permute-start | bytes 4915208 | tf_op jit(solution)/shard_map/ppermute | solution.py:78
  151.4 504.0 %reduce-scatter.2.cloned.1.call-start = ((), (), s32[]{:S(2)}) async-start(), calls=%async_computation.2 | async-start | bytes 6553600 | tf_op jit(solution)/shard_map/reduce_scatter | solution.py:486
  153.9 27.5 %collective-permute-start.28 = (bf16[128,2560]{1,0:T(8,128)(2,1)}, bf16[128,2560]{1,0:T(8,128)(2,1)}, u32[]{:S(2)}, u32[]{:S(2)}) collective-permute-start(bf16[128,2560]{1,0:T(8,128)(2,1)} %get-tuple-element.720), channel_id=1, source_target_pairs={{0,8},{1,9},{2,10},{3,11},{4,12},{5,13},{6,14},{7,15},{8,16},{9,17... | collective-permute-start | bytes 1966088 | tf_op jit(solution)/shard_map/ppermute | solution.py:100
  155.0 26.3 %collective-permute-start.26 = (bf16[120,2560]{1,0:T(8,128)(2,1)}, bf16[120,2560]{1,0:T(8,128)(2,1)}, u32[]{:S(2)}, u32[]{:S(2)}) collective-permute-start(bf16[120,2560]{1,0:T(8,128)(2,1)} %get-tuple-element.1361), channel_id=1, source_target_pairs={{0,4},{1,5},{2,6},{3,7},{4,0},{5,1},{6,2},{7,3},{8,12},{9,13},{10,... | collective-permute-start | bytes 1843208 | tf_op jit(solution)/shard_map/ppermute | solution.py:78
  155.6 25.8 %collective-permute-start.25 = (bf16[120,2560]{1,0:T(8,128)(2,1)}, bf16[120,2560]{1,0:T(8,128)(2,1)}, u32[]{:S(2)}, u32[]{:S(2)}) collective-permute-start(bf16[120,2560]{1,0:T(8,128)(2,1)} %get-tuple-element.1362), channel_id=1, source_target_pairs={{0,2},{1,3},{2,0},{3,1},{4,6},{5,7},{6,4},{7,5},{8,10},{9,11},{10,... | collective-permute-start | bytes 1843208 | tf_op jit(solution)/shard_map/ppermute | solution.py:78
  157.0 24.3 %collective-permute-start.24 = (bf16[80,2560]{1,0:T(8,128)(2,1)S(1)}, bf16[80,2560]{1,0:T(8,128)(2,1)S(1)}, u32[]{:S(2)}, u32[]{:S(2)}) collective-permute-start(bf16[80,2560]{1,0:T(8,128)(2,1)S(1)} %copy-done.51), channel_id=1, source_target_pairs={{0,8},{1,9},{2,10},{3,11},{4,12},{5,13},{6,14},{7,15},{8,16},{9,17... | collective-permute-start | bytes 1228808 | tf_op jit(solution)/shard_map/ppermute | solution.py:100
  186.2 36.7 %collective-permute-start.31 = (bf16[320,2560]{1,0:T(8,128)(2,1)S(1)}, bf16[320,2560]{1,0:T(8,128)(2,1)}, u32[]{:S(2)}, u32[]{:S(2)}) collective-permute-start(bf16[320,2560]{1,0:T(8,128)(2,1)S(1)} %slice_dynamic-update-slice_fusion.20.mine), channel_id=1, source_target_pairs={{0,1},{1,0},{2,3},{3,2},{4,5},{5,4},{6,7},{7,6},{8,9},{9,8},{10,11... | collective-permute-start | bytes 4915208 | tf_op jit(solution)/shard_map/ppermute | solution.py:78
  191.2 31.6 %collective-permute-start.32 = (bf16[128,2560]{1,0:T(8,128)(2,1)}, bf16[128,2560]{1,0:T(8,128)(2,1)}, u32[]{:S(2)}, u32[]{:S(2)}) collective-permute-start(bf16[128,2560]{1,0:T(8,128)(2,1)} %collective-permute-done.13), channel_id=1, source_target_pairs={{0,8},{1,9},{2,10},{3,11},{4,12},{5,13},{6,14},{7,15},{8,16},{9,17... | collective-permute-start | bytes 1966088 | tf_op jit(solution)/shard_map/ppermute | solution.py:100
  192.4 30.0 %collective-permute-start.30 = (bf16[120,2560]{1,0:T(8,128)(2,1)}, bf16[120,2560]{1,0:T(8,128)(2,1)}, u32[]{:S(2)}, u32[]{:S(2)}) collective-permute-start(bf16[120,2560]{1,0:T(8,128)(2,1)} %get-tuple-element.1359), channel_id=1, source_target_pairs={{0,4},{1,5},{2,6},{3,7},{4,0},{5,1},{6,2},{7,3},{8,12},{9,13},{10,... | collective-permute-start | bytes 1843208 | tf_op jit(solution)/shard_map/ppermute | solution.py:78
  192.9 29.9 %collective-permute-start.29 = (bf16[120,2560]{1,0:T(8,128)(2,1)}, bf16[120,2560]{1,0:T(8,128)(2,1)}, u32[]{:S(2)}, u32[]{:S(2)}) collective-permute-start(bf16[120,2560]{1,0:T(8,128)(2,1)} %get-tuple-element.1360), channel_id=1, source_target_pairs={{0,2},{1,3},{2,0},{3,1},{4,6},{5,7},{6,4},{7,5},{8,10},{9,11},{10,... | collective-permute-start | bytes 1843208 | tf_op jit(solution)/shard_map/ppermute | solution.py:78
  226.1 34.1 %collective-permute-start.34 = (bf16[40,2560]{1,0:T(8,128)(2,1)}, bf16[40,2560]{1,0:T(8,128)(2,1)}, u32[]{:S(2)}, u32[]{:S(2)}) collective-permute-start(bf16[40,2560]{1,0:T(8,128)(2,1)} %slice.481), channel_id=1, source_target_pairs={{0,2},{1,3},{2,0},{3,1},{4,6},{5,7},{6,4},{7,5},{8,10},{9,11},{10,... | collective-permute-start | bytes 614408 | tf_op jit(solution)/shard_map/ppermute | solution.py:78
  227.5 32.7 %collective-permute-start.33 = (bf16[40,2560]{1,0:T(8,128)(2,1)}, bf16[40,2560]{1,0:T(8,128)(2,1)}, u32[]{:S(2)}, u32[]{:S(2)}) collective-permute-start(bf16[40,2560]{1,0:T(8,128)(2,1)} %slice.480), channel_id=1, source_target_pairs={{0,4},{1,5},{2,6},{3,7},{4,0},{5,1},{6,2},{7,3},{8,12},{9,13},{10,... | collective-permute-start | bytes 614408 | tf_op jit(solution)/shard_map/ppermute | solution.py:78
  228.9 31.3 %collective-permute-start.36 = (bf16[128,2560]{1,0:T(8,128)(2,1)}, bf16[128,2560]{1,0:T(8,128)(2,1)}, u32[]{:S(2)}, u32[]{:S(2)}) collective-permute-start(bf16[128,2560]{1,0:T(8,128)(2,1)} %collective-permute-done.28), channel_id=1, source_target_pairs={{0,8},{1,9},{2,10},{3,11},{4,12},{5,13},{6,14},{7,15},{8,16},{9,17... | collective-permute-start | bytes 1966088 | tf_op jit(solution)/shard_map/ppermute | solution.py:100
  237.2 23.0 %collective-permute-start.35 = (bf16[320,2560]{1,0:T(8,128)(2,1)}, bf16[320,2560]{1,0:T(8,128)(2,1)}, u32[]{:S(2)}, u32[]{:S(2)}) collective-permute-start(bf16[320,2560]{1,0:T(8,128)(2,1)} %slice_dynamic-update-slice_fusion.18.mine), channel_id=1, source_target_pairs={{0,1},{1,0},{2,3},{3,2},{4,5},{5,4},{6,7},{7,6},{8,9},{9,8},{10,11... | collective-permute-start | bytes 4915208 | tf_op jit(solution)/shard_map/ppermute | solution.py:78
  267.8 24.5 %collective-permute-start.37 = (bf16[320,2560]{1,0:T(8,128)(2,1)}, bf16[320,2560]{1,0:T(8,128)(2,1)}, u32[]{:S(2)}, u32[]{:S(2)}) collective-permute-start(bf16[320,2560]{1,0:T(8,128)(2,1)} %constant_dynamic-update-slice_fusion.13.mine), channel_id=1, source_target_pairs={{0,1},{1,0},{2,3},{3,2},{4,5},{5,4},{6,7},{7,6},{8,9},{9,8},{10,11... | collective-permute-start | bytes 4915208 | tf_op jit(solution)/shard_map/ppermute | solution.py:78
  318.2 33.0 %collective-permute-start.40 = (bf16[256,2560]{1,0:T(8,128)(2,1)S(1)}, bf16[256,2560]{1,0:T(8,128)(2,1)}, u32[]{:S(2)}, u32[]{:S(2)}) collective-permute-start(bf16[256,2560]{1,0:T(8,128)(2,1)S(1)} %multiply_convert_fusion), channel_id=1, source_target_pairs={{0,8},{1,9},{2,10},{3,11},{4,12},{5,13},{6,14},{7,15},{8,16},{9,17... | collective-permute-start | bytes 3932168 | tf_op jit(solution)/shard_map/ppermute | solution.py:100
  351.2 29.0 %collective-permute-start.45 = (bf16[256,2560]{1,0:T(8,128)(2,1)}, bf16[256,2560]{1,0:T(8,128)(2,1)}, u32[]{:S(2)}, u32[]{:S(2)}) collective-permute-start(bf16[256,2560]{1,0:T(8,128)(2,1)} %collective-permute-done.40), channel_id=1, source_target_pairs={{0,1},{1,0},{2,3},{3,2},{4,5},{5,4},{6,7},{7,6},{8,9},{9,8},{10,11... | collective-permute-start | bytes 3932168 | tf_op jit(solution)/shard_map/ppermute | solution.py:78
  351.2 33.7 %collective-permute-start.44 = (bf16[256,2560]{1,0:T(8,128)(2,1)}, bf16[256,2560]{1,0:T(8,128)(2,1)}, u32[]{:S(2)}, u32[]{:S(2)}) collective-permute-start(bf16[256,2560]{1,0:T(8,128)(2,1)} %collective-permute-done.40), channel_id=1, source_target_pairs={{0,8},{1,9},{2,10},{3,11},{4,12},{5,13},{6,14},{7,15},{8,16},{9,17... | collective-permute-start | bytes 3932168 | tf_op jit(solution)/shard_map/ppermute | solution.py:100
  351.6 25.1 %collective-permute-start.46 = (bf16[256,2560]{1,0:T(8,128)(2,1)}, bf16[256,2560]{1,0:T(8,128)(2,1)}, u32[]{:S(2)}, u32[]{:S(2)}) collective-permute-start(bf16[256,2560]{1,0:T(8,128)(2,1)} %pad_maximum_fusion.15), channel_id=1, source_target_pairs={{0,1},{1,0},{2,3},{3,2},{4,5},{5,4},{6,7},{7,6},{8,9},{9,8},{10,11... | collective-permute-start | bytes 3932168 | tf_op jit(solution)/shard_map/ppermute | solution.py:78
  384.9 23.6 %collective-permute-start.49 = (bf16[256,2560]{1,0:T(8,128)(2,1)}, bf16[256,2560]{1,0:T(8,128)(2,1)S(1)}, u32[]{:S(2)}, u32[]{:S(2)}) collective-permute-start(bf16[256,2560]{1,0:T(8,128)(2,1)} %collective-permute-done.44), channel_id=1, source_target_pairs={{0,1},{1,0},{2,3},{3,2},{4,5},{5,4},{6,7},{7,6},{8,9},{9,8},{10,11... | collective-permute-start | bytes 3932168 | tf_op jit(solution)/shard_map/ppermute | solution.py:78
  384.9 33.5 %collective-permute-start.48 = (bf16[256,2560]{1,0:T(8,128)(2,1)}, bf16[256,2560]{1,0:T(8,128)(2,1)}, u32[]{:S(2)}, u32[]{:S(2)}) collective-permute-start(bf16[256,2560]{1,0:T(8,128)(2,1)} %collective-permute-done.44), channel_id=1, source_target_pairs={{0,8},{1,9},{2,10},{3,11},{4,12},{5,13},{6,14},{7,15},{8,16},{9,17... | collective-permute-start | bytes 3932168 | tf_op jit(solution)/shard_map/ppermute | solution.py:100
  427.0 32.5 %collective-permute-start.55 = (bf16[256,2560]{1,0:T(8,128)(2,1)}, bf16[256,2560]{1,0:T(8,128)(2,1)}, u32[]{:S(2)}, u32[]{:S(2)}) collective-permute-start(bf16[256,2560]{1,0:T(8,128)(2,1)} %add_convert_fusion.6), channel_id=1, source_target_pairs={{0,8},{1,9},{2,10},{3,11},{4,12},{5,13},{6,14},{7,15},{8,16},{9,17... | collective-permute-start | bytes 3932168 | tf_op jit(solution)/shard_map/ppermute | solution.py:100
  470.9 31.6 %collective-permute-start.58 = (bf16[256,2560]{1,0:T(8,128)(2,1)}, bf16[256,2560]{1,0:T(8,128)(2,1)}, u32[]{:S(2)}, u32[]{:S(2)}) collective-permute-start(bf16[256,2560]{1,0:T(8,128)(2,1)} %add_convert_fusion.5), channel_id=1, source_target_pairs={{0,8},{1,9},{2,10},{3,11},{4,12},{5,13},{6,14},{7,15},{8,16},{9,17... | collective-permute-start | bytes 3932168 | tf_op jit(solution)/shard_map/ppermute | solution.py:100
  518.0 34.0 %collective-permute-start.60 = (bf16[4,256,2560]{2,1,0:T(8,128)(2,1)}, bf16[4,256,2560]{2,1,0:T(8,128)(2,1)}, u32[]{:S(2)}, u32[]{:S(2)}) collective-permute-start(bf16[4,256,2560]{2,1,0:T(8,128)(2,1)} %bitcast.65), channel_id=1, source_target_pairs={{0,1},{1,0},{2,3},{3,2},{4,5},{5,4},{6,7},{7,6},{8,9},{9,8},{10,11... | collective-permute-start | bytes 15728648 | tf_op jit(solution)/shard_map/ppermute | solution.py:78
  518.7 33.3 %collective-permute-start.59 = (bf16[256,2560]{1,0:T(8,128)(2,1)}, bf16[256,2560]{1,0:T(8,128)(2,1)}, u32[]{:S(2)}, u32[]{:S(2)}) collective-permute-start(bf16[256,2560]{1,0:T(8,128)(2,1)} %add_convert_fusion.4), channel_id=1, source_target_pairs={{0,8},{1,9},{2,10},{3,11},{4,12},{5,13},{6,14},{7,15},{8,16},{9,17... | collective-permute-start | bytes 3932168 | tf_op jit(solution)/shard_map/ppermute | solution.py:100
  560.5 33.1 %collective-permute-start.62 = (bf16[256,2560]{1,0:T(8,128)(2,1)S(1)}, bf16[256,2560]{1,0:T(8,128)(2,1)}, u32[]{:S(2)}, u32[]{:S(2)}) collective-permute-start(bf16[256,2560]{1,0:T(8,128)(2,1)S(1)} %fusion.81), channel_id=1, source_target_pairs={{0,8},{1,9},{2,10},{3,11},{4,12},{5,13},{6,14},{7,15},{8,16},{9,17... | collective-permute-start | bytes 3932168 | tf_op jit(solution)/shard_map/ppermute | solution.py:100
  609.0 46.3 %collective-permute-start.63 = (bf16[640,1280]{1,0:T(8,128)(2,1)}, bf16[640,1280]{1,0:T(8,128)(2,1)}, u32[]{:S(2)}, u32[]{:S(2)}) collective-permute-start(bf16[640,1280]{1,0:T(8,128)(2,1)} %constant_dynamic-slice_fusion.44), channel_id=1, source_target_pairs={{0,8},{1,9},{2,10},{3,11},{4,12},{5,13},{6,14},{7,15},{8,16},{9,17... | collective-permute-start | bytes 4915208 | tf_op jit(solution)/shard_map/ppermute | solution.py:100
  622.4 45.2 %collective-permute-start.66 = (bf16[256,1280]{1,0:T(8,128)(2,1)}, bf16[256,1280]{1,0:T(8,128)(2,1)}, u32[]{:S(2)}, u32[]{:S(2)}) collective-permute-start(bf16[256,1280]{1,0:T(8,128)(2,1)} %get-tuple-element.1342), channel_id=1, source_target_pairs={{0,1},{1,0},{2,3},{3,2},{4,5},{5,4},{6,7},{7,6},{8,9},{9,8},{10,11... | collective-permute-start | bytes 1966088 | tf_op jit(solution)/shard_map/ppermute | solution.py:78
  659.6 31.6 %collective-permute-start.64 = (bf16[256,2560]{1,0:T(8,128)(2,1)}, bf16[256,2560]{1,0:T(8,128)(2,1)}, u32[]{:S(2)}, u32[]{:S(2)}) collective-permute-start(bf16[256,2560]{1,0:T(8,128)(2,1)} %pad_maximum_fusion.18), channel_id=1, source_target_pairs={{0,2},{1,3},{2,0},{3,1},{4,6},{5,7},{6,4},{7,5},{8,10},{9,11},{10,... | collective-permute-start | bytes 3932168 | tf_op jit(solution)/shard_map/ppermute | solution.py:78
  659.9 31.4 %collective-permute-start.65 = (bf16[256,2560]{1,0:T(8,128)(2,1)}, bf16[256,2560]{1,0:T(8,128)(2,1)}, u32[]{:S(2)}, u32[]{:S(2)}) collective-permute-start(bf16[256,2560]{1,0:T(8,128)(2,1)} %pad_maximum_fusion.19), channel_id=1, source_target_pairs={{0,4},{1,5},{2,6},{3,7},{4,0},{5,1},{6,2},{7,3},{8,12},{9,13},{10,... | collective-permute-start | bytes 3932168 | tf_op jit(solution)/shard_map/ppermute | solution.py:78
  664.5 40.4 %collective-permute-start.68 = (bf16[640,1280]{1,0:T(8,128)(2,1)}, bf16[640,1280]{1,0:T(8,128)(2,1)}, u32[]{:S(2)}, u32[]{:S(2)}) collective-permute-start(bf16[640,1280]{1,0:T(8,128)(2,1)} %add_convert_fusion.2), channel_id=1, source_target_pairs={{0,8},{1,9},{2,10},{3,11},{4,12},{5,13},{6,14},{7,15},{8,16},{9,17... | collective-permute-start | bytes 4915208 | tf_op jit(solution)/shard_map/ppermute | solution.py:100
  706.7 38.4 %collective-permute-start.71 = (bf16[160,1536]{1,0:T(8,128)(2,1)}, bf16[160,1536]{1,0:T(8,128)(2,1)S(1)}, u32[]{:S(2)}, u32[]{:S(2)}) collective-permute-start(bf16[160,1536]{1,0:T(8,128)(2,1)} %pad_maximum_fusion.45), channel_id=1, source_target_pairs={{0,2},{1,3},{2,0},{3,1},{4,6},{5,7},{6,4},{7,5},{8,10},{9,11},{10,... | collective-permute-start | bytes 1474568 | tf_op jit(solution)/shard_map/ppermute | solution.py:78
  707.3 37.9 %collective-permute-start.72 = (bf16[160,1536]{1,0:T(8,128)(2,1)}, bf16[160,1536]{1,0:T(8,128)(2,1)}, u32[]{:S(2)}, u32[]{:S(2)}) collective-permute-start(bf16[160,1536]{1,0:T(8,128)(2,1)} %pad_maximum_fusion.46), channel_id=1, source_target_pairs={{0,4},{1,5},{2,6},{3,7},{4,0},{5,1},{6,2},{7,3},{8,12},{9,13},{10,... | collective-permute-start | bytes 1474568 | tf_op jit(solution)/shard_map/ppermute | solution.py:78
  717.4 38.9 %collective-permute-start.73 = (bf16[640,1280]{1,0:T(8,128)(2,1)}, bf16[640,1280]{1,0:T(8,128)(2,1)}, u32[]{:S(2)}, u32[]{:S(2)}) collective-permute-start(bf16[640,1280]{1,0:T(8,128)(2,1)} %add_convert_fusion.1), channel_id=1, source_target_pairs={{0,8},{1,9},{2,10},{3,11},{4,12},{5,13},{6,14},{7,15},{8,16},{9,17... | collective-permute-start | bytes 4915208 | tf_op jit(solution)/shard_map/ppermute | solution.py:100
  717.6 44.4 %collective-permute-start.69 = (bf16[384,2560]{1,0:T(8,128)(2,1)}, bf16[384,2560]{1,0:T(8,128)(2,1)}, u32[]{:S(2)}, u32[]{:S(2)}) collective-permute-start(bf16[384,2560]{1,0:T(8,128)(2,1)} %pad_maximum_fusion.13), channel_id=1, source_target_pairs={{0,2},{1,3},{2,0},{3,1},{4,6},{5,7},{6,4},{7,5},{8,10},{9,11},{10,... | collective-permute-start | bytes 5898248 | tf_op jit(solution)/shard_map/ppermute | solution.py:78
  718.1 44.0 %collective-permute-start.70 = (bf16[384,2560]{1,0:T(8,128)(2,1)}, bf16[384,2560]{1,0:T(8,128)(2,1)}, u32[]{:S(2)}, u32[]{:S(2)}) collective-permute-start(bf16[384,2560]{1,0:T(8,128)(2,1)} %pad_maximum_fusion.14), channel_id=1, source_target_pairs={{0,4},{1,5},{2,6},{3,7},{4,0},{5,1},{6,2},{7,3},{8,12},{9,13},{10,... | collective-permute-start | bytes 5898248 | tf_op jit(solution)/shard_map/ppermute | solution.py:78
  766.9 32.7 %collective-permute-start.78 = (bf16[240,1536]{1,0:T(8,128)(2,1)S(1)}, bf16[240,1536]{1,0:T(8,128)(2,1)S(1)}, u32[]{:S(2)}, u32[]{:S(2)}) collective-permute-start(bf16[240,1536]{1,0:T(8,128)(2,1)S(1)} %pad_maximum_fusion.33), channel_id=1, source_target_pairs={{0,2},{1,3},{2,0},{3,1},{4,6},{5,7},{6,4},{7,5},{8,10},{9,11},{10,... | collective-permute-start | bytes 2211848 | tf_op jit(solution)/shard_map/ppermute | solution.py:78
  768.7 30.9 %collective-permute-start.79 = (bf16[240,1536]{1,0:T(8,128)(2,1)S(1)}, bf16[240,1536]{1,0:T(8,128)(2,1)S(1)}, u32[]{:S(2)}, u32[]{:S(2)}) collective-permute-start(bf16[240,1536]{1,0:T(8,128)(2,1)S(1)} %pad_maximum_fusion.34), channel_id=1, source_target_pairs={{0,4},{1,5},{2,6},{3,7},{4,0},{5,1},{6,2},{7,3},{8,12},{9,13},{10,... | collective-permute-start | bytes 2211848 | tf_op jit(solution)/shard_map/ppermute | solution.py:78
  773.9 30.0 %collective-permute-start.75 = (bf16[256,2560]{1,0:T(8,128)(2,1)S(1)}, bf16[256,2560]{1,0:T(8,128)(2,1)S(1)}, u32[]{:S(2)}, u32[]{:S(2)}) collective-permute-start(bf16[256,2560]{1,0:T(8,128)(2,1)S(1)} %fusion.36), channel_id=1, source_target_pairs={{0,8},{1,9},{2,10},{3,11},{4,12},{5,13},{6,14},{7,15},{8,16},{9,17... | collective-permute-start | bytes 3932168 | tf_op jit(solution)/shard_map/ppermute | solution.py:100
  807.0 39.5 %collective-permute-start.82 = (bf16[256,2560]{1,0:T(8,128)(2,1)S(1)}, bf16[256,2560]{1,0:T(8,128)(2,1)S(1)}, u32[]{:S(2)}, u32[]{:S(2)}) collective-permute-start(bf16[256,2560]{1,0:T(8,128)(2,1)S(1)} %fusion.35), channel_id=1, source_target_pairs={{0,8},{1,9},{2,10},{3,11},{4,12},{5,13},{6,14},{7,15},{8,16},{9,17... | collective-permute-start | bytes 3932168 | tf_op jit(solution)/shard_map/ppermute | solution.py:100
  812.0 34.5 %collective-permute-start.85 = (bf16[160,1536]{1,0:T(8,128)(2,1)S(1)}, bf16[160,1536]{1,0:T(8,128)(2,1)S(1)}, u32[]{:S(2)}, u32[]{:S(2)}) collective-permute-start(bf16[160,1536]{1,0:T(8,128)(2,1)S(1)} %add_convert_fusion.13), channel_id=1, source_target_pairs={{0,8},{1,9},{2,10},{3,11},{4,12},{5,13},{6,14},{7,15},{8,16},{9,17... | collective-permute-start | bytes 1474568 | tf_op jit(solution)/shard_map/ppermute | solution.py:100
  814.3 32.1 %collective-permute-start.83 = (bf16[240,1536]{1,0:T(8,128)(2,1)S(1)}, bf16[240,1536]{1,0:T(8,128)(2,1)S(1)}, u32[]{:S(2)}, u32[]{:S(2)}) collective-permute-start(bf16[240,1536]{1,0:T(8,128)(2,1)S(1)} %pad_maximum_fusion.35), channel_id=1, source_target_pairs={{0,2},{1,3},{2,0},{3,1},{4,6},{5,7},{6,4},{7,5},{8,10},{9,11},{10,... | collective-permute-start | bytes 2211848 | tf_op jit(solution)/shard_map/ppermute | solution.py:78
  815.0 31.5 %collective-permute-start.84 = (bf16[240,1536]{1,0:T(8,128)(2,1)S(1)}, bf16[240,1536]{1,0:T(8,128)(2,1)S(1)}, u32[]{:S(2)}, u32[]{:S(2)}) collective-permute-start(bf16[240,1536]{1,0:T(8,128)(2,1)S(1)} %pad_maximum_fusion.36), channel_id=1, source_target_pairs={{0,4},{1,5},{2,6},{3,7},{4,0},{5,1},{6,2},{7,3},{8,12},{9,13},{10,... | collective-permute-start | bytes 2211848 | tf_op jit(solution)/shard_map/ppermute | solution.py:78
  848.9 23.4 %collective-permute-start.91 = (bf16[160,1536]{1,0:T(8,128)(2,1)S(1)}, bf16[160,1536]{1,0:T(8,128)(2,1)S(1)}, u32[]{:S(2)}, u32[]{:S(2)}) collective-permute-start(bf16[160,1536]{1,0:T(8,128)(2,1)S(1)} %add_convert_fusion.12), channel_id=1, source_target_pairs={{0,8},{1,9},{2,10},{3,11},{4,12},{5,13},{6,14},{7,15},{8,16},{9,17... | collective-permute-start | bytes 1474568 | tf_op jit(solution)/shard_map/ppermute | solution.py:100
  848.9 23.4 %collective-permute-start.89 = (bf16[240,1536]{1,0:T(8,128)(2,1)S(1)}, bf16[240,1536]{1,0:T(8,128)(2,1)S(1)}, u32[]{:S(2)}, u32[]{:S(2)}) collective-permute-start(bf16[240,1536]{1,0:T(8,128)(2,1)S(1)} %pad_maximum_fusion.37), channel_id=1, source_target_pairs={{0,2},{1,3},{2,0},{3,1},{4,6},{5,7},{6,4},{7,5},{8,10},{9,11},{10,... | collective-permute-start | bytes 2211848 | tf_op jit(solution)/shard_map/ppermute | solution.py:78
  849.6 22.7 %collective-permute-start.90 = (bf16[240,1536]{1,0:T(8,128)(2,1)S(1)}, bf16[240,1536]{1,0:T(8,128)(2,1)S(1)}, u32[]{:S(2)}, u32[]{:S(2)}) collective-permute-start(bf16[240,1536]{1,0:T(8,128)(2,1)S(1)} %pad_maximum_fusion.38), channel_id=1, source_target_pairs={{0,4},{1,5},{2,6},{3,7},{4,0},{5,1},{6,2},{7,3},{8,12},{9,13},{10,... | collective-permute-start | bytes 2211848 | tf_op jit(solution)/shard_map/ppermute | solution.py:78
  (196 other events, 2113.8 us)
Sparse Core Ops, SparseCore 0:
  151.5 167.4 all-gather.1
  552.1 59.8 reduce-scatter.1

commit v5 on v4

--- a/solution.py
+++ b/solution.py
@@ -498,10 +498,11 @@
         grad_hidden_b = grad_hidden.astype(BF)
 
         out_partial = dot_tn(attended_both, core_half(mv, grad_hidden_b), BF)
-        out_partial, grad_hidden_b, grads_all, norm_all, branch_ring = fence(
-            (out_partial, grad_hidden_b, grads_all, norm_all, branch_ring)
+        grad_attended = dot_nt(grad_hidden_b, w_out).astype(BF)
+        out_partial, grad_attended, grads_all, norm_all, branch_ring = fence(
+            (out_partial, grad_attended, grads_all, norm_all, branch_ring)
         )
-        held = {"grads": grads_all, "norm": norm_all, "out": out_partial, "branch": branch_ring}
+        held = {"attended": grad_attended, "grads": grads_all, "norm": norm_all, "out": out_partial, "branch": branch_ring}
 
         def scores_back(grad_attended):
             grad_probs = jnp.einsum(
@@ -656,12 +657,12 @@
                 held["out1"] = got_out
             if at == 0:
                 held["down_sum"] = down_sum
+                held["attended"] = held["attended"].reshape(seqs, LENGTH, H, HD)
+                held["scores"] = scores_back(held["attended"])
                 partials = [dot_tn(v, held["norm"], BF) for v in held["grads"]]
                 held["partials"] = partials
             if at == 1:
-                grad_attended = dot_nt(grad_hidden_b, w_out).astype(BF)
-                grad_attended = grad_attended.reshape(seqs, LENGTH, H, HD)
-                held["q"], held["kv"] = lin_back(scores_back(grad_attended), grad_attended)
+                held["q"], held["kv"] = lin_back(held.pop("scores"), held.pop("attended"))
             if at == 1:
                 both = jnp.concatenate([core_half(mv, held["q"]), core_half(mv, held["kv"])], 1)
                 held["lin"] = dot_tn(norm_both, both, BF)

time: 917 us -> 901 us (0.983)
  waiting for transfers between devices: 314 us -> 288 us
    ppermute x73, waiting for transfers between devices: 123 us -> 108 us  [flip(): return lax.ppermute(value, 'dp', [(i, i ^ bit) for i in range(self.n)])]
    ppermute x30, waiting for transfers between devices: 190 us -> 180 us  [up(): lax.ppermute(value, 'dp', [(i, (i + 8 * steps) % self.n) for i in range(s...]
    unnamed x297 -> x281, local copies, waits for them, and re-layouts: 57.6 us -> 54.4 us
  transfers between devices with their start and end apart: 105 -> 105, of which waited for: 48 -> 47; matrix products, arithmetic and copies ran while one was open for 39% -> 41% of each run, Pallas kernels for 7% -> 7%
where the time goes in v5:
time: 901 us; the launch traced here: 891 us
  waiting for transfers between devices  288 us (32%)
  matrix products  210 us (23%)
  other arithmetic  130 us (14%)
  local copies, waits for them, and re-layouts  115 us (13%)
  starting transfers between devices  69.6 us (8%)
  Pallas kernels  60 us (7%)
  between operations  17.1 us (2%)
    ppermute x30, waiting for transfers between devices, up(): lax.ppermute(value, 'dp', [(i, (i + 8 * steps) % self.n) for i in range(s...  180 us
    ppermute x73, waiting for transfers between devices, flip(): return lax.ppermute(value, 'dp', [(i, i ^ bit) for i in range(self.n)])  108 us
    dot_general x15, matrix products, dot_nt(): lax.dot_general(left, right, (((1,), (1,)), ((), ())), preferred_element_...  81.1 us
    dot_general x13, matrix products, dot_nn(): return jnp.dot(left, right, preferred_element_type=F32)  62.7 us
    pallas_call x8, Pallas kernels, put(): pl.pallas_call(place_kernel, out_shape=self.shape, grid_spec=pltpu.Prefet...  60 us
    dot_general x5, matrix products, dot_tn(): lax.dot_general(left, right, (((0,), (0,)), ((), ())), preferred_element_...  58.3 us
    unnamed x281, local copies, waits for them, and re-layouts  54.4 us
    ppermute x73, starting transfers between devices, flip(): return lax.ppermute(value, 'dp', [(i, i ^ bit) for i in range(self.n)])  52.2 us
  transfers between devices with their start and end apart: 105, of which 47 were waited for; matrix products, arithmetic and copies ran while one was open for 41% of the time, Pallas kernels for 7%

profile of v5, /device:TPU:0, one launch (start us, length us, event | category | flops | bytes accessed | tf_op | source)
XLA Modules:
  0.0 891.0 jit_solution(5788535073737659173)
XLA Ops:
  21.3 8.6 collective-permute-done.2
  35.7 13.4 %collective-permute-done.3 = bf16[80,3200]{1,0:T(8,128)(2,1)S(1)} collective-permute-done((bf16[80,3200]{1,0:T(8,128)(2,1)S(1)}, bf16[80,3200]{1,0:T(8,128)(2,1)S(1)}, u32[]{:S(2)}, u32[]{:S(2)}) %collective-permute-start.3) | collective-permute-done | bytes 512032 | tf_op jit(solution)/shard_map/ppermute | solution.py:100
  54.9 15.3 %collective-permute-done.6 = bf16[80,3200]{1,0:T(8,128)(2,1)S(1)} collective-permute-done((bf16[80,3200]{1,0:T(8,128)(2,1)S(1)}, bf16[80,3200]{1,0:T(8,128)(2,1)S(1)}, u32[]{:S(2)}, u32[]{:S(2)}) %collective-permute-start.6) | collective-permute-done | bytes 512032 | tf_op jit(solution)/shard_map/ppermute | solution.py:100
  81.1 7.8 place_rows.8.refs_0_
  88.8 10.3 %collective-permute-done.13 = bf16[128,2560]{1,0:T(8,128)(2,1)} collective-permute-done((bf16[128,2560]{1,0:T(8,128)(2,1)}, bf16[128,2560]{1,0:T(8,128)(2,1)}, u32[]{:S(2)}, u32[]{:S(2)}) %collective-permute-start.13) | collective-permute-done | bytes 655392 | tf_op jit(solution)/shard_map/ppermute | solution.py:100
  107.5 4.9 collective-permute-done.18
  114.3 7.7 place_rows.9.refs_0_
  131.4 7.7 place_rows.10.refs_0_
  157.8 8.2 place_rows.11
  166.1 15.2 %collective-permute-done.24 = bf16[80,2560]{1,0:T(8,128)(2,1)S(1)} collective-permute-done((bf16[80,2560]{1,0:T(8,128)(2,1)S(1)}, bf16[80,2560]{1,0:T(8,128)(2,1)S(1)}, u32[]{:S(2)}, u32[]{:S(2)}) %collective-permute-start.24) | collective-permute-done | bytes 409632 | tf_op jit(solution)/shard_map/ppermute | solution.py:100
  195.4 7.3 place_rows.12.refs_0_
  202.7 19.7 %collective-permute-done.30 = bf16[120,2560]{1,0:T(8,128)(2,1)} collective-permute-done((bf16[120,2560]{1,0:T(8,128)(2,1)}, bf16[120,2560]{1,0:T(8,128)(2,1)}, u32[]{:S(2)}, u32[]{:S(2)}) %collective-permute-start.30) | collective-permute-done | bytes 614432 | tf_op jit(solution)/shard_map/ppermute | solution.py:78
  243.0 8.9 fusion.2
  252.9 7.1 place_rows.13.refs_0_
  279.2 7.1 place_rows.14.refs_0_
  296.5 7.1 place_rows.15
  326.1 26.7 %collective-permute-done.40 = bf16[256,2560]{1,0:T(8,128)(2,1)} collective-permute-done((bf16[256,2560]{1,0:T(8,128)(2,1)S(1)}, bf16[256,2560]{1,0:T(8,128)(2,1)}, u32[]{:S(2)}, u32[]{:S(2)}) %collective-permute-start.40) | collective-permute-done | bytes 1310752 | tf_op jit(solution)/shard_map/ppermute | solution.py:100
  354.6 6.4 fusion.165
  366.8 5.6 fusion.52
  394.4 6.9 fusion.59
  430.4 7.4 fusion.66
  451.6 10.7 %collective-permute-done.55 = bf16[256,2560]{1,0:T(8,128)(2,1)} collective-permute-done((bf16[256,2560]{1,0:T(8,128)(2,1)}, bf16[256,2560]{1,0:T(8,128)(2,1)}, u32[]{:S(2)}, u32[]{:S(2)}) %collective-permute-start.55) | collective-permute-done | bytes 1310752 | tf_op jit(solution)/shard_map/ppermute | solution.py:100
  472.4 7.3 fusion.73
  494.8 9.1 %collective-permute-done.58 = bf16[256,2560]{1,0:T(8,128)(2,1)} collective-permute-done((bf16[256,2560]{1,0:T(8,128)(2,1)}, bf16[256,2560]{1,0:T(8,128)(2,1)}, u32[]{:S(2)}, u32[]{:S(2)}) %collective-permute-start.58) | collective-permute-done | bytes 1310752 | tf_op jit(solution)/shard_map/ppermute | solution.py:100
  513.0 7.5 convolution_convert_fusion.4
  520.6 4.8 pad_maximum_fusion
  525.4 16.1 %fusion.14 = bf16[1024,2560]{1,0:T(8,128)(2,1)} fusion(bf16[2048,1024]{1,0:T(8,128)(2,1)S(1)} %constant_dynamic-update-slice_fusion.16, bf16[512,2560]{1,0:T(8,128)(2,1)} %copy-done.47, bf16[512,2560]{1,0:T(8,128)(2,1)} %copy-done.46, bf16[512,2560]{1,0:T(8,128)(2,1)} %copy-done.45, bf16[512,2560]{1,0:T(8,128)(2,1)} %pad_maximum_fusion.4), kind=kOutput, calls=%fused_computation.23 | convolution fusion | flops 10781982720 | bytes 19922944 | tf_op jit(solution)/shard_map/dot_general | solution.py:50
  541.5 5.5 pad_maximum_fusion.1
  547.0 10.0 %convolution_convert_fusion.5 = bf16[1024,2560]{1,0:T(8,128)(2,1)} fusion(bf16[1024,1024]{1,0:T(8,128)(2,1)S(1)} %bitcast.327, bf16[1024,2560]{1,0:T(8,128)(2,1)} %bitcast.313), kind=kOutput, calls=%fused_computation.25 | convolution fusion | flops 5371330560 | bytes 12582912 | tf_op jit(solution)/shard_map/dot_general | solution.py:60
  567.6 10.0 %convolution_convert_fusion.6 = bf16[256,2560]{1,0:T(8,128)(2,1)} fusion(bf16[256,2560]{1,0:T(8,128)(2,1)S(1)} %fusion.162, bf16[2560,2560]{1,0:T(8,128)(2,1)} %place_rows.15), kind=kOutput, calls=%fused_computation.43 | convolution fusion | flops 3356098560 | bytes 15728640 | tf_op jit(solution)/shard_map/dot_general | solution.py:56
  577.6 5.5 convolution_convert_fusion.1
  583.2 17.2 %collective-permute-done.62 = bf16[256,2560]{1,0:T(8,128)(2,1)} collective-permute-done((bf16[256,2560]{1,0:T(8,128)(2,1)S(1)}, bf16[256,2560]{1,0:T(8,128)(2,1)}, u32[]{:S(2)}, u32[]{:S(2)}) %collective-permute-start.62) | collective-permute-done | bytes 1310752 | tf_op jit(solution)/shard_map/ppermute | solution.py:100
  609.7 16.8 %convolution_convert_fusion.3 = bf16[1024,2560]{1,0:T(8,128)(2,1)} fusion(bf16[2048,1024]{1,0:T(8,128)(2,1)S(1)} %copy-done.14, bf16[2048,2560]{1,0:T(8,128)(2,1)} %pad_maximum_fusion), kind=kOutput, calls=%fused_computation.22 | convolution fusion | flops 10740039680 | bytes 19922944 | tf_op jit(solution)/shard_map/dot_general | solution.py:50
  626.5 13.6 %convolution_convert_fusion.2 = bf16[1024,2560]{1,0:T(8,128)(2,1)} fusion(bf16[2048,1024]{1,0:T(8,128)(2,1)S(1)} %copy-done.12, bf16[2048,2560]{1,0:T(8,128)(2,1)S(1)} %bitcast.294), kind=kOutput, calls=%fused_computation.21 | convolution fusion | flops 10740039680 | bytes 19922944 | tf_op jit(solution)/shard_map/dot_general | solution.py:50
  666.6 6.2 convolution_convert_fusion
  672.9 5.6 collective-permute-done.64
  678.6 12.5 %collective-permute-done.68 = bf16[640,1280]{1,0:T(8,128)(2,1)} collective-permute-done((bf16[640,1280]{1,0:T(8,128)(2,1)}, bf16[640,1280]{1,0:T(8,128)(2,1)}, u32[]{:S(2)}, u32[]{:S(2)}) %collective-permute-start.68) | collective-permute-done | bytes 1638432 | tf_op jit(solution)/shard_map/ppermute | solution.py:100
  711.5 11.1 %fusion.26 = (f32[2560]{0:T(1024)S(1)}, f32[256]{0:T(256)S(1)}, f32[256,2560]{1,0:T(8,128)}) fusion(bf16[256,2560]{1,0:T(8,128)(2,1)S(1)} %copy-done.9, f32[256]{0:T(256)S(1)} %copy-done.101, f32[2560]{0:T(1024)S(1)} %copy-done.94, f32[256,2560]{1,0:T(8,128)} %fusion.40, bf16[256,2560]{0,1:T(8,128)(2,1)S(1)} %bitcast.308, bf16[2560,3200]{1,0:T(8,128)(2,1)} %place_rows.11), kind=kOutput, calls=%fused_computation.60 | convolution fusion | flops 3360683264 | bytes 20994048 | tf_op jit(solution)/shard_map/dot_general | solution.py:56
  725.6 6.5 convert_reduce_fusion.2
  733.1 9.7 %collective-permute-done.73 = bf16[640,1280]{1,0:T(8,128)(2,1)} collective-permute-done((bf16[640,1280]{1,0:T(8,128)(2,1)}, bf16[640,1280]{1,0:T(8,128)(2,1)}, u32[]{:S(2)}, u32[]{:S(2)}) %collective-permute-start.73) | collective-permute-done | bytes 1638432 | tf_op jit(solution)/shard_map/ppermute | solution.py:100
  742.7 5.3 collective-permute-done.69
  777.2 4.8 collective-permute-done.76
  783.6 5.3 collective-permute-done.75
  808.1 12.8 %collective-permute-done.87 = bf16[160,1280]{1,0:T(8,128)(2,1)S(1)} collective-permute-done((bf16[160,1280]{1,0:T(8,128)(2,1)S(1)}, bf16[160,1280]{1,0:T(8,128)(2,1)S(1)}, u32[]{:S(2)}, u32[]{:S(2)}) %collective-permute-start.87) | collective-permute-done | bytes 409632 | tf_op jit(solution)/shard_map/ppermute | solution.py:78
  820.9 9.1 %collective-permute-done.85 = bf16[160,1536]{1,0:T(8,128)(2,1)S(1)} collective-permute-done((bf16[160,1536]{1,0:T(8,128)(2,1)S(1)}, bf16[160,1536]{1,0:T(8,128)(2,1)S(1)}, u32[]{:S(2)}, u32[]{:S(2)}) %collective-permute-start.85) | collective-permute-done | bytes 491552 | tf_op jit(solution)/shard_map/ppermute | solution.py:100
  838.5 17.3 %collective-permute-done.93 = bf16[80,1280]{1,0:T(8,128)(2,1)S(1)} collective-permute-done((bf16[80,1280]{1,0:T(8,128)(2,1)S(1)}, bf16[80,1280]{1,0:T(8,128)(2,1)S(1)}, u32[]{:S(2)}, u32[]{:S(2)}) %collective-permute-start.93) | collective-permute-done | bytes 204832 | tf_op jit(solution)/shard_map/ppermute | solution.py:78
  867.5 5.0 collective-permute-done.96
  872.5 7.1 collective-permute-done.97
  (725 shorter events, 412.1 us)
Async XLA Ops:
  7.2 346.6 %all-gather.2.cloned.1.call-start = ((), (), s32[]{:S(2)}) async-start(), calls=%async_computation.1 | async-start | bytes 19660800 | tf_op jit(solution)/shard_map/all_gather | solution.py:367
  77.8 23.0 %collective-permute-start.12 = (bf16[320,3200]{1,0:T(8,128)(2,1)}, bf16[320,3200]{1,0:T(8,128)(2,1)}, u32[]{:S(2)}, u32[]{:S(2)}) collective-permute-start(bf16[320,3200]{1,0:T(8,128)(2,1)} %slice_dynamic-update-slice_fusion.14.mine), channel_id=1, source_target_pairs={{0,1},{1,0},{2,3},{3,2},{4,5},{5,4},{6,7},{7,6},{8,9},{9,8},{10,11... | collective-permute-start | bytes 6144008 | tf_op jit(solution)/shard_map/ppermute | solution.py:78
  151.3 30.0 %collective-permute-start.27 = (bf16[320,2560]{1,0:T(8,128)(2,1)S(1)}, bf16[320,2560]{1,0:T(8,128)(2,1)}, u32[]{:S(2)}, u32[]{:S(2)}) collective-permute-start(bf16[320,2560]{1,0:T(8,128)(2,1)S(1)} %slice_dynamic-update-slice_fusion.22.mine), channel_id=1, source_target_pairs={{0,1},{1,0},{2,3},{3,2},{4,5},{5,4},{6,7},{7,6},{8,9},{9,8},{10,11... | collective-permute-start | bytes 4915208 | tf_op jit(solution)/shard_map/ppermute | solution.py:78
  151.4 492.2 %reduce-scatter.2.cloned.1.call-start = ((), (), s32[]{:S(2)}) async-start(), calls=%async_computation.2 | async-start | bytes 6553600 | tf_op jit(solution)/shard_map/reduce_scatter | solution.py:486
  153.8 27.5 %collective-permute-start.28 = (bf16[128,2560]{1,0:T(8,128)(2,1)}, bf16[128,2560]{1,0:T(8,128)(2,1)}, u32[]{:S(2)}, u32[]{:S(2)}) collective-permute-start(bf16[128,2560]{1,0:T(8,128)(2,1)} %get-tuple-element.725), channel_id=1, source_target_pairs={{0,8},{1,9},{2,10},{3,11},{4,12},{5,13},{6,14},{7,15},{8,16},{9,17... | collective-permute-start | bytes 1966088 | tf_op jit(solution)/shard_map/ppermute | solution.py:100
  155.0 26.3 %collective-permute-start.26 = (bf16[120,2560]{1,0:T(8,128)(2,1)}, bf16[120,2560]{1,0:T(8,128)(2,1)}, u32[]{:S(2)}, u32[]{:S(2)}) collective-permute-start(bf16[120,2560]{1,0:T(8,128)(2,1)} %get-tuple-element.1371), channel_id=1, source_target_pairs={{0,4},{1,5},{2,6},{3,7},{4,0},{5,1},{6,2},{7,3},{8,12},{9,13},{10,... | collective-permute-start | bytes 1843208 | tf_op jit(solution)/shard_map/ppermute | solution.py:78
  155.5 25.8 %collective-permute-start.25 = (bf16[120,2560]{1,0:T(8,128)(2,1)}, bf16[120,2560]{1,0:T(8,128)(2,1)}, u32[]{:S(2)}, u32[]{:S(2)}) collective-permute-start(bf16[120,2560]{1,0:T(8,128)(2,1)} %get-tuple-element.1372), channel_id=1, source_target_pairs={{0,2},{1,3},{2,0},{3,1},{4,6},{5,7},{6,4},{7,5},{8,10},{9,11},{10,... | collective-permute-start | bytes 1843208 | tf_op jit(solution)/shard_map/ppermute | solution.py:78
  157.0 24.3 %collective-permute-start.24 = (bf16[80,2560]{1,0:T(8,128)(2,1)S(1)}, bf16[80,2560]{1,0:T(8,128)(2,1)S(1)}, u32[]{:S(2)}, u32[]{:S(2)}) collective-permute-start(bf16[80,2560]{1,0:T(8,128)(2,1)S(1)} %copy-done.53), channel_id=1, source_target_pairs={{0,8},{1,9},{2,10},{3,11},{4,12},{5,13},{6,14},{7,15},{8,16},{9,17... | collective-permute-start | bytes 1228808 | tf_op jit(solution)/shard_map/ppermute | solution.py:100
  186.2 36.7 %collective-permute-start.31 = (bf16[320,2560]{1,0:T(8,128)(2,1)S(1)}, bf16[320,2560]{1,0:T(8,128)(2,1)}, u32[]{:S(2)}, u32[]{:S(2)}) collective-permute-start(bf16[320,2560]{1,0:T(8,128)(2,1)S(1)} %slice_dynamic-update-slice_fusion.20.mine), channel_id=1, source_target_pairs={{0,1},{1,0},{2,3},{3,2},{4,5},{5,4},{6,7},{7,6},{8,9},{9,8},{10,11... | collective-permute-start | bytes 4915208 | tf_op jit(solution)/shard_map/ppermute | solution.py:78
  191.2 31.6 %collective-permute-start.32 = (bf16[128,2560]{1,0:T(8,128)(2,1)}, bf16[128,2560]{1,0:T(8,128)(2,1)}, u32[]{:S(2)}, u32[]{:S(2)}) collective-permute-start(bf16[128,2560]{1,0:T(8,128)(2,1)} %collective-permute-done.13), channel_id=1, source_target_pairs={{0,8},{1,9},{2,10},{3,11},{4,12},{5,13},{6,14},{7,15},{8,16},{9,17... | collective-permute-start | bytes 1966088 | tf_op jit(solution)/shard_map/ppermute | solution.py:100
  192.4 30.0 %collective-permute-start.30 = (bf16[120,2560]{1,0:T(8,128)(2,1)}, bf16[120,2560]{1,0:T(8,128)(2,1)}, u32[]{:S(2)}, u32[]{:S(2)}) collective-permute-start(bf16[120,2560]{1,0:T(8,128)(2,1)} %get-tuple-element.1369), channel_id=1, source_target_pairs={{0,4},{1,5},{2,6},{3,7},{4,0},{5,1},{6,2},{7,3},{8,12},{9,13},{10,... | collective-permute-start | bytes 1843208 | tf_op jit(solution)/shard_map/ppermute | solution.py:78
  192.9 29.9 %collective-permute-start.29 = (bf16[120,2560]{1,0:T(8,128)(2,1)}, bf16[120,2560]{1,0:T(8,128)(2,1)}, u32[]{:S(2)}, u32[]{:S(2)}) collective-permute-start(bf16[120,2560]{1,0:T(8,128)(2,1)} %get-tuple-element.1370), channel_id=1, source_target_pairs={{0,2},{1,3},{2,0},{3,1},{4,6},{5,7},{6,4},{7,5},{8,10},{9,11},{10,... | collective-permute-start | bytes 1843208 | tf_op jit(solution)/shard_map/ppermute | solution.py:78
  226.1 35.3 %collective-permute-start.34 = (bf16[40,2560]{1,0:T(8,128)(2,1)}, bf16[40,2560]{1,0:T(8,128)(2,1)}, u32[]{:S(2)}, u32[]{:S(2)}) collective-permute-start(bf16[40,2560]{1,0:T(8,128)(2,1)} %slice.481), channel_id=1, source_target_pairs={{0,2},{1,3},{2,0},{3,1},{4,6},{5,7},{6,4},{7,5},{8,10},{9,11},{10,... | collective-permute-start | bytes 614408 | tf_op jit(solution)/shard_map/ppermute | solution.py:78
  227.6 33.8 %collective-permute-start.33 = (bf16[40,2560]{1,0:T(8,128)(2,1)}, bf16[40,2560]{1,0:T(8,128)(2,1)}, u32[]{:S(2)}, u32[]{:S(2)}) collective-permute-start(bf16[40,2560]{1,0:T(8,128)(2,1)} %slice.480), channel_id=1, source_target_pairs={{0,4},{1,5},{2,6},{3,7},{4,0},{5,1},{6,2},{7,3},{8,12},{9,13},{10,... | collective-permute-start | bytes 614408 | tf_op jit(solution)/shard_map/ppermute | solution.py:78
  229.0 32.4 %collective-permute-start.36 = (bf16[128,2560]{1,0:T(8,128)(2,1)}, bf16[128,2560]{1,0:T(8,128)(2,1)}, u32[]{:S(2)}, u32[]{:S(2)}) collective-permute-start(bf16[128,2560]{1,0:T(8,128)(2,1)} %collective-permute-done.28), channel_id=1, source_target_pairs={{0,8},{1,9},{2,10},{3,11},{4,12},{5,13},{6,14},{7,15},{8,16},{9,17... | collective-permute-start | bytes 1966088 | tf_op jit(solution)/shard_map/ppermute | solution.py:100
  237.2 24.2 %collective-permute-start.35 = (bf16[320,2560]{1,0:T(8,128)(2,1)}, bf16[320,2560]{1,0:T(8,128)(2,1)}, u32[]{:S(2)}, u32[]{:S(2)}) collective-permute-start(bf16[320,2560]{1,0:T(8,128)(2,1)} %slice_dynamic-update-slice_fusion.18.mine), channel_id=1, source_target_pairs={{0,1},{1,0},{2,3},{3,2},{4,5},{5,4},{6,7},{7,6},{8,9},{9,8},{10,11... | collective-permute-start | bytes 4915208 | tf_op jit(solution)/shard_map/ppermute | solution.py:78
  269.0 24.8 %collective-permute-start.37 = (bf16[320,2560]{1,0:T(8,128)(2,1)}, bf16[320,2560]{1,0:T(8,128)(2,1)}, u32[]{:S(2)}, u32[]{:S(2)}) collective-permute-start(bf16[320,2560]{1,0:T(8,128)(2,1)} %constant_dynamic-update-slice_fusion.13.mine), channel_id=1, source_target_pairs={{0,1},{1,0},{2,3},{3,2},{4,5},{5,4},{6,7},{7,6},{8,9},{9,8},{10,11... | collective-permute-start | bytes 4915208 | tf_op jit(solution)/shard_map/ppermute | solution.py:78
  293.7 22.1 %collective-permute-start.39 = (bf16[128,2560]{1,0:T(8,128)(2,1)}, bf16[128,2560]{1,0:T(8,128)(2,1)}, u32[]{:S(2)}, u32[]{:S(2)}) collective-permute-start(bf16[128,2560]{1,0:T(8,128)(2,1)} %collective-permute-done.36), channel_id=1, source_target_pairs={{0,8},{1,9},{2,10},{3,11},{4,12},{5,13},{6,14},{7,15},{8,16},{9,17... | collective-permute-start | bytes 1966088 | tf_op jit(solution)/shard_map/ppermute | solution.py:100
  319.7 33.0 %collective-permute-start.40 = (bf16[256,2560]{1,0:T(8,128)(2,1)S(1)}, bf16[256,2560]{1,0:T(8,128)(2,1)}, u32[]{:S(2)}, u32[]{:S(2)}) collective-permute-start(bf16[256,2560]{1,0:T(8,128)(2,1)S(1)} %multiply_convert_fusion), channel_id=1, source_target_pairs={{0,8},{1,9},{2,10},{3,11},{4,12},{5,13},{6,14},{7,15},{8,16},{9,17... | collective-permute-start | bytes 3932168 | tf_op jit(solution)/shard_map/ppermute | solution.py:100
  352.7 30.9 %collective-permute-start.45 = (bf16[256,2560]{1,0:T(8,128)(2,1)}, bf16[256,2560]{1,0:T(8,128)(2,1)}, u32[]{:S(2)}, u32[]{:S(2)}) collective-permute-start(bf16[256,2560]{1,0:T(8,128)(2,1)} %collective-permute-done.40), channel_id=1, source_target_pairs={{0,1},{1,0},{2,3},{3,2},{4,5},{5,4},{6,7},{7,6},{8,9},{9,8},{10,11... | collective-permute-start | bytes 3932168 | tf_op jit(solution)/shard_map/ppermute | solution.py:78
  352.7 33.8 %collective-permute-start.44 = (bf16[256,2560]{1,0:T(8,128)(2,1)}, bf16[256,2560]{1,0:T(8,128)(2,1)}, u32[]{:S(2)}, u32[]{:S(2)}) collective-permute-start(bf16[256,2560]{1,0:T(8,128)(2,1)} %collective-permute-done.40), channel_id=1, source_target_pairs={{0,8},{1,9},{2,10},{3,11},{4,12},{5,13},{6,14},{7,15},{8,16},{9,17... | collective-permute-start | bytes 3932168 | tf_op jit(solution)/shard_map/ppermute | solution.py:100
  353.2 26.9 %collective-permute-start.46 = (bf16[256,2560]{1,0:T(8,128)(2,1)}, bf16[256,2560]{1,0:T(8,128)(2,1)}, u32[]{:S(2)}, u32[]{:S(2)}) collective-permute-start(bf16[256,2560]{1,0:T(8,128)(2,1)} %pad_maximum_fusion.15), channel_id=1, source_target_pairs={{0,1},{1,0},{2,3},{3,2},{4,5},{5,4},{6,7},{7,6},{8,9},{9,8},{10,11... | collective-permute-start | bytes 3932168 | tf_op jit(solution)/shard_map/ppermute | solution.py:78
  386.5 26.1 %collective-permute-start.49 = (bf16[256,2560]{1,0:T(8,128)(2,1)}, bf16[256,2560]{1,0:T(8,128)(2,1)}, u32[]{:S(2)}, u32[]{:S(2)}) collective-permute-start(bf16[256,2560]{1,0:T(8,128)(2,1)} %collective-permute-done.44), channel_id=1, source_target_pairs={{0,1},{1,0},{2,3},{3,2},{4,5},{5,4},{6,7},{7,6},{8,9},{9,8},{10,11... | collective-permute-start | bytes 3932168 | tf_op jit(solution)/shard_map/ppermute | solution.py:78
  386.6 33.4 %collective-permute-start.48 = (bf16[256,2560]{1,0:T(8,128)(2,1)}, bf16[256,2560]{1,0:T(8,128)(2,1)S(1)}, u32[]{:S(2)}, u32[]{:S(2)}) collective-permute-start(bf16[256,2560]{1,0:T(8,128)(2,1)} %collective-permute-done.44), channel_id=1, source_target_pairs={{0,8},{1,9},{2,10},{3,11},{4,12},{5,13},{6,14},{7,15},{8,16},{9,17... | collective-permute-start | bytes 3932168 | tf_op jit(solution)/shard_map/ppermute | solution.py:100
  429.8 32.4 %collective-permute-start.55 = (bf16[256,2560]{1,0:T(8,128)(2,1)}, bf16[256,2560]{1,0:T(8,128)(2,1)}, u32[]{:S(2)}, u32[]{:S(2)}) collective-permute-start(bf16[256,2560]{1,0:T(8,128)(2,1)} %add_convert_fusion.6), channel_id=1, source_target_pairs={{0,8},{1,9},{2,10},{3,11},{4,12},{5,13},{6,14},{7,15},{8,16},{9,17... | collective-permute-start | bytes 3932168 | tf_op jit(solution)/shard_map/ppermute | solution.py:100
  472.3 31.5 %collective-permute-start.58 = (bf16[256,2560]{1,0:T(8,128)(2,1)}, bf16[256,2560]{1,0:T(8,128)(2,1)}, u32[]{:S(2)}, u32[]{:S(2)}) collective-permute-start(bf16[256,2560]{1,0:T(8,128)(2,1)} %add_convert_fusion.5), channel_id=1, source_target_pairs={{0,8},{1,9},{2,10},{3,11},{4,12},{5,13},{6,14},{7,15},{8,16},{9,17... | collective-permute-start | bytes 3932168 | tf_op jit(solution)/shard_map/ppermute | solution.py:100
  507.2 49.8 %collective-permute-start.59 = (bf16[256,2560]{1,0:T(8,128)(2,1)}, bf16[256,2560]{1,0:T(8,128)(2,1)}, u32[]{:S(2)}, u32[]{:S(2)}) collective-permute-start(bf16[256,2560]{1,0:T(8,128)(2,1)} %add_convert_fusion.4), channel_id=1, source_target_pairs={{0,8},{1,9},{2,10},{3,11},{4,12},{5,13},{6,14},{7,15},{8,16},{9,17... | collective-permute-start | bytes 3932168 | tf_op jit(solution)/shard_map/ppermute | solution.py:100
  520.5 36.5 %collective-permute-start.60 = (bf16[4,256,2560]{2,1,0:T(8,128)(2,1)}, bf16[4,256,2560]{2,1,0:T(8,128)(2,1)}, u32[]{:S(2)}, u32[]{:S(2)}) collective-permute-start(bf16[4,256,2560]{2,1,0:T(8,128)(2,1)} %bitcast.65), channel_id=1, source_target_pairs={{0,1},{1,0},{2,3},{3,2},{4,5},{5,4},{6,7},{7,6},{8,9},{9,8},{10,11... | collective-permute-start | bytes 15728648 | tf_op jit(solution)/shard_map/ppermute | solution.py:78
  567.6 32.7 %collective-permute-start.62 = (bf16[256,2560]{1,0:T(8,128)(2,1)S(1)}, bf16[256,2560]{1,0:T(8,128)(2,1)}, u32[]{:S(2)}, u32[]{:S(2)}) collective-permute-start(bf16[256,2560]{1,0:T(8,128)(2,1)S(1)} %fusion.81), channel_id=1, source_target_pairs={{0,8},{1,9},{2,10},{3,11},{4,12},{5,13},{6,14},{7,15},{8,16},{9,17... | collective-permute-start | bytes 3932168 | tf_op jit(solution)/shard_map/ppermute | solution.py:100
  604.4 39.1 %collective-permute-start.63 = (bf16[640,1280]{1,0:T(8,128)(2,1)S(1)}, bf16[640,1280]{1,0:T(8,128)(2,1)}, u32[]{:S(2)}, u32[]{:S(2)}) collective-permute-start(bf16[640,1280]{1,0:T(8,128)(2,1)S(1)} %constant_dynamic-slice_fusion.44), channel_id=1, source_target_pairs={{0,8},{1,9},{2,10},{3,11},{4,12},{5,13},{6,14},{7,15},{8,16},{9,17... | collective-permute-start | bytes 4915208 | tf_op jit(solution)/shard_map/ppermute | solution.py:100
  648.9 29.6 %collective-permute-start.64 = (bf16[256,2560]{1,0:T(8,128)(2,1)}, bf16[256,2560]{1,0:T(8,128)(2,1)}, u32[]{:S(2)}, u32[]{:S(2)}) collective-permute-start(bf16[256,2560]{1,0:T(8,128)(2,1)} %pad_maximum_fusion.18), channel_id=1, source_target_pairs={{0,2},{1,3},{2,0},{3,1},{4,6},{5,7},{6,4},{7,5},{8,10},{9,11},{10,... | collective-permute-start | bytes 3932168 | tf_op jit(solution)/shard_map/ppermute | solution.py:78
  649.1 29.5 %collective-permute-start.65 = (bf16[256,2560]{1,0:T(8,128)(2,1)}, bf16[256,2560]{1,0:T(8,128)(2,1)}, u32[]{:S(2)}, u32[]{:S(2)}) collective-permute-start(bf16[256,2560]{1,0:T(8,128)(2,1)} %pad_maximum_fusion.19), channel_id=1, source_target_pairs={{0,4},{1,5},{2,6},{3,7},{4,0},{5,1},{6,2},{7,3},{8,12},{9,13},{10,... | collective-permute-start | bytes 3932168 | tf_op jit(solution)/shard_map/ppermute | solution.py:78
  653.4 37.7 %collective-permute-start.68 = (bf16[640,1280]{1,0:T(8,128)(2,1)}, bf16[640,1280]{1,0:T(8,128)(2,1)}, u32[]{:S(2)}, u32[]{:S(2)}) collective-permute-start(bf16[640,1280]{1,0:T(8,128)(2,1)} %add_convert_fusion.2), channel_id=1, source_target_pairs={{0,8},{1,9},{2,10},{3,11},{4,12},{5,13},{6,14},{7,15},{8,16},{9,17... | collective-permute-start | bytes 4915208 | tf_op jit(solution)/shard_map/ppermute | solution.py:100
  694.6 38.4 %collective-permute-start.71 = (bf16[160,1536]{1,0:T(8,128)(2,1)}, bf16[160,1536]{1,0:T(8,128)(2,1)S(1)}, u32[]{:S(2)}, u32[]{:S(2)}) collective-permute-start(bf16[160,1536]{1,0:T(8,128)(2,1)} %pad_maximum_fusion.45), channel_id=1, source_target_pairs={{0,2},{1,3},{2,0},{3,1},{4,6},{5,7},{6,4},{7,5},{8,10},{9,11},{10,... | collective-permute-start | bytes 1474568 | tf_op jit(solution)/shard_map/ppermute | solution.py:78
  696.1 36.9 %collective-permute-start.72 = (bf16[160,1536]{1,0:T(8,128)(2,1)}, bf16[160,1536]{1,0:T(8,128)(2,1)}, u32[]{:S(2)}, u32[]{:S(2)}) collective-permute-start(bf16[160,1536]{1,0:T(8,128)(2,1)} %pad_maximum_fusion.46), channel_id=1, source_target_pairs={{0,4},{1,5},{2,6},{3,7},{4,0},{5,1},{6,2},{7,3},{8,12},{9,13},{10,... | collective-permute-start | bytes 1474568 | tf_op jit(solution)/shard_map/ppermute | solution.py:78
  706.1 36.6 %collective-permute-start.73 = (bf16[640,1280]{1,0:T(8,128)(2,1)}, bf16[640,1280]{1,0:T(8,128)(2,1)}, u32[]{:S(2)}, u32[]{:S(2)}) collective-permute-start(bf16[640,1280]{1,0:T(8,128)(2,1)} %add_convert_fusion.1), channel_id=1, source_target_pairs={{0,8},{1,9},{2,10},{3,11},{4,12},{5,13},{6,14},{7,15},{8,16},{9,17... | collective-permute-start | bytes 4915208 | tf_op jit(solution)/shard_map/ppermute | solution.py:100
  706.4 41.6 %collective-permute-start.69 = (bf16[384,2560]{1,0:T(8,128)(2,1)}, bf16[384,2560]{1,0:T(8,128)(2,1)}, u32[]{:S(2)}, u32[]{:S(2)}) collective-permute-start(bf16[384,2560]{1,0:T(8,128)(2,1)} %pad_maximum_fusion.13), channel_id=1, source_target_pairs={{0,2},{1,3},{2,0},{3,1},{4,6},{5,7},{6,4},{7,5},{8,10},{9,11},{10,... | collective-permute-start | bytes 5898248 | tf_op jit(solution)/shard_map/ppermute | solution.py:78
  706.8 41.8 %collective-permute-start.70 = (bf16[384,2560]{1,0:T(8,128)(2,1)}, bf16[384,2560]{1,0:T(8,128)(2,1)}, u32[]{:S(2)}, u32[]{:S(2)}) collective-permute-start(bf16[384,2560]{1,0:T(8,128)(2,1)} %pad_maximum_fusion.14), channel_id=1, source_target_pairs={{0,4},{1,5},{2,6},{3,7},{4,0},{5,1},{6,2},{7,3},{8,12},{9,13},{10,... | collective-permute-start | bytes 5898248 | tf_op jit(solution)/shard_map/ppermute | solution.py:78
  753.5 30.1 %collective-permute-start.78 = (bf16[240,1536]{1,0:T(8,128)(2,1)S(1)}, bf16[240,1536]{1,0:T(8,128)(2,1)S(1)}, u32[]{:S(2)}, u32[]{:S(2)}) collective-permute-start(bf16[240,1536]{1,0:T(8,128)(2,1)S(1)} %pad_maximum_fusion.33), channel_id=1, source_target_pairs={{0,2},{1,3},{2,0},{3,1},{4,6},{5,7},{6,4},{7,5},{8,10},{9,11},{10,... | collective-permute-start | bytes 2211848 | tf_op jit(solution)/shard_map/ppermute | solution.py:78
  754.6 28.9 %collective-permute-start.79 = (bf16[240,1536]{1,0:T(8,128)(2,1)S(1)}, bf16[240,1536]{1,0:T(8,128)(2,1)S(1)}, u32[]{:S(2)}, u32[]{:S(2)}) collective-permute-start(bf16[240,1536]{1,0:T(8,128)(2,1)S(1)} %pad_maximum_fusion.34), channel_id=1, source_target_pairs={{0,4},{1,5},{2,6},{3,7},{4,0},{5,1},{6,2},{7,3},{8,12},{9,13},{10,... | collective-permute-start | bytes 2211848 | tf_op jit(solution)/shard_map/ppermute | solution.py:78
  760.4 28.5 %collective-permute-start.75 = (bf16[256,2560]{1,0:T(8,128)(2,1)S(1)}, bf16[256,2560]{1,0:T(8,128)(2,1)S(1)}, u32[]{:S(2)}, u32[]{:S(2)}) collective-permute-start(bf16[256,2560]{1,0:T(8,128)(2,1)S(1)} %fusion.36), channel_id=1, source_target_pairs={{0,8},{1,9},{2,10},{3,11},{4,12},{5,13},{6,14},{7,15},{8,16},{9,17... | collective-permute-start | bytes 3932168 | tf_op jit(solution)/shard_map/ppermute | solution.py:100
  792.1 38.0 %collective-permute-start.82 = (bf16[256,2560]{1,0:T(8,128)(2,1)S(1)}, bf16[256,2560]{1,0:T(8,128)(2,1)S(1)}, u32[]{:S(2)}, u32[]{:S(2)}) collective-permute-start(bf16[256,2560]{1,0:T(8,128)(2,1)S(1)} %fusion.35), channel_id=1, source_target_pairs={{0,8},{1,9},{2,10},{3,11},{4,12},{5,13},{6,14},{7,15},{8,16},{9,17... | collective-permute-start | bytes 3932168 | tf_op jit(solution)/shard_map/ppermute | solution.py:100
  797.0 33.0 %collective-permute-start.85 = (bf16[160,1536]{1,0:T(8,128)(2,1)S(1)}, bf16[160,1536]{1,0:T(8,128)(2,1)S(1)}, u32[]{:S(2)}, u32[]{:S(2)}) collective-permute-start(bf16[160,1536]{1,0:T(8,128)(2,1)S(1)} %add_convert_fusion.13), channel_id=1, source_target_pairs={{0,8},{1,9},{2,10},{3,11},{4,12},{5,13},{6,14},{7,15},{8,16},{9,17... | collective-permute-start | bytes 1474568 | tf_op jit(solution)/shard_map/ppermute | solution.py:100
  799.4 30.6 %collective-permute-start.83 = (bf16[240,1536]{1,0:T(8,128)(2,1)S(1)}, bf16[240,1536]{1,0:T(8,128)(2,1)S(1)}, u32[]{:S(2)}, u32[]{:S(2)}) collective-permute-start(bf16[240,1536]{1,0:T(8,128)(2,1)S(1)} %pad_maximum_fusion.35), channel_id=1, source_target_pairs={{0,2},{1,3},{2,0},{3,1},{4,6},{5,7},{6,4},{7,5},{8,10},{9,11},{10,... | collective-permute-start | bytes 2211848 | tf_op jit(solution)/shard_map/ppermute | solution.py:78
  800.0 30.0 %collective-permute-start.84 = (bf16[240,1536]{1,0:T(8,128)(2,1)S(1)}, bf16[240,1536]{1,0:T(8,128)(2,1)S(1)}, u32[]{:S(2)}, u32[]{:S(2)}) collective-permute-start(bf16[240,1536]{1,0:T(8,128)(2,1)S(1)} %pad_maximum_fusion.36), channel_id=1, source_target_pairs={{0,4},{1,5},{2,6},{3,7},{4,0},{5,1},{6,2},{7,3},{8,12},{9,13},{10,... | collective-permute-start | bytes 2211848 | tf_op jit(solution)/shard_map/ppermute | solution.py:78
  832.5 23.4 %collective-permute-start.91 = (bf16[160,1536]{1,0:T(8,128)(2,1)S(1)}, bf16[160,1536]{1,0:T(8,128)(2,1)S(1)}, u32[]{:S(2)}, u32[]{:S(2)}) collective-permute-start(bf16[160,1536]{1,0:T(8,128)(2,1)S(1)} %add_convert_fusion.12), channel_id=1, source_target_pairs={{0,8},{1,9},{2,10},{3,11},{4,12},{5,13},{6,14},{7,15},{8,16},{9,17... | collective-permute-start | bytes 1474568 | tf_op jit(solution)/shard_map/ppermute | solution.py:100
  832.5 23.3 %collective-permute-start.89 = (bf16[240,1536]{1,0:T(8,128)(2,1)S(1)}, bf16[240,1536]{1,0:T(8,128)(2,1)S(1)}, u32[]{:S(2)}, u32[]{:S(2)}) collective-permute-start(bf16[240,1536]{1,0:T(8,128)(2,1)S(1)} %pad_maximum_fusion.37), channel_id=1, source_target_pairs={{0,2},{1,3},{2,0},{3,1},{4,6},{5,7},{6,4},{7,5},{8,10},{9,11},{10,... | collective-permute-start | bytes 2211848 | tf_op jit(solution)/shard_map/ppermute | solution.py:78
  833.2 22.7 %collective-permute-start.90 = (bf16[240,1536]{1,0:T(8,128)(2,1)S(1)}, bf16[240,1536]{1,0:T(8,128)(2,1)S(1)}, u32[]{:S(2)}, u32[]{:S(2)}) collective-permute-start(bf16[240,1536]{1,0:T(8,128)(2,1)S(1)} %pad_maximum_fusion.38), channel_id=1, source_target_pairs={{0,4},{1,5},{2,6},{3,7},{4,0},{5,1},{6,2},{7,3},{8,12},{9,13},{10,... | collective-permute-start | bytes 2211848 | tf_op jit(solution)/shard_map/ppermute | solution.py:78
  (188 other events, 1985.2 us)
Sparse Core Ops, SparseCore 0:
  151.5 167.4 all-gather.1
  557.2 59.9 reduce-scatter.1

commit v6 on v5

--- a/solution.py
+++ b/solution.py
@@ -353,7 +353,7 @@
             mv,
             [jnp.concatenate([q_weight, kv_weight, small], 1), out_weight],
             ffn,
-            rounds - 2,
+            rounds - 1,
             cotangent,
             [mv.planes - 1, *range(rounds - 2, rounds + 3)],
             held,

time: 901 us -> 897 us (level)
  transfers between devices with their start and end apart: 105 -> 105, of which waited for: 47 -> 48; matrix products, arithmetic and copies ran while one was open for 41% -> 41% of each run, Pallas kernels for 7% -> 7%
where the time goes in v6:
time: 897 us; the launch traced here: 887 us
  waiting for transfers between devices  291 us (32%)
  matrix products  210 us (23%)
  other arithmetic  130 us (14%)
  local copies, waits for them, and re-layouts  115 us (13%)
  starting transfers between devices  63.6 us (7%)
  Pallas kernels  59.5 us (7%)
  between operations  17.1 us (2%)
    ppermute x30, waiting for transfers between devices, up(): lax.ppermute(value, 'dp', [(i, (i + 8 * steps) % self.n) for i in range(s...  183 us
    ppermute x73, waiting for transfers between devices, flip(): return lax.ppermute(value, 'dp', [(i, i ^ bit) for i in range(self.n)])  108 us
    dot_general x15, matrix products, dot_nt(): lax.dot_general(left, right, (((1,), (1,)), ((), ())), preferred_element_...  81.1 us
    dot_general x13, matrix products, dot_nn(): return jnp.dot(left, right, preferred_element_type=F32)  62.7 us
    pallas_call x8, Pallas kernels, put(): pl.pallas_call(place_kernel, out_shape=self.shape, grid_spec=pltpu.Prefet...  59.5 us
    dot_general x5, matrix products, dot_tn(): lax.dot_general(left, right, (((0,), (0,)), ((), ())), preferred_element_...  58.3 us
    unnamed x281, local copies, waits for them, and re-layouts  54.7 us
    ppermute x73, starting transfers between devices, flip(): return lax.ppermute(value, 'dp', [(i, i ^ bit) for i in range(self.n)])  49.7 us
  transfers between devices with their start and end apart: 105, of which 48 were waited for; matrix products, arithmetic and copies ran while one was open for 41% of the time, Pallas kernels for 7%

profile of v6, /device:TPU:0, one launch (start us, length us, event | category | flops | bytes accessed | tf_op | source)
XLA Modules:
  0.0 886.9 jit_solution(13300995905307622925)
XLA Ops:
  21.3 8.6 collective-permute-done.2
  35.7 13.4 %collective-permute-done.3 = bf16[80,3200]{1,0:T(8,128)(2,1)S(1)} collective-permute-done((bf16[80,3200]{1,0:T(8,128)(2,1)S(1)}, bf16[80,3200]{1,0:T(8,128)(2,1)S(1)}, u32[]{:S(2)}, u32[]{:S(2)}) %collective-permute-start.3) | collective-permute-done | bytes 512032 | tf_op jit(solution)/shard_map/ppermute | solution.py:100
  54.9 15.3 %collective-permute-done.6 = bf16[80,3200]{1,0:T(8,128)(2,1)S(1)} collective-permute-done((bf16[80,3200]{1,0:T(8,128)(2,1)S(1)}, bf16[80,3200]{1,0:T(8,128)(2,1)S(1)}, u32[]{:S(2)}, u32[]{:S(2)}) %collective-permute-start.6) | collective-permute-done | bytes 512032 | tf_op jit(solution)/shard_map/ppermute | solution.py:100
  81.1 7.8 place_rows.8.refs_0_
  88.8 10.3 %collective-permute-done.13 = bf16[128,2560]{1,0:T(8,128)(2,1)} collective-permute-done((bf16[128,2560]{1,0:T(8,128)(2,1)}, bf16[128,2560]{1,0:T(8,128)(2,1)}, u32[]{:S(2)}, u32[]{:S(2)}) %collective-permute-start.13) | collective-permute-done | bytes 655392 | tf_op jit(solution)/shard_map/ppermute | solution.py:100
  107.5 4.9 collective-permute-done.18
  114.3 7.7 place_rows.9.refs_0_
  131.4 7.7 place_rows.10.refs_0_
  157.6 7.7 place_rows.11
  165.3 16.0 %collective-permute-done.24 = bf16[80,2560]{1,0:T(8,128)(2,1)S(1)} collective-permute-done((bf16[80,2560]{1,0:T(8,128)(2,1)S(1)}, bf16[80,2560]{1,0:T(8,128)(2,1)S(1)}, u32[]{:S(2)}, u32[]{:S(2)}) %collective-permute-start.24) | collective-permute-done | bytes 409632 | tf_op jit(solution)/shard_map/ppermute | solution.py:100
  195.5 7.3 place_rows.12.refs_0_
  202.8 19.9 %collective-permute-done.30 = bf16[120,2560]{1,0:T(8,128)(2,1)} collective-permute-done((bf16[120,2560]{1,0:T(8,128)(2,1)}, bf16[120,2560]{1,0:T(8,128)(2,1)}, u32[]{:S(2)}, u32[]{:S(2)}) %collective-permute-start.30) | collective-permute-done | bytes 614432 | tf_op jit(solution)/shard_map/ppermute | solution.py:78
  241.9 8.9 fusion.2
  251.8 7.1 place_rows.13.refs_0_
  274.0 7.1 place_rows.14.refs_0_
  285.1 7.5 collective-permute-done.38
  293.3 7.1 place_rows.15
  322.8 26.7 %collective-permute-done.40 = bf16[256,2560]{1,0:T(8,128)(2,1)} collective-permute-done((bf16[256,2560]{1,0:T(8,128)(2,1)S(1)}, bf16[256,2560]{1,0:T(8,128)(2,1)}, u32[]{:S(2)}, u32[]{:S(2)}) %collective-permute-start.40) | collective-permute-done | bytes 1310752 | tf_op jit(solution)/shard_map/ppermute | solution.py:100
  351.5 6.4 fusion.165
  363.7 5.7 fusion.52
  391.4 6.9 fusion.59
  427.3 7.5 fusion.66
  448.5 10.5 %collective-permute-done.55 = bf16[256,2560]{1,0:T(8,128)(2,1)} collective-permute-done((bf16[256,2560]{1,0:T(8,128)(2,1)}, bf16[256,2560]{1,0:T(8,128)(2,1)}, u32[]{:S(2)}, u32[]{:S(2)}) %collective-permute-start.55) | collective-permute-done | bytes 1310752 | tf_op jit(solution)/shard_map/ppermute | solution.py:100
  469.0 7.3 fusion.73
  491.5 8.8 collective-permute-done.58
  509.4 7.5 convolution_convert_fusion.4
  517.0 4.8 pad_maximum_fusion
  521.8 16.1 %fusion.14 = bf16[1024,2560]{1,0:T(8,128)(2,1)} fusion(bf16[2048,1024]{1,0:T(8,128)(2,1)S(1)} %constant_dynamic-update-slice_fusion.16, bf16[512,2560]{1,0:T(8,128)(2,1)} %copy-done.47, bf16[512,2560]{1,0:T(8,128)(2,1)} %copy-done.46, bf16[512,2560]{1,0:T(8,128)(2,1)} %copy-done.45, bf16[512,2560]{1,0:T(8,128)(2,1)} %pad_maximum_fusion.4), kind=kOutput, calls=%fused_computation.23 | convolution fusion | flops 10781982720 | bytes 19922944 | tf_op jit(solution)/shard_map/dot_general | solution.py:50
  537.9 5.5 pad_maximum_fusion.1
  543.4 10.0 %convolution_convert_fusion.5 = bf16[1024,2560]{1,0:T(8,128)(2,1)} fusion(bf16[1024,1024]{1,0:T(8,128)(2,1)S(1)} %bitcast.327, bf16[1024,2560]{1,0:T(8,128)(2,1)} %bitcast.313), kind=kOutput, calls=%fused_computation.25 | convolution fusion | flops 5371330560 | bytes 12582912 | tf_op jit(solution)/shard_map/dot_general | solution.py:60
  564.5 10.0 %convolution_convert_fusion.6 = bf16[256,2560]{1,0:T(8,128)(2,1)} fusion(bf16[256,2560]{1,0:T(8,128)(2,1)S(1)} %fusion.162, bf16[2560,2560]{1,0:T(8,128)(2,1)} %place_rows.15), kind=kOutput, calls=%fused_computation.43 | convolution fusion | flops 3356098560 | bytes 15728640 | tf_op jit(solution)/shard_map/dot_general | solution.py:56
  574.5 5.5 convolution_convert_fusion.1
  580.1 17.1 %collective-permute-done.62 = bf16[256,2560]{1,0:T(8,128)(2,1)} collective-permute-done((bf16[256,2560]{1,0:T(8,128)(2,1)S(1)}, bf16[256,2560]{1,0:T(8,128)(2,1)}, u32[]{:S(2)}, u32[]{:S(2)}) %collective-permute-start.62) | collective-permute-done | bytes 1310752 | tf_op jit(solution)/shard_map/ppermute | solution.py:100
  606.6 16.8 %convolution_convert_fusion.3 = bf16[1024,2560]{1,0:T(8,128)(2,1)} fusion(bf16[2048,1024]{1,0:T(8,128)(2,1)S(1)} %copy-done.14, bf16[2048,2560]{1,0:T(8,128)(2,1)} %pad_maximum_fusion), kind=kOutput, calls=%fused_computation.22 | convolution fusion | flops 10740039680 | bytes 19922944 | tf_op jit(solution)/shard_map/dot_general | solution.py:50
  623.4 13.6 %convolution_convert_fusion.2 = bf16[1024,2560]{1,0:T(8,128)(2,1)} fusion(bf16[2048,1024]{1,0:T(8,128)(2,1)S(1)} %copy-done.12, bf16[2048,2560]{1,0:T(8,128)(2,1)S(1)} %bitcast.294), kind=kOutput, calls=%fused_computation.21 | convolution fusion | flops 10740039680 | bytes 19922944 | tf_op jit(solution)/shard_map/dot_general | solution.py:50
  664.3 6.2 convolution_convert_fusion
  670.6 5.0 collective-permute-done.64
  676.9 12.3 %collective-permute-done.68 = bf16[640,1280]{1,0:T(8,128)(2,1)} collective-permute-done((bf16[640,1280]{1,0:T(8,128)(2,1)}, bf16[640,1280]{1,0:T(8,128)(2,1)}, u32[]{:S(2)}, u32[]{:S(2)}) %collective-permute-start.68) | collective-permute-done | bytes 1638432 | tf_op jit(solution)/shard_map/ppermute | solution.py:100
  709.7 11.1 %fusion.26 = (f32[2560]{0:T(1024)S(1)}, f32[256]{0:T(256)S(1)}, f32[256,2560]{1,0:T(8,128)}) fusion(bf16[256,2560]{1,0:T(8,128)(2,1)S(1)} %copy-done.9, f32[256]{0:T(256)S(1)} %copy-done.101, f32[2560]{0:T(1024)S(1)} %copy-done.94, f32[256,2560]{1,0:T(8,128)} %fusion.40, bf16[256,2560]{0,1:T(8,128)(2,1)S(1)} %bitcast.308, bf16[2560,3200]{1,0:T(8,128)(2,1)} %place_rows.11), kind=kOutput, calls=%fused_computation.60 | convolution fusion | flops 3360683264 | bytes 20994048 | tf_op jit(solution)/shard_map/dot_general | solution.py:56
  723.7 6.5 convert_reduce_fusion.2
  731.2 8.6 collective-permute-done.73
  739.8 5.9 collective-permute-done.69
  774.4 5.3 collective-permute-done.76
  781.1 5.1 collective-permute-done.75
  805.6 11.8 %collective-permute-done.87 = bf16[160,1280]{1,0:T(8,128)(2,1)S(1)} collective-permute-done((bf16[160,1280]{1,0:T(8,128)(2,1)S(1)}, bf16[160,1280]{1,0:T(8,128)(2,1)S(1)}, u32[]{:S(2)}, u32[]{:S(2)}) %collective-permute-start.87) | collective-permute-done | bytes 409632 | tf_op jit(solution)/shard_map/ppermute | solution.py:78
  817.4 9.1 %collective-permute-done.85 = bf16[160,1536]{1,0:T(8,128)(2,1)S(1)} collective-permute-done((bf16[160,1536]{1,0:T(8,128)(2,1)S(1)}, bf16[160,1536]{1,0:T(8,128)(2,1)S(1)}, u32[]{:S(2)}, u32[]{:S(2)}) %collective-permute-start.85) | collective-permute-done | bytes 491552 | tf_op jit(solution)/shard_map/ppermute | solution.py:100
  835.0 17.3 %collective-permute-done.93 = bf16[80,1280]{1,0:T(8,128)(2,1)S(1)} collective-permute-done((bf16[80,1280]{1,0:T(8,128)(2,1)S(1)}, bf16[80,1280]{1,0:T(8,128)(2,1)S(1)}, u32[]{:S(2)}, u32[]{:S(2)}) %collective-permute-start.93) | collective-permute-done | bytes 204832 | tf_op jit(solution)/shard_map/ppermute | solution.py:78
  868.4 7.2 collective-permute-done.97
  (725 shorter events, 407.5 us)
Async XLA Ops:
  7.2 343.5 %all-gather.2.cloned.1.call-start = ((), (), s32[]{:S(2)}) async-start(), calls=%async_computation.1 | async-start | bytes 19660800 | tf_op jit(solution)/shard_map/all_gather | solution.py:367
  52.6 21.1 %collective-permute-start.9 = (bf16[320,3200]{1,0:T(8,128)(2,1)S(1)}, bf16[320,3200]{1,0:T(8,128)(2,1)S(1)}, u32[]{:S(2)}, u32[]{:S(2)}) collective-permute-start(bf16[320,3200]{1,0:T(8,128)(2,1)S(1)} %slice_dynamic-update-slice_fusion.16.mine), channel_id=1, source_target_pairs={{0,1},{1,0},{2,3},{3,2},{4,5},{5,4},{6,7},{7,6},{8,9},{9,8},{10,11... | collective-permute-start | bytes 6144008 | tf_op jit(solution)/shard_map/ppermute | solution.py:78
  77.8 23.0 %collective-permute-start.12 = (bf16[320,3200]{1,0:T(8,128)(2,1)}, bf16[320,3200]{1,0:T(8,128)(2,1)}, u32[]{:S(2)}, u32[]{:S(2)}) collective-permute-start(bf16[320,3200]{1,0:T(8,128)(2,1)} %slice_dynamic-update-slice_fusion.14.mine), channel_id=1, source_target_pairs={{0,1},{1,0},{2,3},{3,2},{4,5},{5,4},{6,7},{7,6},{8,9},{9,8},{10,11... | collective-permute-start | bytes 6144008 | tf_op jit(solution)/shard_map/ppermute | solution.py:78
  151.3 30.0 %collective-permute-start.27 = (bf16[320,2560]{1,0:T(8,128)(2,1)S(1)}, bf16[320,2560]{1,0:T(8,128)(2,1)}, u32[]{:S(2)}, u32[]{:S(2)}) collective-permute-start(bf16[320,2560]{1,0:T(8,128)(2,1)S(1)} %slice_dynamic-update-slice_fusion.22.mine), channel_id=1, source_target_pairs={{0,1},{1,0},{2,3},{3,2},{4,5},{5,4},{6,7},{7,6},{8,9},{9,8},{10,11... | collective-permute-start | bytes 4915208 | tf_op jit(solution)/shard_map/ppermute | solution.py:78
  153.5 27.7 %collective-permute-start.28 = (bf16[128,2560]{1,0:T(8,128)(2,1)}, bf16[128,2560]{1,0:T(8,128)(2,1)}, u32[]{:S(2)}, u32[]{:S(2)}) collective-permute-start(bf16[128,2560]{1,0:T(8,128)(2,1)} %get-tuple-element.727), channel_id=1, source_target_pairs={{0,8},{1,9},{2,10},{3,11},{4,12},{5,13},{6,14},{7,15},{8,16},{9,17... | collective-permute-start | bytes 1966088 | tf_op jit(solution)/shard_map/ppermute | solution.py:100
  154.7 26.5 %collective-permute-start.26 = (bf16[120,2560]{1,0:T(8,128)(2,1)}, bf16[120,2560]{1,0:T(8,128)(2,1)}, u32[]{:S(2)}, u32[]{:S(2)}) collective-permute-start(bf16[120,2560]{1,0:T(8,128)(2,1)} %get-tuple-element.1373), channel_id=1, source_target_pairs={{0,4},{1,5},{2,6},{3,7},{4,0},{5,1},{6,2},{7,3},{8,12},{9,13},{10,... | collective-permute-start | bytes 1843208 | tf_op jit(solution)/shard_map/ppermute | solution.py:78
  155.3 26.0 %collective-permute-start.25 = (bf16[120,2560]{1,0:T(8,128)(2,1)}, bf16[120,2560]{1,0:T(8,128)(2,1)}, u32[]{:S(2)}, u32[]{:S(2)}) collective-permute-start(bf16[120,2560]{1,0:T(8,128)(2,1)} %get-tuple-element.1374), channel_id=1, source_target_pairs={{0,2},{1,3},{2,0},{3,1},{4,6},{5,7},{6,4},{7,5},{8,10},{9,11},{10,... | collective-permute-start | bytes 1843208 | tf_op jit(solution)/shard_map/ppermute | solution.py:78
  156.7 24.5 %collective-permute-start.24 = (bf16[80,2560]{1,0:T(8,128)(2,1)S(1)}, bf16[80,2560]{1,0:T(8,128)(2,1)S(1)}, u32[]{:S(2)}, u32[]{:S(2)}) collective-permute-start(bf16[80,2560]{1,0:T(8,128)(2,1)S(1)} %copy-done.53), channel_id=1, source_target_pairs={{0,8},{1,9},{2,10},{3,11},{4,12},{5,13},{6,14},{7,15},{8,16},{9,17... | collective-permute-start | bytes 1228808 | tf_op jit(solution)/shard_map/ppermute | solution.py:100
  181.3 459.2 %reduce-scatter.2.cloned.1.call-start = ((), (), s32[]{:S(2)}) async-start(), calls=%async_computation.2 | async-start | bytes 6553600 | tf_op jit(solution)/shard_map/reduce_scatter | solution.py:486
  186.3 36.7 %collective-permute-start.31 = (bf16[320,2560]{1,0:T(8,128)(2,1)S(1)}, bf16[320,2560]{1,0:T(8,128)(2,1)}, u32[]{:S(2)}, u32[]{:S(2)}) collective-permute-start(bf16[320,2560]{1,0:T(8,128)(2,1)S(1)} %slice_dynamic-update-slice_fusion.20.mine), channel_id=1, source_target_pairs={{0,1},{1,0},{2,3},{3,2},{4,5},{5,4},{6,7},{7,6},{8,9},{9,8},{10,11... | collective-permute-start | bytes 4915208 | tf_op jit(solution)/shard_map/ppermute | solution.py:78
  191.4 31.5 %collective-permute-start.32 = (bf16[128,2560]{1,0:T(8,128)(2,1)}, bf16[128,2560]{1,0:T(8,128)(2,1)}, u32[]{:S(2)}, u32[]{:S(2)}) collective-permute-start(bf16[128,2560]{1,0:T(8,128)(2,1)} %collective-permute-done.13), channel_id=1, source_target_pairs={{0,8},{1,9},{2,10},{3,11},{4,12},{5,13},{6,14},{7,15},{8,16},{9,17... | collective-permute-start | bytes 1966088 | tf_op jit(solution)/shard_map/ppermute | solution.py:100
  192.6 30.0 %collective-permute-start.30 = (bf16[120,2560]{1,0:T(8,128)(2,1)}, bf16[120,2560]{1,0:T(8,128)(2,1)}, u32[]{:S(2)}, u32[]{:S(2)}) collective-permute-start(bf16[120,2560]{1,0:T(8,128)(2,1)} %get-tuple-element.1371), channel_id=1, source_target_pairs={{0,4},{1,5},{2,6},{3,7},{4,0},{5,1},{6,2},{7,3},{8,12},{9,13},{10,... | collective-permute-start | bytes 1843208 | tf_op jit(solution)/shard_map/ppermute | solution.py:78
  193.0 29.9 %collective-permute-start.29 = (bf16[120,2560]{1,0:T(8,128)(2,1)}, bf16[120,2560]{1,0:T(8,128)(2,1)}, u32[]{:S(2)}, u32[]{:S(2)}) collective-permute-start(bf16[120,2560]{1,0:T(8,128)(2,1)} %get-tuple-element.1372), channel_id=1, source_target_pairs={{0,2},{1,3},{2,0},{3,1},{4,6},{5,7},{6,4},{7,5},{8,10},{9,11},{10,... | collective-permute-start | bytes 1843208 | tf_op jit(solution)/shard_map/ppermute | solution.py:78
  226.2 34.0 %collective-permute-start.34 = (bf16[40,2560]{1,0:T(8,128)(2,1)}, bf16[40,2560]{1,0:T(8,128)(2,1)}, u32[]{:S(2)}, u32[]{:S(2)}) collective-permute-start(bf16[40,2560]{1,0:T(8,128)(2,1)} %slice.481), channel_id=1, source_target_pairs={{0,2},{1,3},{2,0},{3,1},{4,6},{5,7},{6,4},{7,5},{8,10},{9,11},{10,... | collective-permute-start | bytes 614408 | tf_op jit(solution)/shard_map/ppermute | solution.py:78
  227.7 32.5 %collective-permute-start.33 = (bf16[40,2560]{1,0:T(8,128)(2,1)}, bf16[40,2560]{1,0:T(8,128)(2,1)}, u32[]{:S(2)}, u32[]{:S(2)}) collective-permute-start(bf16[40,2560]{1,0:T(8,128)(2,1)} %slice.480), channel_id=1, source_target_pairs={{0,4},{1,5},{2,6},{3,7},{4,0},{5,1},{6,2},{7,3},{8,12},{9,13},{10,... | collective-permute-start | bytes 614408 | tf_op jit(solution)/shard_map/ppermute | solution.py:78
  228.2 32.0 %collective-permute-start.36 = (bf16[128,2560]{1,0:T(8,128)(2,1)}, bf16[128,2560]{1,0:T(8,128)(2,1)}, u32[]{:S(2)}, u32[]{:S(2)}) collective-permute-start(bf16[128,2560]{1,0:T(8,128)(2,1)} %collective-permute-done.28), channel_id=1, source_target_pairs={{0,8},{1,9},{2,10},{3,11},{4,12},{5,13},{6,14},{7,15},{8,16},{9,17... | collective-permute-start | bytes 1966088 | tf_op jit(solution)/shard_map/ppermute | solution.py:100
  236.0 24.2 %collective-permute-start.35 = (bf16[320,2560]{1,0:T(8,128)(2,1)}, bf16[320,2560]{1,0:T(8,128)(2,1)}, u32[]{:S(2)}, u32[]{:S(2)}) collective-permute-start(bf16[320,2560]{1,0:T(8,128)(2,1)} %slice_dynamic-update-slice_fusion.18.mine), channel_id=1, source_target_pairs={{0,1},{1,0},{2,3},{3,2},{4,5},{5,4},{6,7},{7,6},{8,9},{9,8},{10,11... | collective-permute-start | bytes 4915208 | tf_op jit(solution)/shard_map/ppermute | solution.py:78
  267.9 24.6 %collective-permute-start.37 = (bf16[320,2560]{1,0:T(8,128)(2,1)}, bf16[320,2560]{1,0:T(8,128)(2,1)}, u32[]{:S(2)}, u32[]{:S(2)}) collective-permute-start(bf16[320,2560]{1,0:T(8,128)(2,1)} %constant_dynamic-update-slice_fusion.13.mine), channel_id=1, source_target_pairs={{0,1},{1,0},{2,3},{3,2},{4,5},{5,4},{6,7},{7,6},{8,9},{9,8},{10,11... | collective-permute-start | bytes 4915208 | tf_op jit(solution)/shard_map/ppermute | solution.py:78
  316.5 33.0 %collective-permute-start.40 = (bf16[256,2560]{1,0:T(8,128)(2,1)S(1)}, bf16[256,2560]{1,0:T(8,128)(2,1)}, u32[]{:S(2)}, u32[]{:S(2)}) collective-permute-start(bf16[256,2560]{1,0:T(8,128)(2,1)S(1)} %multiply_convert_fusion), channel_id=1, source_target_pairs={{0,8},{1,9},{2,10},{3,11},{4,12},{5,13},{6,14},{7,15},{8,16},{9,17... | collective-permute-start | bytes 3932168 | tf_op jit(solution)/shard_map/ppermute | solution.py:100
  349.5 31.1 %collective-permute-start.45 = (bf16[256,2560]{1,0:T(8,128)(2,1)}, bf16[256,2560]{1,0:T(8,128)(2,1)}, u32[]{:S(2)}, u32[]{:S(2)}) collective-permute-start(bf16[256,2560]{1,0:T(8,128)(2,1)} %collective-permute-done.40), channel_id=1, source_target_pairs={{0,1},{1,0},{2,3},{3,2},{4,5},{5,4},{6,7},{7,6},{8,9},{9,8},{10,11... | collective-permute-start | bytes 3932168 | tf_op jit(solution)/shard_map/ppermute | solution.py:78
  349.5 33.9 %collective-permute-start.44 = (bf16[256,2560]{1,0:T(8,128)(2,1)}, bf16[256,2560]{1,0:T(8,128)(2,1)}, u32[]{:S(2)}, u32[]{:S(2)}) collective-permute-start(bf16[256,2560]{1,0:T(8,128)(2,1)} %collective-permute-done.40), channel_id=1, source_target_pairs={{0,8},{1,9},{2,10},{3,11},{4,12},{5,13},{6,14},{7,15},{8,16},{9,17... | collective-permute-start | bytes 3932168 | tf_op jit(solution)/shard_map/ppermute | solution.py:100
  350.5 26.8 %collective-permute-start.46 = (bf16[256,2560]{1,0:T(8,128)(2,1)}, bf16[256,2560]{1,0:T(8,128)(2,1)}, u32[]{:S(2)}, u32[]{:S(2)}) collective-permute-start(bf16[256,2560]{1,0:T(8,128)(2,1)} %pad_maximum_fusion.15), channel_id=1, source_target_pairs={{0,1},{1,0},{2,3},{3,2},{4,5},{5,4},{6,7},{7,6},{8,9},{9,8},{10,11... | collective-permute-start | bytes 3932168 | tf_op jit(solution)/shard_map/ppermute | solution.py:78
  383.4 26.2 %collective-permute-start.49 = (bf16[256,2560]{1,0:T(8,128)(2,1)}, bf16[256,2560]{1,0:T(8,128)(2,1)}, u32[]{:S(2)}, u32[]{:S(2)}) collective-permute-start(bf16[256,2560]{1,0:T(8,128)(2,1)} %collective-permute-done.44), channel_id=1, source_target_pairs={{0,1},{1,0},{2,3},{3,2},{4,5},{5,4},{6,7},{7,6},{8,9},{9,8},{10,11... | collective-permute-start | bytes 3932168 | tf_op jit(solution)/shard_map/ppermute | solution.py:78
  383.8 33.1 %collective-permute-start.48 = (bf16[256,2560]{1,0:T(8,128)(2,1)}, bf16[256,2560]{1,0:T(8,128)(2,1)S(1)}, u32[]{:S(2)}, u32[]{:S(2)}) collective-permute-start(bf16[256,2560]{1,0:T(8,128)(2,1)} %collective-permute-done.44), channel_id=1, source_target_pairs={{0,8},{1,9},{2,10},{3,11},{4,12},{5,13},{6,14},{7,15},{8,16},{9,17... | collective-permute-start | bytes 3932168 | tf_op jit(solution)/shard_map/ppermute | solution.py:100
  426.7 32.2 %collective-permute-start.55 = (bf16[256,2560]{1,0:T(8,128)(2,1)}, bf16[256,2560]{1,0:T(8,128)(2,1)}, u32[]{:S(2)}, u32[]{:S(2)}) collective-permute-start(bf16[256,2560]{1,0:T(8,128)(2,1)} %add_convert_fusion.6), channel_id=1, source_target_pairs={{0,8},{1,9},{2,10},{3,11},{4,12},{5,13},{6,14},{7,15},{8,16},{9,17... | collective-permute-start | bytes 3932168 | tf_op jit(solution)/shard_map/ppermute | solution.py:100
  469.0 31.3 %collective-permute-start.58 = (bf16[256,2560]{1,0:T(8,128)(2,1)}, bf16[256,2560]{1,0:T(8,128)(2,1)}, u32[]{:S(2)}, u32[]{:S(2)}) collective-permute-start(bf16[256,2560]{1,0:T(8,128)(2,1)} %add_convert_fusion.5), channel_id=1, source_target_pairs={{0,8},{1,9},{2,10},{3,11},{4,12},{5,13},{6,14},{7,15},{8,16},{9,17... | collective-permute-start | bytes 3932168 | tf_op jit(solution)/shard_map/ppermute | solution.py:100
  503.6 49.8 %collective-permute-start.59 = (bf16[256,2560]{1,0:T(8,128)(2,1)}, bf16[256,2560]{1,0:T(8,128)(2,1)}, u32[]{:S(2)}, u32[]{:S(2)}) collective-permute-start(bf16[256,2560]{1,0:T(8,128)(2,1)} %add_convert_fusion.4), channel_id=1, source_target_pairs={{0,8},{1,9},{2,10},{3,11},{4,12},{5,13},{6,14},{7,15},{8,16},{9,17... | collective-permute-start | bytes 3932168 | tf_op jit(solution)/shard_map/ppermute | solution.py:100
  516.9 36.5 %collective-permute-start.60 = (bf16[4,256,2560]{2,1,0:T(8,128)(2,1)}, bf16[4,256,2560]{2,1,0:T(8,128)(2,1)}, u32[]{:S(2)}, u32[]{:S(2)}) collective-permute-start(bf16[4,256,2560]{2,1,0:T(8,128)(2,1)} %bitcast.65), channel_id=1, source_target_pairs={{0,1},{1,0},{2,3},{3,2},{4,5},{5,4},{6,7},{7,6},{8,9},{9,8},{10,11... | collective-permute-start | bytes 15728648 | tf_op jit(solution)/shard_map/ppermute | solution.py:78
  564.5 32.7 %collective-permute-start.62 = (bf16[256,2560]{1,0:T(8,128)(2,1)S(1)}, bf16[256,2560]{1,0:T(8,128)(2,1)}, u32[]{:S(2)}, u32[]{:S(2)}) collective-permute-start(bf16[256,2560]{1,0:T(8,128)(2,1)S(1)} %fusion.81), channel_id=1, source_target_pairs={{0,8},{1,9},{2,10},{3,11},{4,12},{5,13},{6,14},{7,15},{8,16},{9,17... | collective-permute-start | bytes 3932168 | tf_op jit(solution)/shard_map/ppermute | solution.py:100
  601.3 39.2 %collective-permute-start.63 = (bf16[640,1280]{1,0:T(8,128)(2,1)S(1)}, bf16[640,1280]{1,0:T(8,128)(2,1)}, u32[]{:S(2)}, u32[]{:S(2)}) collective-permute-start(bf16[640,1280]{1,0:T(8,128)(2,1)S(1)} %constant_dynamic-slice_fusion.44), channel_id=1, source_target_pairs={{0,8},{1,9},{2,10},{3,11},{4,12},{5,13},{6,14},{7,15},{8,16},{9,17... | collective-permute-start | bytes 4915208 | tf_op jit(solution)/shard_map/ppermute | solution.py:100
  645.9 29.7 %collective-permute-start.64 = (bf16[256,2560]{1,0:T(8,128)(2,1)}, bf16[256,2560]{1,0:T(8,128)(2,1)}, u32[]{:S(2)}, u32[]{:S(2)}) collective-permute-start(bf16[256,2560]{1,0:T(8,128)(2,1)} %pad_maximum_fusion.18), channel_id=1, source_target_pairs={{0,2},{1,3},{2,0},{3,1},{4,6},{5,7},{6,4},{7,5},{8,10},{9,11},{10,... | collective-permute-start | bytes 3932168 | tf_op jit(solution)/shard_map/ppermute | solution.py:78
  647.6 29.3 %collective-permute-start.65 = (bf16[256,2560]{1,0:T(8,128)(2,1)}, bf16[256,2560]{1,0:T(8,128)(2,1)}, u32[]{:S(2)}, u32[]{:S(2)}) collective-permute-start(bf16[256,2560]{1,0:T(8,128)(2,1)} %pad_maximum_fusion.19), channel_id=1, source_target_pairs={{0,4},{1,5},{2,6},{3,7},{4,0},{5,1},{6,2},{7,3},{8,12},{9,13},{10,... | collective-permute-start | bytes 3932168 | tf_op jit(solution)/shard_map/ppermute | solution.py:78
  651.1 38.1 %collective-permute-start.68 = (bf16[640,1280]{1,0:T(8,128)(2,1)}, bf16[640,1280]{1,0:T(8,128)(2,1)}, u32[]{:S(2)}, u32[]{:S(2)}) collective-permute-start(bf16[640,1280]{1,0:T(8,128)(2,1)} %add_convert_fusion.2), channel_id=1, source_target_pairs={{0,8},{1,9},{2,10},{3,11},{4,12},{5,13},{6,14},{7,15},{8,16},{9,17... | collective-permute-start | bytes 4915208 | tf_op jit(solution)/shard_map/ppermute | solution.py:100
  692.8 38.4 %collective-permute-start.71 = (bf16[160,1536]{1,0:T(8,128)(2,1)}, bf16[160,1536]{1,0:T(8,128)(2,1)S(1)}, u32[]{:S(2)}, u32[]{:S(2)}) collective-permute-start(bf16[160,1536]{1,0:T(8,128)(2,1)} %pad_maximum_fusion.45), channel_id=1, source_target_pairs={{0,2},{1,3},{2,0},{3,1},{4,6},{5,7},{6,4},{7,5},{8,10},{9,11},{10,... | collective-permute-start | bytes 1474568 | tf_op jit(solution)/shard_map/ppermute | solution.py:78
  694.3 36.9 %collective-permute-start.72 = (bf16[160,1536]{1,0:T(8,128)(2,1)}, bf16[160,1536]{1,0:T(8,128)(2,1)}, u32[]{:S(2)}, u32[]{:S(2)}) collective-permute-start(bf16[160,1536]{1,0:T(8,128)(2,1)} %pad_maximum_fusion.46), channel_id=1, source_target_pairs={{0,4},{1,5},{2,6},{3,7},{4,0},{5,1},{6,2},{7,3},{8,12},{9,13},{10,... | collective-permute-start | bytes 1474568 | tf_op jit(solution)/shard_map/ppermute | solution.py:78
  703.2 36.7 %collective-permute-start.73 = (bf16[640,1280]{1,0:T(8,128)(2,1)}, bf16[640,1280]{1,0:T(8,128)(2,1)}, u32[]{:S(2)}, u32[]{:S(2)}) collective-permute-start(bf16[640,1280]{1,0:T(8,128)(2,1)} %add_convert_fusion.1), channel_id=1, source_target_pairs={{0,8},{1,9},{2,10},{3,11},{4,12},{5,13},{6,14},{7,15},{8,16},{9,17... | collective-permute-start | bytes 4915208 | tf_op jit(solution)/shard_map/ppermute | solution.py:100
  703.5 42.3 %collective-permute-start.69 = (bf16[384,2560]{1,0:T(8,128)(2,1)}, bf16[384,2560]{1,0:T(8,128)(2,1)}, u32[]{:S(2)}, u32[]{:S(2)}) collective-permute-start(bf16[384,2560]{1,0:T(8,128)(2,1)} %pad_maximum_fusion.13), channel_id=1, source_target_pairs={{0,2},{1,3},{2,0},{3,1},{4,6},{5,7},{6,4},{7,5},{8,10},{9,11},{10,... | collective-permute-start | bytes 5898248 | tf_op jit(solution)/shard_map/ppermute | solution.py:78
  705.2 41.4 %collective-permute-start.70 = (bf16[384,2560]{1,0:T(8,128)(2,1)}, bf16[384,2560]{1,0:T(8,128)(2,1)}, u32[]{:S(2)}, u32[]{:S(2)}) collective-permute-start(bf16[384,2560]{1,0:T(8,128)(2,1)} %pad_maximum_fusion.14), channel_id=1, source_target_pairs={{0,4},{1,5},{2,6},{3,7},{4,0},{5,1},{6,2},{7,3},{8,12},{9,13},{10,... | collective-permute-start | bytes 5898248 | tf_op jit(solution)/shard_map/ppermute | solution.py:78
  751.4 29.8 %collective-permute-start.78 = (bf16[240,1536]{1,0:T(8,128)(2,1)S(1)}, bf16[240,1536]{1,0:T(8,128)(2,1)S(1)}, u32[]{:S(2)}, u32[]{:S(2)}) collective-permute-start(bf16[240,1536]{1,0:T(8,128)(2,1)S(1)} %pad_maximum_fusion.33), channel_id=1, source_target_pairs={{0,2},{1,3},{2,0},{3,1},{4,6},{5,7},{6,4},{7,5},{8,10},{9,11},{10,... | collective-permute-start | bytes 2211848 | tf_op jit(solution)/shard_map/ppermute | solution.py:78
  752.4 28.8 %collective-permute-start.79 = (bf16[240,1536]{1,0:T(8,128)(2,1)S(1)}, bf16[240,1536]{1,0:T(8,128)(2,1)S(1)}, u32[]{:S(2)}, u32[]{:S(2)}) collective-permute-start(bf16[240,1536]{1,0:T(8,128)(2,1)S(1)} %pad_maximum_fusion.34), channel_id=1, source_target_pairs={{0,4},{1,5},{2,6},{3,7},{4,0},{5,1},{6,2},{7,3},{8,12},{9,13},{10,... | collective-permute-start | bytes 2211848 | tf_op jit(solution)/shard_map/ppermute | solution.py:78
  758.6 27.6 %collective-permute-start.75 = (bf16[256,2560]{1,0:T(8,128)(2,1)S(1)}, bf16[256,2560]{1,0:T(8,128)(2,1)S(1)}, u32[]{:S(2)}, u32[]{:S(2)}) collective-permute-start(bf16[256,2560]{1,0:T(8,128)(2,1)S(1)} %fusion.36), channel_id=1, source_target_pairs={{0,8},{1,9},{2,10},{3,11},{4,12},{5,13},{6,14},{7,15},{8,16},{9,17... | collective-permute-start | bytes 3932168 | tf_op jit(solution)/shard_map/ppermute | solution.py:100
  789.4 37.1 %collective-permute-start.82 = (bf16[256,2560]{1,0:T(8,128)(2,1)S(1)}, bf16[256,2560]{1,0:T(8,128)(2,1)S(1)}, u32[]{:S(2)}, u32[]{:S(2)}) collective-permute-start(bf16[256,2560]{1,0:T(8,128)(2,1)S(1)} %fusion.35), channel_id=1, source_target_pairs={{0,8},{1,9},{2,10},{3,11},{4,12},{5,13},{6,14},{7,15},{8,16},{9,17... | collective-permute-start | bytes 3932168 | tf_op jit(solution)/shard_map/ppermute | solution.py:100
  793.5 33.0 %collective-permute-start.85 = (bf16[160,1536]{1,0:T(8,128)(2,1)S(1)}, bf16[160,1536]{1,0:T(8,128)(2,1)S(1)}, u32[]{:S(2)}, u32[]{:S(2)}) collective-permute-start(bf16[160,1536]{1,0:T(8,128)(2,1)S(1)} %add_convert_fusion.13), channel_id=1, source_target_pairs={{0,8},{1,9},{2,10},{3,11},{4,12},{5,13},{6,14},{7,15},{8,16},{9,17... | collective-permute-start | bytes 1474568 | tf_op jit(solution)/shard_map/ppermute | solution.py:100
  795.8 30.7 %collective-permute-start.83 = (bf16[240,1536]{1,0:T(8,128)(2,1)S(1)}, bf16[240,1536]{1,0:T(8,128)(2,1)S(1)}, u32[]{:S(2)}, u32[]{:S(2)}) collective-permute-start(bf16[240,1536]{1,0:T(8,128)(2,1)S(1)} %pad_maximum_fusion.35), channel_id=1, source_target_pairs={{0,2},{1,3},{2,0},{3,1},{4,6},{5,7},{6,4},{7,5},{8,10},{9,11},{10,... | collective-permute-start | bytes 2211848 | tf_op jit(solution)/shard_map/ppermute | solution.py:78
  797.3 29.1 %collective-permute-start.84 = (bf16[240,1536]{1,0:T(8,128)(2,1)S(1)}, bf16[240,1536]{1,0:T(8,128)(2,1)S(1)}, u32[]{:S(2)}, u32[]{:S(2)}) collective-permute-start(bf16[240,1536]{1,0:T(8,128)(2,1)S(1)} %pad_maximum_fusion.36), channel_id=1, source_target_pairs={{0,4},{1,5},{2,6},{3,7},{4,0},{5,1},{6,2},{7,3},{8,12},{9,13},{10,... | collective-permute-start | bytes 2211848 | tf_op jit(solution)/shard_map/ppermute | solution.py:78
  828.3 24.1 %collective-permute-start.91 = (bf16[160,1536]{1,0:T(8,128)(2,1)S(1)}, bf16[160,1536]{1,0:T(8,128)(2,1)S(1)}, u32[]{:S(2)}, u32[]{:S(2)}) collective-permute-start(bf16[160,1536]{1,0:T(8,128)(2,1)S(1)} %add_convert_fusion.12), channel_id=1, source_target_pairs={{0,8},{1,9},{2,10},{3,11},{4,12},{5,13},{6,14},{7,15},{8,16},{9,17... | collective-permute-start | bytes 1474568 | tf_op jit(solution)/shard_map/ppermute | solution.py:100
  828.3 24.0 %collective-permute-start.89 = (bf16[240,1536]{1,0:T(8,128)(2,1)S(1)}, bf16[240,1536]{1,0:T(8,128)(2,1)S(1)}, u32[]{:S(2)}, u32[]{:S(2)}) collective-permute-start(bf16[240,1536]{1,0:T(8,128)(2,1)S(1)} %pad_maximum_fusion.37), channel_id=1, source_target_pairs={{0,2},{1,3},{2,0},{3,1},{4,6},{5,7},{6,4},{7,5},{8,10},{9,11},{10,... | collective-permute-start | bytes 2211848 | tf_op jit(solution)/shard_map/ppermute | solution.py:78
  829.7 22.7 %collective-permute-start.90 = (bf16[240,1536]{1,0:T(8,128)(2,1)S(1)}, bf16[240,1536]{1,0:T(8,128)(2,1)S(1)}, u32[]{:S(2)}, u32[]{:S(2)}) collective-permute-start(bf16[240,1536]{1,0:T(8,128)(2,1)S(1)} %pad_maximum_fusion.38), channel_id=1, source_target_pairs={{0,4},{1,5},{2,6},{3,7},{4,0},{5,1},{6,2},{7,3},{8,12},{9,13},{10,... | collective-permute-start | bytes 2211848 | tf_op jit(solution)/shard_map/ppermute | solution.py:78
  (188 other events, 1968.2 us)
Sparse Core Ops, SparseCore 0:
  181.4 163.4 all-gather.1
  553.6 61.0 reduce-scatter.1

commit v7 on v6

--- a/solution.py
+++ b/solution.py
@@ -353,7 +353,7 @@
             mv,
             [jnp.concatenate([q_weight, kv_weight, small], 1), out_weight],
             ffn,
-            rounds - 1,
+            rounds,
             cotangent,
             [mv.planes - 1, *range(rounds - 2, rounds + 3)],
             held,

time: 897 us -> 902 us (level)
    all_gather x1, waiting for transfers between devices: 0.01 us -> 17.8 us  [body(): lax.all_gather(ffn, 'dp', axis=0, tiled=True, axis_index_groups=mv.square...]
    ppermute x73, waiting for transfers between devices: 108 us -> 94.2 us  [flip(): return lax.ppermute(value, 'dp', [(i, i ^ bit) for i in range(self.n)])]
    unnamed x281 -> x269, local copies, waits for them, and re-layouts: 54.7 us -> 53.7 us
  transfers between devices with their start and end apart: 105 -> 105, of which waited for: 48 -> 49; matrix products, arithmetic and copies ran while one was open for 41% -> 41% of each run, Pallas kernels for 7% -> 7%
where the time goes in v7:
time: 902 us; the launch traced here: 892 us
  waiting for transfers between devices  297 us (33%)
  matrix products  211 us (23%)
  other arithmetic  130 us (14%)
  local copies, waits for them, and re-layouts  112 us (12%)
  starting transfers between devices  64.3 us (7%)
  Pallas kernels  59.4 us (7%)
  between operations  17.1 us (2%)
    ppermute x30, waiting for transfers between devices, up(): lax.ppermute(value, 'dp', [(i, (i + 8 * steps) % self.n) for i in range(s...  185 us
    ppermute x73, waiting for transfers between devices, flip(): return lax.ppermute(value, 'dp', [(i, i ^ bit) for i in range(self.n)])  94.2 us
    dot_general x15, matrix products, dot_nt(): lax.dot_general(left, right, (((1,), (1,)), ((), ())), preferred_element_...  81.1 us
    dot_general x13, matrix products, dot_nn(): return jnp.dot(left, right, preferred_element_type=F32)  63.3 us
    pallas_call x8, Pallas kernels, put(): pl.pallas_call(place_kernel, out_shape=self.shape, grid_spec=pltpu.Prefet...  59.4 us
    dot_general x5, matrix products, dot_tn(): lax.dot_general(left, right, (((0,), (0,)), ((), ())), preferred_element_...  58.1 us
    unnamed x269, local copies, waits for them, and re-layouts  53.7 us
    ppermute x73, starting transfers between devices, flip(): return lax.ppermute(value, 'dp', [(i, i ^ bit) for i in range(self.n)])  51.5 us
  transfers between devices with their start and end apart: 105, of which 49 were waited for; matrix products, arithmetic and copies ran while one was open for 41% of the time, Pallas kernels for 7%

profile of v7, /device:TPU:0, one launch (start us, length us, event | category | flops | bytes accessed | tf_op | source)
XLA Modules:
  0.0 891.8 jit_solution(3619522640499854481)
XLA Ops:
  21.3 8.6 collective-permute-done.2
  35.7 13.4 %collective-permute-done.3 = bf16[80,3200]{1,0:T(8,128)(2,1)S(1)} collective-permute-done((bf16[80,3200]{1,0:T(8,128)(2,1)S(1)}, bf16[80,3200]{1,0:T(8,128)(2,1)S(1)}, u32[]{:S(2)}, u32[]{:S(2)}) %collective-permute-start.3) | collective-permute-done | bytes 512032 | tf_op jit(solution)/shard_map/ppermute | solution.py:100
  55.0 15.3 %collective-permute-done.6 = bf16[80,3200]{1,0:T(8,128)(2,1)S(1)} collective-permute-done((bf16[80,3200]{1,0:T(8,128)(2,1)S(1)}, bf16[80,3200]{1,0:T(8,128)(2,1)S(1)}, u32[]{:S(2)}, u32[]{:S(2)}) %collective-permute-start.6) | collective-permute-done | bytes 512032 | tf_op jit(solution)/shard_map/ppermute | solution.py:100
  81.0 7.8 place_rows.8.refs_0_
  88.8 10.3 %collective-permute-done.13 = bf16[128,2560]{1,0:T(8,128)(2,1)} collective-permute-done((bf16[128,2560]{1,0:T(8,128)(2,1)}, bf16[128,2560]{1,0:T(8,128)(2,1)}, u32[]{:S(2)}, u32[]{:S(2)}) %collective-permute-start.13) | collective-permute-done | bytes 655392 | tf_op jit(solution)/shard_map/ppermute | solution.py:100
  107.5 4.9 collective-permute-done.18
  114.4 7.6 place_rows.9.refs_0_
  131.4 7.7 place_rows.10.refs_0_
  157.6 7.8 place_rows.11
  165.3 15.9 %collective-permute-done.24 = bf16[80,2560]{1,0:T(8,128)(2,1)S(1)} collective-permute-done((bf16[80,2560]{1,0:T(8,128)(2,1)S(1)}, bf16[80,2560]{1,0:T(8,128)(2,1)S(1)}, u32[]{:S(2)}, u32[]{:S(2)}) %collective-permute-start.24) | collective-permute-done | bytes 409632 | tf_op jit(solution)/shard_map/ppermute | solution.py:100
  191.5 7.1 place_rows.12.refs_0_
  198.6 7.1 collective-permute-done.30
  229.8 8.7 fusion.2
  238.8 7.2 place_rows.13.refs_0_
  260.2 7.1 place_rows.14.refs_0_
  271.0 8.2 collective-permute-done.38
  279.7 7.1 place_rows.15
  309.4 26.9 %collective-permute-done.40 = bf16[256,2560]{1,0:T(8,128)(2,1)} collective-permute-done((bf16[256,2560]{1,0:T(8,128)(2,1)S(1)}, bf16[256,2560]{1,0:T(8,128)(2,1)}, u32[]{:S(2)}, u32[]{:S(2)}) %collective-permute-start.40) | collective-permute-done | bytes 1310752 | tf_op jit(solution)/shard_map/ppermute | solution.py:100
  337.3 17.8 %all-gather.2.cloned.1.call-done = bf16[3072,2560]{1,0:T(8,128)(2,1)} async-done(((bf16[768,2560]{1,0:T(8,128)(2,1)}), bf16[3072,2560]{1,0:T(8,128)(2,1)}) %all-gather.2.cloned.1.call-update) | async-done | bytes 15728656 | tf_op jit(solution)/shard_map/all_gather | solution.py:367
  356.0 6.4 fusion.165
  368.2 5.7 fusion.52
  397.0 6.9 fusion.59
  431.7 7.4 fusion.66
  452.9 10.8 %collective-permute-done.55 = bf16[256,2560]{1,0:T(8,128)(2,1)} collective-permute-done((bf16[256,2560]{1,0:T(8,128)(2,1)}, bf16[256,2560]{1,0:T(8,128)(2,1)}, u32[]{:S(2)}, u32[]{:S(2)}) %collective-permute-start.55) | collective-permute-done | bytes 1310752 | tf_op jit(solution)/shard_map/ppermute | solution.py:100
  473.8 7.3 fusion.73
  496.2 9.1 %collective-permute-done.58 = bf16[256,2560]{1,0:T(8,128)(2,1)} collective-permute-done((bf16[256,2560]{1,0:T(8,128)(2,1)}, bf16[256,2560]{1,0:T(8,128)(2,1)}, u32[]{:S(2)}, u32[]{:S(2)}) %collective-permute-start.58) | collective-permute-done | bytes 1310752 | tf_op jit(solution)/shard_map/ppermute | solution.py:100
  514.4 7.5 convolution_convert_fusion.4
  526.7 16.0 %fusion.14 = bf16[1024,2560]{1,0:T(8,128)(2,1)} fusion(bf16[2048,1024]{1,0:T(8,128)(2,1)S(1)} %constant_dynamic-update-slice_fusion.16, bf16[512,2560]{1,0:T(8,128)(2,1)} %copy-done.47, bf16[512,2560]{1,0:T(8,128)(2,1)} %copy-done.46, bf16[512,2560]{1,0:T(8,128)(2,1)} %copy-done.45, bf16[512,2560]{1,0:T(8,128)(2,1)} %pad_maximum_fusion.4), kind=kOutput, calls=%fused_computation.23 | convolution fusion | flops 10781982720 | bytes 19922944 | tf_op jit(solution)/shard_map/dot_general | solution.py:50
  542.8 5.5 pad_maximum_fusion.1
  548.3 10.0 %convolution_convert_fusion.5 = bf16[1024,2560]{1,0:T(8,128)(2,1)} fusion(bf16[1024,1024]{1,0:T(8,128)(2,1)S(1)} %bitcast.327, bf16[1024,2560]{1,0:T(8,128)(2,1)} %bitcast.313), kind=kOutput, calls=%fused_computation.25 | convolution fusion | flops 5371330560 | bytes 12582912 | tf_op jit(solution)/shard_map/dot_general | solution.py:60
  569.3 10.0 %convolution_convert_fusion.6 = bf16[256,2560]{1,0:T(8,128)(2,1)} fusion(bf16[256,2560]{1,0:T(8,128)(2,1)S(1)} %fusion.162, bf16[2560,2560]{1,0:T(8,128)(2,1)} %place_rows.15), kind=kOutput, calls=%fused_computation.43 | convolution fusion | flops 3356098560 | bytes 15728640 | tf_op jit(solution)/shard_map/dot_general | solution.py:56
  579.3 5.5 convolution_convert_fusion.1
  584.8 17.2 %collective-permute-done.62 = bf16[256,2560]{1,0:T(8,128)(2,1)} collective-permute-done((bf16[256,2560]{1,0:T(8,128)(2,1)S(1)}, bf16[256,2560]{1,0:T(8,128)(2,1)}, u32[]{:S(2)}, u32[]{:S(2)}) %collective-permute-start.62) | collective-permute-done | bytes 1310752 | tf_op jit(solution)/shard_map/ppermute | solution.py:100
  611.4 16.8 %convolution_convert_fusion.3 = bf16[1024,2560]{1,0:T(8,128)(2,1)} fusion(bf16[2048,1024]{1,0:T(8,128)(2,1)S(1)} %copy-done.14, bf16[2048,2560]{1,0:T(8,128)(2,1)} %pad_maximum_fusion), kind=kOutput, calls=%fused_computation.22 | convolution fusion | flops 10740039680 | bytes 19922944 | tf_op jit(solution)/shard_map/dot_general | solution.py:50
  628.2 13.6 %convolution_convert_fusion.2 = bf16[1024,2560]{1,0:T(8,128)(2,1)} fusion(bf16[2048,1024]{1,0:T(8,128)(2,1)S(1)} %copy-done.12, bf16[2048,2560]{1,0:T(8,128)(2,1)S(1)} %bitcast.294), kind=kOutput, calls=%fused_computation.21 | convolution fusion | flops 10740039680 | bytes 19922944 | tf_op jit(solution)/shard_map/dot_general | solution.py:50
  669.1 6.2 convolution_convert_fusion
  675.3 5.1 collective-permute-done.64
  681.6 12.4 %collective-permute-done.68 = bf16[640,1280]{1,0:T(8,128)(2,1)} collective-permute-done((bf16[640,1280]{1,0:T(8,128)(2,1)}, bf16[640,1280]{1,0:T(8,128)(2,1)}, u32[]{:S(2)}, u32[]{:S(2)}) %collective-permute-start.68) | collective-permute-done | bytes 1638432 | tf_op jit(solution)/shard_map/ppermute | solution.py:100
  714.4 11.1 %fusion.26 = (f32[2560]{0:T(1024)S(1)}, f32[256]{0:T(256)S(1)}, f32[256,2560]{1,0:T(8,128)}) fusion(bf16[256,2560]{1,0:T(8,128)(2,1)S(1)} %copy-done.9, f32[256]{0:T(256)S(1)} %copy-done.97, f32[2560]{0:T(1024)S(1)} %copy-done.91, f32[256,2560]{1,0:T(8,128)} %fusion.40, bf16[256,2560]{0,1:T(8,128)(2,1)S(1)} %bitcast.308, bf16[2560,3200]{1,0:T(8,128)(2,1)} %place_rows.11), kind=kOutput, calls=%fused_computation.60 | convolution fusion | flops 3360683264 | bytes 20994048 | tf_op jit(solution)/shard_map/dot_general | solution.py:56
  728.5 6.5 convert_reduce_fusion.2
  736.0 8.8 collective-permute-done.73
  744.7 5.8 collective-permute-done.69
  779.1 5.6 collective-permute-done.76
  785.8 4.8 collective-permute-done.75
  810.2 11.3 %collective-permute-done.87 = bf16[160,1280]{1,0:T(8,128)(2,1)S(1)} collective-permute-done((bf16[160,1280]{1,0:T(8,128)(2,1)S(1)}, bf16[160,1280]{1,0:T(8,128)(2,1)S(1)}, u32[]{:S(2)}, u32[]{:S(2)}) %collective-permute-start.87) | collective-permute-done | bytes 409632 | tf_op jit(solution)/shard_map/ppermute | solution.py:78
  821.5 9.1 %collective-permute-done.85 = bf16[160,1536]{1,0:T(8,128)(2,1)S(1)} collective-permute-done((bf16[160,1536]{1,0:T(8,128)(2,1)S(1)}, bf16[160,1536]{1,0:T(8,128)(2,1)S(1)}, u32[]{:S(2)}, u32[]{:S(2)}) %collective-permute-start.85) | collective-permute-done | bytes 491552 | tf_op jit(solution)/shard_map/ppermute | solution.py:100
  839.2 17.3 %collective-permute-done.93 = bf16[80,1280]{1,0:T(8,128)(2,1)S(1)} collective-permute-done((bf16[80,1280]{1,0:T(8,128)(2,1)S(1)}, bf16[80,1280]{1,0:T(8,128)(2,1)S(1)}, u32[]{:S(2)}, u32[]{:S(2)}) %collective-permute-start.93) | collective-permute-done | bytes 204832 | tf_op jit(solution)/shard_map/ppermute | solution.py:78
  872.8 7.6 collective-permute-done.97
  (713 shorter events, 411.1 us)
Async XLA Ops:
  7.2 348.0 %all-gather.2.cloned.1.call-start = ((), (), s32[]{:S(2)}) async-start(), calls=%async_computation.1 | async-start | bytes 19660800 | tf_op jit(solution)/shard_map/all_gather | solution.py:367
  52.6 21.1 %collective-permute-start.9 = (bf16[320,3200]{1,0:T(8,128)(2,1)S(1)}, bf16[320,3200]{1,0:T(8,128)(2,1)S(1)}, u32[]{:S(2)}, u32[]{:S(2)}) collective-permute-start(bf16[320,3200]{1,0:T(8,128)(2,1)S(1)} %slice_dynamic-update-slice_fusion.16.mine), channel_id=1, source_target_pairs={{0,1},{1,0},{2,3},{3,2},{4,5},{5,4},{6,7},{7,6},{8,9},{9,8},{10,11... | collective-permute-start | bytes 6144008 | tf_op jit(solution)/shard_map/ppermute | solution.py:78
  77.8 23.0 %collective-permute-start.12 = (bf16[320,3200]{1,0:T(8,128)(2,1)}, bf16[320,3200]{1,0:T(8,128)(2,1)}, u32[]{:S(2)}, u32[]{:S(2)}) collective-permute-start(bf16[320,3200]{1,0:T(8,128)(2,1)} %slice_dynamic-update-slice_fusion.14.mine), channel_id=1, source_target_pairs={{0,1},{1,0},{2,3},{3,2},{4,5},{5,4},{6,7},{7,6},{8,9},{9,8},{10,11... | collective-permute-start | bytes 6144008 | tf_op jit(solution)/shard_map/ppermute | solution.py:78
  79.1 20.0 %collective-permute-start.11 = (bf16[120,3200]{1,0:T(8,128)(2,1)}, bf16[120,3200]{1,0:T(8,128)(2,1)S(1)}, u32[]{:S(2)}, u32[]{:S(2)}) collective-permute-start(bf16[120,3200]{1,0:T(8,128)(2,1)} %get-tuple-element.1367), channel_id=1, source_target_pairs={{0,4},{1,5},{2,6},{3,7},{4,0},{5,1},{6,2},{7,3},{8,12},{9,13},{10,... | collective-permute-start | bytes 2304008 | tf_op jit(solution)/shard_map/ppermute | solution.py:78
  125.4 20.9 %collective-permute-start.23 = (bf16[320,3200]{1,0:T(8,128)(2,1)S(1)}, bf16[320,3200]{1,0:T(8,128)(2,1)}, u32[]{:S(2)}, u32[]{:S(2)}) collective-permute-start(bf16[320,3200]{1,0:T(8,128)(2,1)S(1)} %constant_dynamic-update-slice_fusion.5.mine), channel_id=1, source_target_pairs={{0,1},{1,0},{2,3},{3,2},{4,5},{5,4},{6,7},{7,6},{8,9},{9,8},{10,11... | collective-permute-start | bytes 6144008 | tf_op jit(solution)/shard_map/ppermute | solution.py:78
  151.3 30.7 %collective-permute-start.27 = (bf16[320,2560]{1,0:T(8,128)(2,1)S(1)}, bf16[320,2560]{1,0:T(8,128)(2,1)}, u32[]{:S(2)}, u32[]{:S(2)}) collective-permute-start(bf16[320,2560]{1,0:T(8,128)(2,1)S(1)} %slice_dynamic-update-slice_fusion.22.mine), channel_id=1, source_target_pairs={{0,1},{1,0},{2,3},{3,2},{4,5},{5,4},{6,7},{7,6},{8,9},{9,8},{10,11... | collective-permute-start | bytes 4915208 | tf_op jit(solution)/shard_map/ppermute | solution.py:78
  153.5 27.7 %collective-permute-start.28 = (bf16[128,2560]{1,0:T(8,128)(2,1)}, bf16[128,2560]{1,0:T(8,128)(2,1)}, u32[]{:S(2)}, u32[]{:S(2)}) collective-permute-start(bf16[128,2560]{1,0:T(8,128)(2,1)} %get-tuple-element.728), channel_id=1, source_target_pairs={{0,8},{1,9},{2,10},{3,11},{4,12},{5,13},{6,14},{7,15},{8,16},{9,17... | collective-permute-start | bytes 1966088 | tf_op jit(solution)/shard_map/ppermute | solution.py:100
  154.7 26.5 %collective-permute-start.26 = (bf16[120,2560]{1,0:T(8,128)(2,1)}, bf16[120,2560]{1,0:T(8,128)(2,1)}, u32[]{:S(2)}, u32[]{:S(2)}) collective-permute-start(bf16[120,2560]{1,0:T(8,128)(2,1)} %get-tuple-element.1375), channel_id=1, source_target_pairs={{0,4},{1,5},{2,6},{3,7},{4,0},{5,1},{6,2},{7,3},{8,12},{9,13},{10,... | collective-permute-start | bytes 1843208 | tf_op jit(solution)/shard_map/ppermute | solution.py:78
  155.2 26.0 %collective-permute-start.25 = (bf16[120,2560]{1,0:T(8,128)(2,1)}, bf16[120,2560]{1,0:T(8,128)(2,1)}, u32[]{:S(2)}, u32[]{:S(2)}) collective-permute-start(bf16[120,2560]{1,0:T(8,128)(2,1)} %get-tuple-element.1376), channel_id=1, source_target_pairs={{0,2},{1,3},{2,0},{3,1},{4,6},{5,7},{6,4},{7,5},{8,10},{9,11},{10,... | collective-permute-start | bytes 1843208 | tf_op jit(solution)/shard_map/ppermute | solution.py:78
  156.7 24.5 %collective-permute-start.24 = (bf16[80,2560]{1,0:T(8,128)(2,1)S(1)}, bf16[80,2560]{1,0:T(8,128)(2,1)S(1)}, u32[]{:S(2)}, u32[]{:S(2)}) collective-permute-start(bf16[80,2560]{1,0:T(8,128)(2,1)S(1)} %collective-permute-done.20), channel_id=1, source_target_pairs={{0,8},{1,9},{2,10},{3,11},{4,12},{5,13},{6,14},{7,15},{8,16},{9,17... | collective-permute-start | bytes 1228808 | tf_op jit(solution)/shard_map/ppermute | solution.py:100
  186.0 21.3 %collective-permute-start.31 = (bf16[320,2560]{1,0:T(8,128)(2,1)S(1)}, bf16[320,2560]{1,0:T(8,128)(2,1)}, u32[]{:S(2)}, u32[]{:S(2)}) collective-permute-start(bf16[320,2560]{1,0:T(8,128)(2,1)S(1)} %slice_dynamic-update-slice_fusion.20.mine), channel_id=1, source_target_pairs={{0,1},{1,0},{2,3},{3,2},{4,5},{5,4},{6,7},{7,6},{8,9},{9,8},{10,11... | collective-permute-start | bytes 4915208 | tf_op jit(solution)/shard_map/ppermute | solution.py:78
  207.3 438.0 %reduce-scatter.2.cloned.1.call-start = ((), (), s32[]{:S(2)}) async-start(), calls=%async_computation.2 | async-start | bytes 6553600 | tf_op jit(solution)/shard_map/reduce_scatter | solution.py:486
  213.0 34.2 %collective-permute-start.34 = (bf16[40,2560]{1,0:T(8,128)(2,1)}, bf16[40,2560]{1,0:T(8,128)(2,1)}, u32[]{:S(2)}, u32[]{:S(2)}) collective-permute-start(bf16[40,2560]{1,0:T(8,128)(2,1)} %slice.481), channel_id=1, source_target_pairs={{0,2},{1,3},{2,0},{3,1},{4,6},{5,7},{6,4},{7,5},{8,10},{9,11},{10,... | collective-permute-start | bytes 614408 | tf_op jit(solution)/shard_map/ppermute | solution.py:78
  213.5 33.7 %collective-permute-start.33 = (bf16[40,2560]{1,0:T(8,128)(2,1)}, bf16[40,2560]{1,0:T(8,128)(2,1)}, u32[]{:S(2)}, u32[]{:S(2)}) collective-permute-start(bf16[40,2560]{1,0:T(8,128)(2,1)} %slice.480), channel_id=1, source_target_pairs={{0,4},{1,5},{2,6},{3,7},{4,0},{5,1},{6,2},{7,3},{8,12},{9,13},{10,... | collective-permute-start | bytes 614408 | tf_op jit(solution)/shard_map/ppermute | solution.py:78
  215.1 32.2 %collective-permute-start.36 = (bf16[128,2560]{1,0:T(8,128)(2,1)}, bf16[128,2560]{1,0:T(8,128)(2,1)S(1)}, u32[]{:S(2)}, u32[]{:S(2)}) collective-permute-start(bf16[128,2560]{1,0:T(8,128)(2,1)} %collective-permute-done.28), channel_id=1, source_target_pairs={{0,8},{1,9},{2,10},{3,11},{4,12},{5,13},{6,14},{7,15},{8,16},{9,17... | collective-permute-start | bytes 1966088 | tf_op jit(solution)/shard_map/ppermute | solution.py:100
  223.2 24.1 %collective-permute-start.35 = (bf16[320,2560]{1,0:T(8,128)(2,1)}, bf16[320,2560]{1,0:T(8,128)(2,1)}, u32[]{:S(2)}, u32[]{:S(2)}) collective-permute-start(bf16[320,2560]{1,0:T(8,128)(2,1)} %slice_dynamic-update-slice_fusion.18.mine), channel_id=1, source_target_pairs={{0,1},{1,0},{2,3},{3,2},{4,5},{5,4},{6,7},{7,6},{8,9},{9,8},{10,11... | collective-permute-start | bytes 4915208 | tf_op jit(solution)/shard_map/ppermute | solution.py:78
  254.9 24.4 %collective-permute-start.37 = (bf16[320,2560]{1,0:T(8,128)(2,1)}, bf16[320,2560]{1,0:T(8,128)(2,1)}, u32[]{:S(2)}, u32[]{:S(2)}) collective-permute-start(bf16[320,2560]{1,0:T(8,128)(2,1)} %constant_dynamic-update-slice_fusion.13.mine), channel_id=1, source_target_pairs={{0,1},{1,0},{2,3},{3,2},{4,5},{5,4},{6,7},{7,6},{8,9},{9,8},{10,11... | collective-permute-start | bytes 4915208 | tf_op jit(solution)/shard_map/ppermute | solution.py:78
  279.2 19.7 %collective-permute-start.39 = (bf16[128,2560]{1,0:T(8,128)(2,1)S(1)}, bf16[128,2560]{1,0:T(8,128)(2,1)}, u32[]{:S(2)}, u32[]{:S(2)}) collective-permute-start(bf16[128,2560]{1,0:T(8,128)(2,1)S(1)} %collective-permute-done.36), channel_id=1, source_target_pairs={{0,8},{1,9},{2,10},{3,11},{4,12},{5,13},{6,14},{7,15},{8,16},{9,17... | collective-permute-start | bytes 1966088 | tf_op jit(solution)/shard_map/ppermute | solution.py:100
  303.0 33.3 %collective-permute-start.40 = (bf16[256,2560]{1,0:T(8,128)(2,1)S(1)}, bf16[256,2560]{1,0:T(8,128)(2,1)}, u32[]{:S(2)}, u32[]{:S(2)}) collective-permute-start(bf16[256,2560]{1,0:T(8,128)(2,1)S(1)} %multiply_convert_fusion), channel_id=1, source_target_pairs={{0,8},{1,9},{2,10},{3,11},{4,12},{5,13},{6,14},{7,15},{8,16},{9,17... | collective-permute-start | bytes 3932168 | tf_op jit(solution)/shard_map/ppermute | solution.py:100
  336.3 48.8 %collective-permute-start.45 = (bf16[256,2560]{1,0:T(8,128)(2,1)}, bf16[256,2560]{1,0:T(8,128)(2,1)}, u32[]{:S(2)}, u32[]{:S(2)}) collective-permute-start(bf16[256,2560]{1,0:T(8,128)(2,1)} %collective-permute-done.40), channel_id=1, source_target_pairs={{0,1},{1,0},{2,3},{3,2},{4,5},{5,4},{6,7},{7,6},{8,9},{9,8},{10,11... | collective-permute-start | bytes 3932168 | tf_op jit(solution)/shard_map/ppermute | solution.py:78
  336.3 51.6 %collective-permute-start.44 = (bf16[256,2560]{1,0:T(8,128)(2,1)}, bf16[256,2560]{1,0:T(8,128)(2,1)}, u32[]{:S(2)}, u32[]{:S(2)}) collective-permute-start(bf16[256,2560]{1,0:T(8,128)(2,1)} %collective-permute-done.40), channel_id=1, source_target_pairs={{0,8},{1,9},{2,10},{3,11},{4,12},{5,13},{6,14},{7,15},{8,16},{9,17... | collective-permute-start | bytes 3932168 | tf_op jit(solution)/shard_map/ppermute | solution.py:100
  336.7 44.7 %collective-permute-start.46 = (bf16[256,2560]{1,0:T(8,128)(2,1)}, bf16[256,2560]{1,0:T(8,128)(2,1)}, u32[]{:S(2)}, u32[]{:S(2)}) collective-permute-start(bf16[256,2560]{1,0:T(8,128)(2,1)} %pad_maximum_fusion.15), channel_id=1, source_target_pairs={{0,1},{1,0},{2,3},{3,2},{4,5},{5,4},{6,7},{7,6},{8,9},{9,8},{10,11... | collective-permute-start | bytes 3932168 | tf_op jit(solution)/shard_map/ppermute | solution.py:78
  387.9 27.3 %collective-permute-start.49 = (bf16[256,2560]{1,0:T(8,128)(2,1)}, bf16[256,2560]{1,0:T(8,128)(2,1)}, u32[]{:S(2)}, u32[]{:S(2)}) collective-permute-start(bf16[256,2560]{1,0:T(8,128)(2,1)} %collective-permute-done.44), channel_id=1, source_target_pairs={{0,1},{1,0},{2,3},{3,2},{4,5},{5,4},{6,7},{7,6},{8,9},{9,8},{10,11... | collective-permute-start | bytes 3932168 | tf_op jit(solution)/shard_map/ppermute | solution.py:78
  388.0 33.4 %collective-permute-start.48 = (bf16[256,2560]{1,0:T(8,128)(2,1)}, bf16[256,2560]{1,0:T(8,128)(2,1)S(1)}, u32[]{:S(2)}, u32[]{:S(2)}) collective-permute-start(bf16[256,2560]{1,0:T(8,128)(2,1)} %collective-permute-done.44), channel_id=1, source_target_pairs={{0,8},{1,9},{2,10},{3,11},{4,12},{5,13},{6,14},{7,15},{8,16},{9,17... | collective-permute-start | bytes 3932168 | tf_op jit(solution)/shard_map/ppermute | solution.py:100
  431.2 32.4 %collective-permute-start.55 = (bf16[256,2560]{1,0:T(8,128)(2,1)}, bf16[256,2560]{1,0:T(8,128)(2,1)}, u32[]{:S(2)}, u32[]{:S(2)}) collective-permute-start(bf16[256,2560]{1,0:T(8,128)(2,1)} %add_convert_fusion.6), channel_id=1, source_target_pairs={{0,8},{1,9},{2,10},{3,11},{4,12},{5,13},{6,14},{7,15},{8,16},{9,17... | collective-permute-start | bytes 3932168 | tf_op jit(solution)/shard_map/ppermute | solution.py:100
  473.7 31.5 %collective-permute-start.58 = (bf16[256,2560]{1,0:T(8,128)(2,1)}, bf16[256,2560]{1,0:T(8,128)(2,1)}, u32[]{:S(2)}, u32[]{:S(2)}) collective-permute-start(bf16[256,2560]{1,0:T(8,128)(2,1)} %add_convert_fusion.5), channel_id=1, source_target_pairs={{0,8},{1,9},{2,10},{3,11},{4,12},{5,13},{6,14},{7,15},{8,16},{9,17... | collective-permute-start | bytes 3932168 | tf_op jit(solution)/shard_map/ppermute | solution.py:100
  508.6 49.6 %collective-permute-start.59 = (bf16[256,2560]{1,0:T(8,128)(2,1)}, bf16[256,2560]{1,0:T(8,128)(2,1)}, u32[]{:S(2)}, u32[]{:S(2)}) collective-permute-start(bf16[256,2560]{1,0:T(8,128)(2,1)} %add_convert_fusion.4), channel_id=1, source_target_pairs={{0,8},{1,9},{2,10},{3,11},{4,12},{5,13},{6,14},{7,15},{8,16},{9,17... | collective-permute-start | bytes 3932168 | tf_op jit(solution)/shard_map/ppermute | solution.py:100
  521.9 36.4 %collective-permute-start.60 = (bf16[4,256,2560]{2,1,0:T(8,128)(2,1)}, bf16[4,256,2560]{2,1,0:T(8,128)(2,1)}, u32[]{:S(2)}, u32[]{:S(2)}) collective-permute-start(bf16[4,256,2560]{2,1,0:T(8,128)(2,1)} %bitcast.65), channel_id=1, source_target_pairs={{0,1},{1,0},{2,3},{3,2},{4,5},{5,4},{6,7},{7,6},{8,9},{9,8},{10,11... | collective-permute-start | bytes 15728648 | tf_op jit(solution)/shard_map/ppermute | solution.py:78
  569.3 32.7 %collective-permute-start.62 = (bf16[256,2560]{1,0:T(8,128)(2,1)S(1)}, bf16[256,2560]{1,0:T(8,128)(2,1)}, u32[]{:S(2)}, u32[]{:S(2)}) collective-permute-start(bf16[256,2560]{1,0:T(8,128)(2,1)S(1)} %fusion.81), channel_id=1, source_target_pairs={{0,8},{1,9},{2,10},{3,11},{4,12},{5,13},{6,14},{7,15},{8,16},{9,17... | collective-permute-start | bytes 3932168 | tf_op jit(solution)/shard_map/ppermute | solution.py:100
  606.1 39.2 %collective-permute-start.63 = (bf16[640,1280]{1,0:T(8,128)(2,1)S(1)}, bf16[640,1280]{1,0:T(8,128)(2,1)}, u32[]{:S(2)}, u32[]{:S(2)}) collective-permute-start(bf16[640,1280]{1,0:T(8,128)(2,1)S(1)} %constant_dynamic-slice_fusion.44), channel_id=1, source_target_pairs={{0,8},{1,9},{2,10},{3,11},{4,12},{5,13},{6,14},{7,15},{8,16},{9,17... | collective-permute-start | bytes 4915208 | tf_op jit(solution)/shard_map/ppermute | solution.py:100
  650.7 29.7 %collective-permute-start.64 = (bf16[256,2560]{1,0:T(8,128)(2,1)}, bf16[256,2560]{1,0:T(8,128)(2,1)}, u32[]{:S(2)}, u32[]{:S(2)}) collective-permute-start(bf16[256,2560]{1,0:T(8,128)(2,1)} %pad_maximum_fusion.18), channel_id=1, source_target_pairs={{0,2},{1,3},{2,0},{3,1},{4,6},{5,7},{6,4},{7,5},{8,10},{9,11},{10,... | collective-permute-start | bytes 3932168 | tf_op jit(solution)/shard_map/ppermute | solution.py:78
  652.3 29.3 %collective-permute-start.65 = (bf16[256,2560]{1,0:T(8,128)(2,1)}, bf16[256,2560]{1,0:T(8,128)(2,1)}, u32[]{:S(2)}, u32[]{:S(2)}) collective-permute-start(bf16[256,2560]{1,0:T(8,128)(2,1)} %pad_maximum_fusion.19), channel_id=1, source_target_pairs={{0,4},{1,5},{2,6},{3,7},{4,0},{5,1},{6,2},{7,3},{8,12},{9,13},{10,... | collective-permute-start | bytes 3932168 | tf_op jit(solution)/shard_map/ppermute | solution.py:78
  655.8 38.1 %collective-permute-start.68 = (bf16[640,1280]{1,0:T(8,128)(2,1)}, bf16[640,1280]{1,0:T(8,128)(2,1)}, u32[]{:S(2)}, u32[]{:S(2)}) collective-permute-start(bf16[640,1280]{1,0:T(8,128)(2,1)} %add_convert_fusion.2), channel_id=1, source_target_pairs={{0,8},{1,9},{2,10},{3,11},{4,12},{5,13},{6,14},{7,15},{8,16},{9,17... | collective-permute-start | bytes 4915208 | tf_op jit(solution)/shard_map/ppermute | solution.py:100
  697.5 38.4 %collective-permute-start.71 = (bf16[160,1536]{1,0:T(8,128)(2,1)}, bf16[160,1536]{1,0:T(8,128)(2,1)S(1)}, u32[]{:S(2)}, u32[]{:S(2)}) collective-permute-start(bf16[160,1536]{1,0:T(8,128)(2,1)} %pad_maximum_fusion.45), channel_id=1, source_target_pairs={{0,2},{1,3},{2,0},{3,1},{4,6},{5,7},{6,4},{7,5},{8,10},{9,11},{10,... | collective-permute-start | bytes 1474568 | tf_op jit(solution)/shard_map/ppermute | solution.py:78
  699.2 36.7 %collective-permute-start.72 = (bf16[160,1536]{1,0:T(8,128)(2,1)}, bf16[160,1536]{1,0:T(8,128)(2,1)}, u32[]{:S(2)}, u32[]{:S(2)}) collective-permute-start(bf16[160,1536]{1,0:T(8,128)(2,1)} %pad_maximum_fusion.46), channel_id=1, source_target_pairs={{0,4},{1,5},{2,6},{3,7},{4,0},{5,1},{6,2},{7,3},{8,12},{9,13},{10,... | collective-permute-start | bytes 1474568 | tf_op jit(solution)/shard_map/ppermute | solution.py:78
  708.1 36.7 %collective-permute-start.73 = (bf16[640,1280]{1,0:T(8,128)(2,1)}, bf16[640,1280]{1,0:T(8,128)(2,1)}, u32[]{:S(2)}, u32[]{:S(2)}) collective-permute-start(bf16[640,1280]{1,0:T(8,128)(2,1)} %add_convert_fusion.1), channel_id=1, source_target_pairs={{0,8},{1,9},{2,10},{3,11},{4,12},{5,13},{6,14},{7,15},{8,16},{9,17... | collective-permute-start | bytes 4915208 | tf_op jit(solution)/shard_map/ppermute | solution.py:100
  708.3 42.2 %collective-permute-start.69 = (bf16[384,2560]{1,0:T(8,128)(2,1)}, bf16[384,2560]{1,0:T(8,128)(2,1)}, u32[]{:S(2)}, u32[]{:S(2)}) collective-permute-start(bf16[384,2560]{1,0:T(8,128)(2,1)} %pad_maximum_fusion.13), channel_id=1, source_target_pairs={{0,2},{1,3},{2,0},{3,1},{4,6},{5,7},{6,4},{7,5},{8,10},{9,11},{10,... | collective-permute-start | bytes 5898248 | tf_op jit(solution)/shard_map/ppermute | solution.py:78
  709.9 41.7 %collective-permute-start.70 = (bf16[384,2560]{1,0:T(8,128)(2,1)}, bf16[384,2560]{1,0:T(8,128)(2,1)}, u32[]{:S(2)}, u32[]{:S(2)}) collective-permute-start(bf16[384,2560]{1,0:T(8,128)(2,1)} %pad_maximum_fusion.14), channel_id=1, source_target_pairs={{0,4},{1,5},{2,6},{3,7},{4,0},{5,1},{6,2},{7,3},{8,12},{9,13},{10,... | collective-permute-start | bytes 5898248 | tf_op jit(solution)/shard_map/ppermute | solution.py:78
  756.4 29.4 %collective-permute-start.78 = (bf16[240,1536]{1,0:T(8,128)(2,1)S(1)}, bf16[240,1536]{1,0:T(8,128)(2,1)S(1)}, u32[]{:S(2)}, u32[]{:S(2)}) collective-permute-start(bf16[240,1536]{1,0:T(8,128)(2,1)S(1)} %pad_maximum_fusion.33), channel_id=1, source_target_pairs={{0,2},{1,3},{2,0},{3,1},{4,6},{5,7},{6,4},{7,5},{8,10},{9,11},{10,... | collective-permute-start | bytes 2211848 | tf_op jit(solution)/shard_map/ppermute | solution.py:78
  757.1 28.7 %collective-permute-start.79 = (bf16[240,1536]{1,0:T(8,128)(2,1)S(1)}, bf16[240,1536]{1,0:T(8,128)(2,1)S(1)}, u32[]{:S(2)}, u32[]{:S(2)}) collective-permute-start(bf16[240,1536]{1,0:T(8,128)(2,1)S(1)} %pad_maximum_fusion.34), channel_id=1, source_target_pairs={{0,4},{1,5},{2,6},{3,7},{4,0},{5,1},{6,2},{7,3},{8,12},{9,13},{10,... | collective-permute-start | bytes 2211848 | tf_op jit(solution)/shard_map/ppermute | solution.py:78
  763.3 27.4 %collective-permute-start.75 = (bf16[256,2560]{1,0:T(8,128)(2,1)S(1)}, bf16[256,2560]{1,0:T(8,128)(2,1)S(1)}, u32[]{:S(2)}, u32[]{:S(2)}) collective-permute-start(bf16[256,2560]{1,0:T(8,128)(2,1)S(1)} %fusion.36), channel_id=1, source_target_pairs={{0,8},{1,9},{2,10},{3,11},{4,12},{5,13},{6,14},{7,15},{8,16},{9,17... | collective-permute-start | bytes 3932168 | tf_op jit(solution)/shard_map/ppermute | solution.py:100
  793.8 36.8 %collective-permute-start.82 = (bf16[256,2560]{1,0:T(8,128)(2,1)S(1)}, bf16[256,2560]{1,0:T(8,128)(2,1)S(1)}, u32[]{:S(2)}, u32[]{:S(2)}) collective-permute-start(bf16[256,2560]{1,0:T(8,128)(2,1)S(1)} %fusion.35), channel_id=1, source_target_pairs={{0,8},{1,9},{2,10},{3,11},{4,12},{5,13},{6,14},{7,15},{8,16},{9,17... | collective-permute-start | bytes 3932168 | tf_op jit(solution)/shard_map/ppermute | solution.py:100
  798.2 32.4 %collective-permute-start.85 = (bf16[160,1536]{1,0:T(8,128)(2,1)S(1)}, bf16[160,1536]{1,0:T(8,128)(2,1)S(1)}, u32[]{:S(2)}, u32[]{:S(2)}) collective-permute-start(bf16[160,1536]{1,0:T(8,128)(2,1)S(1)} %add_convert_fusion.13), channel_id=1, source_target_pairs={{0,8},{1,9},{2,10},{3,11},{4,12},{5,13},{6,14},{7,15},{8,16},{9,17... | collective-permute-start | bytes 1474568 | tf_op jit(solution)/shard_map/ppermute | solution.py:100
  800.5 30.1 %collective-permute-start.83 = (bf16[240,1536]{1,0:T(8,128)(2,1)S(1)}, bf16[240,1536]{1,0:T(8,128)(2,1)S(1)}, u32[]{:S(2)}, u32[]{:S(2)}) collective-permute-start(bf16[240,1536]{1,0:T(8,128)(2,1)S(1)} %pad_maximum_fusion.35), channel_id=1, source_target_pairs={{0,2},{1,3},{2,0},{3,1},{4,6},{5,7},{6,4},{7,5},{8,10},{9,11},{10,... | collective-permute-start | bytes 2211848 | tf_op jit(solution)/shard_map/ppermute | solution.py:78
  802.0 28.6 %collective-permute-start.84 = (bf16[240,1536]{1,0:T(8,128)(2,1)S(1)}, bf16[240,1536]{1,0:T(8,128)(2,1)S(1)}, u32[]{:S(2)}, u32[]{:S(2)}) collective-permute-start(bf16[240,1536]{1,0:T(8,128)(2,1)S(1)} %pad_maximum_fusion.36), channel_id=1, source_target_pairs={{0,4},{1,5},{2,6},{3,7},{4,0},{5,1},{6,2},{7,3},{8,12},{9,13},{10,... | collective-permute-start | bytes 2211848 | tf_op jit(solution)/shard_map/ppermute | solution.py:78
  832.8 23.7 %collective-permute-start.91 = (bf16[160,1536]{1,0:T(8,128)(2,1)S(1)}, bf16[160,1536]{1,0:T(8,128)(2,1)S(1)}, u32[]{:S(2)}, u32[]{:S(2)}) collective-permute-start(bf16[160,1536]{1,0:T(8,128)(2,1)S(1)} %add_convert_fusion.12), channel_id=1, source_target_pairs={{0,8},{1,9},{2,10},{3,11},{4,12},{5,13},{6,14},{7,15},{8,16},{9,17... | collective-permute-start | bytes 1474568 | tf_op jit(solution)/shard_map/ppermute | solution.py:100
  832.9 23.6 %collective-permute-start.89 = (bf16[240,1536]{1,0:T(8,128)(2,1)S(1)}, bf16[240,1536]{1,0:T(8,128)(2,1)S(1)}, u32[]{:S(2)}, u32[]{:S(2)}) collective-permute-start(bf16[240,1536]{1,0:T(8,128)(2,1)S(1)} %pad_maximum_fusion.37), channel_id=1, source_target_pairs={{0,2},{1,3},{2,0},{3,1},{4,6},{5,7},{6,4},{7,5},{8,10},{9,11},{10,... | collective-permute-start | bytes 2211848 | tf_op jit(solution)/shard_map/ppermute | solution.py:78
  833.8 22.7 %collective-permute-start.90 = (bf16[240,1536]{1,0:T(8,128)(2,1)S(1)}, bf16[240,1536]{1,0:T(8,128)(2,1)S(1)}, u32[]{:S(2)}, u32[]{:S(2)}) collective-permute-start(bf16[240,1536]{1,0:T(8,128)(2,1)S(1)} %pad_maximum_fusion.38), channel_id=1, source_target_pairs={{0,4},{1,5},{2,6},{3,7},{4,0},{5,1},{6,2},{7,3},{8,12},{9,13},{10,... | collective-permute-start | bytes 2211848 | tf_op jit(solution)/shard_map/ppermute | solution.py:78
  (182 other events, 1967.4 us)
Sparse Core Ops, SparseCore 0:
  207.4 147.6 all-gather.1
  558.5 60.8 reduce-scatter.1
